TPU v7x, 32 devices: a whole 2x2x4 slice. The times are simulated.
32 devices in a mesh: dp: 2 (over x), section: 4 (over z), seq: 4 (over y, core).
Axes of the slice: x: 2, y: 2, z: 4, core: 2. Of those that a mesh axis runs over, the one named last changes fastest.
Arguments:
- section_inputs: bfloat16 [4, 3, 2, 512, 768], P('section', None, 'dp', 'seq'), may hold values from -6 to 6
- cotangent: bfloat16 [3, 2, 512, 768], P(None, 'dp', 'seq'), may hold values from -6 to 6
- conv_weight: bfloat16 [4, 3, 768, 384], P('section'), may hold values from -0.125 to 0.125
- out_weight: bfloat16 [4, 384, 768], P('section'), may hold values from -0.3125 to 0.3125
- norm_scale: float32 [4, 768], P('section'), may hold values from 0.25 to 1.75
- norm_shift: float32 [4, 768], P('section'), may hold values from -3 to 3
- inner_scale: float32 [4, 384], P('section'), may hold values from 0.25 to 1.75
- inner_shift: float32 [4, 384], P('section'), may hold values from -3 to 3
Outputs:
- grad_in: bfloat16 [4, 3, 2, 512, 768], P('section', None, 'dp', 'seq')
- grad_conv: float32 [4, 3, 768, 384], P('section', None, 'seq')
- grad_out: float32 [4, 384, 768], P('section', None, 'seq')
All inputs are finite; a program needn't handle non-finite values.
Results may differ from a plain program's by a relative error of at most 0.025.
Values may be sent and summed in bfloat16 or wider, within the bound.
No kernel may reach another device: no remote copies, remote signals or barrier semaphores. Data moves between devices by JAX's collectives and lax.ppermute only.
A program may use at most 64 MiB of HBM per device.

v0:
```python
import jax
import jax.numpy as jnp
from jax import lax
from jax.sharding import PartitionSpec as P

BASE_DILATION = 32


gelu_coeff = 0.7978845608028654
cubic_coeff = 0.044715


def with_halo(block, sides, width):
    for axis, dim in sides:
        count = lax.axis_size(axis)
        forward = [(i, i + 1) for i in range(count - 1)]
        backward = [(target, source) for source, target in forward]
        low = lax.ppermute(
            lax.slice_in_dim(block, block.shape[dim] - width, None, axis=dim), axis, forward
        )
        high = lax.ppermute(lax.slice_in_dim(block, 0, width, axis=dim), axis, backward)
        block = jnp.concatenate([low, block, high], axis=dim)
    return block


def shifted(value, axis, by):
    length = lax.axis_size(axis)
    pairs = [(i, i + by) for i in range(length) if 0 <= i + by < length]
    return lax.ppermute(value, axis, pairs)


def gelu_pair(inputs):
    inner_arg = gelu_coeff * (inputs + cubic_coeff * inputs * inputs * inputs)
    tanh_val = jnp.tanh(inner_arg)
    result = 0.5 * inputs * (1.0 + tanh_val)
    slope_val = 0.5 * (1.0 + tanh_val) + 0.5 * inputs * (1.0 - tanh_val * tanh_val) * gelu_coeff * (
        1.0 + 3.0 * cubic_coeff * inputs * inputs
    )
    return (result, slope_val)


def put_row(buffer, update, index, is_valid):
    current = lax.dynamic_index_in_dim(buffer, index, 0, keepdims=False)
    return lax.dynamic_update_index_in_dim(buffer, jnp.where(is_valid, update, current), index, 0)


def on_device(
    section_inputs,
    cotangent,
    conv_weight,
    out_weight,
    norm_scale,
    norm_shift,
    inner_scale,
    inner_shift,
):
    sections = lax.axis_size("section")
    windows = lax.axis_size("dp")
    section_number = lax.axis_index("section")
    inputs = section_inputs[0, :, 0]
    top_grads = cotangent[:, 0]
    micro_count, row_count, channels = inputs.shape
    convolution_kernel = conv_weight[0]
    inner_width = convolution_kernel.shape[2]
    conv_flat = convolution_kernel.reshape(3 * channels, inner_width)
    out_w = out_weight[0]
    scale_one = norm_scale[0]
    shift_one = norm_shift[0]
    scale_two = inner_scale[0]
    shift_two = inner_shift[0]
    border_margin = 2 * BASE_DILATION
    dilation_rate = BASE_DILATION * (1 + section_number % 2)
    is_last = section_number == sections - 1
    tick_count = micro_count + sections - 1
    stashed = ()

    def tick(state_in, tick_num):
        received, grads_out, acc_conv, acc_out, kept = state_in
        micro_idx = tick_num - (sections - 1 - section_number)
        is_valid = jnp.logical_and(micro_idx >= 0, micro_idx < micro_count)
        safe_idx = jnp.clip(micro_idx, 0, micro_count - 1)
        block_in = lax.dynamic_index_in_dim(inputs, safe_idx, 0, keepdims=False)
        top_grad = lax.dynamic_index_in_dim(top_grads, safe_idx, 0, keepdims=False)
        grad_top = jnp.where(is_last, top_grad, received)
        pre_norm = block_in.astype(jnp.float32) * scale_one + shift_one
        act_val, act_slope = gelu_pair(pre_norm)
        hidden = act_val.astype(jnp.bfloat16)
        padded = with_halo(hidden, (("seq", 0),), border_margin)
        tap_rows = jnp.concatenate(
            [
                lax.dynamic_slice_in_dim(
                    padded, border_margin + (tap_number - 1) * dilation_rate, row_count, 0
                )
                for tap_number in range(3)
            ],
            axis=1,
        )
        inner_pre = (
            jnp.dot(tap_rows, conv_flat, preferred_element_type=jnp.float32) * scale_two + shift_two
        )
        inner_val, inner_slope = gelu_pair(inner_pre)
        inner_act = inner_val.astype(jnp.bfloat16)
        grad_inner = lax.dot_general(
            grad_top, out_w, (((1,), (1,)), ((), ())), preferred_element_type=jnp.float32
        )
        grad_conv = (grad_inner * inner_slope * scale_two).astype(jnp.bfloat16)
        grad_pad = with_halo(grad_conv, (("seq", 0),), border_margin)
        back_taps = jnp.stack(
            [
                lax.dynamic_slice_in_dim(
                    grad_pad, border_margin - (tap_number - 1) * dilation_rate, row_count, 0
                )
                for tap_number in range(3)
            ],
            axis=1,
        )
        grad_hidden = lax.dot_general(
            back_taps,
            convolution_kernel,
            (((1, 2), (0, 2)), ((), ())),
            preferred_element_type=jnp.float32,
        )
        grad_block = (grad_top.astype(jnp.float32) + grad_hidden * act_slope * scale_one).astype(
            jnp.bfloat16
        )
        handed_forward = shifted(grad_block, "section", -1)
        grads_out = put_row(grads_out, grad_block, safe_idx, is_valid)
        masked_conv = jnp.where(is_valid, grad_conv, jnp.zeros_like(grad_conv))
        masked_top = jnp.where(is_valid, grad_top, jnp.zeros_like(grad_top))
        acc_conv = acc_conv + lax.dot_general(
            tap_rows, masked_conv, (((0,), (0,)), ((), ())), preferred_element_type=jnp.float32
        )
        acc_out = acc_out + lax.dot_general(
            inner_act, masked_top, (((0,), (0,)), ((), ())), preferred_element_type=jnp.float32
        )
        return ((handed_forward, grads_out, acc_conv, acc_out, kept), None)

    starting_value = (
        jnp.zeros((row_count, channels), jnp.bfloat16),
        jnp.zeros((micro_count, row_count, channels), jnp.bfloat16),
        jnp.zeros((3 * channels, inner_width), jnp.float32),
        jnp.zeros((inner_width, channels), jnp.float32),
        stashed,
    )
    final_state, unused = lax.scan(tick, starting_value, jnp.arange(tick_count, dtype=jnp.int32))
    received, grads_out, acc_conv, acc_out, kept = final_state
    conv_part = acc_conv.reshape(3, channels, inner_width)
    shares = (
        lax.psum_scatter(
            conv_part.astype(jnp.bfloat16), "seq", scatter_dimension=1, tiled=True
        ).astype(jnp.float32),
        lax.psum_scatter(
            acc_out.astype(jnp.bfloat16), "seq", scatter_dimension=1, tiled=True
        ).astype(jnp.float32),
    )
    conv_total, out_total = (
        lax.psum(shares[0].astype(jnp.bfloat16), "dp").astype(jnp.float32),
        lax.psum(shares[1].astype(jnp.bfloat16), "dp").astype(jnp.float32),
    )
    factor = 1.0 / float(micro_count * windows)
    return (
        grads_out.reshape(section_inputs.shape),
        (conv_total * factor)[None],
        (out_total * factor)[None],
    )


def solution(mesh):
    return jax.shard_map(
        on_device,
        mesh=mesh,
        in_specs=(
            P("section", None, "dp", "seq", None),
            P(None, "dp", "seq", None),
            P("section", None, None, None),
            P("section", None, None),
            P("section", None),
            P("section", None),
            P("section", None),
            P("section", None),
        ),
        out_specs=(
            P("section", None, "dp", "seq", None),
            P("section", None, "seq", None),
            P("section", None, "seq"),
        ),
        check_vma=False,
    )
```

profile of v0, /device:TPU:0, one launch (start us, length us, event | category | flops | bytes accessed | tf_op | source)
XLA Modules:
  0.0 320.8 jit_solution(2454830737139336015)
XLA Ops:
  8.8 211.6 %while.20 = (s32[]{:T(128)}, bf16[128,768]{1,0:T(8,128)(2,1)}, bf16[3,128,768]{2,1,0:T(8,128)(2,1)}, f32[2304,384]{1,0:T(8,128)S(1)}, f32[384,768]{1,0:T(8,128)}...) while((s32[]{:T(128)}, bf16[128,768]{1,0:T(8,128)(2,1)}, ...), condition=%wide.region_1.2_spmd.clone, body=%wide.region_0.1_spmd.clone.sunk | while | flops 843939840 | bytes 44764652 | solution.py:145
  15.2 3.7 %collective-permute-start.1 = (bf16[64,768]{1,0:T(8,128)(2,1)}, bf16[64,768]{1,0:T(8,128)(2,1)}, u32[]{:S(2)}, u32[]{:S(2)}) collective-permute-start(bf16[64,768]{1,0:T(8,128)(2,1)} %get-tuple-element.581), channel_id=1, source_target_pairs={{0,1},{1,2},{2,3},{4,5},{5,6},{6,7},{8,9},{9,10},{10,11},{12,13},{... | collective-permute-start | bytes 294920 | tf_op jit(solution)/shard_map/while/body/eval_jaxpr/ppermute | solution.py:18
  26.4 4.5 %collective-permute-start.3 = (bf16[64,384]{1,0:T(8,128)(2,1)S(1)}, bf16[64,384]{1,0:T(8,128)(2,1)S(1)}, u32[]{:S(2)}, u32[]{:S(2)}) collective-permute-start(bf16[64,384]{1,0:T(8,128)(2,1)S(1)} %get-tuple-element.585), channel_id=1, source_target_pairs={{0,1},{1,2},{2,3},{4,5},{5,6},{6,7},{8,9},{9,10},{10,11},{12,13},{... | collective-permute-start | bytes 147464 | tf_op jit(solution)/shard_map/while/body/eval_jaxpr/ppermute | solution.py:18
  32.6 2.5 bitcast_dynamic-update-slice_fusion.2
  37.1 7.0 %collective-permute-done.4 = bf16[128,768]{1,0:T(8,128)(2,1)S(1)} collective-permute-done((bf16[128,768]{1,0:T(8,128)(2,1)S(1)}, bf16[128,768]{1,0:T(8,128)(2,1)S(1)}, u32[]{:S(2)}, u32[]{:S(2)}) %collective-permute-start.4) | collective-permute-done | bytes 196640 | tf_op jit(solution)/shard_map/while/body/eval_jaxpr/ppermute | solution.py:29
  51.2 3.7 %collective-permute-start.1 = (bf16[64,768]{1,0:T(8,128)(2,1)}, bf16[64,768]{1,0:T(8,128)(2,1)}, u32[]{:S(2)}, u32[]{:S(2)}) collective-permute-start(bf16[64,768]{1,0:T(8,128)(2,1)} %get-tuple-element.581), channel_id=1, source_target_pairs={{0,1},{1,2},{2,3},{4,5},{5,6},{6,7},{8,9},{9,10},{10,11},{12,13},{... | collective-permute-start | bytes 294920 | tf_op jit(solution)/shard_map/while/body/eval_jaxpr/ppermute | solution.py:18
  62.3 3.7 %collective-permute-start.3 = (bf16[64,384]{1,0:T(8,128)(2,1)S(1)}, bf16[64,384]{1,0:T(8,128)(2,1)S(1)}, u32[]{:S(2)}, u32[]{:S(2)}) collective-permute-start(bf16[64,384]{1,0:T(8,128)(2,1)S(1)} %get-tuple-element.585), channel_id=1, source_target_pairs={{0,1},{1,2},{2,3},{4,5},{5,6},{6,7},{8,9},{9,10},{10,11},{12,13},{... | collective-permute-start | bytes 147464 | tf_op jit(solution)/shard_map/while/body/eval_jaxpr/ppermute | solution.py:18
  66.0 1.7 convolution_add_fusion.4
  67.8 2.5 bitcast_dynamic-update-slice_fusion.2
  72.2 7.0 %collective-permute-done.4 = bf16[128,768]{1,0:T(8,128)(2,1)S(1)} collective-permute-done((bf16[128,768]{1,0:T(8,128)(2,1)S(1)}, bf16[128,768]{1,0:T(8,128)(2,1)S(1)}, u32[]{:S(2)}, u32[]{:S(2)}) %collective-permute-start.4) | collective-permute-done | bytes 196640 | tf_op jit(solution)/shard_map/while/body/eval_jaxpr/ppermute | solution.py:29
  86.3 3.7 %collective-permute-start.1 = (bf16[64,768]{1,0:T(8,128)(2,1)}, bf16[64,768]{1,0:T(8,128)(2,1)}, u32[]{:S(2)}, u32[]{:S(2)}) collective-permute-start(bf16[64,768]{1,0:T(8,128)(2,1)} %get-tuple-element.581), channel_id=1, source_target_pairs={{0,1},{1,2},{2,3},{4,5},{5,6},{6,7},{8,9},{9,10},{10,11},{12,13},{... | collective-permute-start | bytes 294920 | tf_op jit(solution)/shard_map/while/body/eval_jaxpr/ppermute | solution.py:18
  97.5 3.7 %collective-permute-start.3 = (bf16[64,384]{1,0:T(8,128)(2,1)S(1)}, bf16[64,384]{1,0:T(8,128)(2,1)S(1)}, u32[]{:S(2)}, u32[]{:S(2)}) collective-permute-start(bf16[64,384]{1,0:T(8,128)(2,1)S(1)} %get-tuple-element.585), channel_id=1, source_target_pairs={{0,1},{1,2},{2,3},{4,5},{5,6},{6,7},{8,9},{9,10},{10,11},{12,13},{... | collective-permute-start | bytes 147464 | tf_op jit(solution)/shard_map/while/body/eval_jaxpr/ppermute | solution.py:18
  101.2 1.7 convolution_add_fusion.4
  102.9 2.5 bitcast_dynamic-update-slice_fusion.2
  107.4 7.0 %collective-permute-done.4 = bf16[128,768]{1,0:T(8,128)(2,1)S(1)} collective-permute-done((bf16[128,768]{1,0:T(8,128)(2,1)S(1)}, bf16[128,768]{1,0:T(8,128)(2,1)S(1)}, u32[]{:S(2)}, u32[]{:S(2)}) %collective-permute-start.4) | collective-permute-done | bytes 196640 | tf_op jit(solution)/shard_map/while/body/eval_jaxpr/ppermute | solution.py:29
  121.5 3.7 %collective-permute-start.1 = (bf16[64,768]{1,0:T(8,128)(2,1)}, bf16[64,768]{1,0:T(8,128)(2,1)}, u32[]{:S(2)}, u32[]{:S(2)}) collective-permute-start(bf16[64,768]{1,0:T(8,128)(2,1)} %get-tuple-element.581), channel_id=1, source_target_pairs={{0,1},{1,2},{2,3},{4,5},{5,6},{6,7},{8,9},{9,10},{10,11},{12,13},{... | collective-permute-start | bytes 294920 | tf_op jit(solution)/shard_map/while/body/eval_jaxpr/ppermute | solution.py:18
  132.6 3.7 %collective-permute-start.3 = (bf16[64,384]{1,0:T(8,128)(2,1)S(1)}, bf16[64,384]{1,0:T(8,128)(2,1)S(1)}, u32[]{:S(2)}, u32[]{:S(2)}) collective-permute-start(bf16[64,384]{1,0:T(8,128)(2,1)S(1)} %get-tuple-element.585), channel_id=1, source_target_pairs={{0,1},{1,2},{2,3},{4,5},{5,6},{6,7},{8,9},{9,10},{10,11},{12,13},{... | collective-permute-start | bytes 147464 | tf_op jit(solution)/shard_map/while/body/eval_jaxpr/ppermute | solution.py:18
  138.1 2.5 bitcast_dynamic-update-slice_fusion.2
  142.5 7.0 %collective-permute-done.4 = bf16[128,768]{1,0:T(8,128)(2,1)S(1)} collective-permute-done((bf16[128,768]{1,0:T(8,128)(2,1)S(1)}, bf16[128,768]{1,0:T(8,128)(2,1)S(1)}, u32[]{:S(2)}, u32[]{:S(2)}) %collective-permute-start.4) | collective-permute-done | bytes 196640 | tf_op jit(solution)/shard_map/while/body/eval_jaxpr/ppermute | solution.py:29
  156.6 3.7 %collective-permute-start.1 = (bf16[64,768]{1,0:T(8,128)(2,1)}, bf16[64,768]{1,0:T(8,128)(2,1)}, u32[]{:S(2)}, u32[]{:S(2)}) collective-permute-start(bf16[64,768]{1,0:T(8,128)(2,1)} %get-tuple-element.581), channel_id=1, source_target_pairs={{0,1},{1,2},{2,3},{4,5},{5,6},{6,7},{8,9},{9,10},{10,11},{12,13},{... | collective-permute-start | bytes 294920 | tf_op jit(solution)/shard_map/while/body/eval_jaxpr/ppermute | solution.py:18
  167.8 3.7 %collective-permute-start.3 = (bf16[64,384]{1,0:T(8,128)(2,1)S(1)}, bf16[64,384]{1,0:T(8,128)(2,1)S(1)}, u32[]{:S(2)}, u32[]{:S(2)}) collective-permute-start(bf16[64,384]{1,0:T(8,128)(2,1)S(1)} %get-tuple-element.585), channel_id=1, source_target_pairs={{0,1},{1,2},{2,3},{4,5},{5,6},{6,7},{8,9},{9,10},{10,11},{12,13},{... | collective-permute-start | bytes 147464 | tf_op jit(solution)/shard_map/while/body/eval_jaxpr/ppermute | solution.py:18
  173.2 2.5 bitcast_dynamic-update-slice_fusion.2
  177.6 7.0 %collective-permute-done.4 = bf16[128,768]{1,0:T(8,128)(2,1)S(1)} collective-permute-done((bf16[128,768]{1,0:T(8,128)(2,1)S(1)}, bf16[128,768]{1,0:T(8,128)(2,1)S(1)}, u32[]{:S(2)}, u32[]{:S(2)}) %collective-permute-start.4) | collective-permute-done | bytes 196640 | tf_op jit(solution)/shard_map/while/body/eval_jaxpr/ppermute | solution.py:29
  191.7 3.7 %collective-permute-start.1 = (bf16[64,768]{1,0:T(8,128)(2,1)}, bf16[64,768]{1,0:T(8,128)(2,1)}, u32[]{:S(2)}, u32[]{:S(2)}) collective-permute-start(bf16[64,768]{1,0:T(8,128)(2,1)} %get-tuple-element.581), channel_id=1, source_target_pairs={{0,1},{1,2},{2,3},{4,5},{5,6},{6,7},{8,9},{9,10},{10,11},{12,13},{... | collective-permute-start | bytes 294920 | tf_op jit(solution)/shard_map/while/body/eval_jaxpr/ppermute | solution.py:18
  202.9 3.7 %collective-permute-start.3 = (bf16[64,384]{1,0:T(8,128)(2,1)S(1)}, bf16[64,384]{1,0:T(8,128)(2,1)S(1)}, u32[]{:S(2)}, u32[]{:S(2)}) collective-permute-start(bf16[64,384]{1,0:T(8,128)(2,1)S(1)} %get-tuple-element.585), channel_id=1, source_target_pairs={{0,1},{1,2},{2,3},{4,5},{5,6},{6,7},{8,9},{9,10},{10,11},{12,13},{... | collective-permute-start | bytes 147464 | tf_op jit(solution)/shard_map/while/body/eval_jaxpr/ppermute | solution.py:18
  208.3 2.5 bitcast_dynamic-update-slice_fusion.2
  212.8 7.0 %collective-permute-done.4 = bf16[128,768]{1,0:T(8,128)(2,1)S(1)} collective-permute-done((bf16[128,768]{1,0:T(8,128)(2,1)S(1)}, bf16[128,768]{1,0:T(8,128)(2,1)S(1)}, u32[]{:S(2)}, u32[]{:S(2)}) %collective-permute-start.4) | collective-permute-done | bytes 196640 | tf_op jit(solution)/shard_map/while/body/eval_jaxpr/ppermute | solution.py:29
  220.5 2.3 copy.11
  224.3 21.4 %reduce-scatter.5.cloned.1.call-done = bf16[384,192]{0,1:T(8,128)(2,1)} async-done(((bf16[384,768]{0,1:T(8,128)(2,1)}), bf16[384,192]{0,1:T(8,128)(2,1)}) %reduce-scatter.5.cloned.1.call-update) | async-done | bytes 147472 | tf_op jit(solution)/shard_map/reduce_scatter | solution.py:152
  245.8 32.0 %reduce-scatter.3.cloned.1.call-done = bf16[3,192,384]{2,1,0:T(8,128)(2,1)} async-done(((bf16[3,768,384]{2,1,0:T(8,128)(2,1)}), bf16[3,192,384]{2,1,0:T(8,128)(2,1)}) %reduce-scatter.3.cloned.1.call-update) | async-done | bytes 442384 | tf_op jit(solution)/shard_map/reduce_scatter | solution.py:149
  277.8 32.8 %all-reduce.3.cloned.1.call-done = (bf16[3,192,384]{2,1,0:T(8,128)(2,1)}, bf16[384,192]{0,1:T(8,128)(2,1)}) async-done(((bf16[3,192,384]{2,1,0:T(8,128)(2,1)}, bf16[384,192]{0,1:T(8,128)(2,1)}), (bf16[3,192,384]{2,1,0:T(8,128)(2,1)}, bf16[384,192]{0,1:T(8,128)(2,1)})) %all-reduce.3.cloned.1.call-update) | async-done | bytes 589840 | tf_op jit(solution)/shard_map/psum | solution.py:157
  312.2 2.0 multiply_bitcast_fusion
  (269 shorter events, 105.7 us)
Async XLA Ops:
  7.2 238.6 %reduce-scatter.5.cloned.1.call-start = ((), (), s32[]{:S(2)}) async-start(), calls=%async_computation.3 | async-start | bytes 737280 | tf_op jit(solution)/shard_map/reduce_scatter | solution.py:152
  14.0 8.5 %collective-permute-start = (bf16[64,768]{1,0:T(8,128)(2,1)}, bf16[64,768]{1,0:T(8,128)(2,1)}, u32[]{:S(2)}, u32[]{:S(2)}) collective-permute-start(bf16[64,768]{1,0:T(8,128)(2,1)} %get-tuple-element.580), channel_id=1, source_target_pairs={{1,0},{2,1},{3,2},{5,4},{6,5},{7,6},{9,8},{10,9},{11,10},{13,12},{... | collective-permute-start | bytes 294920 | tf_op jit(solution)/shard_map/while/body/eval_jaxpr/ppermute | solution.py:21
  15.2 7.3 %collective-permute-start.1 = (bf16[64,768]{1,0:T(8,128)(2,1)}, bf16[64,768]{1,0:T(8,128)(2,1)}, u32[]{:S(2)}, u32[]{:S(2)}) collective-permute-start(bf16[64,768]{1,0:T(8,128)(2,1)} %get-tuple-element.581), channel_id=1, source_target_pairs={{0,1},{1,2},{2,3},{4,5},{5,6},{6,7},{8,9},{9,10},{10,11},{12,13},{... | collective-permute-start | bytes 294920 | tf_op jit(solution)/shard_map/while/body/eval_jaxpr/ppermute | solution.py:18
  25.1 7.5 %collective-permute-start.2 = (bf16[64,384]{1,0:T(8,128)(2,1)S(1)}, bf16[64,384]{1,0:T(8,128)(2,1)S(1)}, u32[]{:S(2)}, u32[]{:S(2)}) collective-permute-start(bf16[64,384]{1,0:T(8,128)(2,1)S(1)} %get-tuple-element.584), channel_id=1, source_target_pairs={{1,0},{2,1},{3,2},{5,4},{6,5},{7,6},{9,8},{10,9},{11,10},{13,12},{... | collective-permute-start | bytes 147464 | tf_op jit(solution)/shard_map/while/body/eval_jaxpr/ppermute | solution.py:21
  26.4 6.2 %collective-permute-start.3 = (bf16[64,384]{1,0:T(8,128)(2,1)S(1)}, bf16[64,384]{1,0:T(8,128)(2,1)S(1)}, u32[]{:S(2)}, u32[]{:S(2)}) collective-permute-start(bf16[64,384]{1,0:T(8,128)(2,1)S(1)} %get-tuple-element.585), channel_id=1, source_target_pairs={{0,1},{1,2},{2,3},{4,5},{5,6},{6,7},{8,9},{9,10},{10,11},{12,13},{... | collective-permute-start | bytes 147464 | tf_op jit(solution)/shard_map/while/body/eval_jaxpr/ppermute | solution.py:18
  35.1 8.9 %collective-permute-start.4 = (bf16[128,768]{1,0:T(8,128)(2,1)S(1)}, bf16[128,768]{1,0:T(8,128)(2,1)S(1)}, u32[]{:S(2)}, u32[]{:S(2)}) collective-permute-start(bf16[128,768]{1,0:T(8,128)(2,1)S(1)} %get-tuple-element.588), channel_id=1, source_target_pairs={{4,0},{8,4},{12,8},{5,1},{9,5},{13,9},{6,2},{10,6},{14,10},{7,3},{... | collective-permute-start | bytes 589832 | tf_op jit(solution)/shard_map/while/body/eval_jaxpr/ppermute | solution.py:29
  49.9 8.6 %collective-permute-start = (bf16[64,768]{1,0:T(8,128)(2,1)}, bf16[64,768]{1,0:T(8,128)(2,1)}, u32[]{:S(2)}, u32[]{:S(2)}) collective-permute-start(bf16[64,768]{1,0:T(8,128)(2,1)} %get-tuple-element.580), channel_id=1, source_target_pairs={{1,0},{2,1},{3,2},{5,4},{6,5},{7,6},{9,8},{10,9},{11,10},{13,12},{... | collective-permute-start | bytes 294920 | tf_op jit(solution)/shard_map/while/body/eval_jaxpr/ppermute | solution.py:21
  51.2 7.3 %collective-permute-start.1 = (bf16[64,768]{1,0:T(8,128)(2,1)}, bf16[64,768]{1,0:T(8,128)(2,1)}, u32[]{:S(2)}, u32[]{:S(2)}) collective-permute-start(bf16[64,768]{1,0:T(8,128)(2,1)} %get-tuple-element.581), channel_id=1, source_target_pairs={{0,1},{1,2},{2,3},{4,5},{5,6},{6,7},{8,9},{9,10},{10,11},{12,13},{... | collective-permute-start | bytes 294920 | tf_op jit(solution)/shard_map/while/body/eval_jaxpr/ppermute | solution.py:18
  61.0 6.6 %collective-permute-start.2 = (bf16[64,384]{1,0:T(8,128)(2,1)S(1)}, bf16[64,384]{1,0:T(8,128)(2,1)S(1)}, u32[]{:S(2)}, u32[]{:S(2)}) collective-permute-start(bf16[64,384]{1,0:T(8,128)(2,1)S(1)} %get-tuple-element.584), channel_id=1, source_target_pairs={{1,0},{2,1},{3,2},{5,4},{6,5},{7,6},{9,8},{10,9},{11,10},{13,12},{... | collective-permute-start | bytes 147464 | tf_op jit(solution)/shard_map/while/body/eval_jaxpr/ppermute | solution.py:21
  70.3 8.9 %collective-permute-start.4 = (bf16[128,768]{1,0:T(8,128)(2,1)S(1)}, bf16[128,768]{1,0:T(8,128)(2,1)S(1)}, u32[]{:S(2)}, u32[]{:S(2)}) collective-permute-start(bf16[128,768]{1,0:T(8,128)(2,1)S(1)} %get-tuple-element.588), channel_id=1, source_target_pairs={{4,0},{8,4},{12,8},{5,1},{9,5},{13,9},{6,2},{10,6},{14,10},{7,3},{... | collective-permute-start | bytes 589832 | tf_op jit(solution)/shard_map/while/body/eval_jaxpr/ppermute | solution.py:29
  85.0 8.6 %collective-permute-start = (bf16[64,768]{1,0:T(8,128)(2,1)}, bf16[64,768]{1,0:T(8,128)(2,1)}, u32[]{:S(2)}, u32[]{:S(2)}) collective-permute-start(bf16[64,768]{1,0:T(8,128)(2,1)} %get-tuple-element.580), channel_id=1, source_target_pairs={{1,0},{2,1},{3,2},{5,4},{6,5},{7,6},{9,8},{10,9},{11,10},{13,12},{... | collective-permute-start | bytes 294920 | tf_op jit(solution)/shard_map/while/body/eval_jaxpr/ppermute | solution.py:21
  86.3 7.3 %collective-permute-start.1 = (bf16[64,768]{1,0:T(8,128)(2,1)}, bf16[64,768]{1,0:T(8,128)(2,1)}, u32[]{:S(2)}, u32[]{:S(2)}) collective-permute-start(bf16[64,768]{1,0:T(8,128)(2,1)} %get-tuple-element.581), channel_id=1, source_target_pairs={{0,1},{1,2},{2,3},{4,5},{5,6},{6,7},{8,9},{9,10},{10,11},{12,13},{... | collective-permute-start | bytes 294920 | tf_op jit(solution)/shard_map/while/body/eval_jaxpr/ppermute | solution.py:18
  96.2 6.6 %collective-permute-start.2 = (bf16[64,384]{1,0:T(8,128)(2,1)S(1)}, bf16[64,384]{1,0:T(8,128)(2,1)S(1)}, u32[]{:S(2)}, u32[]{:S(2)}) collective-permute-start(bf16[64,384]{1,0:T(8,128)(2,1)S(1)} %get-tuple-element.584), channel_id=1, source_target_pairs={{1,0},{2,1},{3,2},{5,4},{6,5},{7,6},{9,8},{10,9},{11,10},{13,12},{... | collective-permute-start | bytes 147464 | tf_op jit(solution)/shard_map/while/body/eval_jaxpr/ppermute | solution.py:21
  97.5 5.3 %collective-permute-start.3 = (bf16[64,384]{1,0:T(8,128)(2,1)S(1)}, bf16[64,384]{1,0:T(8,128)(2,1)S(1)}, u32[]{:S(2)}, u32[]{:S(2)}) collective-permute-start(bf16[64,384]{1,0:T(8,128)(2,1)S(1)} %get-tuple-element.585), channel_id=1, source_target_pairs={{0,1},{1,2},{2,3},{4,5},{5,6},{6,7},{8,9},{9,10},{10,11},{12,13},{... | collective-permute-start | bytes 147464 | tf_op jit(solution)/shard_map/while/body/eval_jaxpr/ppermute | solution.py:18
  105.4 8.9 %collective-permute-start.4 = (bf16[128,768]{1,0:T(8,128)(2,1)S(1)}, bf16[128,768]{1,0:T(8,128)(2,1)S(1)}, u32[]{:S(2)}, u32[]{:S(2)}) collective-permute-start(bf16[128,768]{1,0:T(8,128)(2,1)S(1)} %get-tuple-element.588), channel_id=1, source_target_pairs={{4,0},{8,4},{12,8},{5,1},{9,5},{13,9},{6,2},{10,6},{14,10},{7,3},{... | collective-permute-start | bytes 589832 | tf_op jit(solution)/shard_map/while/body/eval_jaxpr/ppermute | solution.py:29
  120.2 8.6 %collective-permute-start = (bf16[64,768]{1,0:T(8,128)(2,1)}, bf16[64,768]{1,0:T(8,128)(2,1)}, u32[]{:S(2)}, u32[]{:S(2)}) collective-permute-start(bf16[64,768]{1,0:T(8,128)(2,1)} %get-tuple-element.580), channel_id=1, source_target_pairs={{1,0},{2,1},{3,2},{5,4},{6,5},{7,6},{9,8},{10,9},{11,10},{13,12},{... | collective-permute-start | bytes 294920 | tf_op jit(solution)/shard_map/while/body/eval_jaxpr/ppermute | solution.py:21
  121.5 7.3 %collective-permute-start.1 = (bf16[64,768]{1,0:T(8,128)(2,1)}, bf16[64,768]{1,0:T(8,128)(2,1)}, u32[]{:S(2)}, u32[]{:S(2)}) collective-permute-start(bf16[64,768]{1,0:T(8,128)(2,1)} %get-tuple-element.581), channel_id=1, source_target_pairs={{0,1},{1,2},{2,3},{4,5},{5,6},{6,7},{8,9},{9,10},{10,11},{12,13},{... | collective-permute-start | bytes 294920 | tf_op jit(solution)/shard_map/while/body/eval_jaxpr/ppermute | solution.py:18
  131.3 6.6 %collective-permute-start.2 = (bf16[64,384]{1,0:T(8,128)(2,1)S(1)}, bf16[64,384]{1,0:T(8,128)(2,1)S(1)}, u32[]{:S(2)}, u32[]{:S(2)}) collective-permute-start(bf16[64,384]{1,0:T(8,128)(2,1)S(1)} %get-tuple-element.584), channel_id=1, source_target_pairs={{1,0},{2,1},{3,2},{5,4},{6,5},{7,6},{9,8},{10,9},{11,10},{13,12},{... | collective-permute-start | bytes 147464 | tf_op jit(solution)/shard_map/while/body/eval_jaxpr/ppermute | solution.py:21
  132.6 5.3 %collective-permute-start.3 = (bf16[64,384]{1,0:T(8,128)(2,1)S(1)}, bf16[64,384]{1,0:T(8,128)(2,1)S(1)}, u32[]{:S(2)}, u32[]{:S(2)}) collective-permute-start(bf16[64,384]{1,0:T(8,128)(2,1)S(1)} %get-tuple-element.585), channel_id=1, source_target_pairs={{0,1},{1,2},{2,3},{4,5},{5,6},{6,7},{8,9},{9,10},{10,11},{12,13},{... | collective-permute-start | bytes 147464 | tf_op jit(solution)/shard_map/while/body/eval_jaxpr/ppermute | solution.py:18
  140.6 8.9 %collective-permute-start.4 = (bf16[128,768]{1,0:T(8,128)(2,1)S(1)}, bf16[128,768]{1,0:T(8,128)(2,1)S(1)}, u32[]{:S(2)}, u32[]{:S(2)}) collective-permute-start(bf16[128,768]{1,0:T(8,128)(2,1)S(1)} %get-tuple-element.588), channel_id=1, source_target_pairs={{4,0},{8,4},{12,8},{5,1},{9,5},{13,9},{6,2},{10,6},{14,10},{7,3},{... | collective-permute-start | bytes 589832 | tf_op jit(solution)/shard_map/while/body/eval_jaxpr/ppermute | solution.py:29
  155.3 8.6 %collective-permute-start = (bf16[64,768]{1,0:T(8,128)(2,1)}, bf16[64,768]{1,0:T(8,128)(2,1)}, u32[]{:S(2)}, u32[]{:S(2)}) collective-permute-start(bf16[64,768]{1,0:T(8,128)(2,1)} %get-tuple-element.580), channel_id=1, source_target_pairs={{1,0},{2,1},{3,2},{5,4},{6,5},{7,6},{9,8},{10,9},{11,10},{13,12},{... | collective-permute-start | bytes 294920 | tf_op jit(solution)/shard_map/while/body/eval_jaxpr/ppermute | solution.py:21
  156.6 7.3 %collective-permute-start.1 = (bf16[64,768]{1,0:T(8,128)(2,1)}, bf16[64,768]{1,0:T(8,128)(2,1)}, u32[]{:S(2)}, u32[]{:S(2)}) collective-permute-start(bf16[64,768]{1,0:T(8,128)(2,1)} %get-tuple-element.581), channel_id=1, source_target_pairs={{0,1},{1,2},{2,3},{4,5},{5,6},{6,7},{8,9},{9,10},{10,11},{12,13},{... | collective-permute-start | bytes 294920 | tf_op jit(solution)/shard_map/while/body/eval_jaxpr/ppermute | solution.py:18
  166.5 6.6 %collective-permute-start.2 = (bf16[64,384]{1,0:T(8,128)(2,1)S(1)}, bf16[64,384]{1,0:T(8,128)(2,1)S(1)}, u32[]{:S(2)}, u32[]{:S(2)}) collective-permute-start(bf16[64,384]{1,0:T(8,128)(2,1)S(1)} %get-tuple-element.584), channel_id=1, source_target_pairs={{1,0},{2,1},{3,2},{5,4},{6,5},{7,6},{9,8},{10,9},{11,10},{13,12},{... | collective-permute-start | bytes 147464 | tf_op jit(solution)/shard_map/while/body/eval_jaxpr/ppermute | solution.py:21
  167.8 5.3 %collective-permute-start.3 = (bf16[64,384]{1,0:T(8,128)(2,1)S(1)}, bf16[64,384]{1,0:T(8,128)(2,1)S(1)}, u32[]{:S(2)}, u32[]{:S(2)}) collective-permute-start(bf16[64,384]{1,0:T(8,128)(2,1)S(1)} %get-tuple-element.585), channel_id=1, source_target_pairs={{0,1},{1,2},{2,3},{4,5},{5,6},{6,7},{8,9},{9,10},{10,11},{12,13},{... | collective-permute-start | bytes 147464 | tf_op jit(solution)/shard_map/while/body/eval_jaxpr/ppermute | solution.py:18
  175.7 8.9 %collective-permute-start.4 = (bf16[128,768]{1,0:T(8,128)(2,1)S(1)}, bf16[128,768]{1,0:T(8,128)(2,1)S(1)}, u32[]{:S(2)}, u32[]{:S(2)}) collective-permute-start(bf16[128,768]{1,0:T(8,128)(2,1)S(1)} %get-tuple-element.588), channel_id=1, source_target_pairs={{4,0},{8,4},{12,8},{5,1},{9,5},{13,9},{6,2},{10,6},{14,10},{7,3},{... | collective-permute-start | bytes 589832 | tf_op jit(solution)/shard_map/while/body/eval_jaxpr/ppermute | solution.py:29
  190.4 8.6 %collective-permute-start = (bf16[64,768]{1,0:T(8,128)(2,1)}, bf16[64,768]{1,0:T(8,128)(2,1)}, u32[]{:S(2)}, u32[]{:S(2)}) collective-permute-start(bf16[64,768]{1,0:T(8,128)(2,1)} %get-tuple-element.580), channel_id=1, source_target_pairs={{1,0},{2,1},{3,2},{5,4},{6,5},{7,6},{9,8},{10,9},{11,10},{13,12},{... | collective-permute-start | bytes 294920 | tf_op jit(solution)/shard_map/while/body/eval_jaxpr/ppermute | solution.py:21
  191.7 7.3 %collective-permute-start.1 = (bf16[64,768]{1,0:T(8,128)(2,1)}, bf16[64,768]{1,0:T(8,128)(2,1)}, u32[]{:S(2)}, u32[]{:S(2)}) collective-permute-start(bf16[64,768]{1,0:T(8,128)(2,1)} %get-tuple-element.581), channel_id=1, source_target_pairs={{0,1},{1,2},{2,3},{4,5},{5,6},{6,7},{8,9},{9,10},{10,11},{12,13},{... | collective-permute-start | bytes 294920 | tf_op jit(solution)/shard_map/while/body/eval_jaxpr/ppermute | solution.py:18
  201.6 6.6 %collective-permute-start.2 = (bf16[64,384]{1,0:T(8,128)(2,1)S(1)}, bf16[64,384]{1,0:T(8,128)(2,1)S(1)}, u32[]{:S(2)}, u32[]{:S(2)}) collective-permute-start(bf16[64,384]{1,0:T(8,128)(2,1)S(1)} %get-tuple-element.584), channel_id=1, source_target_pairs={{1,0},{2,1},{3,2},{5,4},{6,5},{7,6},{9,8},{10,9},{11,10},{13,12},{... | collective-permute-start | bytes 147464 | tf_op jit(solution)/shard_map/while/body/eval_jaxpr/ppermute | solution.py:21
  202.9 5.3 %collective-permute-start.3 = (bf16[64,384]{1,0:T(8,128)(2,1)S(1)}, bf16[64,384]{1,0:T(8,128)(2,1)S(1)}, u32[]{:S(2)}, u32[]{:S(2)}) collective-permute-start(bf16[64,384]{1,0:T(8,128)(2,1)S(1)} %get-tuple-element.585), channel_id=1, source_target_pairs={{0,1},{1,2},{2,3},{4,5},{5,6},{6,7},{8,9},{9,10},{10,11},{12,13},{... | collective-permute-start | bytes 147464 | tf_op jit(solution)/shard_map/while/body/eval_jaxpr/ppermute | solution.py:18
  210.8 8.9 %collective-permute-start.4 = (bf16[128,768]{1,0:T(8,128)(2,1)S(1)}, bf16[128,768]{1,0:T(8,128)(2,1)S(1)}, u32[]{:S(2)}, u32[]{:S(2)}) collective-permute-start(bf16[128,768]{1,0:T(8,128)(2,1)S(1)} %get-tuple-element.588), channel_id=1, source_target_pairs={{4,0},{8,4},{12,8},{5,1},{9,5},{13,9},{6,2},{10,6},{14,10},{7,3},{... | collective-permute-start | bytes 589832 | tf_op jit(solution)/shard_map/while/body/eval_jaxpr/ppermute | solution.py:29
  222.8 55.0 %reduce-scatter.3.cloned.1.call-start = ((), (), s32[]{:S(2)}) async-start(), calls=%async_computation.2 | async-start | bytes 2211840 | tf_op jit(solution)/shard_map/reduce_scatter | solution.py:149
  224.3 86.3 %all-reduce.3.cloned.1.call-start = ((), (), s32[]{:S(2)}) async-start(), calls=%async_computation.4 | async-start | bytes 1179648 | tf_op jit(solution)/shard_map/psum | solution.py:157
  (55 other events, 235.0 us)
Sparse Core Ops, SparseCore 0:
  222.9 22.8 reduce-scatter.4
  248.4 29.3 reduce-scatter.2
  280.4 30.1 all-reduce.2
where the time goes:
time: 323 us; the launch traced here: 321 us
  waiting for transfers between devices  128 us (40%)
  starting transfers between devices  68.4 us (21%)
  other arithmetic  42.1 us (13%)
  matrix products  33.5 us (10%)
  local copies, waits for them, and re-layouts  29.4 us (9%)
  between operations  13.8 us (4%)
  loops' own time  5.31 us (2%)
    ppermute x12, starting transfers between devices, with_halo(): lax.ppermute(lax.slice_in_dim(block, block.shape[dim] - width, None, axis...  45.2 us
    ppermute x6, waiting for transfers between devices, shifted(): return lax.ppermute(value, axis, pairs)  41.9 us
    psum x1, waiting for transfers between devices, on_device(): lax.psum(shares[0].astype(jnp.bfloat16), 'dp').astype(jnp.float32)  32.8 us
    reduce_scatter x1, waiting for transfers between devices, on_device(): lax.psum_scatter(conv_part.astype(jnp.bfloat16), 'seq', scatter_dimension...  32 us
    reduce_scatter x1, waiting for transfers between devices, on_device(): lax.psum_scatter(acc_out.astype(jnp.bfloat16), 'seq', scatter_dimension=1...  21.4 us
    ppermute x12, starting transfers between devices, with_halo(): lax.ppermute(lax.slice_in_dim(block, 0, width, axis=dim), axis, backward)  15.4 us
    dot_general x6, matrix products, tick(): lax.dot_general(back_taps, convolution_kernel, (((1, 2), (0, 2)), ((), ()...  15 us
    while x108, local copies, waits for them, and re-layouts  11.7 us
  transfers between devices with their start and end apart: 33, of which 9 were waited for; matrix products, arithmetic and copies ran while one was open for 11% of the time, Pallas kernels for 0%

commit v1 on v0

v1 whole, which is shorter than its diff:
```python
import jax
import jax.numpy as jnp
from jax import lax
from jax.sharding import PartitionSpec as P

BASE_DILATION = 32
LAG = 2


gelu_coeff = 0.7978845608028654
cubic_coeff = 0.044715


def gelu_pair(inputs):
    squared = inputs * inputs
    inner_arg = gelu_coeff * (inputs + cubic_coeff * inputs * squared)
    tanh_val = jnp.tanh(inner_arg)
    result = 0.5 * inputs * (1.0 + tanh_val)
    slope_val = 0.5 * (1.0 + tanh_val) + 0.5 * inputs * (1.0 - tanh_val * tanh_val) * gelu_coeff * (
        1.0 + 3.0 * cubic_coeff * squared
    )
    return (result, slope_val)


def seq_swap(value, bit):
    count = lax.axis_size("seq")
    return lax.ppermute(value, "seq", [(i, i ^ bit) for i in range(count)])


def dp_swap(value):
    return lax.ppermute(value, "dp", [(0, 1), (1, 0)])


def pick(value, index, axis):
    return lax.dynamic_index_in_dim(value, index, axis, keepdims=False)


def exchange(value, number):
    count = lax.axis_size("seq")
    bit = 1
    while bit < count:
        batch, source, inner, target, rest, channels = value.shape
        split = value.reshape(batch, source, inner, target // 2, 2, rest, channels)
        mine = (number // bit) % 2
        keep = pick(split, mine, 4)
        come = seq_swap(pick(split, 1 - mine, 4), bit)
        first = jnp.where(mine == 0, keep, come)
        second = jnp.where(mine == 0, come, keep)
        value = jnp.stack([first, second], axis=1).reshape(
            batch, 2 * source, inner, target // 2, rest, channels
        )
        bit *= 2
    return value[:, :, :, 0]


def to_residues(value, number):
    batch, rows, channels = value.shape
    count = lax.axis_size("seq")
    value = value.reshape(batch, 1, rows // BASE_DILATION, count, BASE_DILATION // count, channels)
    return exchange(value, number).reshape(batch, rows, channels)


def from_residues(value, number):
    batch, rows, channels = value.shape
    count = lax.axis_size("seq")
    own = BASE_DILATION // count
    inner = rows // BASE_DILATION
    value = value.reshape(batch, 1, count, inner, own, channels).transpose(0, 1, 3, 2, 4, 5)
    value = exchange(value, number)
    return value.transpose(0, 2, 1, 3, 4).reshape(batch, rows, channels)


def shifts(value, step):
    rows = value.shape[-2]
    width = 2 * step[1]
    pad = [(0, 0)] * (value.ndim - 2) + [(width, width), (0, 0)]
    padded = jnp.pad(value, pad)
    axis = value.ndim - 2
    return [
        lax.dynamic_slice_in_dim(padded, width - (tap - 1) * step[0], rows, axis) for tap in range(3)
    ]


def on_device(
    section_inputs,
    cotangent,
    conv_weight,
    out_weight,
    norm_scale,
    norm_shift,
    inner_scale,
    inner_shift,
):
    sections = lax.axis_size("section")
    windows = lax.axis_size("dp")
    count = lax.axis_size("seq")
    section = lax.axis_index("section")
    number = lax.axis_index("seq")
    window = lax.axis_index("dp")
    inputs = section_inputs[0, :, 0]
    top = cotangent[:, 0]
    micro, rows, channels = inputs.shape
    kernel = conv_weight[0]
    inner = kernel.shape[2]
    kernel_flat = kernel.reshape(3 * channels, inner)
    back_kernel = kernel.transpose(0, 2, 1).reshape(3 * inner, channels)
    out_w = out_weight[0]
    own = BASE_DILATION // count
    step = (own * (1 + section % 2), own)
    gathered = count == 4 and windows == 2

    def forward(block_in):
        pre = block_in.astype(jnp.float32) * norm_scale[0] + norm_shift[0]
        act, slope = gelu_pair(pre)
        hidden = act.astype(jnp.bfloat16)
        up, same, down = shifts(hidden, step)
        taps = jnp.concatenate([down, same, up], axis=-1)
        inner_pre = (
            jnp.dot(taps, kernel_flat, preferred_element_type=jnp.float32) * inner_scale[0]
            + inner_shift[0]
        )
        inner_act, inner_slope = gelu_pair(inner_pre)
        return (
            hidden,
            slope * norm_scale[0],
            inner_act.astype(jnp.bfloat16),
            inner_slope * inner_scale[0],
        )

    first = to_residues(jnp.stack([inputs[0], top[0]]), number)
    rest = to_residues(jnp.concatenate([inputs[1:], top[1:]]), number)
    block_in = [first[0]] + [rest[m] for m in range(micro - 1)]
    top = jnp.stack([first[1]] + [rest[micro - 1 + m] for m in range(micro - 1)])
    parts = [forward(one) for one in block_in]
    hidden = [one[0] for one in parts]
    inner_act = [one[2] for one in parts]
    slope = jnp.stack([one[1] for one in parts])
    inner_slope = jnp.stack([one[3] for one in parts])

    if gathered:
        half = channels // 2
        side = number // 2
        wide = jnp.stack(hidden).reshape(micro, rows, 2, half)
        near = jnp.stack([pick(wide, side, 2), seq_swap(pick(wide, 1 - side, 2), 2)])
        far = dp_swap(near)
        hidden_all = jnp.stack(
            [jnp.where(window == 0, near, far), jnp.where(window == 0, far, near)]
        )

    def tick(index, received):
        grad_top = jnp.where(section == sections - 1, pick(top, index, 0), received)
        grad_inner = lax.dot_general(
            grad_top, out_w, (((1,), (1,)), ((), ())), preferred_element_type=jnp.float32
        )
        grad_conv = (grad_inner * pick(inner_slope, index, 0)).astype(jnp.bfloat16)
        back = jnp.concatenate(shifts(grad_conv, step), axis=-1)
        grad_hidden = jnp.dot(back, back_kernel, preferred_element_type=jnp.float32)
        grad_block = (
            grad_top.astype(jnp.float32) + grad_hidden * pick(slope, index, 0)
        ).astype(jnp.bfloat16)
        return grad_top, grad_conv, grad_block

    ticks = micro + LAG * (sections - 1)
    down_pairs = [(i + 1, i) for i in range(sections - 1)]
    sent = []
    done = []
    for number_of in range(ticks):
        index = jnp.clip(number_of - LAG * (sections - 1 - section), 0, micro - 1)
        if number_of == 0:
            index = 0
        received = sent[number_of - LAG] if number_of >= LAG else jnp.zeros_like(top[0])
        result = tick(index, received)
        done.append(result)
        if number_of + LAG < ticks:
            sent.append(lax.ppermute(result[2], "section", down_pairs))

    def of_section(m, which):
        value = done[m][which]
        for below in range(1, sections):
            value = jnp.where(
                section == sections - 1 - below, done[m + LAG * below][which], value
            )
        return value

    grads_out = []
    conv_total = 0.0
    out_part = 0.0
    for m in range(micro):
        grad_top, grad_conv, grad_block = (of_section(m, which) for which in range(3))
        out_part = out_part + lax.dot_general(
            inner_act[m], grad_top, (((0,), (0,)), ((), ())), preferred_element_type=jnp.float32
        )
        if gathered:
            near = jnp.stack([grad_conv, seq_swap(grad_conv, 2)])
            far = dp_swap(near)
            both = jnp.stack(
                [jnp.where(window == 0, near, far), jnp.where(window == 0, far, near)]
            )
            back = jnp.concatenate(shifts(both, step), axis=-1)
            conv_total = conv_total + lax.dot_general(
                hidden_all[:, :, m].reshape(4 * rows, half),
                back.reshape(4 * rows, 3 * inner),
                (((0,), (0,)), ((), ())),
                preferred_element_type=jnp.float32,
            )
        else:
            back = jnp.concatenate(shifts(grad_conv, step), axis=-1)
            conv_total = conv_total + lax.dot_general(
                hidden[m], back, (((0,), (0,)), ((), ())), preferred_element_type=jnp.float32
            )
        grads_out.append(from_residues(grad_block[None], number)[0])

    factor = 1.0 / float(micro * windows)
    if gathered:
        core = number % 2
        share = channels // 4
        split = conv_total.reshape(2, share, 3 * inner)
        come = seq_swap(pick(split, 1 - core, 0).astype(jnp.bfloat16), 1)
        conv_sum = pick(split, core, 0) + come.astype(jnp.float32)
        conv_sum = conv_sum.reshape(share, 3, inner).transpose(1, 0, 2)
        columns = out_part.reshape(inner, 2, 2, share)
        come = seq_swap(pick(columns, 1 - core, 2).astype(jnp.bfloat16), 1)
        columns = pick(columns, core, 2) + come.astype(jnp.float32)
        come = seq_swap(pick(columns, 1 - side, 1).astype(jnp.bfloat16), 2)
        columns = (pick(columns, side, 1) + come.astype(jnp.float32)).astype(jnp.bfloat16)
        out_sum = columns.astype(jnp.float32) + dp_swap(columns).astype(jnp.float32)
    else:
        conv_part = conv_total.reshape(channels, 3, inner).transpose(1, 0, 2)
        conv_sum, out_sum = (
            lax.psum(
                lax.psum_scatter(part.astype(jnp.bfloat16), "seq", scatter_dimension=1, tiled=True),
                "dp",
            ).astype(jnp.float32)
            for part in (conv_part, out_part)
        )
    return (
        jnp.stack(grads_out).reshape(section_inputs.shape),
        (conv_sum * factor)[None],
        (out_sum * factor)[None],
    )


def solution(mesh):
    return jax.shard_map(
        on_device,
        mesh=mesh,
        in_specs=(
            P("section", None, "dp", "seq", None),
            P(None, "dp", "seq", None),
            P("section", None, None, None),
            P("section", None, None),
            P("section", None),
            P("section", None),
            P("section", None),
            P("section", None),
        ),
        out_specs=(
            P("section", None, "dp", "seq", None),
            P("section", None, "seq", None),
            P("section", None, "seq"),
        ),
        check_vma=False,
    )
```

time: 323 us -> 135 us (0.42)
  waiting for transfers between devices: 128 us -> 44.9 us
  starting transfers between devices: 68.4 us -> 29.7 us
  other arithmetic: 42.1 us -> 22.5 us
  matrix products: 33.5 us -> 14.3 us
  between operations: 13.8 us -> 2.09 us
  local copies, waits for them, and re-layouts: 29.4 us -> 20 us
  loops' own time: 5.31 us -> 0 us
    reduce_scatter x2 -> x0, waiting for transfers between devices: 53.5 us -> none  [the longest x1 32 us: on_device(): lax.psum_scatter(conv_part.astype(jnp.bfloat16), 'seq', scatter_dimension...]
    ppermute x30 -> x29, starting transfers between devices: 68.3 us -> 29.7 us  [the longest x17 13.5 us: seq_swap(): return lax.ppermute(value, 'seq', [(i, i ^ bit) for i in range(count)])]
    psum x1 -> x0, waiting for transfers between devices: 32.8 us -> none  [on_device(): lax.psum(shares[0].astype(jnp.bfloat16), 'dp').astype(jnp.float32)]
    dot_general x24 -> x18, matrix products: 31.5 us -> 11.4 us  [the longest x9 5.79 us: tick(): grad_hidden = jnp.dot(back, back_kernel, preferred_element_type=jnp.float32)]
    while x109 -> x0, local copies, waits for them, and re-layouts: 14 us -> none
    another operation x0 -> x35, other arithmetic: none -> 13.1 us  [the longest x18 5.22 us: exchange(): jnp.stack([first, second], axis=1)]
    unnamed x0 -> x122, local copies, waits for them, and re-layouts: none -> 9.26 us
    add x12 -> x1, other arithmetic: 8.38 us -> 0.06 us  [on_device(): columns = pick(columns, core, 2) + come.astype(jnp.float32)]
  transfers between devices with their start and end apart: 33 -> 29, of which waited for: 9 -> 13; matrix products, arithmetic and copies ran while one was open for 11% -> 27% of each run, Pallas kernels for 0% -> 0%
where the time goes in v1:
time: 135 us; the launch traced here: 134 us
  waiting for transfers between devices  44.9 us (33%)
  starting transfers between devices  29.7 us (22%)
  other arithmetic  22.5 us (17%)
  local copies, waits for them, and re-layouts  20 us (15%)
  matrix products  14.3 us (11%)
  between operations  2.09 us (2%)
    ppermute x7, waiting for transfers between devices, on_device(): sent.append(lax.ppermute(result[2], 'section', down_pairs))  26 us
    ppermute x17, starting transfers between devices, seq_swap(): return lax.ppermute(value, 'seq', [(i, i ^ bit) for i in range(count)])  13.5 us
    ppermute x5, waiting for transfers between devices, dp_swap(): return lax.ppermute(value, 'dp', [(0, 1), (1, 0)])  11.4 us
    ppermute x7, starting transfers between devices, on_device(): sent.append(lax.ppermute(result[2], 'section', down_pairs))  9.47 us
    unnamed x122, local copies, waits for them, and re-layouts  9.26 us
    ppermute x17, waiting for transfers between devices, seq_swap(): return lax.ppermute(value, 'seq', [(i, i ^ bit) for i in range(count)])  7.58 us
    ppermute x5, starting transfers between devices, dp_swap(): return lax.ppermute(value, 'dp', [(0, 1), (1, 0)])  6.73 us
    dot_general x9, matrix products, tick(): grad_hidden = jnp.dot(back, back_kernel, preferred_element_type=jnp.float32)  5.79 us
  transfers between devices with their start and end apart: 29, of which 13 were waited for; matrix products, arithmetic and copies ran while one was open for 27% of the time, Pallas kernels for 0%

profile of v1, /device:TPU:0, one launch (start us, length us, event | category | flops | bytes accessed | tf_op | source)
XLA Modules:
  0.0 133.6 jit_solution(12659648090208788324)
XLA Ops:
  5.9 2.9 %collective-permute-start.1 = (bf16[2,2,4,1,8,768]{5,4,2,1,0,3:T(8,128)(2,1)}, bf16[2,2,4,1,8,768]{5,4,2,1,0,3:T(8,128)(2,1)}, u32[]{:S(2)}, u32[]{:S(2)}) collective-permute-start(bf16[2,2,4,1,8,768]{5,4,2,1,0,3:T(8,128)(2,1)} %bitcast.392), channel_id=1, source_target_pairs={{0,2},{1,3},{2,0},{3,1},{4,6},{5,7},{6,4},{7,5},{8,10},{9,11},{10,... | collective-permute-start | bytes 589832 | tf_op jit(solution)/shard_map/ppermute | solution.py:27
  9.6 2.6 %copy.64 = bf16[1,3,768,384]{2,3,1,0:T(8,128)(2,1)S(1)} copy(bf16[1,3,768,384]{3,2,1,0:T(8,128)(2,1)} %param.10) | data formatting | bytes 3538944 | tf_op args[2]
  13.5 1.3 collective-permute-done.1
  17.5 5.2 %collective-permute-done.3 = bf16[4,2,4,1,8,768]{5,4,2,1,0,3:T(8,128)(2,1)} collective-permute-done((bf16[4,2,4,1,8,768]{5,4,2,1,0,3:T(8,128)(2,1)S(1)}, bf16[4,2,4,1,8,768]{5,4,2,1,0,3:T(8,128)(2,1)}, u32[]{:S(2)}, u32[]{:S(2)}) %collective-permute-start.3) | collective-permute-done | bytes 393248 | tf_op jit(solution)/shard_map/ppermute | solution.py:27
  25.6 1.3 multiply_convert_fusion.4
  29.6 1.4 %fusion.7 = f32[128,384]{1,0:T(8,128)S(1)} fusion(bf16[2304,384]{1,0:T(8,128)(2,1)S(1)} %bitcast.420, bf16[128,768]{1,0:T(8,128)(2,1)S(1)} %get-tuple-element.81, bf16[128,768]{1,0:T(8,128)(2,1)} %get-tuple-element.103, bf16[128,768]{1,0:T(8,128)(2,1)S(1)} %get-tuple-element.80, f32[384]{0:T(512)S(1)} %copy-done.53, f32[384]{0:T(512)S(1)} %copy-done.50), kind=kOutput, calls=%fused_computation.40 | convolution fusion | flops 228360192 | bytes 2558976 | tf_op jit(solution)/shard_map/dot_general | solution.py:119
  36.0 1.4 %collective-permute-start.9 = (bf16[128,768]{1,0:T(8,128)(2,1)S(1)}, bf16[128,768]{1,0:T(8,128)(2,1)S(1)}, u32[]{:S(2)}, u32[]{:S(2)}) collective-permute-start(bf16[128,768]{1,0:T(8,128)(2,1)S(1)} %fusion.3), channel_id=1, source_target_pairs={{4,0},{8,4},{12,8},{5,1},{9,5},{13,9},{6,2},{10,6},{14,10},{7,3},{... | collective-permute-start | bytes 589832 | tf_op jit(solution)/shard_map/ppermute | solution.py:175
  38.5 1.3 collective-permute-start.4
  40.3 5.4 %collective-permute-done.9 = bf16[128,768]{1,0:T(8,128)(2,1)S(1)} collective-permute-done((bf16[128,768]{1,0:T(8,128)(2,1)S(1)}, bf16[128,768]{1,0:T(8,128)(2,1)S(1)}, u32[]{:S(2)}, u32[]{:S(2)}) %collective-permute-start.9) | collective-permute-done | bytes 196640 | tf_op jit(solution)/shard_map/ppermute | solution.py:175
  48.9 1.4 %collective-permute-start.17 = (bf16[3,128,384]{2,1,0:T(8,128)(2,1)}, bf16[3,128,384]{2,1,0:T(8,128)(2,1)}, u32[]{:S(2)}, u32[]{:S(2)}) collective-permute-start(bf16[3,128,384]{2,1,0:T(8,128)(2,1)} %get-tuple-element.32), channel_id=1, source_target_pairs={{0,2},{1,3},{2,0},{3,1},{4,6},{5,7},{6,4},{7,5},{8,10},{9,11},{10,... | collective-permute-start | bytes 884744 | tf_op jit(solution)/shard_map/ppermute | solution.py:27
  50.4 3.8 %collective-permute-done.10 = bf16[128,768]{1,0:T(8,128)(2,1)S(1)} collective-permute-done((bf16[128,768]{1,0:T(8,128)(2,1)S(1)}, bf16[128,768]{1,0:T(8,128)(2,1)S(1)}, u32[]{:S(2)}, u32[]{:S(2)}) %collective-permute-start.10) | collective-permute-done | bytes 196640 | tf_op jit(solution)/shard_map/ppermute | solution.py:175
  56.5 1.3 collective-permute-start.5
  58.9 1.5 %collective-permute-start.18 = (bf16[2,3,128,384]{3,2,1,0:T(8,128)(2,1)S(1)}, bf16[2,3,128,384]{3,2,1,0:T(8,128)(2,1)S(1)}, u32[]{:S(2)}, u32[]{:S(2)}) collective-permute-start(bf16[2,3,128,384]{3,2,1,0:T(8,128)(2,1)S(1)} %pad_maximum_fusion.7), channel_id=1, source_target_pairs={{0,16},{16,0},{1,17},{17,1},{2,18},{18,2},{3,19},{19,3},{4,20},{20... | collective-permute-start | bytes 1769480 | tf_op jit(solution)/shard_map/ppermute | solution.py:31
  60.4 3.9 %collective-permute-done.5 = bf16[128,768]{1,0:T(8,128)(2,1)} collective-permute-done((bf16[128,768]{1,0:T(8,128)(2,1)}, bf16[128,768]{1,0:T(8,128)(2,1)}, u32[]{:S(2)}, u32[]{:S(2)}) %collective-permute-start.5) | collective-permute-done | bytes 196640 | tf_op jit(solution)/shard_map/ppermute | solution.py:175
  66.1 1.3 collective-permute-start.6
  67.8 5.9 %collective-permute-done.6 = bf16[128,768]{1,0:T(8,128)(2,1)S(1)} collective-permute-done((bf16[128,768]{1,0:T(8,128)(2,1)S(1)}, bf16[128,768]{1,0:T(8,128)(2,1)S(1)}, u32[]{:S(2)}, u32[]{:S(2)}) %collective-permute-start.6) | collective-permute-done | bytes 196640 | tf_op jit(solution)/shard_map/ppermute | solution.py:175
  75.1 1.6 %collective-permute-start.11 = (bf16[128,768]{1,0:T(8,128)(2,1)S(1)}, bf16[128,768]{1,0:T(8,128)(2,1)S(1)}, u32[]{:S(2)}, u32[]{:S(2)}) collective-permute-start(bf16[128,768]{1,0:T(8,128)(2,1)S(1)} %add_convert_fusion.2), channel_id=1, source_target_pairs={{4,0},{8,4},{12,8},{5,1},{9,5},{13,9},{6,2},{10,6},{14,10},{7,3},{... | collective-permute-start | bytes 589832 | tf_op jit(solution)/shard_map/ppermute | solution.py:175
  76.8 1.3 collective-permute-start.14
  78.1 1.5 %collective-permute-start.8 = (bf16[1,2,4,1,8,768]{5,4,1,2,3,0:T(8,128)(2,1)S(1)}, bf16[1,2,4,1,8,768]{5,4,1,2,3,0:T(8,128)(2,1)S(1)}, u32[]{:S(2)}, u32[]{:S(2)}) collective-permute-start(bf16[1,2,4,1,8,768]{5,4,1,2,3,0:T(8,128)(2,1)S(1)} %bitcast.456), channel_id=1, source_target_pairs={{0,2},{1,3},{2,0},{3,1},{4,6},{5,7},{6,4},{7,5},{8,10},{9,11},{10,... | collective-permute-start | bytes 294920 | tf_op jit(solution)/shard_map/ppermute | solution.py:27
  81.9 3.2 %collective-permute-done.11 = bf16[128,768]{1,0:T(8,128)(2,1)S(1)} collective-permute-done((bf16[128,768]{1,0:T(8,128)(2,1)S(1)}, bf16[128,768]{1,0:T(8,128)(2,1)S(1)}, u32[]{:S(2)}, u32[]{:S(2)}) %collective-permute-start.11) | collective-permute-done | bytes 196640 | tf_op jit(solution)/shard_map/ppermute | solution.py:175
  85.0 3.8 %collective-permute-done.14 = bf16[128,768]{1,0:T(8,128)(2,1)S(1)} collective-permute-done((bf16[128,768]{1,0:T(8,128)(2,1)S(1)}, bf16[128,768]{1,0:T(8,128)(2,1)S(1)}, u32[]{:S(2)}, u32[]{:S(2)}) %collective-permute-start.14) | collective-permute-done | bytes 196640 | tf_op jit(solution)/shard_map/ppermute | solution.py:175
  91.4 1.5 %fusion.119 = bf16[128,768]{1,0:T(8,128)(2,1)S(1)} fusion(f32[3,128,768]{2,1,0:T(8,128)S(1)} %copy-done.2, s32[]{:T(128)S(6)} %min.32, bf16[1152,768]{1,0:T(8,128)(2,1)S(1)} %bitcast.403, bf16[128,768]{1,0:T(8,128)(2,1)S(1)} %get-tuple-element.34, bf16[128,384]{1,0:T(8,128)(2,1)S(1)} %get-tuple-element.82, bf16[128,384]{1,0:T(8,128)(2,1)S(1)} %fusion.16, ...), kind=kOutput, calls=%fused_computation.204 | convolution fusion | flops 228065280 | bytes 3440647 | tf_op jit(solution)/shard_map/dot_general | solution.py:157
  95.3 1.5 %collective-permute-start.19 = (bf16[128,384]{1,0:T(8,128)(2,1)S(1)}, bf16[128,384]{1,0:T(8,128)(2,1)}, u32[]{:S(2)}, u32[]{:S(2)}) collective-permute-start(bf16[128,384]{1,0:T(8,128)(2,1)S(1)} %get-tuple-element.57), channel_id=1, source_target_pairs={{0,2},{1,3},{2,0},{3,1},{4,6},{5,7},{6,4},{7,5},{8,10},{9,11},{10,... | collective-permute-start | bytes 294920 | tf_op jit(solution)/shard_map/ppermute | solution.py:27
  97.4 1.5 %collective-permute-start.23 = (bf16[128,384]{1,0:T(8,128)(2,1)S(1)}, bf16[128,384]{1,0:T(8,128)(2,1)S(1)}, u32[]{:S(2)}, u32[]{:S(2)}) collective-permute-start(bf16[128,384]{1,0:T(8,128)(2,1)S(1)} %get-tuple-element.56), channel_id=1, source_target_pairs={{0,2},{1,3},{2,0},{3,1},{4,6},{5,7},{6,4},{7,5},{8,10},{9,11},{10,... | collective-permute-start | bytes 294920 | tf_op jit(solution)/shard_map/ppermute | solution.py:27
  102.5 1.5 %collective-permute-start.13 = (bf16[1,2,4,1,8,768]{5,4,1,2,3,0:T(8,128)(2,1)S(1)}, bf16[1,2,4,1,8,768]{5,4,1,2,3,0:T(8,128)(2,1)S(1)}, u32[]{:S(2)}, u32[]{:S(2)}) collective-permute-start(bf16[1,2,4,1,8,768]{5,4,1,2,3,0:T(8,128)(2,1)S(1)} %bitcast.457), channel_id=1, source_target_pairs={{0,2},{1,3},{2,0},{3,1},{4,6},{5,7},{6,4},{7,5},{8,10},{9,11},{10,... | collective-permute-start | bytes 294920 | tf_op jit(solution)/shard_map/ppermute | solution.py:27
  104.9 1.5 %collective-permute-start.20 = (bf16[2,128,384]{2,1,0:T(8,128)(2,1)S(1)}, bf16[2,128,384]{2,1,0:T(8,128)(2,1)S(1)}, u32[]{:S(2)}, u32[]{:S(2)}) collective-permute-start(bf16[2,128,384]{2,1,0:T(8,128)(2,1)S(1)} %pad_maximum_fusion.14), channel_id=1, source_target_pairs={{0,16},{16,0},{1,17},{17,1},{2,18},{18,2},{3,19},{19,3},{4,20},{20... | collective-permute-start | bytes 589832 | tf_op jit(solution)/shard_map/ppermute | solution.py:31
  108.0 1.5 %collective-permute-start.24 = (bf16[2,128,384]{2,1,0:T(8,128)(2,1)S(1)}, bf16[2,128,384]{2,1,0:T(8,128)(2,1)S(1)}, u32[]{:S(2)}, u32[]{:S(2)}) collective-permute-start(bf16[2,128,384]{2,1,0:T(8,128)(2,1)S(1)} %pad_maximum_fusion.16), channel_id=1, source_target_pairs={{0,16},{16,0},{1,17},{17,1},{2,18},{18,2},{3,19},{19,3},{4,20},{20... | collective-permute-start | bytes 589832 | tf_op jit(solution)/shard_map/ppermute | solution.py:31
  110.4 2.4 %collective-permute-done.20 = bf16[2,128,384]{2,1,0:T(8,128)(2,1)S(1)} collective-permute-done((bf16[2,128,384]{2,1,0:T(8,128)(2,1)S(1)}, bf16[2,128,384]{2,1,0:T(8,128)(2,1)S(1)}, u32[]{:S(2)}, u32[]{:S(2)}) %collective-permute-start.20) | collective-permute-done | bytes 196640 | tf_op jit(solution)/shard_map/ppermute | solution.py:31
  113.9 3.1 %collective-permute-done.22 = bf16[2,128,384]{2,1,0:T(8,128)(2,1)S(1)} collective-permute-done((bf16[2,128,384]{2,1,0:T(8,128)(2,1)S(1)}, bf16[2,128,384]{2,1,0:T(8,128)(2,1)S(1)}, u32[]{:S(2)}, u32[]{:S(2)}) %collective-permute-start.22) | collective-permute-done | bytes 196640 | tf_op jit(solution)/shard_map/ppermute | solution.py:31
  118.1 2.1 %collective-permute-done.24 = bf16[2,128,384]{2,1,0:T(8,128)(2,1)S(1)} collective-permute-done((bf16[2,128,384]{2,1,0:T(8,128)(2,1)S(1)}, bf16[2,128,384]{2,1,0:T(8,128)(2,1)S(1)}, u32[]{:S(2)}, u32[]{:S(2)}) %collective-permute-start.24) | collective-permute-done | bytes 196640 | tf_op jit(solution)/shard_map/ppermute | solution.py:31
  125.1 1.5 %collective-permute-start.28 = (bf16[384,192]{0,1:T(8,128)(2,1)S(1)}, bf16[384,192]{0,1:T(8,128)(2,1)S(1)}, u32[]{:S(2)}, u32[]{:S(2)}) collective-permute-start(bf16[384,192]{0,1:T(8,128)(2,1)S(1)} %fusion.126), channel_id=1, source_target_pairs={{0,16},{16,0},{1,17},{17,1},{2,18},{18,2},{3,19},{19,3},{4,20},{20... | collective-permute-start | bytes 442376 | tf_op jit(solution)/shard_map/ppermute | solution.py:31
  127.5 3.8 %collective-permute-done.28 = bf16[384,192]{0,1:T(8,128)(2,1)S(1)} collective-permute-done((bf16[384,192]{0,1:T(8,128)(2,1)S(1)}, bf16[384,192]{0,1:T(8,128)(2,1)S(1)}, u32[]{:S(2)}, u32[]{:S(2)}) %collective-permute-start.28) | collective-permute-done | bytes 147488 | tf_op jit(solution)/shard_map/ppermute | solution.py:31
  (273 shorter events, 56.1 us)
Async XLA Ops:
  0.6 32.9 %copy-start = (bf16[1,384,768]{2,1,0:T(8,128)(2,1)S(1)}, bf16[1,384,768]{2,1,0:T(8,128)(2,1)}, u32[]{:S(2)}) copy-start(bf16[1,384,768]{2,1,0:T(8,128)(2,1)} %param.11) | copy-start | bytes 1769476
  3.4 1.7 %collective-permute-start = (bf16[2,1,4,2,8,768]{5,4,3,2,0,1:T(8,128)(2,1)}, bf16[2,1,4,2,8,768]{5,4,3,2,0,1:T(8,128)(2,1)S(1)}, u32[]{:S(2)}, u32[]{:S(2)}) collective-permute-start(bf16[2,1,4,2,8,768]{5,4,3,2,0,1:T(8,128)(2,1)} %fusion.131), channel_id=1, source_target_pairs={{0,1},{1,0},{2,3},{3,2},{4,5},{5,4},{6,7},{7,6},{8,9},{9,8},{10,11... | collective-permute-start | bytes 589832 | tf_op jit(solution)/shard_map/ppermute | solution.py:27
  4.0 4.8 %collective-permute-start.2 = (bf16[4,1,4,2,8,768]{5,4,3,2,0,1:T(8,128)(2,1)S(1)}, bf16[4,1,4,2,8,768]{5,4,3,2,0,1:T(8,128)(2,1)S(1)}, u32[]{:S(2)}, u32[]{:S(2)}) collective-permute-start(bf16[4,1,4,2,8,768]{5,4,3,2,0,1:T(8,128)(2,1)S(1)} %fusion.47), channel_id=1, source_target_pairs={{0,1},{1,0},{2,3},{3,2},{4,5},{5,4},{6,7},{7,6},{8,9},{9,8},{10,11... | collective-permute-start | bytes 1179656 | tf_op jit(solution)/shard_map/ppermute | solution.py:27
  5.9 8.9 %collective-permute-start.1 = (bf16[2,2,4,1,8,768]{5,4,2,1,0,3:T(8,128)(2,1)}, bf16[2,2,4,1,8,768]{5,4,2,1,0,3:T(8,128)(2,1)}, u32[]{:S(2)}, u32[]{:S(2)}) collective-permute-start(bf16[2,2,4,1,8,768]{5,4,2,1,0,3:T(8,128)(2,1)} %bitcast.392), channel_id=1, source_target_pairs={{0,2},{1,3},{2,0},{3,1},{4,6},{5,7},{6,4},{7,5},{8,10},{9,11},{10,... | collective-permute-start | bytes 589832 | tf_op jit(solution)/shard_map/ppermute | solution.py:27
  9.0 13.7 %collective-permute-start.3 = (bf16[4,2,4,1,8,768]{5,4,2,1,0,3:T(8,128)(2,1)S(1)}, bf16[4,2,4,1,8,768]{5,4,2,1,0,3:T(8,128)(2,1)}, u32[]{:S(2)}, u32[]{:S(2)}) collective-permute-start(bf16[4,2,4,1,8,768]{5,4,2,1,0,3:T(8,128)(2,1)S(1)} %bitcast.447), channel_id=1, source_target_pairs={{0,2},{1,3},{2,0},{3,1},{4,6},{5,7},{6,4},{7,5},{8,10},{9,11},{10,... | collective-permute-start | bytes 1179656 | tf_op jit(solution)/shard_map/ppermute | solution.py:27
  16.6 9.1 %copy-start.3 = (f32[1,2,2,4,1,8,768]{6,5,3,2,0,4,1:T(8,128)}, f32[1,2,2,4,1,8,768]{6,5,3,2,0,4,1:T(8,128)S(1)}, u32[]{:S(2)}) copy-start(f32[1,2,2,4,1,8,768]{6,5,3,2,0,4,1:T(8,128)S(1)} %get-tuple-element.51) | copy-start | bytes 1179652
  35.5 19.8 %copy-start.1 = (f32[3,128,768]{2,1,0:T(8,128)}, f32[3,128,768]{2,1,0:T(8,128)S(1)}, u32[]{:S(2)}) copy-start(f32[3,128,768]{2,1,0:T(8,128)S(1)} %pad_maximum_fusion) | copy-start | bytes 3538948
  36.0 9.6 %collective-permute-start.9 = (bf16[128,768]{1,0:T(8,128)(2,1)S(1)}, bf16[128,768]{1,0:T(8,128)(2,1)S(1)}, u32[]{:S(2)}, u32[]{:S(2)}) collective-permute-start(bf16[128,768]{1,0:T(8,128)(2,1)S(1)} %fusion.3), channel_id=1, source_target_pairs={{4,0},{8,4},{12,8},{5,1},{9,5},{13,9},{6,2},{10,6},{14,10},{7,3},{... | collective-permute-start | bytes 589832 | tf_op jit(solution)/shard_map/ppermute | solution.py:175
  38.5 11.9 %collective-permute-start.4 = (bf16[128,768]{1,0:T(8,128)(2,1)S(1)}, bf16[128,768]{1,0:T(8,128)(2,1)S(1)}, u32[]{:S(2)}, u32[]{:S(2)}) collective-permute-start(bf16[128,768]{1,0:T(8,128)(2,1)S(1)} %fusion.4), channel_id=1, source_target_pairs={{4,0},{8,4},{12,8},{5,1},{9,5},{13,9},{6,2},{10,6},{14,10},{7,3},{... | collective-permute-start | bytes 589832 | tf_op jit(solution)/shard_map/ppermute | solution.py:175
  46.6 7.6 %collective-permute-start.10 = (bf16[128,768]{1,0:T(8,128)(2,1)S(1)}, bf16[128,768]{1,0:T(8,128)(2,1)S(1)}, u32[]{:S(2)}, u32[]{:S(2)}) collective-permute-start(bf16[128,768]{1,0:T(8,128)(2,1)S(1)} %add_convert_fusion.3), channel_id=1, source_target_pairs={{4,0},{8,4},{12,8},{5,1},{9,5},{13,9},{6,2},{10,6},{14,10},{7,3},{... | collective-permute-start | bytes 589832 | tf_op jit(solution)/shard_map/ppermute | solution.py:175
  48.9 8.9 %collective-permute-start.17 = (bf16[3,128,384]{2,1,0:T(8,128)(2,1)}, bf16[3,128,384]{2,1,0:T(8,128)(2,1)}, u32[]{:S(2)}, u32[]{:S(2)}) collective-permute-start(bf16[3,128,384]{2,1,0:T(8,128)(2,1)} %get-tuple-element.32), channel_id=1, source_target_pairs={{0,2},{1,3},{2,0},{3,1},{4,6},{5,7},{6,4},{7,5},{8,10},{9,11},{10,... | collective-permute-start | bytes 884744 | tf_op jit(solution)/shard_map/ppermute | solution.py:27
  56.5 7.9 %collective-permute-start.5 = (bf16[128,768]{1,0:T(8,128)(2,1)}, bf16[128,768]{1,0:T(8,128)(2,1)}, u32[]{:S(2)}, u32[]{:S(2)}) collective-permute-start(bf16[128,768]{1,0:T(8,128)(2,1)} %add_convert_fusion.6), channel_id=1, source_target_pairs={{4,0},{8,4},{12,8},{5,1},{9,5},{13,9},{6,2},{10,6},{14,10},{7,3},{... | collective-permute-start | bytes 589832 | tf_op jit(solution)/shard_map/ppermute | solution.py:175
  58.9 20.7 %collective-permute-start.18 = (bf16[2,3,128,384]{3,2,1,0:T(8,128)(2,1)S(1)}, bf16[2,3,128,384]{3,2,1,0:T(8,128)(2,1)S(1)}, u32[]{:S(2)}, u32[]{:S(2)}) collective-permute-start(bf16[2,3,128,384]{3,2,1,0:T(8,128)(2,1)S(1)} %pad_maximum_fusion.7), channel_id=1, source_target_pairs={{0,16},{16,0},{1,17},{17,1},{2,18},{18,2},{3,19},{19,3},{4,20},{20... | collective-permute-start | bytes 1769480 | tf_op jit(solution)/shard_map/ppermute | solution.py:31
  66.1 7.6 %collective-permute-start.6 = (bf16[128,768]{1,0:T(8,128)(2,1)S(1)}, bf16[128,768]{1,0:T(8,128)(2,1)S(1)}, u32[]{:S(2)}, u32[]{:S(2)}) collective-permute-start(bf16[128,768]{1,0:T(8,128)(2,1)S(1)} %add_convert_fusion.5), channel_id=1, source_target_pairs={{4,0},{8,4},{12,8},{5,1},{9,5},{13,9},{6,2},{10,6},{14,10},{7,3},{... | collective-permute-start | bytes 589832 | tf_op jit(solution)/shard_map/ppermute | solution.py:175
  74.6 3.4 %collective-permute-start.7 = (bf16[1,1,4,2,8,768]{5,4,2,3,1,0:T(8,128)(2,1)S(1)}, bf16[1,1,4,2,8,768]{5,4,2,3,1,0:T(8,128)(2,1)S(1)}, u32[]{:S(2)}, u32[]{:S(2)}) collective-permute-start(bf16[1,1,4,2,8,768]{5,4,2,3,1,0:T(8,128)(2,1)S(1)} %dynamic-slice_bitcast_fusion.4), channel_id=1, source_target_pairs={{0,1},{1,0},{2,3},{3,2},{4,5},{5,4},{6,7},{7,6},{8,9},{9,8},{10,11... | collective-permute-start | bytes 294920 | tf_op jit(solution)/shard_map/ppermute | solution.py:27
  75.1 9.9 %collective-permute-start.11 = (bf16[128,768]{1,0:T(8,128)(2,1)S(1)}, bf16[128,768]{1,0:T(8,128)(2,1)S(1)}, u32[]{:S(2)}, u32[]{:S(2)}) collective-permute-start(bf16[128,768]{1,0:T(8,128)(2,1)S(1)} %add_convert_fusion.2), channel_id=1, source_target_pairs={{4,0},{8,4},{12,8},{5,1},{9,5},{13,9},{6,2},{10,6},{14,10},{7,3},{... | collective-permute-start | bytes 589832 | tf_op jit(solution)/shard_map/ppermute | solution.py:175
  76.8 12.1 %collective-permute-start.14 = (bf16[128,768]{1,0:T(8,128)(2,1)S(1)}, bf16[128,768]{1,0:T(8,128)(2,1)S(1)}, u32[]{:S(2)}, u32[]{:S(2)}) collective-permute-start(bf16[128,768]{1,0:T(8,128)(2,1)S(1)} %get-tuple-element.115), channel_id=1, source_target_pairs={{4,0},{8,4},{12,8},{5,1},{9,5},{13,9},{6,2},{10,6},{14,10},{7,3},{... | collective-permute-start | bytes 589832 | tf_op jit(solution)/shard_map/ppermute | solution.py:175
  78.1 17.1 %collective-permute-start.8 = (bf16[1,2,4,1,8,768]{5,4,1,2,3,0:T(8,128)(2,1)S(1)}, bf16[1,2,4,1,8,768]{5,4,1,2,3,0:T(8,128)(2,1)S(1)}, u32[]{:S(2)}, u32[]{:S(2)}) collective-permute-start(bf16[1,2,4,1,8,768]{5,4,1,2,3,0:T(8,128)(2,1)S(1)} %bitcast.456), channel_id=1, source_target_pairs={{0,2},{1,3},{2,0},{3,1},{4,6},{5,7},{6,4},{7,5},{8,10},{9,11},{10,... | collective-permute-start | bytes 294920 | tf_op jit(solution)/shard_map/ppermute | solution.py:27
  93.5 6.2 %collective-permute-start.15 = (bf16[1,1,4,2,8,768]{5,4,2,3,1,0:T(8,128)(2,1)}, bf16[1,1,4,2,8,768]{5,4,2,3,1,0:T(8,128)(2,1)}, u32[]{:S(2)}, u32[]{:S(2)}) collective-permute-start(bf16[1,1,4,2,8,768]{5,4,2,3,1,0:T(8,128)(2,1)} %dynamic-slice_bitcast_fusion.2), channel_id=1, source_target_pairs={{0,1},{1,0},{2,3},{3,2},{4,5},{5,4},{6,7},{7,6},{8,9},{9,8},{10,11... | collective-permute-start | bytes 294920 | tf_op jit(solution)/shard_map/ppermute | solution.py:27
  94.8 6.0 %collective-permute-start.12 = (bf16[1,1,4,2,8,768]{5,4,2,3,1,0:T(8,128)(2,1)}, bf16[1,1,4,2,8,768]{5,4,2,3,1,0:T(8,128)(2,1)}, u32[]{:S(2)}, u32[]{:S(2)}) collective-permute-start(bf16[1,1,4,2,8,768]{5,4,2,3,1,0:T(8,128)(2,1)} %dynamic-slice_bitcast_fusion.3), channel_id=1, source_target_pairs={{0,1},{1,0},{2,3},{3,2},{4,5},{5,4},{6,7},{7,6},{8,9},{9,8},{10,11... | collective-permute-start | bytes 294920 | tf_op jit(solution)/shard_map/ppermute | solution.py:27
  95.3 7.1 %collective-permute-start.19 = (bf16[128,384]{1,0:T(8,128)(2,1)S(1)}, bf16[128,384]{1,0:T(8,128)(2,1)}, u32[]{:S(2)}, u32[]{:S(2)}) collective-permute-start(bf16[128,384]{1,0:T(8,128)(2,1)S(1)} %get-tuple-element.57), channel_id=1, source_target_pairs={{0,2},{1,3},{2,0},{3,1},{4,6},{5,7},{6,4},{7,5},{8,10},{9,11},{10,... | collective-permute-start | bytes 294920 | tf_op jit(solution)/shard_map/ppermute | solution.py:27
  96.8 8.0 %collective-permute-start.21 = (bf16[128,384]{1,0:T(8,128)(2,1)S(1)}, bf16[128,384]{1,0:T(8,128)(2,1)}, u32[]{:S(2)}, u32[]{:S(2)}) collective-permute-start(bf16[128,384]{1,0:T(8,128)(2,1)S(1)} %get-tuple-element.84), channel_id=1, source_target_pairs={{0,2},{1,3},{2,0},{3,1},{4,6},{5,7},{6,4},{7,5},{8,10},{9,11},{10,... | collective-permute-start | bytes 294920 | tf_op jit(solution)/shard_map/ppermute | solution.py:27
  97.4 9.9 %collective-permute-start.23 = (bf16[128,384]{1,0:T(8,128)(2,1)S(1)}, bf16[128,384]{1,0:T(8,128)(2,1)S(1)}, u32[]{:S(2)}, u32[]{:S(2)}) collective-permute-start(bf16[128,384]{1,0:T(8,128)(2,1)S(1)} %get-tuple-element.56), channel_id=1, source_target_pairs={{0,2},{1,3},{2,0},{3,1},{4,6},{5,7},{6,4},{7,5},{8,10},{9,11},{10,... | collective-permute-start | bytes 294920 | tf_op jit(solution)/shard_map/ppermute | solution.py:27
  99.7 10.0 %collective-permute-start.26 = (bf16[384,2,192]{0,2,1:T(8,128)(2,1)S(1)}, bf16[384,2,192]{0,2,1:T(8,128)(2,1)S(1)}, u32[]{:S(2)}, u32[]{:S(2)}) collective-permute-start(bf16[384,2,192]{0,2,1:T(8,128)(2,1)S(1)} %fusion.60), channel_id=1, source_target_pairs={{0,1},{1,0},{2,3},{3,2},{4,5},{5,4},{6,7},{7,6},{8,9},{9,8},{10,11... | collective-permute-start | bytes 884744 | tf_op jit(solution)/shard_map/ppermute | solution.py:27
  101.8 6.2 %collective-permute-start.16 = (bf16[1,2,4,1,8,768]{5,4,1,2,3,0:T(8,128)(2,1)S(1)}, bf16[1,2,4,1,8,768]{5,4,1,2,3,0:T(8,128)(2,1)S(1)}, u32[]{:S(2)}, u32[]{:S(2)}) collective-permute-start(bf16[1,2,4,1,8,768]{5,4,1,2,3,0:T(8,128)(2,1)S(1)} %bitcast.458), channel_id=1, source_target_pairs={{0,2},{1,3},{2,0},{3,1},{4,6},{5,7},{6,4},{7,5},{8,10},{9,11},{10,... | collective-permute-start | bytes 294920 | tf_op jit(solution)/shard_map/ppermute | solution.py:27
  102.5 7.2 %collective-permute-start.13 = (bf16[1,2,4,1,8,768]{5,4,1,2,3,0:T(8,128)(2,1)S(1)}, bf16[1,2,4,1,8,768]{5,4,1,2,3,0:T(8,128)(2,1)S(1)}, u32[]{:S(2)}, u32[]{:S(2)}) collective-permute-start(bf16[1,2,4,1,8,768]{5,4,1,2,3,0:T(8,128)(2,1)S(1)} %bitcast.457), channel_id=1, source_target_pairs={{0,2},{1,3},{2,0},{3,1},{4,6},{5,7},{6,4},{7,5},{8,10},{9,11},{10,... | collective-permute-start | bytes 294920 | tf_op jit(solution)/shard_map/ppermute | solution.py:27
  104.9 7.8 %collective-permute-start.20 = (bf16[2,128,384]{2,1,0:T(8,128)(2,1)S(1)}, bf16[2,128,384]{2,1,0:T(8,128)(2,1)S(1)}, u32[]{:S(2)}, u32[]{:S(2)}) collective-permute-start(bf16[2,128,384]{2,1,0:T(8,128)(2,1)S(1)} %pad_maximum_fusion.14), channel_id=1, source_target_pairs={{0,16},{16,0},{1,17},{17,1},{2,18},{18,2},{3,19},{19,3},{4,20},{20... | collective-permute-start | bytes 589832 | tf_op jit(solution)/shard_map/ppermute | solution.py:31
  107.4 9.6 %collective-permute-start.22 = (bf16[2,128,384]{2,1,0:T(8,128)(2,1)S(1)}, bf16[2,128,384]{2,1,0:T(8,128)(2,1)S(1)}, u32[]{:S(2)}, u32[]{:S(2)}) collective-permute-start(bf16[2,128,384]{2,1,0:T(8,128)(2,1)S(1)} %pad_maximum_fusion.15), channel_id=1, source_target_pairs={{0,16},{16,0},{1,17},{17,1},{2,18},{18,2},{3,19},{19,3},{4,20},{20... | collective-permute-start | bytes 589832 | tf_op jit(solution)/shard_map/ppermute | solution.py:31
  108.0 12.1 %collective-permute-start.24 = (bf16[2,128,384]{2,1,0:T(8,128)(2,1)S(1)}, bf16[2,128,384]{2,1,0:T(8,128)(2,1)S(1)}, u32[]{:S(2)}, u32[]{:S(2)}) collective-permute-start(bf16[2,128,384]{2,1,0:T(8,128)(2,1)S(1)} %pad_maximum_fusion.16), channel_id=1, source_target_pairs={{0,16},{16,0},{1,17},{17,1},{2,18},{18,2},{3,19},{19,3},{4,20},{20... | collective-permute-start | bytes 589832 | tf_op jit(solution)/shard_map/ppermute | solution.py:31
  109.8 15.2 %collective-permute-start.27 = (bf16[384,192]{0,1:T(8,128)(2,1)S(1)}, bf16[384,192]{0,1:T(8,128)(2,1)S(1)}, u32[]{:S(2)}, u32[]{:S(2)}) collective-permute-start(bf16[384,192]{0,1:T(8,128)(2,1)S(1)} %fusion.163), channel_id=1, source_target_pairs={{0,2},{1,3},{2,0},{3,1},{4,6},{5,7},{6,4},{7,5},{8,10},{9,11},{10,... | collective-permute-start | bytes 442376 | tf_op jit(solution)/shard_map/ppermute | solution.py:27
  124.9 7.2 %collective-permute-start.25 = (bf16[192,1152]{1,0:T(8,128)(2,1)S(1)}, bf16[192,1152]{1,0:T(8,128)(2,1)S(1)}, u32[]{:S(2)}, u32[]{:S(2)}) collective-permute-start(bf16[192,1152]{1,0:T(8,128)(2,1)S(1)} %fusion.43), channel_id=1, source_target_pairs={{0,1},{1,0},{2,3},{3,2},{4,5},{5,4},{6,7},{7,6},{8,9},{9,8},{10,11... | collective-permute-start | bytes 1327112 | tf_op jit(solution)/shard_map/ppermute | solution.py:27
  125.1 6.3 %collective-permute-start.28 = (bf16[384,192]{0,1:T(8,128)(2,1)S(1)}, bf16[384,192]{0,1:T(8,128)(2,1)S(1)}, u32[]{:S(2)}, u32[]{:S(2)}) collective-permute-start(bf16[384,192]{0,1:T(8,128)(2,1)S(1)} %fusion.126), channel_id=1, source_target_pairs={{0,16},{16,0},{1,17},{17,1},{2,18},{18,2},{3,19},{19,3},{4,20},{20... | collective-permute-start | bytes 442376 | tf_op jit(solution)/shard_map/ppermute | solution.py:31
  (57 other events, 139.1 us)

commit v2 on v1

--- a/solution.py
+++ b/solution.py
@@ -1,6 +1,7 @@
 import jax
 import jax.numpy as jnp
 from jax import lax
+from jax.experimental import pallas as pl
 from jax.sharding import PartitionSpec as P
 
 BASE_DILATION = 32
@@ -81,6 +82,21 @@
     ]
 
 
+def passed(value):
+    def kernel(value_ref, out_ref):
+        out_ref[...] = value_ref[...]
+
+    return pl.pallas_call(kernel, out_shape=jax.ShapeDtypeStruct(value.shape, value.dtype))(value)
+
+
+def after(value, *events):
+    return lax.optimization_barrier((value,) + events)[0]
+
+
+def choose(flag, first, second):
+    return jnp.where(flag, first, second)
+
+
 def on_device(
     section_inputs,
     cotangent,
@@ -91,6 +107,7 @@
     inner_scale,
     inner_shift,
 ):
+    norm_scale = passed(norm_scale)
     sections = lax.axis_size("section")
     windows = lax.axis_size("dp")
     count = lax.axis_size("seq")
@@ -108,6 +125,9 @@
     own = BASE_DILATION // count
     step = (own * (1 + section % 2), own)
     gathered = count == 4 and windows == 2
+    core, side = number % 2, number // 2
+    ticks = micro + LAG * (sections - 1)
+    down_pairs = [(i + 1, i) for i in range(sections - 1)]
 
     def forward(block_in):
         pre = block_in.astype(jnp.float32) * norm_scale[0] + norm_shift[0]
@@ -120,59 +140,61 @@
             + inner_shift[0]
         )
         inner_act, inner_slope = gelu_pair(inner_pre)
-        return (
-            hidden,
-            slope * norm_scale[0],
-            inner_act.astype(jnp.bfloat16),
-            inner_slope * inner_scale[0],
-        )
-
-    first = to_residues(jnp.stack([inputs[0], top[0]]), number)
-    rest = to_residues(jnp.concatenate([inputs[1:], top[1:]]), number)
-    block_in = [first[0]] + [rest[m] for m in range(micro - 1)]
-    top = jnp.stack([first[1]] + [rest[micro - 1 + m] for m in range(micro - 1)])
-    parts = [forward(one) for one in block_in]
-    hidden = [one[0] for one in parts]
-    inner_act = [one[2] for one in parts]
-    slope = jnp.stack([one[1] for one in parts])
-    inner_slope = jnp.stack([one[3] for one in parts])
-
-    if gathered:
-        half = channels // 2
-        side = number // 2
-        wide = jnp.stack(hidden).reshape(micro, rows, 2, half)
-        near = jnp.stack([pick(wide, side, 2), seq_swap(pick(wide, 1 - side, 2), 2)])
-        far = dp_swap(near)
-        hidden_all = jnp.stack(
-            [jnp.where(window == 0, near, far), jnp.where(window == 0, far, near)]
-        )
+        return lax.optimization_barrier(
+            (
+                hidden,
+                slope * norm_scale[0],
+                inner_act.astype(jnp.bfloat16),
+                inner_slope * inner_scale[0],
+            )
+        )
+
+    both_in = jnp.concatenate([inputs, top])
+    if count == 4:
+        blocks = both_in.reshape(2 * micro, rows // BASE_DILATION, 2, 2, own, channels)
+        keep = pick(blocks, core, 3)
+        come = seq_swap(pick(blocks, 1 - core, 3), 1)
+        halves = jnp.stack([choose(core == 0, keep, come), choose(core == 0, come, keep)], 1)
+        sends, keeps = [], []
+        for m in range(micro):
+            pair = jnp.stack([halves[m], halves[micro + m]])
+            sends.append(pick(pair, 1 - side, 3))
+            keeps.append(pick(pair, side, 3))
+        comes = [seq_swap(one, 2) for one in sends]
+
+        def arrived(m, *events):
+            keep = keeps[m]
+            come = after(comes[m], *events)
+            pair = jnp.stack([choose(side == 0, keep, come), choose(side == 0, come, keep)], 1)
+            return pair[0].reshape(rows, channels), pair[1].reshape(rows, channels)
+    else:
+        swapped = to_residues(both_in, number)
+
+        def arrived(m, *events):
+            return swapped[m], swapped[micro + m]
+
+    tops, hidden, slope, inner_act, inner_slope = [], [], [], [], []
 
     def tick(index, received):
-        grad_top = jnp.where(section == sections - 1, pick(top, index, 0), received)
+        def of_index(values):
+            value = values[0]
+            for m in range(1, len(values)):
+                value = jnp.where(index >= m, values[m], value)
+            return value
+
+        grad_top = of_index(tops)
+        if received is not None:
+            grad_top = jnp.where(section == sections - 1, grad_top, received)
         grad_inner = lax.dot_general(
             grad_top, out_w, (((1,), (1,)), ((), ())), preferred_element_type=jnp.float32
         )
-        grad_conv = (grad_inner * pick(inner_slope, index, 0)).astype(jnp.bfloat16)
+        grad_conv = (grad_inner * of_index(inner_slope)).astype(jnp.bfloat16)
         back = jnp.concatenate(shifts(grad_conv, step), axis=-1)
         grad_hidden = jnp.dot(back, back_kernel, preferred_element_type=jnp.float32)
-        grad_block = (
-            grad_top.astype(jnp.float32) + grad_hidden * pick(slope, index, 0)
-        ).astype(jnp.bfloat16)
-        return grad_top, grad_conv, grad_block
-
-    ticks = micro + LAG * (sections - 1)
-    down_pairs = [(i + 1, i) for i in range(sections - 1)]
-    sent = []
-    done = []
-    for number_of in range(ticks):
-        index = jnp.clip(number_of - LAG * (sections - 1 - section), 0, micro - 1)
-        if number_of == 0:
-            index = 0
-        received = sent[number_of - LAG] if number_of >= LAG else jnp.zeros_like(top[0])
-        result = tick(index, received)
-        done.append(result)
-        if number_of + LAG < ticks:
-            sent.append(lax.ppermute(result[2], "section", down_pairs))
+        grad_block = (grad_top.astype(jnp.float32) + grad_hidden * of_index(slope)).astype(
+            jnp.bfloat16
+        )
+        return lax.optimization_barrier((grad_top, grad_conv, grad_block))
 
     def of_section(m, which):
         value = done[m][which]
@@ -182,48 +204,96 @@
             )
         return value
 
-    grads_out = []
+    def exchange_rows(value, far_value):
+        return jnp.concatenate(
+            [choose(window == 0, value, far_value), choose(window == 0, far_value, value)]
+        )
+
+    half = channels // 2
+    share = half // 2
+    sent, done = [], []
+    near_hidden = far_hidden = None
+    near_grad, far_grad = [None] * micro, [None] * micro
+    back_half = [None] * micro
     conv_total = 0.0
     out_part = 0.0
+    for now in range(ticks):
+        if now < micro:
+            block_in, one_top = arrived(now, *([done[now - 1]] if now else []))
+            one = forward(block_in)
+            tops.append(one_top)
+            hidden.append(one[0])
+            slope.append(one[1])
+            inner_act.append(one[2])
+            inner_slope.append(one[3])
+        received = sent[now - LAG] if now >= LAG else None
+        if received is not None:
+            received = after(received, done[now - 1])
+        done.append(tick(now - LAG * (sections - 1 - section), received))
+        if now + LAG < ticks:
+            sent.append(lax.ppermute(done[now][2], "section", down_pairs))
+        if gathered and now == micro:
+            wide = jnp.concatenate(hidden)
+            mine = choose(side == 0, wide[:, :half], wide[:, half:])
+            other = choose(side == 0, wide[:, half:], wide[:, :half])
+            mine, other = after((mine, other), done[now])
+            near_hidden = (mine, seq_swap(other, 2))
+        if gathered and now == micro + 2:
+            near_hidden = after(near_hidden, done[now])
+            near_hidden = jnp.concatenate(
+                [one.reshape(micro, rows, half) for one in near_hidden], axis=1
+            )
+            far_hidden = dp_swap(near_hidden)
+        m = now - LAG * (sections - 1)
+        if m >= 0:
+            grad_conv = of_section(m, 1)
+            if gathered:
+                near_grad[m] = (grad_conv, seq_swap(grad_conv, 2))
+        if gathered and m >= 1:
+            near_grad[m - 1] = jnp.concatenate(after(near_grad[m - 1], done[now]))
+            far_grad[m - 1] = dp_swap(near_grad[m - 1])
+
+    if gathered:
+        near_grad[-1] = jnp.concatenate(near_grad[-1])
+        far_grad[-1] = dp_swap(near_grad[-1])
     for m in range(micro):
-        grad_top, grad_conv, grad_block = (of_section(m, which) for which in range(3))
         out_part = out_part + lax.dot_general(
-            inner_act[m], grad_top, (((0,), (0,)), ((), ())), preferred_element_type=jnp.float32
-        )
+            inner_act[m],
+            of_section(m, 0),
+            (((0,), (0,)), ((), ())),
+            preferred_element_type=jnp.float32,
+        )
+    if gathered:
+        halves = [out_part[:, :half], out_part[:, half:]]
+        quarters = [[one[:, :share], one[:, share:]] for one in halves]
+        send = [choose(core == 0, one[1], one[0]).astype(jnp.bfloat16) for one in quarters]
+        keep = [choose(core == 0, one[0], one[1]) for one in quarters]
+        come = seq_swap(jnp.stack(send), 1).astype(jnp.float32)
+        columns = [keep[0] + come[0], keep[1] + come[1]]
+        send = choose(side == 0, columns[1], columns[0]).astype(jnp.bfloat16)
+        keep = choose(side == 0, columns[0], columns[1])
+        come = seq_swap(send, 2)
+        columns = (keep + come.astype(jnp.float32)).astype(jnp.bfloat16)
+        out_sum = columns.astype(jnp.float32) + dp_swap(columns).astype(jnp.float32)
+    grads_out = [from_residues(of_section(m, 2)[None], number)[0] for m in range(micro)]
+    for m in range(micro):
         if gathered:
-            near = jnp.stack([grad_conv, seq_swap(grad_conv, 2)])
-            far = dp_swap(near)
-            both = jnp.stack(
-                [jnp.where(window == 0, near, far), jnp.where(window == 0, far, near)]
-            )
-            back = jnp.concatenate(shifts(both, step), axis=-1)
-            conv_total = conv_total + lax.dot_general(
-                hidden_all[:, :, m].reshape(4 * rows, half),
-                back.reshape(4 * rows, 3 * inner),
-                (((0,), (0,)), ((), ())),
-                preferred_element_type=jnp.float32,
-            )
+            all_hidden = exchange_rows(near_hidden[m], far_hidden[m])
+            all_grad = exchange_rows(near_grad[m], far_grad[m]).reshape(4, rows, inner)
+            back = jnp.concatenate(shifts(all_grad, step), axis=-1).reshape(4 * rows, 3 * inner)
         else:
-            back = jnp.concatenate(shifts(grad_conv, step), axis=-1)
-            conv_total = conv_total + lax.dot_general(
-                hidden[m], back, (((0,), (0,)), ((), ())), preferred_element_type=jnp.float32
-            )
-        grads_out.append(from_residues(grad_block[None], number)[0])
+            all_hidden = hidden[m]
+            back = jnp.concatenate(shifts(of_section(m, 1), step), axis=-1)
+        conv_total = conv_total + lax.dot_general(
+            all_hidden, back, (((0,), (0,)), ((), ())), preferred_element_type=jnp.float32
+        )
 
     factor = 1.0 / float(micro * windows)
     if gathered:
-        core = number % 2
-        share = channels // 4
-        split = conv_total.reshape(2, share, 3 * inner)
-        come = seq_swap(pick(split, 1 - core, 0).astype(jnp.bfloat16), 1)
-        conv_sum = pick(split, core, 0) + come.astype(jnp.float32)
-        conv_sum = conv_sum.reshape(share, 3, inner).transpose(1, 0, 2)
-        columns = out_part.reshape(inner, 2, 2, share)
-        come = seq_swap(pick(columns, 1 - core, 2).astype(jnp.bfloat16), 1)
-        columns = pick(columns, core, 2) + come.astype(jnp.float32)
-        come = seq_swap(pick(columns, 1 - side, 1).astype(jnp.bfloat16), 2)
-        columns = (pick(columns, side, 1) + come.astype(jnp.float32)).astype(jnp.bfloat16)
-        out_sum = columns.astype(jnp.float32) + dp_swap(columns).astype(jnp.float32)
+        low, high = conv_total[:share], conv_total[share:]
+        come = seq_swap(choose(core == 0, high, low).astype(jnp.bfloat16), 1)
+        conv_sum = choose(core == 0, low, high) + come.astype(jnp.float32)
+        conv_sum = jnp.stack([conv_sum[:, k * inner : (k + 1) * inner] for k in range(3)])
     else:
         conv_part = conv_total.reshape(channels, 3, inner).transpose(1, 0, 2)
         conv_sum, out_sum = (

time: 135 us -> 95.5 us (0.71)
  local copies, waits for them, and re-layouts: 20 us -> 5 us
  other arithmetic: 22.5 us -> 10.5 us
  waiting for transfers between devices: 44.9 us -> 33.4 us
  matrix products: 14.3 us -> 11.9 us
  starting transfers between devices: 29.7 us -> 31.3 us
    ppermute x7, waiting for transfers between devices: 26 us -> 11.8 us  [on_device(): sent.append(lax.ppermute(done[now][2], 'section', down_pairs))]
    another operation x17 -> x12, other arithmetic: 7.89 us -> 1.81 us  [the longest x2 1.26 us: on_device(): jnp.stack([choose(core == 0, keep, come), choose(core == 0, come, keep)], 1)]
    unnamed x122 -> x20, local copies, waits for them, and re-layouts: 9.26 us -> 3.68 us
    another operation x18 -> x11, other arithmetic: 5.22 us -> 0.27 us  [exchange(): jnp.stack([first, second], axis=1)]
    ppermute x17, waiting for transfers between devices: 7.58 us -> 11.4 us  [seq_swap(): return lax.ppermute(value, 'seq', [(i, i ^ bit) for i in range(count)])]
    convert_element_type x6 -> x0, local copies, waits for them, and re-layouts: 3.03 us -> none  [the longest x3 2.9 us: forward(): pre = block_in.astype(jnp.float32) * norm_scale[0] + norm_shift[0]]
    slice x4 -> x0, local copies, waits for them, and re-layouts: 2.06 us -> none  [the longest x2 2 us: on_device(): first = to_residues(jnp.stack([inputs[0], top[0]]), number)]
    dot_general x9, matrix products: 5.79 us -> 4.12 us  [tick(): grad_hidden = jnp.dot(back, back_kernel, preferred_element_type=jnp.float32)]
  transfers between devices with their start and end apart: 29 -> 29, of which waited for: 13 -> 16; matrix products, arithmetic and copies ran while one was open for 27% -> 24% of each run, Pallas kernels for 0% -> 1%
where the time goes in v2:
time: 95.5 us; the launch traced here: 95.1 us
  waiting for transfers between devices  33.4 us (35%)
  starting transfers between devices  31.3 us (33%)
  matrix products  11.9 us (12%)
  other arithmetic  10.5 us (11%)
  local copies, waits for them, and re-layouts  5 us (5%)
  between operations  1.7 us (2%)
  Pallas kernels  1.26 us (1%)
    ppermute x17, starting transfers between devices, seq_swap(): return lax.ppermute(value, 'seq', [(i, i ^ bit) for i in range(count)])  14.8 us
    ppermute x7, waiting for transfers between devices, on_device(): sent.append(lax.ppermute(done[now][2], 'section', down_pairs))  11.8 us
    ppermute x17, waiting for transfers between devices, seq_swap(): return lax.ppermute(value, 'seq', [(i, i ^ bit) for i in range(count)])  11.4 us
    ppermute x5, waiting for transfers between devices, dp_swap(): return lax.ppermute(value, 'dp', [(0, 1), (1, 0)])  10.2 us
    ppermute x7, starting transfers between devices, on_device(): sent.append(lax.ppermute(done[now][2], 'section', down_pairs))  9.23 us
    ppermute x5, starting transfers between devices, dp_swap(): return lax.ppermute(value, 'dp', [(0, 1), (1, 0)])  7.28 us
    dot_general x9, matrix products, tick(): grad_hidden = jnp.dot(back, back_kernel, preferred_element_type=jnp.float32)  4.12 us
    unnamed x20, local copies, waits for them, and re-layouts  3.68 us
  transfers between devices with their start and end apart: 29, of which 16 were waited for; matrix products, arithmetic and copies ran while one was open for 24% of the time, Pallas kernels for 1%

profile of v2, /device:TPU:0, one launch (start us, length us, event | category | flops | bytes accessed | tf_op | source)
XLA Modules:
  0.0 95.1 jit_solution(9984158466575967556)
XLA Ops:
  0.7 2.0 %fusion.41 = bf16[6,4,2,8,768]{4,3,2,1,0:T(8,128)(2,1)} fusion(s32[]{:T(128)S(6)} %select_n.743, bf16[3,4,2,2,8,768]{5,4,3,2,1,0:T(8,128)(2,1)} %bitcast.346, bf16[3,4,2,2,8,768]{5,4,3,2,1,0:T(8,128)(2,1)} %bitcast.348), kind=kLoop, calls=%fused_computation.91 | loop fusion | flops 294912 | bytes 1769476 | tf_op jit(solution)/shard_map/jit(dynamic_index_in_dim)/squeeze | solution.py:36
  3.2 1.3 %shard_map.103 = f32[1,768]{1,0:T(1,128)} custom-call(f32[1,768]{1,0:T(1,128)} %value_ref.1), custom_call_target="tpu_custom_call" | custom-call | tf_op jit(solution)/shard_map/pallas_call | solution.py:89
  5.2 2.7 %copy.43 = bf16[1,3,768,384]{2,3,1,0:T(8,128)(2,1)S(1)} copy(bf16[1,3,768,384]{3,2,1,0:T(8,128)(2,1)} %param.10) | data formatting | bytes 3538944 | tf_op args[2]
  8.0 1.2 %select_bitcast_fusion.1 = (bf16[6,1,4,2,8,768]{5,4,3,2,0,1:T(8,128)(2,1)S(1)}, bf16[6,1,4,2,8,768]{5,4,3,2,0,1:T(8,128)(2,1)S(1)}) fusion(bf16[6,4,2,8,768]{4,3,2,1,0:T(8,128)(2,1)} %collective-permute-done, pred[]{:T(512)S(6)} %eq.26, s32[]{:T(128)S(6)} %select_n.742, bf16[3,4,2,2,8,768]{5,4,3,2,1,0:T(8,128)(2,1)S(1)} %bitcast.349, ...), kind=kLoop, calls=%fused_computation.120 | loop fusion | flops 1179648 | bytes 2949125 | tf_op jit(solution)/shard_map/stack | solution.py:157
  9.4 2.6 %collective-permute-start.3 = (bf16[2,2,4,8,768]{4,3,2,1,0:T(8,128)(2,1)S(1)}, bf16[2,2,4,8,768]{4,3,2,1,0:T(8,128)(2,1)S(1)}, u32[]{:S(2)}, u32[]{:S(2)}) collective-permute-start(bf16[2,2,4,8,768]{4,3,2,1,0:T(8,128)(2,1)S(1)} %bitcast.376), channel_id=1, source_target_pairs={{0,2},{1,3},{2,0},{3,1},{4,6},{5,7},{6,4},{7,5},{8,10},{9,11},{10,... | collective-permute-start | bytes 589832 | tf_op jit(solution)/shard_map/ppermute | solution.py:28
  12.2 2.0 %collective-permute-start.2 = (bf16[2,2,4,8,768]{4,3,2,1,0:T(8,128)(2,1)S(1)}, bf16[2,2,4,8,768]{4,3,2,1,0:T(8,128)(2,1)S(1)}, u32[]{:S(2)}, u32[]{:S(2)}) collective-permute-start(bf16[2,2,4,8,768]{4,3,2,1,0:T(8,128)(2,1)S(1)} %bitcast.375), channel_id=1, source_target_pairs={{0,2},{1,3},{2,0},{3,1},{4,6},{5,7},{6,4},{7,5},{8,10},{9,11},{10,... | collective-permute-start | bytes 589832 | tf_op jit(solution)/shard_map/ppermute | solution.py:28
  14.2 3.5 %collective-permute-done.3 = bf16[2,2,4,8,768]{4,3,2,1,0:T(8,128)(2,1)S(1)} collective-permute-done((bf16[2,2,4,8,768]{4,3,2,1,0:T(8,128)(2,1)S(1)}, bf16[2,2,4,8,768]{4,3,2,1,0:T(8,128)(2,1)S(1)}, u32[]{:S(2)}, u32[]{:S(2)}) %collective-permute-start.3) | collective-permute-done | bytes 196640 | tf_op jit(solution)/shard_map/ppermute | solution.py:28
  19.6 1.3 %collective-permute-start.4 = (bf16[128,768]{1,0:T(8,128)(2,1)S(1)}, bf16[128,768]{1,0:T(8,128)(2,1)S(1)}, u32[]{:S(2)}, u32[]{:S(2)}) collective-permute-start(bf16[128,768]{1,0:T(8,128)(2,1)S(1)} %fusion.25), channel_id=1, source_target_pairs={{4,0},{8,4},{12,8},{5,1},{9,5},{13,9},{6,2},{10,6},{14,10},{7,3},{... | collective-permute-start | bytes 589832 | tf_op jit(solution)/shard_map/ppermute | solution.py:234
  20.9 5.0 %collective-permute-done.2 = bf16[2,2,4,8,768]{4,3,2,1,0:T(8,128)(2,1)S(1)} collective-permute-done((bf16[2,2,4,8,768]{4,3,2,1,0:T(8,128)(2,1)S(1)}, bf16[2,2,4,8,768]{4,3,2,1,0:T(8,128)(2,1)S(1)}, u32[]{:S(2)}, u32[]{:S(2)}) %collective-permute-start.2) | collective-permute-done | bytes 196640 | tf_op jit(solution)/shard_map/ppermute | solution.py:28
  27.9 1.3 %collective-permute-start.6 = (bf16[128,768]{1,0:T(8,128)(2,1)S(1)}, bf16[128,768]{1,0:T(8,128)(2,1)S(1)}, u32[]{:S(2)}, u32[]{:S(2)}) collective-permute-start(bf16[128,768]{1,0:T(8,128)(2,1)S(1)} %fusion.24), channel_id=1, source_target_pairs={{4,0},{8,4},{12,8},{5,1},{9,5},{13,9},{6,2},{10,6},{14,10},{7,3},{... | collective-permute-start | bytes 589832 | tf_op jit(solution)/shard_map/ppermute | solution.py:234
  31.4 1.3 %collective-permute-start.5 = (bf16[128,768]{1,0:T(8,128)(2,1)S(1)}, bf16[128,768]{1,0:T(8,128)(2,1)S(1)}, u32[]{:S(2)}, u32[]{:S(2)}) collective-permute-start(bf16[128,768]{1,0:T(8,128)(2,1)S(1)} %add_convert_fusion.7), channel_id=1, source_target_pairs={{4,0},{8,4},{12,8},{5,1},{9,5},{13,9},{6,2},{10,6},{14,10},{7,3},{... | collective-permute-start | bytes 589832 | tf_op jit(solution)/shard_map/ppermute | solution.py:234
  32.7 3.9 %collective-permute-done.6 = bf16[128,768]{1,0:T(8,128)(2,1)S(1)} collective-permute-done((bf16[128,768]{1,0:T(8,128)(2,1)S(1)}, bf16[128,768]{1,0:T(8,128)(2,1)S(1)}, u32[]{:S(2)}, u32[]{:S(2)}) %collective-permute-start.6) | collective-permute-done | bytes 196640 | tf_op jit(solution)/shard_map/ppermute | solution.py:234
  37.5 1.3 %collective-permute-start.8 = (bf16[128,768]{1,0:T(8,128)(2,1)S(1)}, bf16[128,768]{1,0:T(8,128)(2,1)S(1)}, u32[]{:S(2)}, u32[]{:S(2)}) collective-permute-start(bf16[128,768]{1,0:T(8,128)(2,1)S(1)} %add_convert_fusion.6), channel_id=1, source_target_pairs={{4,0},{8,4},{12,8},{5,1},{9,5},{13,9},{6,2},{10,6},{14,10},{7,3},{... | collective-permute-start | bytes 589832 | tf_op jit(solution)/shard_map/ppermute | solution.py:234
  38.8 1.6 %collective-permute-start.17 = (bf16[384,384]{1,0:T(8,128)(2,1)S(1)}, bf16[384,384]{1,0:T(8,128)(2,1)S(1)}, u32[]{:S(2)}, u32[]{:S(2)}) collective-permute-start(bf16[384,384]{1,0:T(8,128)(2,1)S(1)} %get-tuple-element.103), channel_id=1, source_target_pairs={{0,2},{1,3},{2,0},{3,1},{4,6},{5,7},{6,4},{7,5},{8,10},{9,11},{10,... | collective-permute-start | bytes 884744 | tf_op jit(solution)/shard_map/ppermute | solution.py:28
  41.7 1.3 %collective-permute-start.7 = (bf16[128,768]{1,0:T(8,128)(2,1)S(1)}, bf16[128,768]{1,0:T(8,128)(2,1)S(1)}, u32[]{:S(2)}, u32[]{:S(2)}) collective-permute-start(bf16[128,768]{1,0:T(8,128)(2,1)S(1)} %add_convert_fusion.5), channel_id=1, source_target_pairs={{4,0},{8,4},{12,8},{5,1},{9,5},{13,9},{6,2},{10,6},{14,10},{7,3},{... | collective-permute-start | bytes 589832 | tf_op jit(solution)/shard_map/ppermute | solution.py:234
  43.0 2.2 %collective-permute-done.8 = bf16[128,768]{1,0:T(8,128)(2,1)S(1)} collective-permute-done((bf16[128,768]{1,0:T(8,128)(2,1)S(1)}, bf16[128,768]{1,0:T(8,128)(2,1)S(1)}, u32[]{:S(2)}, u32[]{:S(2)}) %collective-permute-start.8) | collective-permute-done | bytes 196640 | tf_op jit(solution)/shard_map/ppermute | solution.py:234
  46.1 1.3 %collective-permute-start.11 = (bf16[128,768]{1,0:T(8,128)(2,1)S(1)}, bf16[128,768]{1,0:T(8,128)(2,1)S(1)}, u32[]{:S(2)}, u32[]{:S(2)}) collective-permute-start(bf16[128,768]{1,0:T(8,128)(2,1)S(1)} %add_convert_fusion.4), channel_id=1, source_target_pairs={{4,0},{8,4},{12,8},{5,1},{9,5},{13,9},{6,2},{10,6},{14,10},{7,3},{... | collective-permute-start | bytes 589832 | tf_op jit(solution)/shard_map/ppermute | solution.py:234
  47.5 1.4 %collective-permute-start.18 = (bf16[3,256,384]{2,1,0:T(8,128)(2,1)S(1)}, bf16[3,256,384]{2,1,0:T(8,128)(2,1)S(1)}, u32[]{:S(2)}, u32[]{:S(2)}) collective-permute-start(bf16[3,256,384]{2,1,0:T(8,128)(2,1)S(1)} %pad_maximum_fusion), channel_id=1, source_target_pairs={{0,16},{16,0},{1,17},{17,1},{2,18},{18,2},{3,19},{19,3},{4,20},{20... | collective-permute-start | bytes 1769480 | tf_op jit(solution)/shard_map/ppermute | solution.py:32
  49.0 1.4 %collective-permute-done.7 = bf16[128,768]{1,0:T(8,128)(2,1)S(1)} collective-permute-done((bf16[128,768]{1,0:T(8,128)(2,1)S(1)}, bf16[128,768]{1,0:T(8,128)(2,1)S(1)}, u32[]{:S(2)}, u32[]{:S(2)}) %collective-permute-start.7) | collective-permute-done | bytes 196640 | tf_op jit(solution)/shard_map/ppermute | solution.py:234
  51.3 1.5 %collective-permute-start.14 = (bf16[128,768]{1,0:T(8,128)(2,1)S(1)}, bf16[128,768]{1,0:T(8,128)(2,1)S(1)}, u32[]{:S(2)}, u32[]{:S(2)}) collective-permute-start(bf16[128,768]{1,0:T(8,128)(2,1)S(1)} %add_convert_fusion.3), channel_id=1, source_target_pairs={{4,0},{8,4},{12,8},{5,1},{9,5},{13,9},{6,2},{10,6},{14,10},{7,3},{... | collective-permute-start | bytes 589832 | tf_op jit(solution)/shard_map/ppermute | solution.py:234
  52.8 2.0 %collective-permute-done.11 = bf16[128,768]{1,0:T(8,128)(2,1)S(1)} collective-permute-done((bf16[128,768]{1,0:T(8,128)(2,1)S(1)}, bf16[128,768]{1,0:T(8,128)(2,1)S(1)}, u32[]{:S(2)}, u32[]{:S(2)}) %collective-permute-start.11) | collective-permute-done | bytes 196640 | tf_op jit(solution)/shard_map/ppermute | solution.py:234
  55.9 1.1 %collective-permute-start.21 = (bf16[128,384]{1,0:T(8,128)(2,1)S(1)}, bf16[128,384]{1,0:T(8,128)(2,1)S(1)}, u32[]{:S(2)}, u32[]{:S(2)}) collective-permute-start(bf16[128,384]{1,0:T(8,128)(2,1)S(1)} %select_select_fusion.4), channel_id=1, source_target_pairs={{0,2},{1,3},{2,0},{3,1},{4,6},{5,7},{6,4},{7,5},{8,10},{9,11},{10,... | collective-permute-start | bytes 294920 | tf_op jit(solution)/shard_map/ppermute | solution.py:28
  57.8 1.9 %collective-permute-done.14 = bf16[128,768]{1,0:T(8,128)(2,1)S(1)} collective-permute-done((bf16[128,768]{1,0:T(8,128)(2,1)S(1)}, bf16[128,768]{1,0:T(8,128)(2,1)S(1)}, u32[]{:S(2)}, u32[]{:S(2)}) %collective-permute-start.14) | collective-permute-done | bytes 196640 | tf_op jit(solution)/shard_map/ppermute | solution.py:234
  64.4 1.6 %collective-permute-start.22 = (bf16[256,384]{1,0:T(8,128)(2,1)S(1)}, bf16[256,384]{1,0:T(8,128)(2,1)S(1)}, u32[]{:S(2)}, u32[]{:S(2)}) collective-permute-start(bf16[256,384]{1,0:T(8,128)(2,1)S(1)} %constant_dynamic-update-slice_fusion.5), channel_id=1, source_target_pairs={{0,16},{16,0},{1,17},{17,1},{2,18},{18,2},{3,19},{19,3},{4,20},{20... | collective-permute-start | bytes 589832 | tf_op jit(solution)/shard_map/ppermute | solution.py:32
  66.4 1.1 %collective-permute-done.19 = bf16[128,384]{1,0:T(8,128)(2,1)S(1)} collective-permute-done((bf16[128,384]{1,0:T(8,128)(2,1)S(1)}, bf16[128,384]{1,0:T(8,128)(2,1)S(1)}, u32[]{:S(2)}, u32[]{:S(2)}) %collective-permute-start.19) | collective-permute-done | bytes 98336 | tf_op jit(solution)/shard_map/ppermute | solution.py:28
  69.7 1.1 %collective-permute-done.22 = bf16[256,384]{1,0:T(8,128)(2,1)S(1)} collective-permute-done((bf16[256,384]{1,0:T(8,128)(2,1)S(1)}, bf16[256,384]{1,0:T(8,128)(2,1)S(1)}, u32[]{:S(2)}, u32[]{:S(2)}) %collective-permute-start.22) | collective-permute-done | bytes 196640 | tf_op jit(solution)/shard_map/ppermute | solution.py:32
  72.0 1.2 %collective-permute-done.10 = bf16[1,2,4,1,8,768]{5,4,1,2,3,0:T(8,128)(2,1)S(1)} collective-permute-done((bf16[1,2,4,1,8,768]{5,4,1,2,3,0:T(8,128)(2,1)S(1)}, bf16[1,2,4,1,8,768]{5,4,1,2,3,0:T(8,128)(2,1)S(1)}, u32[]{:S(2)}, u32[]{:S(2)}) %collective-permute-start.10) | collective-permute-done | bytes 98336 | tf_op jit(solution)/shard_map/ppermute | solution.py:28
  73.2 1.4 %collective-permute-start.24 = (bf16[256,384]{1,0:T(8,128)(2,1)S(1)}, bf16[256,384]{1,0:T(8,128)(2,1)S(1)}, u32[]{:S(2)}, u32[]{:S(2)}) collective-permute-start(bf16[256,384]{1,0:T(8,128)(2,1)S(1)} %pad_maximum_fusion.11), channel_id=1, source_target_pairs={{0,16},{16,0},{1,17},{17,1},{2,18},{18,2},{3,19},{19,3},{4,20},{20... | collective-permute-start | bytes 589832 | tf_op jit(solution)/shard_map/ppermute | solution.py:32
  74.8 1.5 %collective-permute-start.20 = (bf16[256,384]{1,0:T(8,128)(2,1)S(1)}, bf16[256,384]{1,0:T(8,128)(2,1)S(1)}, u32[]{:S(2)}, u32[]{:S(2)}) collective-permute-start(bf16[256,384]{1,0:T(8,128)(2,1)S(1)} %constant_dynamic-update-slice_fusion.3), channel_id=1, source_target_pairs={{0,16},{16,0},{1,17},{17,1},{2,18},{18,2},{3,19},{19,3},{4,20},{20... | collective-permute-start | bytes 589832 | tf_op jit(solution)/shard_map/ppermute | solution.py:32
  77.8 3.9 %collective-permute-done.20 = bf16[256,384]{1,0:T(8,128)(2,1)S(1)} collective-permute-done((bf16[256,384]{1,0:T(8,128)(2,1)S(1)}, bf16[256,384]{1,0:T(8,128)(2,1)S(1)}, u32[]{:S(2)}, u32[]{:S(2)}) %collective-permute-start.20) | collective-permute-done | bytes 196640 | tf_op jit(solution)/shard_map/ppermute | solution.py:32
  85.6 1.3 %collective-permute-start.28 = (bf16[384,192]{1,0:T(8,128)(2,1)S(1)}, bf16[384,192]{1,0:T(8,128)(2,1)S(1)}, u32[]{:S(2)}, u32[]{:S(2)}) collective-permute-start(bf16[384,192]{1,0:T(8,128)(2,1)S(1)} %add_convert_fusion), channel_id=1, source_target_pairs={{0,16},{16,0},{1,17},{17,1},{2,18},{18,2},{3,19},{19,3},{4,20},{20... | collective-permute-start | bytes 442376 | tf_op jit(solution)/shard_map/ppermute | solution.py:32
  87.8 5.2 %collective-permute-done.28 = bf16[384,192]{1,0:T(8,128)(2,1)S(1)} collective-permute-done((bf16[384,192]{1,0:T(8,128)(2,1)S(1)}, bf16[384,192]{1,0:T(8,128)(2,1)S(1)}, u32[]{:S(2)}, u32[]{:S(2)}) %collective-permute-start.28) | collective-permute-done | bytes 147488 | tf_op jit(solution)/shard_map/ppermute | solution.py:32
  (166 shorter events, 30.0 us)
Async XLA Ops:
  0.6 18.1 %copy-start = (bf16[1,384,768]{2,1,0:T(8,128)(2,1)S(1)}, bf16[1,384,768]{2,1,0:T(8,128)(2,1)}, u32[]{:S(2)}) copy-start(bf16[1,384,768]{2,1,0:T(8,128)(2,1)} %param.11) | copy-start | bytes 1769476
  0.7 4.5 %copy-start.4 = (f32[1,768]{1,0:T(1,128)S(1)}, f32[1,768]{1,0:T(1,128)}, u32[]{:S(2)}) copy-start(f32[1,768]{1,0:T(1,128)} %param.13) | copy-start | bytes 9220
  2.7 5.3 %collective-permute-start = (bf16[6,4,2,8,768]{4,3,2,1,0:T(8,128)(2,1)}, bf16[6,4,2,8,768]{4,3,2,1,0:T(8,128)(2,1)}, u32[]{:S(2)}, u32[]{:S(2)}) collective-permute-start(bf16[6,4,2,8,768]{4,3,2,1,0:T(8,128)(2,1)} %fusion.41), channel_id=1, source_target_pairs={{0,1},{1,0},{2,3},{3,2},{4,5},{5,4},{6,7},{7,6},{8,9},{9,8},{10,11... | collective-permute-start | bytes 1769480 | tf_op jit(solution)/shard_map/ppermute | solution.py:28
  9.4 8.3 %collective-permute-start.3 = (bf16[2,2,4,8,768]{4,3,2,1,0:T(8,128)(2,1)S(1)}, bf16[2,2,4,8,768]{4,3,2,1,0:T(8,128)(2,1)S(1)}, u32[]{:S(2)}, u32[]{:S(2)}) collective-permute-start(bf16[2,2,4,8,768]{4,3,2,1,0:T(8,128)(2,1)S(1)} %bitcast.376), channel_id=1, source_target_pairs={{0,2},{1,3},{2,0},{3,1},{4,6},{5,7},{6,4},{7,5},{8,10},{9,11},{10,... | collective-permute-start | bytes 589832 | tf_op jit(solution)/shard_map/ppermute | solution.py:28
  12.1 6.1 %copy-start.3 = (bf16[1,3,768,384]{3,2,1,0:T(8,128)(2,1)S(1)}, bf16[1,3,768,384]{3,2,1,0:T(8,128)(2,1)}, u32[]{:S(2)}) copy-start(bf16[1,3,768,384]{3,2,1,0:T(8,128)(2,1)} %param.10) | copy-start | bytes 5308420
  12.1 17.1 %collective-permute-start.1 = (bf16[2,2,4,8,768]{4,3,2,1,0:T(8,128)(2,1)S(1)}, bf16[2,2,4,8,768]{4,3,2,1,0:T(8,128)(2,1)S(1)}, u32[]{:S(2)}, u32[]{:S(2)}) collective-permute-start(bf16[2,2,4,8,768]{4,3,2,1,0:T(8,128)(2,1)S(1)} %bitcast.374), channel_id=1, source_target_pairs={{0,2},{1,3},{2,0},{3,1},{4,6},{5,7},{6,4},{7,5},{8,10},{9,11},{10,... | collective-permute-start | bytes 589832 | tf_op jit(solution)/shard_map/ppermute | solution.py:28
  12.2 13.7 %collective-permute-start.2 = (bf16[2,2,4,8,768]{4,3,2,1,0:T(8,128)(2,1)S(1)}, bf16[2,2,4,8,768]{4,3,2,1,0:T(8,128)(2,1)S(1)}, u32[]{:S(2)}, u32[]{:S(2)}) collective-permute-start(bf16[2,2,4,8,768]{4,3,2,1,0:T(8,128)(2,1)S(1)} %bitcast.375), channel_id=1, source_target_pairs={{0,2},{1,3},{2,0},{3,1},{4,6},{5,7},{6,4},{7,5},{8,10},{9,11},{10,... | collective-permute-start | bytes 589832 | tf_op jit(solution)/shard_map/ppermute | solution.py:28
  19.6 10.8 %collective-permute-start.4 = (bf16[128,768]{1,0:T(8,128)(2,1)S(1)}, bf16[128,768]{1,0:T(8,128)(2,1)S(1)}, u32[]{:S(2)}, u32[]{:S(2)}) collective-permute-start(bf16[128,768]{1,0:T(8,128)(2,1)S(1)} %fusion.25), channel_id=1, source_target_pairs={{4,0},{8,4},{12,8},{5,1},{9,5},{13,9},{6,2},{10,6},{14,10},{7,3},{... | collective-permute-start | bytes 589832 | tf_op jit(solution)/shard_map/ppermute | solution.py:234
  27.9 8.7 %collective-permute-start.6 = (bf16[128,768]{1,0:T(8,128)(2,1)S(1)}, bf16[128,768]{1,0:T(8,128)(2,1)S(1)}, u32[]{:S(2)}, u32[]{:S(2)}) collective-permute-start(bf16[128,768]{1,0:T(8,128)(2,1)S(1)} %fusion.24), channel_id=1, source_target_pairs={{4,0},{8,4},{12,8},{5,1},{9,5},{13,9},{6,2},{10,6},{14,10},{7,3},{... | collective-permute-start | bytes 589832 | tf_op jit(solution)/shard_map/ppermute | solution.py:234
  31.4 9.4 %collective-permute-start.5 = (bf16[128,768]{1,0:T(8,128)(2,1)S(1)}, bf16[128,768]{1,0:T(8,128)(2,1)S(1)}, u32[]{:S(2)}, u32[]{:S(2)}) collective-permute-start(bf16[128,768]{1,0:T(8,128)(2,1)S(1)} %add_convert_fusion.7), channel_id=1, source_target_pairs={{4,0},{8,4},{12,8},{5,1},{9,5},{13,9},{6,2},{10,6},{14,10},{7,3},{... | collective-permute-start | bytes 589832 | tf_op jit(solution)/shard_map/ppermute | solution.py:234
  37.5 7.7 %collective-permute-start.8 = (bf16[128,768]{1,0:T(8,128)(2,1)S(1)}, bf16[128,768]{1,0:T(8,128)(2,1)S(1)}, u32[]{:S(2)}, u32[]{:S(2)}) collective-permute-start(bf16[128,768]{1,0:T(8,128)(2,1)S(1)} %add_convert_fusion.6), channel_id=1, source_target_pairs={{4,0},{8,4},{12,8},{5,1},{9,5},{13,9},{6,2},{10,6},{14,10},{7,3},{... | collective-permute-start | bytes 589832 | tf_op jit(solution)/shard_map/ppermute | solution.py:234
  38.8 8.6 %collective-permute-start.17 = (bf16[384,384]{1,0:T(8,128)(2,1)S(1)}, bf16[384,384]{1,0:T(8,128)(2,1)S(1)}, u32[]{:S(2)}, u32[]{:S(2)}) collective-permute-start(bf16[384,384]{1,0:T(8,128)(2,1)S(1)} %get-tuple-element.103), channel_id=1, source_target_pairs={{0,2},{1,3},{2,0},{3,1},{4,6},{5,7},{6,4},{7,5},{8,10},{9,11},{10,... | collective-permute-start | bytes 884744 | tf_op jit(solution)/shard_map/ppermute | solution.py:28
  41.7 8.7 %collective-permute-start.7 = (bf16[128,768]{1,0:T(8,128)(2,1)S(1)}, bf16[128,768]{1,0:T(8,128)(2,1)S(1)}, u32[]{:S(2)}, u32[]{:S(2)}) collective-permute-start(bf16[128,768]{1,0:T(8,128)(2,1)S(1)} %add_convert_fusion.5), channel_id=1, source_target_pairs={{4,0},{8,4},{12,8},{5,1},{9,5},{13,9},{6,2},{10,6},{14,10},{7,3},{... | collective-permute-start | bytes 589832 | tf_op jit(solution)/shard_map/ppermute | solution.py:234
  46.1 8.7 %collective-permute-start.11 = (bf16[128,768]{1,0:T(8,128)(2,1)S(1)}, bf16[128,768]{1,0:T(8,128)(2,1)S(1)}, u32[]{:S(2)}, u32[]{:S(2)}) collective-permute-start(bf16[128,768]{1,0:T(8,128)(2,1)S(1)} %add_convert_fusion.4), channel_id=1, source_target_pairs={{4,0},{8,4},{12,8},{5,1},{9,5},{13,9},{6,2},{10,6},{14,10},{7,3},{... | collective-permute-start | bytes 589832 | tf_op jit(solution)/shard_map/ppermute | solution.py:234
  47.5 34.8 %collective-permute-start.18 = (bf16[3,256,384]{2,1,0:T(8,128)(2,1)S(1)}, bf16[3,256,384]{2,1,0:T(8,128)(2,1)S(1)}, u32[]{:S(2)}, u32[]{:S(2)}) collective-permute-start(bf16[3,256,384]{2,1,0:T(8,128)(2,1)S(1)} %pad_maximum_fusion), channel_id=1, source_target_pairs={{0,16},{16,0},{1,17},{17,1},{2,18},{18,2},{3,19},{19,3},{4,20},{20... | collective-permute-start | bytes 1769480 | tf_op jit(solution)/shard_map/ppermute | solution.py:32
  51.3 8.4 %collective-permute-start.14 = (bf16[128,768]{1,0:T(8,128)(2,1)S(1)}, bf16[128,768]{1,0:T(8,128)(2,1)S(1)}, u32[]{:S(2)}, u32[]{:S(2)}) collective-permute-start(bf16[128,768]{1,0:T(8,128)(2,1)S(1)} %add_convert_fusion.3), channel_id=1, source_target_pairs={{4,0},{8,4},{12,8},{5,1},{9,5},{13,9},{6,2},{10,6},{14,10},{7,3},{... | collective-permute-start | bytes 589832 | tf_op jit(solution)/shard_map/ppermute | solution.py:234
  55.8 1.9 %collective-permute-start.12 = (bf16[1,1,4,2,8,768]{5,4,2,3,1,0:T(8,128)(2,1)S(1)}, bf16[1,1,4,2,8,768]{5,4,2,3,1,0:T(8,128)(2,1)S(1)}, u32[]{:S(2)}, u32[]{:S(2)}) collective-permute-start(bf16[1,1,4,2,8,768]{5,4,2,3,1,0:T(8,128)(2,1)S(1)} %dynamic-slice_bitcast_fusion.1), channel_id=1, source_target_pairs={{0,1},{1,0},{2,3},{3,2},{4,5},{5,4},{6,7},{7,6},{8,9},{9,8},{10,11... | collective-permute-start | bytes 294920 | tf_op jit(solution)/shard_map/ppermute | solution.py:28
  55.9 5.2 %collective-permute-start.21 = (bf16[128,384]{1,0:T(8,128)(2,1)S(1)}, bf16[128,384]{1,0:T(8,128)(2,1)S(1)}, u32[]{:S(2)}, u32[]{:S(2)}) collective-permute-start(bf16[128,384]{1,0:T(8,128)(2,1)S(1)} %select_select_fusion.4), channel_id=1, source_target_pairs={{0,2},{1,3},{2,0},{3,1},{4,6},{5,7},{6,4},{7,5},{8,10},{9,11},{10,... | collective-permute-start | bytes 294920 | tf_op jit(solution)/shard_map/ppermute | solution.py:28
  61.2 3.2 %collective-permute-start.9 = (bf16[1,1,4,2,8,768]{5,4,2,3,1,0:T(8,128)(2,1)S(1)}, bf16[1,1,4,2,8,768]{5,4,2,3,1,0:T(8,128)(2,1)S(1)}, u32[]{:S(2)}, u32[]{:S(2)}) collective-permute-start(bf16[1,1,4,2,8,768]{5,4,2,3,1,0:T(8,128)(2,1)S(1)} %dynamic-slice_bitcast_fusion.2), channel_id=1, source_target_pairs={{0,1},{1,0},{2,3},{3,2},{4,5},{5,4},{6,7},{7,6},{8,9},{9,8},{10,11... | collective-permute-start | bytes 294920 | tf_op jit(solution)/shard_map/ppermute | solution.py:28
  61.3 4.9 %collective-permute-start.15 = (bf16[1,1,4,2,8,768]{5,4,2,3,1,0:T(8,128)(2,1)S(1)}, bf16[1,1,4,2,8,768]{5,4,2,3,1,0:T(8,128)(2,1)S(1)}, u32[]{:S(2)}, u32[]{:S(2)}) collective-permute-start(bf16[1,1,4,2,8,768]{5,4,2,3,1,0:T(8,128)(2,1)S(1)} %dynamic-slice_bitcast_fusion), channel_id=1, source_target_pairs={{0,1},{1,0},{2,3},{3,2},{4,5},{5,4},{6,7},{7,6},{8,9},{9,8},{10,11... | collective-permute-start | bytes 294920 | tf_op jit(solution)/shard_map/ppermute | solution.py:28
  61.8 5.7 %collective-permute-start.19 = (bf16[128,384]{1,0:T(8,128)(2,1)S(1)}, bf16[128,384]{1,0:T(8,128)(2,1)S(1)}, u32[]{:S(2)}, u32[]{:S(2)}) collective-permute-start(bf16[128,384]{1,0:T(8,128)(2,1)S(1)} %get-tuple-element.106), channel_id=1, source_target_pairs={{0,2},{1,3},{2,0},{3,1},{4,6},{5,7},{6,4},{7,5},{8,10},{9,11},{10,... | collective-permute-start | bytes 294920 | tf_op jit(solution)/shard_map/ppermute | solution.py:28
  62.8 5.8 %collective-permute-start.23 = (bf16[128,384]{1,0:T(8,128)(2,1)S(1)}, bf16[128,384]{1,0:T(8,128)(2,1)S(1)}, u32[]{:S(2)}, u32[]{:S(2)}) collective-permute-start(bf16[128,384]{1,0:T(8,128)(2,1)S(1)} %get-tuple-element.180), channel_id=1, source_target_pairs={{0,2},{1,3},{2,0},{3,1},{4,6},{5,7},{6,4},{7,5},{8,10},{9,11},{10,... | collective-permute-start | bytes 294920 | tf_op jit(solution)/shard_map/ppermute | solution.py:28
  64.4 6.4 %collective-permute-start.22 = (bf16[256,384]{1,0:T(8,128)(2,1)S(1)}, bf16[256,384]{1,0:T(8,128)(2,1)S(1)}, u32[]{:S(2)}, u32[]{:S(2)}) collective-permute-start(bf16[256,384]{1,0:T(8,128)(2,1)S(1)} %constant_dynamic-update-slice_fusion.5), channel_id=1, source_target_pairs={{0,16},{16,0},{1,17},{17,1},{2,18},{18,2},{3,19},{19,3},{4,20},{20... | collective-permute-start | bytes 589832 | tf_op jit(solution)/shard_map/ppermute | solution.py:32
  66.2 10.2 %collective-permute-start.26 = (bf16[2,384,192]{2,1,0:T(8,128)(2,1)S(1)}, bf16[2,384,192]{2,1,0:T(8,128)(2,1)S(1)}, u32[]{:S(2)}, u32[]{:S(2)}) collective-permute-start(bf16[2,384,192]{2,1,0:T(8,128)(2,1)S(1)} %pad_maximum_fusion.4), channel_id=1, source_target_pairs={{0,1},{1,0},{2,3},{3,2},{4,5},{5,4},{6,7},{7,6},{8,9},{9,8},{10,11... | collective-permute-start | bytes 884744 | tf_op jit(solution)/shard_map/ppermute | solution.py:28
  67.4 5.7 %collective-permute-start.10 = (bf16[1,2,4,1,8,768]{5,4,1,2,3,0:T(8,128)(2,1)S(1)}, bf16[1,2,4,1,8,768]{5,4,1,2,3,0:T(8,128)(2,1)S(1)}, u32[]{:S(2)}, u32[]{:S(2)}) collective-permute-start(bf16[1,2,4,1,8,768]{5,4,1,2,3,0:T(8,128)(2,1)S(1)} %bitcast.378), channel_id=1, source_target_pairs={{0,2},{1,3},{2,0},{3,1},{4,6},{5,7},{6,4},{7,5},{8,10},{9,11},{10,... | collective-permute-start | bytes 294920 | tf_op jit(solution)/shard_map/ppermute | solution.py:28
  68.7 6.1 %collective-permute-start.13 = (bf16[1,2,4,1,8,768]{5,4,1,2,3,0:T(8,128)(2,1)S(1)}, bf16[1,2,4,1,8,768]{5,4,1,2,3,0:T(8,128)(2,1)S(1)}, u32[]{:S(2)}, u32[]{:S(2)}) collective-permute-start(bf16[1,2,4,1,8,768]{5,4,1,2,3,0:T(8,128)(2,1)S(1)} %bitcast.379), channel_id=1, source_target_pairs={{0,2},{1,3},{2,0},{3,1},{4,6},{5,7},{6,4},{7,5},{8,10},{9,11},{10,... | collective-permute-start | bytes 294920 | tf_op jit(solution)/shard_map/ppermute | solution.py:28
  70.8 5.5 %collective-permute-start.16 = (bf16[1,2,4,1,8,768]{5,4,1,2,3,0:T(8,128)(2,1)S(1)}, bf16[1,2,4,1,8,768]{5,4,1,2,3,0:T(8,128)(2,1)S(1)}, u32[]{:S(2)}, u32[]{:S(2)}) collective-permute-start(bf16[1,2,4,1,8,768]{5,4,1,2,3,0:T(8,128)(2,1)S(1)} %bitcast.377), channel_id=1, source_target_pairs={{0,2},{1,3},{2,0},{3,1},{4,6},{5,7},{6,4},{7,5},{8,10},{9,11},{10,... | collective-permute-start | bytes 294920 | tf_op jit(solution)/shard_map/ppermute | solution.py:28
  73.2 8.6 %collective-permute-start.24 = (bf16[256,384]{1,0:T(8,128)(2,1)S(1)}, bf16[256,384]{1,0:T(8,128)(2,1)S(1)}, u32[]{:S(2)}, u32[]{:S(2)}) collective-permute-start(bf16[256,384]{1,0:T(8,128)(2,1)S(1)} %pad_maximum_fusion.11), channel_id=1, source_target_pairs={{0,16},{16,0},{1,17},{17,1},{2,18},{18,2},{3,19},{19,3},{4,20},{20... | collective-permute-start | bytes 589832 | tf_op jit(solution)/shard_map/ppermute | solution.py:32
  74.8 6.9 %collective-permute-start.20 = (bf16[256,384]{1,0:T(8,128)(2,1)S(1)}, bf16[256,384]{1,0:T(8,128)(2,1)S(1)}, u32[]{:S(2)}, u32[]{:S(2)}) collective-permute-start(bf16[256,384]{1,0:T(8,128)(2,1)S(1)} %constant_dynamic-update-slice_fusion.3), channel_id=1, source_target_pairs={{0,16},{16,0},{1,17},{17,1},{2,18},{18,2},{3,19},{19,3},{4,20},{20... | collective-permute-start | bytes 589832 | tf_op jit(solution)/shard_map/ppermute | solution.py:32
  76.7 8.8 %collective-permute-start.27 = (bf16[384,192]{1,0:T(8,128)(2,1)S(1)}, bf16[384,192]{1,0:T(8,128)(2,1)S(1)}, u32[]{:S(2)}, u32[]{:S(2)}) collective-permute-start(bf16[384,192]{1,0:T(8,128)(2,1)S(1)} %get-tuple-element.124), channel_id=1, source_target_pairs={{0,2},{1,3},{2,0},{3,1},{4,6},{5,7},{6,4},{7,5},{8,10},{9,11},{10,... | collective-permute-start | bytes 442376 | tf_op jit(solution)/shard_map/ppermute | solution.py:28
  85.6 8.4 %collective-permute-start.25 = (bf16[192,1152]{1,0:T(8,128)(2,1)}, bf16[192,1152]{1,0:T(8,128)(2,1)S(1)}, u32[]{:S(2)}, u32[]{:S(2)}) collective-permute-start(bf16[192,1152]{1,0:T(8,128)(2,1)} %select_convert_fusion), channel_id=1, source_target_pairs={{0,1},{1,0},{2,3},{3,2},{4,5},{5,4},{6,7},{7,6},{8,9},{9,8},{10,11... | collective-permute-start | bytes 1327112 | tf_op jit(solution)/shard_map/ppermute | solution.py:28
  85.6 7.4 %collective-permute-start.28 = (bf16[384,192]{1,0:T(8,128)(2,1)S(1)}, bf16[384,192]{1,0:T(8,128)(2,1)S(1)}, u32[]{:S(2)}, u32[]{:S(2)}) collective-permute-start(bf16[384,192]{1,0:T(8,128)(2,1)S(1)} %add_convert_fusion), channel_id=1, source_target_pairs={{0,16},{16,0},{1,17},{17,1},{2,18},{18,2},{3,19},{19,3},{4,20},{20... | collective-permute-start | bytes 442376 | tf_op jit(solution)/shard_map/ppermute | solution.py:32
  (4 other events, 10.6 us)

commit v3 on v2

--- a/solution.py
+++ b/solution.py
@@ -2,6 +2,7 @@
 import jax.numpy as jnp
 from jax import lax
 from jax.experimental import pallas as pl
+from jax.experimental.pallas import tpu as pltpu
 from jax.sharding import PartitionSpec as P
 
 BASE_DILATION = 32
@@ -82,11 +83,40 @@
     ]
 
 
-def passed(value):
-    def kernel(value_ref, out_ref):
-        out_ref[...] = value_ref[...]
-
-    return pl.pallas_call(kernel, out_shape=jax.ShapeDtypeStruct(value.shape, value.dtype))(value)
+def split_cores(section_inputs, cotangent, core, first, batch):
+    rows, channels = cotangent.shape[2:]
+    quarter = rows // 4
+    blocks = rows // BASE_DILATION
+
+    def kernel(core_ref, inputs_ref, top_ref, send_ref, keep_ref):
+        low = core_ref[0] == 0
+        for which, value in enumerate((inputs_ref[0, 0, 0], top_ref[0, 0])):
+            value = value.astype(jnp.float32).reshape(blocks, 4, quarter // blocks, channels)
+            for side in range(2):
+                first_part = value[:, 2 * side].reshape(quarter, channels)
+                second_part = value[:, 2 * side + 1].reshape(quarter, channels)
+                keep = jnp.where(low, first_part, second_part)
+                send = jnp.where(low, second_part, first_part)
+                keep_ref[which, side] = keep.astype(keep_ref.dtype)
+                send_ref[which, side] = send.astype(send_ref.dtype)
+
+    out = jax.ShapeDtypeStruct((2 * batch, 2, quarter, channels), cotangent.dtype)
+    part = pl.BlockSpec((2, 2, quarter, channels), lambda m: (m, 0, 0, 0))
+    return pl.pallas_call(
+        kernel,
+        grid=(batch,),
+        in_specs=[
+            pl.BlockSpec(memory_space=pltpu.SMEM),
+            pl.BlockSpec((1, 1, 1, rows, channels), lambda m: (0, first + m, 0, 0, 0)),
+            pl.BlockSpec((1, 1, rows, channels), lambda m: (first + m, 0, 0, 0)),
+        ],
+        out_specs=[part, part],
+        out_shape=[out, out],
+        compiler_params=pltpu.CompilerParams(vmem_limit_bytes=16 * 2**20),
+        cost_estimate=pl.CostEstimate(
+            flops=0, bytes_accessed=8 * batch * rows * channels, transcendentals=0
+        ),
+    )(core.reshape(1).astype(jnp.int32), section_inputs, cotangent)
 
 
 def after(value, *events):
@@ -107,7 +137,6 @@
     inner_scale,
     inner_shift,
 ):
-    norm_scale = passed(norm_scale)
     sections = lax.axis_size("section")
     windows = lax.axis_size("dp")
     count = lax.axis_size("seq")
@@ -120,14 +149,26 @@
     kernel = conv_weight[0]
     inner = kernel.shape[2]
     kernel_flat = kernel.reshape(3 * channels, inner)
-    back_kernel = kernel.transpose(0, 2, 1).reshape(3 * inner, channels)
     out_w = out_weight[0]
     own = BASE_DILATION // count
     step = (own * (1 + section % 2), own)
     gathered = count == 4 and windows == 2
     core, side = number % 2, number // 2
     ticks = micro + LAG * (sections - 1)
-    down_pairs = [(i + 1, i) for i in range(sections - 1)]
+
+    def send_down(value, now):
+        return {
+            hop: lax.ppermute(value, "section", [(sections - 1 - hop, sections - 2 - hop)])
+            for hop in range(sections - 1)
+            if 0 <= now - LAG * hop < micro
+        }
+
+    def receive(comes, *events):
+        value = None
+        for hop, come in comes.items():
+            come = after(come, *events)
+            value = come if value is None else jnp.where(section == sections - 2 - hop, come, value)
+        return value
 
     def forward(block_in):
         pre = block_in.astype(jnp.float32) * norm_scale[0] + norm_shift[0]
@@ -149,30 +190,68 @@
             )
         )
 
-    both_in = jnp.concatenate([inputs, top])
     if count == 4:
-        blocks = both_in.reshape(2 * micro, rows // BASE_DILATION, 2, 2, own, channels)
-        keep = pick(blocks, core, 3)
-        come = seq_swap(pick(blocks, 1 - core, 3), 1)
-        halves = jnp.stack([choose(core == 0, keep, come), choose(core == 0, come, keep)], 1)
-        sends, keeps = [], []
-        for m in range(micro):
-            pair = jnp.stack([halves[m], halves[micro + m]])
-            sends.append(pick(pair, 1 - side, 3))
-            keeps.append(pick(pair, side, 3))
-        comes = [seq_swap(one, 2) for one in sends]
+
+        def swap_sides(keep, come):
+            send = jnp.stack([pick(keep, 1 - side, 1), pick(come, 1 - side, 1)], 1)
+            mine = jnp.stack([pick(keep, side, 1), pick(come, side, 1)], 1)
+            return send, mine
+
+        def settle(mine, come):
+            mine, come = (
+                jnp.stack(
+                    [
+                        choose(core == 0, one[:, 0], one[:, 1]),
+                        choose(core == 0, one[:, 1], one[:, 0]),
+                    ],
+                    1,
+                )
+                for one in (mine, come)
+            )
+            both = jnp.stack([choose(side == 0, mine, come), choose(side == 0, come, mine)], 1)
+            both = both.reshape(-1, rows, channels)
+            return both[0], both[1]
+
+        send, keep = split_cores(section_inputs, cotangent, core, 0, 1)
+        come = seq_swap(send, 1)
+        later_core = after(core, send)
+        later_send, later_keep = split_cores(section_inputs, cotangent, later_core, 1, micro - 1)
+        later_come = seq_swap(later_send, 1)
+        send, mine = swap_sides(keep, come)
+        come = seq_swap(send, 2)
+        later_keep = after(later_keep, send)
+        later_send, later_mine = swap_sides(later_keep, later_come)
+        first_send = send
+        parts = [later_send[2 * m : 2 * m + 2] for m in range(micro - 1)]
+        parts = lax.optimization_barrier(tuple(parts) + (later_mine,))
+        later_mine = parts[-1]
+        come = after(come, *parts)
+        arriving = [(mine, come)]
 
         def arrived(m, *events):
-            keep = keeps[m]
-            come = after(comes[m], *events)
-            pair = jnp.stack([choose(side == 0, keep, come), choose(side == 0, come, keep)], 1)
-            return pair[0].reshape(rows, channels), pair[1].reshape(rows, channels)
+            mine, come = arriving[m]
+            if m + 1 < micro:
+                send = parts[m] if m == 0 else after(parts[m], *events)
+                arriving.append((later_mine[2 * m : 2 * m + 2], seq_swap(send, 2)))
+            return settle(mine, after(come, *events))
     else:
-        swapped = to_residues(both_in, number)
+        swapped = to_residues(jnp.concatenate([inputs, top]), number)
+        first_send = swapped
 
         def arrived(m, *events):
             return swapped[m], swapped[micro + m]
 
+    unit = after(jnp.eye(inner, dtype=jnp.bfloat16), first_send)
+    back_kernel = lax.optimization_barrier(
+        jnp.concatenate(
+            [
+                lax.dot_general(
+                    unit, kernel[tap], (((1,), (1,)), ((), ())), preferred_element_type=jnp.float32
+                ).astype(jnp.bfloat16)
+                for tap in range(3)
+            ]
+        )
+    )
     tops, hidden, slope, inner_act, inner_slope = [], [], [], [], []
 
     def tick(index, received):
@@ -212,9 +291,8 @@
     half = channels // 2
     share = half // 2
     sent, done = [], []
-    near_hidden = far_hidden = None
+    near_hidden, far_hidden = [], []
     near_grad, far_grad = [None] * micro, [None] * micro
-    back_half = [None] * micro
     conv_total = 0.0
     out_part = 0.0
     for now in range(ticks):
@@ -226,67 +304,83 @@
             slope.append(one[1])
             inner_act.append(one[2])
             inner_slope.append(one[3])
-        received = sent[now - LAG] if now >= LAG else None
-        if received is not None:
-            received = after(received, done[now - 1])
+        received = None
+        if now >= LAG:
+            events = [done[now - 1]]
+            if gathered and now == micro + 2:
+                events.append(near_hidden)
+            if gathered and now == ticks - 2:
+                events.append(far_hidden)
+            if gathered and now - LAG * (sections - 1) >= 1:
+                events.append(near_grad[now - LAG * (sections - 1) - 1])
+            received = receive(sent[now - LAG], *events)
         done.append(tick(now - LAG * (sections - 1 - section), received))
         if now + LAG < ticks:
-            sent.append(lax.ppermute(done[now][2], "section", down_pairs))
-        if gathered and now == micro:
-            wide = jnp.concatenate(hidden)
+            sent.append(send_down(done[now][2], now))
+        if gathered and now == micro - 1:
+            wide = jnp.concatenate(after(tuple(hidden), done[now]))
             mine = choose(side == 0, wide[:, :half], wide[:, half:])
             other = choose(side == 0, wide[:, half:], wide[:, :half])
-            mine, other = after((mine, other), done[now])
             near_hidden = (mine, seq_swap(other, 2))
-        if gathered and now == micro + 2:
-            near_hidden = after(near_hidden, done[now])
+        if gathered and now == micro:
             near_hidden = jnp.concatenate(
-                [one.reshape(micro, rows, half) for one in near_hidden], axis=1
+                [one.reshape(micro, rows, half) for one in after(near_hidden, done[now])], axis=1
             )
             far_hidden = dp_swap(near_hidden)
         m = now - LAG * (sections - 1)
         if m >= 0:
+            out_part = out_part + lax.dot_general(
+                of_section(m, 0),
+                inner_act[m],
+                (((0,), (0,)), ((), ())),
+                preferred_element_type=jnp.float32,
+            )
+        if gathered and m >= 0:
             grad_conv = of_section(m, 1)
-            if gathered:
-                near_grad[m] = (grad_conv, seq_swap(grad_conv, 2))
+            near_grad[m] = (grad_conv, seq_swap(grad_conv, 2))
         if gathered and m >= 1:
-            near_grad[m - 1] = jnp.concatenate(after(near_grad[m - 1], done[now]))
+            near_grad[m - 1] = jnp.concatenate(after(near_grad[m - 1], done[now - 1]))
             far_grad[m - 1] = dp_swap(near_grad[m - 1])
 
-    if gathered:
-        near_grad[-1] = jnp.concatenate(near_grad[-1])
-        far_grad[-1] = dp_swap(near_grad[-1])
-    for m in range(micro):
-        out_part = out_part + lax.dot_general(
-            inner_act[m],
-            of_section(m, 0),
-            (((0,), (0,)), ((), ())),
-            preferred_element_type=jnp.float32,
-        )
-    if gathered:
-        halves = [out_part[:, :half], out_part[:, half:]]
-        quarters = [[one[:, :share], one[:, share:]] for one in halves]
-        send = [choose(core == 0, one[1], one[0]).astype(jnp.bfloat16) for one in quarters]
-        keep = [choose(core == 0, one[0], one[1]) for one in quarters]
-        come = seq_swap(jnp.stack(send), 1).astype(jnp.float32)
-        columns = [keep[0] + come[0], keep[1] + come[1]]
-        send = choose(side == 0, columns[1], columns[0]).astype(jnp.bfloat16)
-        keep = choose(side == 0, columns[0], columns[1])
-        come = seq_swap(send, 2)
-        columns = (keep + come.astype(jnp.float32)).astype(jnp.bfloat16)
-        out_sum = columns.astype(jnp.float32) + dp_swap(columns).astype(jnp.float32)
-    grads_out = [from_residues(of_section(m, 2)[None], number)[0] for m in range(micro)]
-    for m in range(micro):
+    def add_conv(total, m, *events):
         if gathered:
             all_hidden = exchange_rows(near_hidden[m], far_hidden[m])
-            all_grad = exchange_rows(near_grad[m], far_grad[m]).reshape(4, rows, inner)
+            all_grad = exchange_rows(near_grad[m], after(far_grad[m], *events))
+            all_grad = all_grad.reshape(4, rows, inner)
             back = jnp.concatenate(shifts(all_grad, step), axis=-1).reshape(4 * rows, 3 * inner)
         else:
             all_hidden = hidden[m]
             back = jnp.concatenate(shifts(of_section(m, 1), step), axis=-1)
-        conv_total = conv_total + lax.dot_general(
+        return total + lax.dot_general(
             all_hidden, back, (((0,), (0,)), ((), ())), preferred_element_type=jnp.float32
         )
+
+    if gathered:
+        quarters = out_part.reshape(2, 2, share, inner)
+        keep = choose(core == 0, quarters[:, 0], quarters[:, 1])
+        send = choose(core == 0, quarters[:, 1], quarters[:, 0]).astype(jnp.bfloat16)
+        come_out = seq_swap(send, 1)
+        far_grad[-2] = after(far_grad[-2], send)
+        near_grad[-1] = jnp.concatenate(after(near_grad[-1], far_grad[-2]))
+        far_grad[-1] = dp_swap(near_grad[-1])
+        come_out = after(come_out, near_grad[-1]).astype(jnp.float32)
+        columns = [keep[0] + come_out[0], keep[1] + come_out[1]]
+        send = choose(side == 0, columns[1], columns[0]).astype(jnp.bfloat16)
+        keep = choose(side == 0, columns[0], columns[1])
+        come = seq_swap(send, 2)
+        grads = jnp.stack([of_section(m, 2) for m in range(micro)])
+        grads_out = from_residues(after(grads, send), number)
+        for m in range(micro - 1):
+            conv_total = lax.optimization_barrier(add_conv(conv_total, m, send))
+        come = after(come, conv_total)
+        columns = (keep + come.astype(jnp.float32)).astype(jnp.bfloat16)
+        come_out = dp_swap(columns)
+        conv_total = add_conv(conv_total, micro - 1, columns)
+        out_sum = (columns.astype(jnp.float32) + come_out.astype(jnp.float32)).T
+    else:
+        for m in range(micro):
+            conv_total = add_conv(conv_total, m)
+        grads_out = from_residues(jnp.stack([of_section(m, 2) for m in range(micro)]), number)
 
     factor = 1.0 / float(micro * windows)
     if gathered:
@@ -295,6 +389,7 @@
         conv_sum = choose(core == 0, low, high) + come.astype(jnp.float32)
         conv_sum = jnp.stack([conv_sum[:, k * inner : (k + 1) * inner] for k in range(3)])
     else:
+        out_part = out_part.T
         conv_part = conv_total.reshape(channels, 3, inner).transpose(1, 0, 2)
         conv_sum, out_sum = (
             lax.psum(
@@ -304,7 +399,7 @@
             for part in (conv_part, out_part)
         )
     return (
-        jnp.stack(grads_out).reshape(section_inputs.shape),
+        grads_out.reshape(section_inputs.shape),
         (conv_sum * factor)[None],
         (out_sum * factor)[None],
     )

time: 95.5 us -> 87.8 us (0.919)
  waiting for transfers between devices: 33.4 us -> 25.2 us
  starting transfers between devices: 31.3 us -> 34.3 us
  other arithmetic: 10.5 us -> 8.18 us
  matrix products: 11.9 us -> 13.6 us
  Pallas kernels: 1.26 us -> 0.25 us
    ppermute x7 -> x9, waiting for transfers between devices: 11.8 us -> 5.11 us  [send_down(): lax.ppermute(value, 'section', [(sections - 1 - hop, sections - 2 - hop)])]
    ppermute x17 -> x14, starting transfers between devices: 14.8 us -> 19.9 us  [seq_swap(): return lax.ppermute(value, 'seq', [(i, i ^ bit) for i in range(count)])]
    ppermute x5, waiting for transfers between devices: 10.2 us -> 5.15 us  [dp_swap(): return lax.ppermute(value, 'dp', [(0, 1), (1, 0)])]
    ppermute x17 -> x14, waiting for transfers between devices: 11.4 us -> 14.9 us  [seq_swap(): return lax.ppermute(value, 'seq', [(i, i ^ bit) for i in range(count)])]
    squeeze x1 -> x0, other arithmetic: 1.97 us -> none  [pick(): return lax.dynamic_index_in_dim(value, index, axis, keepdims=False)]
    dot_general x6 -> x9, matrix products: 3.12 us -> 4.66 us  [the longest x3 2.09 us: add_conv(): lax.dot_general(all_hidden, back, (((0,), (0,)), ((), ())), preferred_ele...]
    unnamed x20 -> x19, local copies, waits for them, and re-layouts: 3.68 us -> 2.27 us
    ppermute x7 -> x9, starting transfers between devices: 9.23 us -> 8.1 us  [send_down(): lax.ppermute(value, 'section', [(sections - 1 - hop, sections - 2 - hop)])]
  transfers between devices with their start and end apart: 29 -> 28, of which waited for: 16 -> 10; matrix products, arithmetic and copies ran while one was open for 24% -> 26% of each run, Pallas kernels for 1% -> 0%
where the time goes in v3:
time: 87.8 us; the launch traced here: 87.4 us
  starting transfers between devices  34.3 us (39%)
  waiting for transfers between devices  25.2 us (29%)
  matrix products  13.6 us (15%)
  other arithmetic  8.18 us (9%)
  local copies, waits for them, and re-layouts  4.34 us (5%)
  between operations  1.62 us (2%)
    ppermute x14, starting transfers between devices, seq_swap(): return lax.ppermute(value, 'seq', [(i, i ^ bit) for i in range(count)])  19.9 us
    ppermute x14, waiting for transfers between devices, seq_swap(): return lax.ppermute(value, 'seq', [(i, i ^ bit) for i in range(count)])  14.9 us
    ppermute x9, starting transfers between devices, send_down(): lax.ppermute(value, 'section', [(sections - 1 - hop, sections - 2 - hop)])  8.1 us
    ppermute x5, starting transfers between devices, dp_swap(): return lax.ppermute(value, 'dp', [(0, 1), (1, 0)])  6.32 us
    ppermute x5, waiting for transfers between devices, dp_swap(): return lax.ppermute(value, 'dp', [(0, 1), (1, 0)])  5.15 us
    ppermute x9, waiting for transfers between devices, send_down(): lax.ppermute(value, 'section', [(sections - 1 - hop, sections - 2 - hop)])  5.11 us
    dot_general x9, matrix products, tick(): grad_hidden = jnp.dot(back, back_kernel, preferred_element_type=jnp.float32)  4.25 us
    dot_general x9, matrix products, tick(): lax.dot_general(grad_top, out_w, (((1,), (1,)), ((), ())), preferred_elem...  2.89 us
  transfers between devices with their start and end apart: 28, of which 10 were waited for; matrix products, arithmetic and copies ran while one was open for 26% of the time, Pallas kernels for 0%

profile of v3, /device:TPU:0, one launch (start us, length us, event | category | flops | bytes accessed | tf_op | source)
XLA Modules:
  0.0 87.4 jit_solution(4178922319181490819)
XLA Ops:
  0.7 1.1 %copy-done.1 = bf16[1,3,1,128,768]{4,3,2,1,0:T(8,128)(2,1)S(1)} copy-done((bf16[1,3,1,128,768]{4,3,2,1,0:T(8,128)(2,1)S(1)}, bf16[1,3,1,128,768]{4,3,2,1,0:T(8,128)(2,1)}, u32[]{:S(2)}) %copy-start.1) | copy-done | bytes 589848
  1.8 1.1 %copy-done.2 = bf16[3,1,128,768]{3,2,1,0:T(8,128)(2,1)S(1)} copy-done((bf16[3,1,128,768]{3,2,1,0:T(8,128)(2,1)S(1)}, bf16[3,1,128,768]{3,2,1,0:T(8,128)(2,1)}, u32[]{:S(2)}) %copy-start.2) | copy-done | bytes 589848
  3.7 0.8 copy.14
  4.6 0.7 reduce.3
  5.4 1.0 %select_bitcast_fusion.16 = (bf16[2,1,1,32,768]{4,3,0,2,1:T(8,128)(2,1)S(1)}, bf16[2,1,1,32,768]{4,3,0,2,1:T(8,128)(2,1)S(1)}, bf16[2,1,32,768]{3,2,0,1:T(8,128)(2,1)S(1)}, bf16[2,1,32,768]{3,2,0,1:T(8,128)(2,1)S(1)}) fusion(pred[]{:T(512)S(6)} %eq.24, bf16[2,2,32,768]{3,2,0,1:T(8,128)(2,1)} %collective-permute-done, s32[]{:T(128)S(6)} %select_n.793, ...), kind=kLoop, calls=%fused_computation.410 | loop fusion | flops 98304 | bytes 786441 | tf_op jit(solution)/shard_map/stack | solution.py:202
  6.4 3.0 %collective-permute-start.2 = (bf16[2,2,32,768]{3,2,0,1:T(8,128)(2,1)S(1)}, bf16[2,2,32,768]{3,2,0,1:T(8,128)(2,1)S(1)}, u32[]{:S(2)}, u32[]{:S(2)}) collective-permute-start(bf16[2,2,32,768]{3,2,0,1:T(8,128)(2,1)S(1)} %pad_maximum_fusion.12), channel_id=1, source_target_pairs={{0,2},{1,3},{2,0},{3,1},{4,6},{5,7},{6,4},{7,5},{8,10},{9,11},{10,... | collective-permute-start | bytes 589832 | tf_op jit(solution)/shard_map/ppermute | solution.py:29
  11.4 3.7 %collective-permute-done.2 = bf16[2,2,32,768]{3,2,0,1:T(8,128)(2,1)S(1)} collective-permute-done((bf16[2,2,32,768]{3,2,0,1:T(8,128)(2,1)S(1)}, bf16[2,2,32,768]{3,2,0,1:T(8,128)(2,1)S(1)}, u32[]{:S(2)}, u32[]{:S(2)}) %collective-permute-start.2) | collective-permute-done | bytes 196640 | tf_op jit(solution)/shard_map/ppermute | solution.py:29
  17.8 2.1 %collective-permute-start.3 = (bf16[2,2,32,768]{3,2,0,1:T(8,128)(2,1)S(1)}, bf16[2,2,32,768]{3,2,0,1:T(8,128)(2,1)S(1)}, u32[]{:S(2)}, u32[]{:S(2)}) collective-permute-start(bf16[2,2,32,768]{3,2,0,1:T(8,128)(2,1)S(1)} %get-tuple-element.99), channel_id=1, source_target_pairs={{0,2},{1,3},{2,0},{3,1},{4,6},{5,7},{6,4},{7,5},{8,10},{9,11},{10,... | collective-permute-start | bytes 589832 | tf_op jit(solution)/shard_map/ppermute | solution.py:29
  22.6 0.9 %collective-permute-done.3 = bf16[2,2,32,768]{3,2,0,1:T(8,128)(2,1)S(1)} collective-permute-done((bf16[2,2,32,768]{3,2,0,1:T(8,128)(2,1)S(1)}, bf16[2,2,32,768]{3,2,0,1:T(8,128)(2,1)S(1)}, u32[]{:S(2)}, u32[]{:S(2)}) %collective-permute-start.3) | collective-permute-done | bytes 196640 | tf_op jit(solution)/shard_map/ppermute | solution.py:29
  27.1 2.0 %collective-permute-start.11 = (bf16[384,384]{1,0:T(8,128)(2,1)S(1)}, bf16[384,384]{1,0:T(8,128)(2,1)S(1)}, u32[]{:S(2)}, u32[]{:S(2)}) collective-permute-start(bf16[384,384]{1,0:T(8,128)(2,1)S(1)} %get-tuple-element.182), channel_id=1, source_target_pairs={{0,2},{1,3},{2,0},{3,1},{4,6},{5,7},{6,4},{7,5},{8,10},{9,11},{10,... | collective-permute-start | bytes 884744 | tf_op jit(solution)/shard_map/ppermute | solution.py:29
  31.8 1.3 %collective-permute-start.9 = (bf16[128,768]{1,0:T(8,128)(2,1)S(1)}, bf16[128,768]{1,0:T(8,128)(2,1)S(1)}, u32[]{:S(2)}, u32[]{:S(2)}) collective-permute-start(bf16[128,768]{1,0:T(8,128)(2,1)S(1)} %fusion.27), channel_id=1, source_target_pairs={{4,0},{5,1},{6,2},{7,3},{20,16},{21,17},{22,18},{23,19}} | collective-permute-start | bytes 589832 | tf_op jit(solution)/shard_map/ppermute | solution.py:161
  34.0 2.0 %collective-permute-start.14 = (bf16[3,256,384]{2,1,0:T(8,128)(2,1)S(1)}, bf16[3,256,384]{2,1,0:T(8,128)(2,1)S(1)}, u32[]{:S(2)}, u32[]{:S(2)}) collective-permute-start(bf16[3,256,384]{2,1,0:T(8,128)(2,1)S(1)} %pad_maximum_fusion.1), channel_id=1, source_target_pairs={{0,16},{16,0},{1,17},{17,1},{2,18},{18,2},{3,19},{19,3},{4,20},{20... | collective-permute-start | bytes 1769480 | tf_op jit(solution)/shard_map/ppermute | solution.py:33
  37.0 1.3 %collective-permute-start.13 = (bf16[128,768]{1,0:T(8,128)(2,1)S(1)}, bf16[128,768]{1,0:T(8,128)(2,1)S(1)}, u32[]{:S(2)}, u32[]{:S(2)}) collective-permute-start(bf16[128,768]{1,0:T(8,128)(2,1)S(1)} %add_convert_fusion.2), channel_id=1, source_target_pairs={{4,0},{5,1},{6,2},{7,3},{20,16},{21,17},{22,18},{23,19}} | collective-permute-start | bytes 589832 | tf_op jit(solution)/shard_map/ppermute | solution.py:161
  38.3 5.1 %collective-permute-done.9 = bf16[128,768]{1,0:T(8,128)(2,1)S(1)} collective-permute-done((bf16[128,768]{1,0:T(8,128)(2,1)S(1)}, bf16[128,768]{1,0:T(8,128)(2,1)S(1)}, u32[]{:S(2)}, u32[]{:S(2)}) %collective-permute-start.9) | collective-permute-done | bytes 196640 | tf_op jit(solution)/shard_map/ppermute | solution.py:161
  44.3 1.5 %collective-permute-start.16 = (bf16[128,768]{1,0:T(8,128)(2,1)S(1)}, bf16[128,768]{1,0:T(8,128)(2,1)S(1)}, u32[]{:S(2)}, u32[]{:S(2)}) collective-permute-start(bf16[128,768]{1,0:T(8,128)(2,1)S(1)} %fusion.26), channel_id=1, source_target_pairs={{4,0},{5,1},{6,2},{7,3},{20,16},{21,17},{22,18},{23,19}} | collective-permute-start | bytes 589832 | tf_op jit(solution)/shard_map/ppermute | solution.py:161
  45.8 3.8 %collective-permute-start.15 = (bf16[128,384]{1,0:T(8,128)(2,1)S(1)}, bf16[128,384]{1,0:T(8,128)(2,1)S(1)}, u32[]{:S(2)}, u32[]{:S(2)}) collective-permute-start(bf16[128,384]{1,0:T(8,128)(2,1)S(1)} %select_select_fusion.2), channel_id=1, source_target_pairs={{0,2},{1,3},{2,0},{3,1},{4,6},{5,7},{6,4},{7,5},{8,10},{9,11},{10,... | collective-permute-start | bytes 294920 | tf_op jit(solution)/shard_map/ppermute | solution.py:29
  50.0 2.2 %collective-permute-done.15 = bf16[128,384]{1,0:T(8,128)(2,1)S(1)} collective-permute-done((bf16[128,384]{1,0:T(8,128)(2,1)S(1)}, bf16[128,384]{1,0:T(8,128)(2,1)S(1)}, u32[]{:S(2)}, u32[]{:S(2)}) %collective-permute-start.15) | collective-permute-done | bytes 98336 | tf_op jit(solution)/shard_map/ppermute | solution.py:29
  52.3 1.6 %collective-permute-start.23 = (bf16[256,384]{1,0:T(8,128)(2,1)S(1)}, bf16[256,384]{1,0:T(8,128)(2,1)S(1)}, u32[]{:S(2)}, u32[]{:S(2)}) collective-permute-start(bf16[256,384]{1,0:T(8,128)(2,1)S(1)} %constant_dynamic-update-slice_fusion.7), channel_id=1, source_target_pairs={{0,16},{16,0},{1,17},{17,1},{2,18},{18,2},{3,19},{19,3},{4,20},{20... | collective-permute-start | bytes 589832 | tf_op jit(solution)/shard_map/ppermute | solution.py:33
  54.8 2.1 %collective-permute-start.17 = (bf16[128,384]{1,0:T(8,128)(2,1)S(1)}, bf16[128,384]{1,0:T(8,128)(2,1)S(1)}, u32[]{:S(2)}, u32[]{:S(2)}) collective-permute-start(bf16[128,384]{1,0:T(8,128)(2,1)S(1)} %select_select_fusion.1), channel_id=1, source_target_pairs={{0,2},{1,3},{2,0},{3,1},{4,6},{5,7},{6,4},{7,5},{8,10},{9,11},{10,... | collective-permute-start | bytes 294920 | tf_op jit(solution)/shard_map/ppermute | solution.py:29
  57.6 1.9 %collective-permute-done.17 = bf16[128,384]{1,0:T(8,128)(2,1)S(1)} collective-permute-done((bf16[128,384]{1,0:T(8,128)(2,1)S(1)}, bf16[128,384]{1,0:T(8,128)(2,1)S(1)}, u32[]{:S(2)}, u32[]{:S(2)}) %collective-permute-start.17) | collective-permute-done | bytes 98336 | tf_op jit(solution)/shard_map/ppermute | solution.py:29
  61.8 2.1 %collective-permute-start.19 = (bf16[128,384]{1,0:T(8,128)(2,1)S(1)}, bf16[128,384]{1,0:T(8,128)(2,1)S(1)}, u32[]{:S(2)}, u32[]{:S(2)}) collective-permute-start(bf16[128,384]{1,0:T(8,128)(2,1)S(1)} %select_select_fusion), channel_id=1, source_target_pairs={{0,2},{1,3},{2,0},{3,1},{4,6},{5,7},{6,4},{7,5},{8,10},{9,11},{10,... | collective-permute-start | bytes 294920 | tf_op jit(solution)/shard_map/ppermute | solution.py:29
  63.9 4.6 %collective-permute-done.20 = bf16[256,384]{1,0:T(8,128)(2,1)S(1)} collective-permute-done((bf16[256,384]{1,0:T(8,128)(2,1)S(1)}, bf16[256,384]{1,0:T(8,128)(2,1)S(1)}, u32[]{:S(2)}, u32[]{:S(2)}) %collective-permute-start.20) | collective-permute-done | bytes 196640 | tf_op jit(solution)/shard_map/ppermute | solution.py:33
  69.3 2.1 %collective-permute-start.25 = (bf16[192,384]{1,0:T(8,128)(2,1)S(1)}, bf16[192,384]{1,0:T(8,128)(2,1)S(1)}, u32[]{:S(2)}, u32[]{:S(2)}) collective-permute-start(bf16[192,384]{1,0:T(8,128)(2,1)S(1)} %fusion.230), channel_id=1, source_target_pairs={{0,2},{1,3},{2,0},{3,1},{4,6},{5,7},{6,4},{7,5},{8,10},{9,11},{10,... | collective-permute-start | bytes 442376 | tf_op jit(solution)/shard_map/ppermute | solution.py:29
  72.6 0.7 convolution_add_fusion.1
  73.3 1.5 %collective-permute-done.25 = bf16[192,384]{1,0:T(8,128)(2,1)S(1)} collective-permute-done((bf16[192,384]{1,0:T(8,128)(2,1)S(1)}, bf16[192,384]{1,0:T(8,128)(2,1)S(1)}, u32[]{:S(2)}, u32[]{:S(2)}) %collective-permute-start.25) | collective-permute-done | bytes 147488 | tf_op jit(solution)/shard_map/ppermute | solution.py:29
  74.9 1.6 %collective-permute-start.27 = (bf16[192,384]{1,0:T(8,128)(2,1)S(1)}, bf16[192,384]{1,0:T(8,128)(2,1)S(1)}, u32[]{:S(2)}, u32[]{:S(2)}) collective-permute-start(bf16[192,384]{1,0:T(8,128)(2,1)S(1)} %fusion.192), channel_id=1, source_target_pairs={{0,16},{16,0},{1,17},{17,1},{2,18},{18,2},{3,19},{19,3},{4,20},{20... | collective-permute-start | bytes 442376 | tf_op jit(solution)/shard_map/ppermute | solution.py:33
  76.7 0.7 convolution_add_fusion
  77.6 1.8 %collective-permute-start.22 = (bf16[3,2,4,1,8,768]{5,4,1,2,0,3:T(8,128)(2,1)S(1)}, bf16[3,2,4,1,8,768]{5,4,1,2,0,3:T(8,128)(2,1)S(1)}, u32[]{:S(2)}, u32[]{:S(2)}) collective-permute-start(bf16[3,2,4,1,8,768]{5,4,1,2,0,3:T(8,128)(2,1)S(1)} %bitcast.305), channel_id=1, source_target_pairs={{0,2},{1,3},{2,0},{3,1},{4,6},{5,7},{6,4},{7,5},{8,10},{9,11},{10,... | collective-permute-start | bytes 884744 | tf_op jit(solution)/shard_map/ppermute | solution.py:29
  80.1 0.8 multiply_bitcast_fusion
  80.8 4.5 %collective-permute-done.22 = bf16[3,2,4,1,8,768]{5,4,1,2,0,3:T(8,128)(2,1)S(1)} collective-permute-done((bf16[3,2,4,1,8,768]{5,4,1,2,0,3:T(8,128)(2,1)S(1)}, bf16[3,2,4,1,8,768]{5,4,1,2,0,3:T(8,128)(2,1)S(1)}, u32[]{:S(2)}, u32[]{:S(2)}) %collective-permute-start.22) | collective-permute-done | bytes 294944 | tf_op jit(solution)/shard_map/ppermute | solution.py:29
  85.4 0.9 pad_maximum_fusion.3
  86.4 1.0 %maximum_multiply_fusion = f32[1,3,192,384]{3,2,1,0:T(8,128)} fusion(f32[1,1,192,384]{3,2,1,0:T(8,128)S(1)} %get-tuple-element.172, f32[1,1,192,384]{3,2,1,0:T(8,128)S(1)} %get-tuple-element.173, f32[1,1,192,384]{3,2,1,0:T(8,128)S(1)} %get-tuple-element.171), kind=kLoop, calls=%fused_computation.71 | loop fusion | flops 663552 | bytes 1769472 | tf_op jit(solution)/shard_map/mul | solution.py:403
  (161 shorter events, 24.4 us)
Async XLA Ops:
  0.6 15.6 %copy-start = (bf16[1,384,768]{2,1,0:T(8,128)(2,1)S(1)}, bf16[1,384,768]{2,1,0:T(8,128)(2,1)}, u32[]{:S(2)}) copy-start(bf16[1,384,768]{2,1,0:T(8,128)(2,1)} %param.11) | copy-start | bytes 1769476
  2.9 1.7 %copy-start.5 = (f32[1,768]{1,0:T(1,128)S(1)}, f32[1,768]{1,0:T(1,128)}, u32[]{:S(2)}) copy-start(f32[1,768]{1,0:T(1,128)} %param.12) | copy-start | bytes 9220
  2.9 1.7 %copy-start.6 = (f32[1,384]{1,0:T(1,128)S(1)}, f32[1,384]{1,0:T(1,128)}, u32[]{:S(2)}) copy-start(f32[1,384]{1,0:T(1,128)} %param.14) | copy-start | bytes 4612
  3.0 2.4 %collective-permute-start = (bf16[2,2,32,768]{3,2,0,1:T(8,128)(2,1)S(1)}, bf16[2,2,32,768]{3,2,0,1:T(8,128)(2,1)}, u32[]{:S(2)}, u32[]{:S(2)}) collective-permute-start(bf16[2,2,32,768]{3,2,0,1:T(8,128)(2,1)S(1)} %copy.12), channel_id=1, source_target_pairs={{0,1},{1,0},{2,3},{3,2},{4,5},{5,4},{6,7},{7,6},{8,9},{9,8},{10,11... | collective-permute-start | bytes 589832 | tf_op jit(solution)/shard_map/ppermute | solution.py:29
  3.5 5.9 %copy-start.3 = (bf16[1,3,768,384]{3,2,1,0:T(8,128)(2,1)S(1)}, bf16[1,3,768,384]{3,2,1,0:T(8,128)(2,1)}, u32[]{:S(2)}) copy-start(bf16[1,3,768,384]{3,2,1,0:T(8,128)(2,1)} %param.10) | copy-start | bytes 5308420
  4.4 6.7 %collective-permute-start.1 = (bf16[4,2,32,768]{3,2,0,1:T(8,128)(2,1)}, bf16[4,2,32,768]{3,2,0,1:T(8,128)(2,1)S(1)}, u32[]{:S(2)}, u32[]{:S(2)}) collective-permute-start(bf16[4,2,32,768]{3,2,0,1:T(8,128)(2,1)} %copy.14), channel_id=1, source_target_pairs={{0,1},{1,0},{2,3},{3,2},{4,5},{5,4},{6,7},{7,6},{8,9},{9,8},{10,11... | collective-permute-start | bytes 1179656 | tf_op jit(solution)/shard_map/ppermute | solution.py:29
  6.4 8.7 %collective-permute-start.2 = (bf16[2,2,32,768]{3,2,0,1:T(8,128)(2,1)S(1)}, bf16[2,2,32,768]{3,2,0,1:T(8,128)(2,1)S(1)}, u32[]{:S(2)}, u32[]{:S(2)}) collective-permute-start(bf16[2,2,32,768]{3,2,0,1:T(8,128)(2,1)S(1)} %pad_maximum_fusion.12), channel_id=1, source_target_pairs={{0,2},{1,3},{2,0},{3,1},{4,6},{5,7},{6,4},{7,5},{8,10},{9,11},{10,... | collective-permute-start | bytes 589832 | tf_op jit(solution)/shard_map/ppermute | solution.py:29
  11.2 8.7 %collective-permute-start.4 = (bf16[2,2,32,768]{3,2,0,1:T(8,128)(2,1)S(1)}, bf16[2,2,32,768]{3,2,0,1:T(8,128)(2,1)S(1)}, u32[]{:S(2)}, u32[]{:S(2)}) collective-permute-start(bf16[2,2,32,768]{3,2,0,1:T(8,128)(2,1)S(1)} %get-tuple-element.91), channel_id=1, source_target_pairs={{0,2},{1,3},{2,0},{3,1},{4,6},{5,7},{6,4},{7,5},{8,10},{9,11},{10,... | collective-permute-start | bytes 589832 | tf_op jit(solution)/shard_map/ppermute | solution.py:29
  17.1 6.5 %collective-permute-start.5 = (bf16[128,768]{1,0:T(8,128)(2,1)S(1)}, bf16[128,768]{1,0:T(8,128)(2,1)S(1)}, u32[]{:S(2)}, u32[]{:S(2)}) collective-permute-start(bf16[128,768]{1,0:T(8,128)(2,1)S(1)} %fusion.29), channel_id=1, source_target_pairs={{12,8},{13,9},{14,10},{15,11},{28,24},{29,25},{30,26},{31,27}} | collective-permute-start | bytes 589832 | tf_op jit(solution)/shard_map/ppermute | solution.py:161
  17.8 5.8 %collective-permute-start.3 = (bf16[2,2,32,768]{3,2,0,1:T(8,128)(2,1)S(1)}, bf16[2,2,32,768]{3,2,0,1:T(8,128)(2,1)S(1)}, u32[]{:S(2)}, u32[]{:S(2)}) collective-permute-start(bf16[2,2,32,768]{3,2,0,1:T(8,128)(2,1)S(1)} %get-tuple-element.99), channel_id=1, source_target_pairs={{0,2},{1,3},{2,0},{3,1},{4,6},{5,7},{6,4},{7,5},{8,10},{9,11},{10,... | collective-permute-start | bytes 589832 | tf_op jit(solution)/shard_map/ppermute | solution.py:29
  21.9 7.2 %collective-permute-start.7 = (bf16[128,768]{1,0:T(8,128)(2,1)S(1)}, bf16[128,768]{1,0:T(8,128)(2,1)S(1)}, u32[]{:S(2)}, u32[]{:S(2)}) collective-permute-start(bf16[128,768]{1,0:T(8,128)(2,1)S(1)} %fusion.28), channel_id=1, source_target_pairs={{12,8},{13,9},{14,10},{15,11},{28,24},{29,25},{30,26},{31,27}} | collective-permute-start | bytes 589832 | tf_op jit(solution)/shard_map/ppermute | solution.py:161
  25.6 5.2 %collective-permute-start.6 = (bf16[128,768]{1,0:T(8,128)(2,1)S(1)}, bf16[128,768]{1,0:T(8,128)(2,1)S(1)}, u32[]{:S(2)}, u32[]{:S(2)}) collective-permute-start(bf16[128,768]{1,0:T(8,128)(2,1)S(1)} %add_convert_fusion.4), channel_id=1, source_target_pairs={{8,4},{9,5},{10,6},{11,7},{24,20},{25,21},{26,22},{27,23}} | collective-permute-start | bytes 589832 | tf_op jit(solution)/shard_map/ppermute | solution.py:161
  26.3 4.5 %collective-permute-start.8 = (bf16[128,768]{1,0:T(8,128)(2,1)S(1)}, bf16[128,768]{1,0:T(8,128)(2,1)S(1)}, u32[]{:S(2)}, u32[]{:S(2)}) collective-permute-start(bf16[128,768]{1,0:T(8,128)(2,1)S(1)} %add_convert_fusion.4), channel_id=1, source_target_pairs={{12,8},{13,9},{14,10},{15,11},{28,24},{29,25},{30,26},{31,27}} | collective-permute-start | bytes 589832 | tf_op jit(solution)/shard_map/ppermute | solution.py:161
  27.1 6.8 %collective-permute-start.11 = (bf16[384,384]{1,0:T(8,128)(2,1)S(1)}, bf16[384,384]{1,0:T(8,128)(2,1)S(1)}, u32[]{:S(2)}, u32[]{:S(2)}) collective-permute-start(bf16[384,384]{1,0:T(8,128)(2,1)S(1)} %get-tuple-element.182), channel_id=1, source_target_pairs={{0,2},{1,3},{2,0},{3,1},{4,6},{5,7},{6,4},{7,5},{8,10},{9,11},{10,... | collective-permute-start | bytes 884744 | tf_op jit(solution)/shard_map/ppermute | solution.py:29
  30.1 5.9 %collective-permute-start.10 = (bf16[128,768]{1,0:T(8,128)(2,1)S(1)}, bf16[128,768]{1,0:T(8,128)(2,1)S(1)}, u32[]{:S(2)}, u32[]{:S(2)}) collective-permute-start(bf16[128,768]{1,0:T(8,128)(2,1)S(1)} %add_convert_fusion.3), channel_id=1, source_target_pairs={{8,4},{9,5},{10,6},{11,7},{24,20},{25,21},{26,22},{27,23}} | collective-permute-start | bytes 589832 | tf_op jit(solution)/shard_map/ppermute | solution.py:161
  31.8 11.5 %collective-permute-start.9 = (bf16[128,768]{1,0:T(8,128)(2,1)S(1)}, bf16[128,768]{1,0:T(8,128)(2,1)S(1)}, u32[]{:S(2)}, u32[]{:S(2)}) collective-permute-start(bf16[128,768]{1,0:T(8,128)(2,1)S(1)} %fusion.27), channel_id=1, source_target_pairs={{4,0},{5,1},{6,2},{7,3},{20,16},{21,17},{22,18},{23,19}} | collective-permute-start | bytes 589832 | tf_op jit(solution)/shard_map/ppermute | solution.py:161
  33.1 10.2 %collective-permute-start.12 = (bf16[128,768]{1,0:T(8,128)(2,1)S(1)}, bf16[128,768]{1,0:T(8,128)(2,1)S(1)}, u32[]{:S(2)}, u32[]{:S(2)}) collective-permute-start(bf16[128,768]{1,0:T(8,128)(2,1)S(1)} %fusion.27), channel_id=1, source_target_pairs={{8,4},{9,5},{10,6},{11,7},{24,20},{25,21},{26,22},{27,23}} | collective-permute-start | bytes 589832 | tf_op jit(solution)/shard_map/ppermute | solution.py:161
  34.0 19.9 %collective-permute-start.14 = (bf16[3,256,384]{2,1,0:T(8,128)(2,1)S(1)}, bf16[3,256,384]{2,1,0:T(8,128)(2,1)S(1)}, u32[]{:S(2)}, u32[]{:S(2)}) collective-permute-start(bf16[3,256,384]{2,1,0:T(8,128)(2,1)S(1)} %pad_maximum_fusion.1), channel_id=1, source_target_pairs={{0,16},{16,0},{1,17},{17,1},{2,18},{18,2},{3,19},{19,3},{4,20},{20... | collective-permute-start | bytes 1769480 | tf_op jit(solution)/shard_map/ppermute | solution.py:33
  37.0 16.9 %collective-permute-start.13 = (bf16[128,768]{1,0:T(8,128)(2,1)S(1)}, bf16[128,768]{1,0:T(8,128)(2,1)S(1)}, u32[]{:S(2)}, u32[]{:S(2)}) collective-permute-start(bf16[128,768]{1,0:T(8,128)(2,1)S(1)} %add_convert_fusion.2), channel_id=1, source_target_pairs={{4,0},{5,1},{6,2},{7,3},{20,16},{21,17},{22,18},{23,19}} | collective-permute-start | bytes 589832 | tf_op jit(solution)/shard_map/ppermute | solution.py:161
  44.3 13.3 %collective-permute-start.16 = (bf16[128,768]{1,0:T(8,128)(2,1)S(1)}, bf16[128,768]{1,0:T(8,128)(2,1)S(1)}, u32[]{:S(2)}, u32[]{:S(2)}) collective-permute-start(bf16[128,768]{1,0:T(8,128)(2,1)S(1)} %fusion.26), channel_id=1, source_target_pairs={{4,0},{5,1},{6,2},{7,3},{20,16},{21,17},{22,18},{23,19}} | collective-permute-start | bytes 589832 | tf_op jit(solution)/shard_map/ppermute | solution.py:161
  45.8 6.4 %collective-permute-start.15 = (bf16[128,384]{1,0:T(8,128)(2,1)S(1)}, bf16[128,384]{1,0:T(8,128)(2,1)S(1)}, u32[]{:S(2)}, u32[]{:S(2)}) collective-permute-start(bf16[128,384]{1,0:T(8,128)(2,1)S(1)} %select_select_fusion.2), channel_id=1, source_target_pairs={{0,2},{1,3},{2,0},{3,1},{4,6},{5,7},{6,4},{7,5},{8,10},{9,11},{10,... | collective-permute-start | bytes 294920 | tf_op jit(solution)/shard_map/ppermute | solution.py:29
  52.3 19.3 %collective-permute-start.23 = (bf16[256,384]{1,0:T(8,128)(2,1)S(1)}, bf16[256,384]{1,0:T(8,128)(2,1)S(1)}, u32[]{:S(2)}, u32[]{:S(2)}) collective-permute-start(bf16[256,384]{1,0:T(8,128)(2,1)S(1)} %constant_dynamic-update-slice_fusion.7), channel_id=1, source_target_pairs={{0,16},{16,0},{1,17},{17,1},{2,18},{18,2},{3,19},{19,3},{4,20},{20... | collective-permute-start | bytes 589832 | tf_op jit(solution)/shard_map/ppermute | solution.py:33
  54.8 4.7 %collective-permute-start.17 = (bf16[128,384]{1,0:T(8,128)(2,1)S(1)}, bf16[128,384]{1,0:T(8,128)(2,1)S(1)}, u32[]{:S(2)}, u32[]{:S(2)}) collective-permute-start(bf16[128,384]{1,0:T(8,128)(2,1)S(1)} %select_select_fusion.1), channel_id=1, source_target_pairs={{0,2},{1,3},{2,0},{3,1},{4,6},{5,7},{6,4},{7,5},{8,10},{9,11},{10,... | collective-permute-start | bytes 294920 | tf_op jit(solution)/shard_map/ppermute | solution.py:29
  61.1 8.1 %collective-permute-start.18 = (bf16[2,192,384]{2,1,0:T(8,128)(2,1)S(1)}, bf16[2,192,384]{2,1,0:T(8,128)(2,1)S(1)}, u32[]{:S(2)}, u32[]{:S(2)}) collective-permute-start(bf16[2,192,384]{2,1,0:T(8,128)(2,1)S(1)} %fusion.134), channel_id=1, source_target_pairs={{0,1},{1,0},{2,3},{3,2},{4,5},{5,4},{6,7},{7,6},{8,9},{9,8},{10,11... | collective-permute-start | bytes 884744 | tf_op jit(solution)/shard_map/ppermute | solution.py:29
  61.2 7.4 %collective-permute-start.20 = (bf16[256,384]{1,0:T(8,128)(2,1)S(1)}, bf16[256,384]{1,0:T(8,128)(2,1)S(1)}, u32[]{:S(2)}, u32[]{:S(2)}) collective-permute-start(bf16[256,384]{1,0:T(8,128)(2,1)S(1)} %constant_dynamic-update-slice_fusion.3), channel_id=1, source_target_pairs={{0,16},{16,0},{1,17},{17,1},{2,18},{18,2},{3,19},{19,3},{4,20},{20... | collective-permute-start | bytes 589832 | tf_op jit(solution)/shard_map/ppermute | solution.py:33
  61.8 6.8 %collective-permute-start.19 = (bf16[128,384]{1,0:T(8,128)(2,1)S(1)}, bf16[128,384]{1,0:T(8,128)(2,1)S(1)}, u32[]{:S(2)}, u32[]{:S(2)}) collective-permute-start(bf16[128,384]{1,0:T(8,128)(2,1)S(1)} %select_select_fusion), channel_id=1, source_target_pairs={{0,2},{1,3},{2,0},{3,1},{4,6},{5,7},{6,4},{7,5},{8,10},{9,11},{10,... | collective-permute-start | bytes 294920 | tf_op jit(solution)/shard_map/ppermute | solution.py:29
  68.6 7.9 %collective-permute-start.24 = (bf16[256,384]{1,0:T(8,128)(2,1)S(1)}, bf16[256,384]{1,0:T(8,128)(2,1)S(1)}, u32[]{:S(2)}, u32[]{:S(2)}) collective-permute-start(bf16[256,384]{1,0:T(8,128)(2,1)S(1)} %constant_dynamic-update-slice_fusion.5), channel_id=1, source_target_pairs={{0,16},{16,0},{1,17},{17,1},{2,18},{18,2},{3,19},{19,3},{4,20},{20... | collective-permute-start | bytes 589832 | tf_op jit(solution)/shard_map/ppermute | solution.py:33
  69.3 5.5 %collective-permute-start.25 = (bf16[192,384]{1,0:T(8,128)(2,1)S(1)}, bf16[192,384]{1,0:T(8,128)(2,1)S(1)}, u32[]{:S(2)}, u32[]{:S(2)}) collective-permute-start(bf16[192,384]{1,0:T(8,128)(2,1)S(1)} %fusion.230), channel_id=1, source_target_pairs={{0,2},{1,3},{2,0},{3,1},{4,6},{5,7},{6,4},{7,5},{8,10},{9,11},{10,... | collective-permute-start | bytes 442376 | tf_op jit(solution)/shard_map/ppermute | solution.py:29
  71.4 6.0 %collective-permute-start.21 = (bf16[3,1,4,2,8,768]{5,4,2,3,0,1:T(8,128)(2,1)S(1)}, bf16[3,1,4,2,8,768]{5,4,2,3,0,1:T(8,128)(2,1)S(1)}, u32[]{:S(2)}, u32[]{:S(2)}) collective-permute-start(bf16[3,1,4,2,8,768]{5,4,2,3,0,1:T(8,128)(2,1)S(1)} %dynamic-slice_bitcast_fusion), channel_id=1, source_target_pairs={{0,1},{1,0},{2,3},{3,2},{4,5},{5,4},{6,7},{7,6},{8,9},{9,8},{10,11... | collective-permute-start | bytes 884744 | tf_op jit(solution)/shard_map/ppermute | solution.py:29
  74.9 5.2 %collective-permute-start.27 = (bf16[192,384]{1,0:T(8,128)(2,1)S(1)}, bf16[192,384]{1,0:T(8,128)(2,1)S(1)}, u32[]{:S(2)}, u32[]{:S(2)}) collective-permute-start(bf16[192,384]{1,0:T(8,128)(2,1)S(1)} %fusion.192), channel_id=1, source_target_pairs={{0,16},{16,0},{1,17},{17,1},{2,18},{18,2},{3,19},{19,3},{4,20},{20... | collective-permute-start | bytes 442376 | tf_op jit(solution)/shard_map/ppermute | solution.py:33
  77.6 7.7 %collective-permute-start.22 = (bf16[3,2,4,1,8,768]{5,4,1,2,0,3:T(8,128)(2,1)S(1)}, bf16[3,2,4,1,8,768]{5,4,1,2,0,3:T(8,128)(2,1)S(1)}, u32[]{:S(2)}, u32[]{:S(2)}) collective-permute-start(bf16[3,2,4,1,8,768]{5,4,1,2,0,3:T(8,128)(2,1)S(1)} %bitcast.305), channel_id=1, source_target_pairs={{0,2},{1,3},{2,0},{3,1},{4,6},{5,7},{6,4},{7,5},{8,10},{9,11},{10,... | collective-permute-start | bytes 884744 | tf_op jit(solution)/shard_map/ppermute | solution.py:29
  79.5 6.8 %collective-permute-start.26 = (bf16[192,1152]{1,0:T(8,128)(2,1)S(1)}, bf16[192,1152]{1,0:T(8,128)(2,1)S(1)}, u32[]{:S(2)}, u32[]{:S(2)}) collective-permute-start(bf16[192,1152]{1,0:T(8,128)(2,1)S(1)} %select_convert_fusion), channel_id=1, source_target_pairs={{0,1},{1,0},{2,3},{3,2},{4,5},{5,4},{6,7},{7,6},{8,9},{9,8},{10,11... | collective-permute-start | bytes 1327112 | tf_op jit(solution)/shard_map/ppermute | solution.py:29
  (3 other events, 3.8 us)

commit v4 on v3

--- a/solution.py
+++ b/solution.py
@@ -7,6 +7,8 @@
 
 BASE_DILATION = 32
 LAG = 2
+NEAR = 5
+FAR = 8
 
 
 gelu_coeff = 0.7978845608028654
@@ -52,14 +54,14 @@
             batch, 2 * source, inner, target // 2, rest, channels
         )
         bit *= 2
-    return value[:, :, :, 0]
+    return value[:, :, :, 0], come
 
 
 def to_residues(value, number):
     batch, rows, channels = value.shape
     count = lax.axis_size("seq")
     value = value.reshape(batch, 1, rows // BASE_DILATION, count, BASE_DILATION // count, channels)
-    return exchange(value, number).reshape(batch, rows, channels)
+    return exchange(value, number)[0].reshape(batch, rows, channels)
 
 
 def from_residues(value, number):
@@ -68,8 +70,8 @@
     own = BASE_DILATION // count
     inner = rows // BASE_DILATION
     value = value.reshape(batch, 1, count, inner, own, channels).transpose(0, 1, 3, 2, 4, 5)
-    value = exchange(value, number)
-    return value.transpose(0, 2, 1, 3, 4).reshape(batch, rows, channels)
+    value, come = exchange(value, number)
+    return value.transpose(0, 2, 1, 3, 4).reshape(batch, rows, channels), come
 
 
 def shifts(value, step):
@@ -157,18 +159,9 @@
     ticks = micro + LAG * (sections - 1)
 
     def send_down(value, now):
-        return {
-            hop: lax.ppermute(value, "section", [(sections - 1 - hop, sections - 2 - hop)])
-            for hop in range(sections - 1)
-            if 0 <= now - LAG * hop < micro
-        }
-
-    def receive(comes, *events):
-        value = None
-        for hop, come in comes.items():
-            come = after(come, *events)
-            value = come if value is None else jnp.where(section == sections - 2 - hop, come, value)
-        return value
+        hops = [hop for hop in range(sections - 1) if 0 <= now - LAG * hop < micro]
+        pairs = [(sections - 1 - hop, sections - 2 - hop) for hop in hops]
+        return lax.ppermute(value, "section", pairs)
 
     def forward(block_in):
         pre = block_in.astype(jnp.float32) * norm_scale[0] + norm_shift[0]
@@ -187,6 +180,21 @@
                 slope * norm_scale[0],
                 inner_act.astype(jnp.bfloat16),
                 inner_slope * inner_scale[0],
+            )
+        )
+
+    def transposed(unit):
+        return lax.optimization_barrier(
+            jnp.concatenate(
+                [
+                    lax.dot_general(
+                        unit,
+                        kernel[tap],
+                        (((1,), (1,)), ((), ())),
+                        preferred_element_type=jnp.float32,
+                    ).astype(jnp.bfloat16)
+                    for tap in range(3)
+                ]
             )
         )
 
@@ -221,10 +229,10 @@
         come = seq_swap(send, 2)
         later_keep = after(later_keep, send)
         later_send, later_mine = swap_sides(later_keep, later_come)
-        first_send = send
         parts = [later_send[2 * m : 2 * m + 2] for m in range(micro - 1)]
         parts = lax.optimization_barrier(tuple(parts) + (later_mine,))
         later_mine = parts[-1]
+        back_kernel = transposed(after(jnp.eye(inner, dtype=jnp.bfloat16), *parts))
         come = after(come, *parts)
         arriving = [(mine, come)]
 
@@ -236,22 +244,11 @@
             return settle(mine, after(come, *events))
     else:
         swapped = to_residues(jnp.concatenate([inputs, top]), number)
-        first_send = swapped
+        back_kernel = kernel.transpose(0, 2, 1).reshape(3 * inner, channels)
 
         def arrived(m, *events):
             return swapped[m], swapped[micro + m]
 
-    unit = after(jnp.eye(inner, dtype=jnp.bfloat16), first_send)
-    back_kernel = lax.optimization_barrier(
-        jnp.concatenate(
-            [
-                lax.dot_general(
-                    unit, kernel[tap], (((1,), (1,)), ((), ())), preferred_element_type=jnp.float32
-                ).astype(jnp.bfloat16)
-                for tap in range(3)
-            ]
-        )
-    )
     tops, hidden, slope, inner_act, inner_slope = [], [], [], [], []
 
     def tick(index, received):
@@ -307,13 +304,15 @@
         received = None
         if now >= LAG:
             events = [done[now - 1]]
-            if gathered and now == micro + 2:
+            if now < micro:
+                events.append(hidden[now])
+            if gathered and now == NEAR:
                 events.append(near_hidden)
-            if gathered and now == ticks - 2:
+            if gathered and now == FAR:
                 events.append(far_hidden)
-            if gathered and now - LAG * (sections - 1) >= 1:
-                events.append(near_grad[now - LAG * (sections - 1) - 1])
-            received = receive(sent[now - LAG], *events)
+            if gathered and now == ticks - 1:
+                events.append(near_grad[0])
+            received = after(sent[now - LAG], *events)
         done.append(tick(now - LAG * (sections - 1 - section), received))
         if now + LAG < ticks:
             sent.append(send_down(done[now][2], now))
@@ -339,7 +338,7 @@
             grad_conv = of_section(m, 1)
             near_grad[m] = (grad_conv, seq_swap(grad_conv, 2))
         if gathered and m >= 1:
-            near_grad[m - 1] = jnp.concatenate(after(near_grad[m - 1], done[now - 1]))
+            near_grad[m - 1] = jnp.concatenate(after(near_grad[m - 1], done[now]))
             far_grad[m - 1] = dp_swap(near_grad[m - 1])
 
     def add_conv(total, m, *events):
@@ -356,11 +355,12 @@
         )
 
     if gathered:
+        out_part = after(out_part, near_grad[1])
         quarters = out_part.reshape(2, 2, share, inner)
         keep = choose(core == 0, quarters[:, 0], quarters[:, 1])
         send = choose(core == 0, quarters[:, 1], quarters[:, 0]).astype(jnp.bfloat16)
         come_out = seq_swap(send, 1)
-        far_grad[-2] = after(far_grad[-2], send)
+        far_grad[-2] = after(far_grad[-2], send, far_grad[0])
         near_grad[-1] = jnp.concatenate(after(near_grad[-1], far_grad[-2]))
         far_grad[-1] = dp_swap(near_grad[-1])
         come_out = after(come_out, near_grad[-1]).astype(jnp.float32)
@@ -369,18 +369,18 @@
         keep = choose(side == 0, columns[0], columns[1])
         come = seq_swap(send, 2)
         grads = jnp.stack([of_section(m, 2) for m in range(micro)])
-        grads_out = from_residues(after(grads, send), number)
+        grads_out, arrived_last = from_residues(after(grads, send), number)
         for m in range(micro - 1):
             conv_total = lax.optimization_barrier(add_conv(conv_total, m, send))
         come = after(come, conv_total)
         columns = (keep + come.astype(jnp.float32)).astype(jnp.bfloat16)
         come_out = dp_swap(columns)
-        conv_total = add_conv(conv_total, micro - 1, columns)
+        conv_total = add_conv(conv_total, micro - 1, columns, arrived_last)
         out_sum = (columns.astype(jnp.float32) + come_out.astype(jnp.float32)).T
     else:
         for m in range(micro):
             conv_total = add_conv(conv_total, m)
-        grads_out = from_residues(jnp.stack([of_section(m, 2) for m in range(micro)]), number)
+        grads_out, _ = from_residues(jnp.stack([of_section(m, 2) for m in range(micro)]), number)
 
     factor = 1.0 / float(micro * windows)
     if gathered:

time: 87.8 us -> 79.3 us (0.903)
  starting transfers between devices: 34.3 us -> 28.2 us
  other arithmetic: 8.18 us -> 6.43 us
    ppermute x14, starting transfers between devices: 19.9 us -> 14.8 us  [seq_swap(): return lax.ppermute(value, 'seq', [(i, i ^ bit) for i in range(count)])]
    ppermute x9 -> x7, waiting for transfers between devices: 5.11 us -> 8.54 us  [send_down(): return lax.ppermute(value, 'section', pairs)]
    ppermute x5, waiting for transfers between devices: 5.15 us -> 2.5 us  [dp_swap(): return lax.ppermute(value, 'dp', [(0, 1), (1, 0)])]
    ppermute x9 -> x7, starting transfers between devices: 8.1 us -> 6.74 us  [send_down(): return lax.ppermute(value, 'section', pairs)]
    another operation x6, other arithmetic: 1.12 us -> 0.18 us  [settle(): jnp.stack([choose(core == 0, one[:, 0], one[:, 1]), choose(core == 0, one...]
    unnamed x19 -> x21, local copies, waits for them, and re-layouts: 2.27 us -> 2.27 us
  transfers between devices with their start and end apart: 28 -> 26, of which waited for: 10 -> 13; matrix products, arithmetic and copies ran while one was open for 26% -> 25% of each run, Pallas kernels for 0% -> 0%
where the time goes in v4:
time: 79.3 us; the launch traced here: 79.1 us
  starting transfers between devices  28.2 us (36%)
  waiting for transfers between devices  25.4 us (32%)
  matrix products  13.5 us (17%)
  other arithmetic  6.43 us (8%)
  local copies, waits for them, and re-layouts  3.6 us (5%)
  between operations  1.74 us (2%)
    ppermute x14, starting transfers between devices, seq_swap(): return lax.ppermute(value, 'seq', [(i, i ^ bit) for i in range(count)])  14.8 us
    ppermute x14, waiting for transfers between devices, seq_swap(): return lax.ppermute(value, 'seq', [(i, i ^ bit) for i in range(count)])  14.3 us
    ppermute x7, waiting for transfers between devices, send_down(): return lax.ppermute(value, 'section', pairs)  8.54 us
    ppermute x7, starting transfers between devices, send_down(): return lax.ppermute(value, 'section', pairs)  6.74 us
    ppermute x5, starting transfers between devices, dp_swap(): return lax.ppermute(value, 'dp', [(0, 1), (1, 0)])  6.68 us
    dot_general x9, matrix products, tick(): grad_hidden = jnp.dot(back, back_kernel, preferred_element_type=jnp.float32)  4.13 us
    dot_general x9, matrix products, tick(): lax.dot_general(grad_top, out_w, (((1,), (1,)), ((), ())), preferred_elem...  2.86 us
    ppermute x5, waiting for transfers between devices, dp_swap(): return lax.ppermute(value, 'dp', [(0, 1), (1, 0)])  2.5 us
  transfers between devices with their start and end apart: 26, of which 13 were waited for; matrix products, arithmetic and copies ran while one was open for 25% of the time, Pallas kernels for 0%

profile of v4, /device:TPU:0, one launch (start us, length us, event | category | flops | bytes accessed | tf_op | source)
XLA Modules:
  0.0 79.1 jit_solution(16428899700243811246)
XLA Ops:
  0.7 1.1 %copy-done.1 = bf16[1,3,1,128,768]{4,3,2,1,0:T(8,128)(2,1)S(1)} copy-done((bf16[1,3,1,128,768]{4,3,2,1,0:T(8,128)(2,1)S(1)}, bf16[1,3,1,128,768]{4,3,2,1,0:T(8,128)(2,1)}, u32[]{:S(2)}) %copy-start.1) | copy-done | bytes 589848
  1.8 1.1 %copy-done.2 = bf16[3,1,128,768]{3,2,1,0:T(8,128)(2,1)S(1)} copy-done((bf16[3,1,128,768]{3,2,1,0:T(8,128)(2,1)S(1)}, bf16[3,1,128,768]{3,2,1,0:T(8,128)(2,1)}, u32[]{:S(2)}) %copy-start.2) | copy-done | bytes 589848
  4.6 3.0 %collective-permute-start.2 = (bf16[2,2,32,768]{3,2,0,1:T(8,128)(2,1)S(1)}, bf16[2,2,32,768]{3,2,0,1:T(8,128)(2,1)S(1)}, u32[]{:S(2)}, u32[]{:S(2)}) collective-permute-start(bf16[2,2,32,768]{3,2,0,1:T(8,128)(2,1)S(1)} %pad_maximum_fusion.12), channel_id=1, source_target_pairs={{0,2},{1,3},{2,0},{3,1},{4,6},{5,7},{6,4},{7,5},{8,10},{9,11},{10,... | collective-permute-start | bytes 589832 | tf_op jit(solution)/shard_map/ppermute | solution.py:31
  9.9 3.4 %collective-permute-done.2 = bf16[2,2,32,768]{3,2,0,1:T(8,128)(2,1)S(1)} collective-permute-done((bf16[2,2,32,768]{3,2,0,1:T(8,128)(2,1)S(1)}, bf16[2,2,32,768]{3,2,0,1:T(8,128)(2,1)S(1)}, u32[]{:S(2)}, u32[]{:S(2)}) %collective-permute-start.2) | collective-permute-done | bytes 196640 | tf_op jit(solution)/shard_map/ppermute | solution.py:31
  15.3 0.7 collective-permute-start.5
  16.0 2.1 %collective-permute-start.3 = (bf16[2,2,32,768]{3,2,0,1:T(8,128)(2,1)S(1)}, bf16[2,2,32,768]{3,2,0,1:T(8,128)(2,1)S(1)}, u32[]{:S(2)}, u32[]{:S(2)}) collective-permute-start(bf16[2,2,32,768]{3,2,0,1:T(8,128)(2,1)S(1)} %get-tuple-element.98), channel_id=1, source_target_pairs={{0,2},{1,3},{2,0},{3,1},{4,6},{5,7},{6,4},{7,5},{8,10},{9,11},{10,... | collective-permute-start | bytes 589832 | tf_op jit(solution)/shard_map/ppermute | solution.py:31
  20.9 1.2 %collective-permute-done.3 = bf16[2,2,32,768]{3,2,0,1:T(8,128)(2,1)S(1)} collective-permute-done((bf16[2,2,32,768]{3,2,0,1:T(8,128)(2,1)S(1)}, bf16[2,2,32,768]{3,2,0,1:T(8,128)(2,1)S(1)}, u32[]{:S(2)}, u32[]{:S(2)}) %collective-permute-start.3) | collective-permute-done | bytes 196640 | tf_op jit(solution)/shard_map/ppermute | solution.py:31
  24.9 1.8 %collective-permute-start.10 = (bf16[384,384]{1,0:T(8,128)(2,1)S(1)}, bf16[384,384]{1,0:T(8,128)(2,1)S(1)}, u32[]{:S(2)}, u32[]{:S(2)}) collective-permute-start(bf16[384,384]{1,0:T(8,128)(2,1)S(1)} %get-tuple-element.180), channel_id=1, source_target_pairs={{0,2},{1,3},{2,0},{3,1},{4,6},{5,7},{6,4},{7,5},{8,10},{9,11},{10,... | collective-permute-start | bytes 884744 | tf_op jit(solution)/shard_map/ppermute | solution.py:31
  29.3 1.3 %collective-permute-start.8 = (bf16[128,768]{1,0:T(8,128)(2,1)S(1)}, bf16[128,768]{1,0:T(8,128)(2,1)S(1)}, u32[]{:S(2)}, u32[]{:S(2)}) collective-permute-start(bf16[128,768]{1,0:T(8,128)(2,1)S(1)} %add_convert_fusion.4), channel_id=1, source_target_pairs={{8,4},{4,0},{9,5},{5,1},{10,6},{6,2},{11,7},{7,3},{24,20},{20,16},... | collective-permute-start | bytes 589832 | tf_op jit(solution)/shard_map/ppermute | solution.py:164
  30.6 1.4 %collective-permute-done.10 = bf16[384,384]{1,0:T(8,128)(2,1)S(1)} collective-permute-done((bf16[384,384]{1,0:T(8,128)(2,1)S(1)}, bf16[384,384]{1,0:T(8,128)(2,1)S(1)}, u32[]{:S(2)}, u32[]{:S(2)}) %collective-permute-start.10) | collective-permute-done | bytes 294944 | tf_op jit(solution)/shard_map/ppermute | solution.py:31
  32.1 1.4 %collective-permute-start.13 = (bf16[3,256,384]{2,1,0:T(8,128)(2,1)S(1)}, bf16[3,256,384]{2,1,0:T(8,128)(2,1)S(1)}, u32[]{:S(2)}, u32[]{:S(2)}) collective-permute-start(bf16[3,256,384]{2,1,0:T(8,128)(2,1)S(1)} %pad_maximum_fusion.1), channel_id=1, source_target_pairs={{0,16},{16,0},{1,17},{17,1},{2,18},{18,2},{3,19},{19,3},{4,20},{20... | collective-permute-start | bytes 1769480 | tf_op jit(solution)/shard_map/ppermute | solution.py:35
  34.5 1.3 %collective-permute-start.11 = (bf16[128,768]{1,0:T(8,128)(2,1)S(1)}, bf16[128,768]{1,0:T(8,128)(2,1)S(1)}, u32[]{:S(2)}, u32[]{:S(2)}) collective-permute-start(bf16[128,768]{1,0:T(8,128)(2,1)S(1)} %add_convert_fusion.3), channel_id=1, source_target_pairs={{4,0},{5,1},{6,2},{7,3},{20,16},{21,17},{22,18},{23,19}} | collective-permute-start | bytes 589832 | tf_op jit(solution)/shard_map/ppermute | solution.py:164
  35.8 7.1 %collective-permute-done.8 = bf16[128,768]{1,0:T(8,128)(2,1)S(1)} collective-permute-done((bf16[128,768]{1,0:T(8,128)(2,1)S(1)}, bf16[128,768]{1,0:T(8,128)(2,1)S(1)}, u32[]{:S(2)}, u32[]{:S(2)}) %collective-permute-start.8) | collective-permute-done | bytes 196640 | tf_op jit(solution)/shard_map/ppermute | solution.py:164
  43.9 2.2 %collective-permute-start.14 = (bf16[128,384]{1,0:T(8,128)(2,1)S(1)}, bf16[128,384]{1,0:T(8,128)(2,1)S(1)}, u32[]{:S(2)}, u32[]{:S(2)}) collective-permute-start(bf16[128,384]{1,0:T(8,128)(2,1)S(1)} %select_select_fusion.2), channel_id=1, source_target_pairs={{0,2},{1,3},{2,0},{3,1},{4,6},{5,7},{6,4},{7,5},{8,10},{9,11},{10,... | collective-permute-start | bytes 294920 | tf_op jit(solution)/shard_map/ppermute | solution.py:31
  46.1 1.5 %collective-permute-start.12 = (bf16[128,768]{1,0:T(8,128)(2,1)S(1)}, bf16[128,768]{1,0:T(8,128)(2,1)S(1)}, u32[]{:S(2)}, u32[]{:S(2)}) collective-permute-start(bf16[128,768]{1,0:T(8,128)(2,1)S(1)} %add_convert_fusion.2), channel_id=1, source_target_pairs={{4,0},{5,1},{6,2},{7,3},{20,16},{21,17},{22,18},{23,19}} | collective-permute-start | bytes 589832 | tf_op jit(solution)/shard_map/ppermute | solution.py:164
  49.5 1.3 %collective-permute-start.15 = (bf16[128,384]{1,0:T(8,128)(2,1)S(1)}, bf16[128,384]{1,0:T(8,128)(2,1)S(1)}, u32[]{:S(2)}, u32[]{:S(2)}) collective-permute-start(bf16[128,384]{1,0:T(8,128)(2,1)S(1)} %select_select_fusion.1), channel_id=1, source_target_pairs={{0,2},{1,3},{2,0},{3,1},{4,6},{5,7},{6,4},{7,5},{8,10},{9,11},{10,... | collective-permute-start | bytes 294920 | tf_op jit(solution)/shard_map/ppermute | solution.py:31
  50.8 1.5 %collective-permute-start.19 = (bf16[256,384]{1,0:T(8,128)(2,1)S(1)}, bf16[256,384]{1,0:T(8,128)(2,1)S(1)}, u32[]{:S(2)}, u32[]{:S(2)}) collective-permute-start(bf16[256,384]{1,0:T(8,128)(2,1)S(1)} %constant_dynamic-update-slice_fusion.3), channel_id=1, source_target_pairs={{0,16},{16,0},{1,17},{17,1},{2,18},{18,2},{3,19},{19,3},{4,20},{20... | collective-permute-start | bytes 589832 | tf_op jit(solution)/shard_map/ppermute | solution.py:35
  52.8 0.9 %collective-permute-done.12 = bf16[128,768]{1,0:T(8,128)(2,1)S(1)} collective-permute-done((bf16[128,768]{1,0:T(8,128)(2,1)S(1)}, bf16[128,768]{1,0:T(8,128)(2,1)S(1)}, u32[]{:S(2)}, u32[]{:S(2)}) %collective-permute-start.12) | collective-permute-done | bytes 196640 | tf_op jit(solution)/shard_map/ppermute | solution.py:164
  54.7 1.5 %collective-permute-start.18 = (bf16[256,384]{1,0:T(8,128)(2,1)S(1)}, bf16[256,384]{1,0:T(8,128)(2,1)S(1)}, u32[]{:S(2)}, u32[]{:S(2)}) collective-permute-start(bf16[256,384]{1,0:T(8,128)(2,1)S(1)} %constant_dynamic-update-slice_fusion.5), channel_id=1, source_target_pairs={{0,16},{16,0},{1,17},{17,1},{2,18},{18,2},{3,19},{19,3},{4,20},{20... | collective-permute-start | bytes 589832 | tf_op jit(solution)/shard_map/ppermute | solution.py:35
  57.1 0.8 collective-permute-start.17
  58.0 2.5 %collective-permute-done.18 = bf16[256,384]{1,0:T(8,128)(2,1)S(1)} collective-permute-done((bf16[256,384]{1,0:T(8,128)(2,1)S(1)}, bf16[256,384]{1,0:T(8,128)(2,1)S(1)}, u32[]{:S(2)}, u32[]{:S(2)}) %collective-permute-start.18) | collective-permute-done | bytes 196640 | tf_op jit(solution)/shard_map/ppermute | solution.py:35
  60.5 1.9 %collective-permute-done.17 = bf16[128,384]{1,0:T(8,128)(2,1)S(1)} collective-permute-done((bf16[128,384]{1,0:T(8,128)(2,1)S(1)}, bf16[128,384]{1,0:T(8,128)(2,1)S(1)}, u32[]{:S(2)}, u32[]{:S(2)}) %collective-permute-start.17) | collective-permute-done | bytes 98336 | tf_op jit(solution)/shard_map/ppermute | solution.py:31
  63.1 0.8 collective-permute-start.23
  64.5 0.7 fusion.2
  65.8 1.4 %collective-permute-start.21 = (bf16[3,2,4,1,8,768]{5,4,1,2,0,3:T(8,128)(2,1)S(1)}, bf16[3,2,4,1,8,768]{5,4,1,2,0,3:T(8,128)(2,1)S(1)}, u32[]{:S(2)}, u32[]{:S(2)}) collective-permute-start(bf16[3,2,4,1,8,768]{5,4,1,2,0,3:T(8,128)(2,1)S(1)} %bitcast.305), channel_id=1, source_target_pairs={{0,2},{1,3},{2,0},{3,1},{4,6},{5,7},{6,4},{7,5},{8,10},{9,11},{10,... | collective-permute-start | bytes 884744 | tf_op jit(solution)/shard_map/ppermute | solution.py:31
  67.2 0.7 convolution_add_fusion.1
  68.5 1.5 %collective-permute-start.25 = (bf16[192,384]{1,0:T(8,128)(2,1)S(1)}, bf16[192,384]{1,0:T(8,128)(2,1)S(1)}, u32[]{:S(2)}, u32[]{:S(2)}) collective-permute-start(bf16[192,384]{1,0:T(8,128)(2,1)S(1)} %fusion.192), channel_id=1, source_target_pairs={{0,16},{16,0},{1,17},{17,1},{2,18},{18,2},{3,19},{19,3},{4,20},{20... | collective-permute-start | bytes 442376 | tf_op jit(solution)/shard_map/ppermute | solution.py:35
  70.0 5.0 %collective-permute-done.21 = bf16[3,2,4,1,8,768]{5,4,1,2,0,3:T(8,128)(2,1)S(1)} collective-permute-done((bf16[3,2,4,1,8,768]{5,4,1,2,0,3:T(8,128)(2,1)S(1)}, bf16[3,2,4,1,8,768]{5,4,1,2,0,3:T(8,128)(2,1)S(1)}, u32[]{:S(2)}, u32[]{:S(2)}) %collective-permute-start.21) | collective-permute-done | bytes 294944 | tf_op jit(solution)/shard_map/ppermute | solution.py:31
  75.2 0.7 convolution_add_fusion
  76.1 0.8 multiply_bitcast_fusion
  76.9 0.9 %pad_maximum_fusion.3 = bf16[3,2,2,4,1,8,768]{6,5,2,1,3,0,4:T(8,128)(2,1)} fusion(bf16[3,1,2,4,1,8,768]{6,5,2,1,3,0,4:T(8,128)(2,1)S(1)} %get-tuple-element.175, bf16[3,1,2,4,1,8,768]{6,5,2,1,3,0,4:T(8,128)(2,1)S(1)} %get-tuple-element.174), kind=kLoop, calls=%fused_computation.99 | loop fusion | flops 294912 | bytes 1179648 | tf_op jit(solution)/shard_map/stack | solution.py:53
  78.1 1.0 %maximum_multiply_fusion = f32[1,3,192,384]{3,2,1,0:T(8,128)} fusion(f32[1,1,192,384]{3,2,1,0:T(8,128)S(1)} %get-tuple-element.170, f32[1,1,192,384]{3,2,1,0:T(8,128)S(1)} %get-tuple-element.171, f32[1,1,192,384]{3,2,1,0:T(8,128)S(1)} %get-tuple-element.169), kind=kLoop, calls=%fused_computation.67 | loop fusion | flops 663552 | bytes 1769472 | tf_op jit(solution)/shard_map/mul | solution.py:403
  (159 shorter events, 23.0 us)
Async XLA Ops:
  0.6 13.7 %copy-start = (bf16[1,384,768]{2,1,0:T(8,128)(2,1)S(1)}, bf16[1,384,768]{2,1,0:T(8,128)(2,1)}, u32[]{:S(2)}) copy-start(bf16[1,384,768]{2,1,0:T(8,128)(2,1)} %param.11) | copy-start | bytes 1769476
  0.7 1.1 %copy-start.1 = (bf16[1,3,1,128,768]{4,3,2,1,0:T(8,128)(2,1)S(1)}, bf16[1,3,1,128,768]{4,3,2,1,0:T(8,128)(2,1)}, u32[]{:S(2)}) copy-start(bf16[1,3,1,128,768]{4,3,2,1,0:T(8,128)(2,1)} %inputs_ref.3) | copy-start | bytes 1769476
  2.9 1.1 %copy-start.7 = (f32[1,384]{1,0:T(1,128)S(1)}, f32[1,384]{1,0:T(1,128)}, u32[]{:S(2)}) copy-start(f32[1,384]{1,0:T(1,128)} %param.15) | copy-start | bytes 4612
  2.9 1.1 %copy-start.4 = (f32[1,768]{1,0:T(1,128)S(1)}, f32[1,768]{1,0:T(1,128)}, u32[]{:S(2)}) copy-start(f32[1,768]{1,0:T(1,128)} %param.12) | copy-start | bytes 9220
  2.9 1.1 %copy-start.5 = (f32[1,768]{1,0:T(1,128)S(1)}, f32[1,768]{1,0:T(1,128)}, u32[]{:S(2)}) copy-start(f32[1,768]{1,0:T(1,128)} %param.13) | copy-start | bytes 9220
  3.0 1.6 %collective-permute-start = (bf16[2,2,32,768]{3,2,0,1:T(8,128)(2,1)S(1)}, bf16[2,2,32,768]{3,2,0,1:T(8,128)(2,1)S(1)}, u32[]{:S(2)}, u32[]{:S(2)}) collective-permute-start(bf16[2,2,32,768]{3,2,0,1:T(8,128)(2,1)S(1)} %copy.12), channel_id=1, source_target_pairs={{0,1},{1,0},{2,3},{3,2},{4,5},{5,4},{6,7},{7,6},{8,9},{9,8},{10,11... | collective-permute-start | bytes 589832 | tf_op jit(solution)/shard_map/ppermute | solution.py:31
  3.7 3.9 %collective-permute-start.1 = (bf16[4,2,32,768]{3,2,0,1:T(8,128)(2,1)S(1)}, bf16[4,2,32,768]{3,2,0,1:T(8,128)(2,1)S(1)}, u32[]{:S(2)}, u32[]{:S(2)}) collective-permute-start(bf16[4,2,32,768]{3,2,0,1:T(8,128)(2,1)S(1)} %copy.14), channel_id=1, source_target_pairs={{0,1},{1,0},{2,3},{3,2},{4,5},{5,4},{6,7},{7,6},{8,9},{9,8},{10,11... | collective-permute-start | bytes 1179656 | tf_op jit(solution)/shard_map/ppermute | solution.py:31
  4.6 3.7 %copy-start.3 = (bf16[1,3,768,384]{3,2,1,0:T(8,128)(2,1)S(1)}, bf16[1,3,768,384]{3,2,1,0:T(8,128)(2,1)}, u32[]{:S(2)}) copy-start(bf16[1,3,768,384]{3,2,1,0:T(8,128)(2,1)} %param.10) | copy-start | bytes 5308420
  4.6 8.6 %collective-permute-start.2 = (bf16[2,2,32,768]{3,2,0,1:T(8,128)(2,1)S(1)}, bf16[2,2,32,768]{3,2,0,1:T(8,128)(2,1)S(1)}, u32[]{:S(2)}, u32[]{:S(2)}) collective-permute-start(bf16[2,2,32,768]{3,2,0,1:T(8,128)(2,1)S(1)} %pad_maximum_fusion.12), channel_id=1, source_target_pairs={{0,2},{1,3},{2,0},{3,1},{4,6},{5,7},{6,4},{7,5},{8,10},{9,11},{10,... | collective-permute-start | bytes 589832 | tf_op jit(solution)/shard_map/ppermute | solution.py:31
  7.8 10.4 %collective-permute-start.4 = (bf16[2,2,32,768]{3,2,0,1:T(8,128)(2,1)S(1)}, bf16[2,2,32,768]{3,2,0,1:T(8,128)(2,1)S(1)}, u32[]{:S(2)}, u32[]{:S(2)}) collective-permute-start(bf16[2,2,32,768]{3,2,0,1:T(8,128)(2,1)S(1)} %get-tuple-element.90), channel_id=1, source_target_pairs={{0,2},{1,3},{2,0},{3,1},{4,6},{5,7},{6,4},{7,5},{8,10},{9,11},{10,... | collective-permute-start | bytes 589832 | tf_op jit(solution)/shard_map/ppermute | solution.py:31
  15.3 7.8 %collective-permute-start.5 = (bf16[128,768]{1,0:T(8,128)(2,1)S(1)}, bf16[128,768]{1,0:T(8,128)(2,1)S(1)}, u32[]{:S(2)}, u32[]{:S(2)}) collective-permute-start(bf16[128,768]{1,0:T(8,128)(2,1)S(1)} %fusion.25), channel_id=1, source_target_pairs={{12,8},{13,9},{14,10},{15,11},{28,24},{29,25},{30,26},{31,27}} | collective-permute-start | bytes 589832 | tf_op jit(solution)/shard_map/ppermute | solution.py:164
  16.0 6.0 %collective-permute-start.3 = (bf16[2,2,32,768]{3,2,0,1:T(8,128)(2,1)S(1)}, bf16[2,2,32,768]{3,2,0,1:T(8,128)(2,1)S(1)}, u32[]{:S(2)}, u32[]{:S(2)}) collective-permute-start(bf16[2,2,32,768]{3,2,0,1:T(8,128)(2,1)S(1)} %get-tuple-element.98), channel_id=1, source_target_pairs={{0,2},{1,3},{2,0},{3,1},{4,6},{5,7},{6,4},{7,5},{8,10},{9,11},{10,... | collective-permute-start | bytes 589832 | tf_op jit(solution)/shard_map/ppermute | solution.py:31
  20.2 6.5 %collective-permute-start.7 = (bf16[128,768]{1,0:T(8,128)(2,1)S(1)}, bf16[128,768]{1,0:T(8,128)(2,1)S(1)}, u32[]{:S(2)}, u32[]{:S(2)}) collective-permute-start(bf16[128,768]{1,0:T(8,128)(2,1)S(1)} %fusion.24), channel_id=1, source_target_pairs={{12,8},{13,9},{14,10},{15,11},{28,24},{29,25},{30,26},{31,27}} | collective-permute-start | bytes 589832 | tf_op jit(solution)/shard_map/ppermute | solution.py:164
  24.1 4.3 %collective-permute-start.6 = (bf16[128,768]{1,0:T(8,128)(2,1)S(1)}, bf16[128,768]{1,0:T(8,128)(2,1)S(1)}, u32[]{:S(2)}, u32[]{:S(2)}) collective-permute-start(bf16[128,768]{1,0:T(8,128)(2,1)S(1)} %add_convert_fusion.6), channel_id=1, source_target_pairs={{12,8},{8,4},{13,9},{9,5},{14,10},{10,6},{15,11},{11,7},{28,24},{2... | collective-permute-start | bytes 589832 | tf_op jit(solution)/shard_map/ppermute | solution.py:164
  24.9 7.2 %collective-permute-start.10 = (bf16[384,384]{1,0:T(8,128)(2,1)S(1)}, bf16[384,384]{1,0:T(8,128)(2,1)S(1)}, u32[]{:S(2)}, u32[]{:S(2)}) collective-permute-start(bf16[384,384]{1,0:T(8,128)(2,1)S(1)} %get-tuple-element.180), channel_id=1, source_target_pairs={{0,2},{1,3},{2,0},{3,1},{4,6},{5,7},{6,4},{7,5},{8,10},{9,11},{10,... | collective-permute-start | bytes 884744 | tf_op jit(solution)/shard_map/ppermute | solution.py:31
  27.7 5.9 %collective-permute-start.9 = (bf16[128,768]{1,0:T(8,128)(2,1)S(1)}, bf16[128,768]{1,0:T(8,128)(2,1)S(1)}, u32[]{:S(2)}, u32[]{:S(2)}) collective-permute-start(bf16[128,768]{1,0:T(8,128)(2,1)S(1)} %add_convert_fusion.5), channel_id=1, source_target_pairs={{8,4},{9,5},{10,6},{11,7},{24,20},{25,21},{26,22},{27,23}} | collective-permute-start | bytes 589832 | tf_op jit(solution)/shard_map/ppermute | solution.py:164
  29.3 13.6 %collective-permute-start.8 = (bf16[128,768]{1,0:T(8,128)(2,1)S(1)}, bf16[128,768]{1,0:T(8,128)(2,1)S(1)}, u32[]{:S(2)}, u32[]{:S(2)}) collective-permute-start(bf16[128,768]{1,0:T(8,128)(2,1)S(1)} %add_convert_fusion.4), channel_id=1, source_target_pairs={{8,4},{4,0},{9,5},{5,1},{10,6},{6,2},{11,7},{7,3},{24,20},{20,16},... | collective-permute-start | bytes 589832 | tf_op jit(solution)/shard_map/ppermute | solution.py:164
  32.1 21.5 %collective-permute-start.13 = (bf16[3,256,384]{2,1,0:T(8,128)(2,1)S(1)}, bf16[3,256,384]{2,1,0:T(8,128)(2,1)S(1)}, u32[]{:S(2)}, u32[]{:S(2)}) collective-permute-start(bf16[3,256,384]{2,1,0:T(8,128)(2,1)S(1)} %pad_maximum_fusion.1), channel_id=1, source_target_pairs={{0,16},{16,0},{1,17},{17,1},{2,18},{18,2},{3,19},{19,3},{4,20},{20... | collective-permute-start | bytes 1769480 | tf_op jit(solution)/shard_map/ppermute | solution.py:35
  34.5 14.0 %collective-permute-start.11 = (bf16[128,768]{1,0:T(8,128)(2,1)S(1)}, bf16[128,768]{1,0:T(8,128)(2,1)S(1)}, u32[]{:S(2)}, u32[]{:S(2)}) collective-permute-start(bf16[128,768]{1,0:T(8,128)(2,1)S(1)} %add_convert_fusion.3), channel_id=1, source_target_pairs={{4,0},{5,1},{6,2},{7,3},{20,16},{21,17},{22,18},{23,19}} | collective-permute-start | bytes 589832 | tf_op jit(solution)/shard_map/ppermute | solution.py:164
  43.9 5.6 %collective-permute-start.14 = (bf16[128,384]{1,0:T(8,128)(2,1)S(1)}, bf16[128,384]{1,0:T(8,128)(2,1)S(1)}, u32[]{:S(2)}, u32[]{:S(2)}) collective-permute-start(bf16[128,384]{1,0:T(8,128)(2,1)S(1)} %select_select_fusion.2), channel_id=1, source_target_pairs={{0,2},{1,3},{2,0},{3,1},{4,6},{5,7},{6,4},{7,5},{8,10},{9,11},{10,... | collective-permute-start | bytes 294920 | tf_op jit(solution)/shard_map/ppermute | solution.py:31
  46.1 7.6 %collective-permute-start.12 = (bf16[128,768]{1,0:T(8,128)(2,1)S(1)}, bf16[128,768]{1,0:T(8,128)(2,1)S(1)}, u32[]{:S(2)}, u32[]{:S(2)}) collective-permute-start(bf16[128,768]{1,0:T(8,128)(2,1)S(1)} %add_convert_fusion.2), channel_id=1, source_target_pairs={{4,0},{5,1},{6,2},{7,3},{20,16},{21,17},{22,18},{23,19}} | collective-permute-start | bytes 589832 | tf_op jit(solution)/shard_map/ppermute | solution.py:164
  49.5 5.2 %collective-permute-start.15 = (bf16[128,384]{1,0:T(8,128)(2,1)S(1)}, bf16[128,384]{1,0:T(8,128)(2,1)S(1)}, u32[]{:S(2)}, u32[]{:S(2)}) collective-permute-start(bf16[128,384]{1,0:T(8,128)(2,1)S(1)} %select_select_fusion.1), channel_id=1, source_target_pairs={{0,2},{1,3},{2,0},{3,1},{4,6},{5,7},{6,4},{7,5},{8,10},{9,11},{10,... | collective-permute-start | bytes 294920 | tf_op jit(solution)/shard_map/ppermute | solution.py:31
  50.8 7.2 %collective-permute-start.19 = (bf16[256,384]{1,0:T(8,128)(2,1)S(1)}, bf16[256,384]{1,0:T(8,128)(2,1)S(1)}, u32[]{:S(2)}, u32[]{:S(2)}) collective-permute-start(bf16[256,384]{1,0:T(8,128)(2,1)S(1)} %constant_dynamic-update-slice_fusion.3), channel_id=1, source_target_pairs={{0,16},{16,0},{1,17},{17,1},{2,18},{18,2},{3,19},{19,3},{4,20},{20... | collective-permute-start | bytes 589832 | tf_op jit(solution)/shard_map/ppermute | solution.py:35
  54.7 5.7 %collective-permute-start.18 = (bf16[256,384]{1,0:T(8,128)(2,1)S(1)}, bf16[256,384]{1,0:T(8,128)(2,1)S(1)}, u32[]{:S(2)}, u32[]{:S(2)}) collective-permute-start(bf16[256,384]{1,0:T(8,128)(2,1)S(1)} %constant_dynamic-update-slice_fusion.5), channel_id=1, source_target_pairs={{0,16},{16,0},{1,17},{17,1},{2,18},{18,2},{3,19},{19,3},{4,20},{20... | collective-permute-start | bytes 589832 | tf_op jit(solution)/shard_map/ppermute | solution.py:35
  56.8 6.3 %collective-permute-start.16 = (bf16[2,192,384]{2,1,0:T(8,128)(2,1)S(1)}, bf16[2,192,384]{2,1,0:T(8,128)(2,1)S(1)}, u32[]{:S(2)}, u32[]{:S(2)}) collective-permute-start(bf16[2,192,384]{2,1,0:T(8,128)(2,1)S(1)} %fusion.130), channel_id=1, source_target_pairs={{0,1},{1,0},{2,3},{3,2},{4,5},{5,4},{6,7},{7,6},{8,9},{9,8},{10,11... | collective-permute-start | bytes 884744 | tf_op jit(solution)/shard_map/ppermute | solution.py:31
  57.1 5.3 %collective-permute-start.17 = (bf16[128,384]{1,0:T(8,128)(2,1)S(1)}, bf16[128,384]{1,0:T(8,128)(2,1)S(1)}, u32[]{:S(2)}, u32[]{:S(2)}) collective-permute-start(bf16[128,384]{1,0:T(8,128)(2,1)S(1)} %select_select_fusion), channel_id=1, source_target_pairs={{0,2},{1,3},{2,0},{3,1},{4,6},{5,7},{6,4},{7,5},{8,10},{9,11},{10,... | collective-permute-start | bytes 294920 | tf_op jit(solution)/shard_map/ppermute | solution.py:31
  62.4 7.6 %collective-permute-start.22 = (bf16[256,384]{1,0:T(8,128)(2,1)S(1)}, bf16[256,384]{1,0:T(8,128)(2,1)S(1)}, u32[]{:S(2)}, u32[]{:S(2)}) collective-permute-start(bf16[256,384]{1,0:T(8,128)(2,1)S(1)} %constant_dynamic-update-slice_fusion.7), channel_id=1, source_target_pairs={{0,16},{16,0},{1,17},{17,1},{2,18},{18,2},{3,19},{19,3},{4,20},{20... | collective-permute-start | bytes 589832 | tf_op jit(solution)/shard_map/ppermute | solution.py:35
  63.1 5.2 %collective-permute-start.23 = (bf16[192,384]{1,0:T(8,128)(2,1)S(1)}, bf16[192,384]{1,0:T(8,128)(2,1)S(1)}, u32[]{:S(2)}, u32[]{:S(2)}) collective-permute-start(bf16[192,384]{1,0:T(8,128)(2,1)S(1)} %fusion.230), channel_id=1, source_target_pairs={{0,2},{1,3},{2,0},{3,1},{4,6},{5,7},{6,4},{7,5},{8,10},{9,11},{10,... | collective-permute-start | bytes 442376 | tf_op jit(solution)/shard_map/ppermute | solution.py:31
  64.1 1.6 %collective-permute-start.20 = (bf16[3,1,4,2,8,768]{5,4,2,3,0,1:T(8,128)(2,1)S(1)}, bf16[3,1,4,2,8,768]{5,4,2,3,0,1:T(8,128)(2,1)S(1)}, u32[]{:S(2)}, u32[]{:S(2)}) collective-permute-start(bf16[3,1,4,2,8,768]{5,4,2,3,0,1:T(8,128)(2,1)S(1)} %dynamic-slice_bitcast_fusion), channel_id=1, source_target_pairs={{0,1},{1,0},{2,3},{3,2},{4,5},{5,4},{6,7},{7,6},{8,9},{9,8},{10,11... | collective-permute-start | bytes 884744 | tf_op jit(solution)/shard_map/ppermute | solution.py:31
  65.8 9.1 %collective-permute-start.21 = (bf16[3,2,4,1,8,768]{5,4,1,2,0,3:T(8,128)(2,1)S(1)}, bf16[3,2,4,1,8,768]{5,4,1,2,0,3:T(8,128)(2,1)S(1)}, u32[]{:S(2)}, u32[]{:S(2)}) collective-permute-start(bf16[3,2,4,1,8,768]{5,4,1,2,0,3:T(8,128)(2,1)S(1)} %bitcast.305), channel_id=1, source_target_pairs={{0,2},{1,3},{2,0},{3,1},{4,6},{5,7},{6,4},{7,5},{8,10},{9,11},{10,... | collective-permute-start | bytes 884744 | tf_op jit(solution)/shard_map/ppermute | solution.py:31
  68.5 7.6 %collective-permute-start.25 = (bf16[192,384]{1,0:T(8,128)(2,1)S(1)}, bf16[192,384]{1,0:T(8,128)(2,1)S(1)}, u32[]{:S(2)}, u32[]{:S(2)}) collective-permute-start(bf16[192,384]{1,0:T(8,128)(2,1)S(1)} %fusion.192), channel_id=1, source_target_pairs={{0,16},{16,0},{1,17},{17,1},{2,18},{18,2},{3,19},{19,3},{4,20},{20... | collective-permute-start | bytes 442376 | tf_op jit(solution)/shard_map/ppermute | solution.py:35
  76.0 1.9 %collective-permute-start.24 = (bf16[192,1152]{1,0:T(8,128)(2,1)S(1)}, bf16[192,1152]{1,0:T(8,128)(2,1)S(1)}, u32[]{:S(2)}, u32[]{:S(2)}) collective-permute-start(bf16[192,1152]{1,0:T(8,128)(2,1)S(1)} %select_convert_fusion), channel_id=1, source_target_pairs={{0,1},{1,0},{2,3},{3,2},{4,5},{5,4},{6,7},{7,6},{8,9},{9,8},{10,11... | collective-permute-start | bytes 1327112 | tf_op jit(solution)/shard_map/ppermute | solution.py:31
  (2 other events, 2.1 us)

commit v5 on v4

--- a/solution.py
+++ b/solution.py
@@ -42,19 +42,21 @@
 def exchange(value, number):
     count = lax.axis_size("seq")
     bit = 1
+    comes = []
     while bit < count:
         batch, source, inner, target, rest, channels = value.shape
         split = value.reshape(batch, source, inner, target // 2, 2, rest, channels)
         mine = (number // bit) % 2
         keep = pick(split, mine, 4)
         come = seq_swap(pick(split, 1 - mine, 4), bit)
+        comes.append(come)
         first = jnp.where(mine == 0, keep, come)
         second = jnp.where(mine == 0, come, keep)
         value = jnp.stack([first, second], axis=1).reshape(
             batch, 2 * source, inner, target // 2, rest, channels
         )
         bit *= 2
-    return value[:, :, :, 0], come
+    return value[:, :, :, 0], comes
 
 
 def to_residues(value, number):
@@ -70,8 +72,8 @@
     own = BASE_DILATION // count
     inner = rows // BASE_DILATION
     value = value.reshape(batch, 1, count, inner, own, channels).transpose(0, 1, 3, 2, 4, 5)
-    value, come = exchange(value, number)
-    return value.transpose(0, 2, 1, 3, 4).reshape(batch, rows, channels), come
+    value, comes = exchange(value, number)
+    return value.transpose(0, 2, 1, 3, 4).reshape(batch, rows, channels), comes
 
 
 def shifts(value, step):
@@ -160,8 +162,18 @@
 
     def send_down(value, now):
         hops = [hop for hop in range(sections - 1) if 0 <= now - LAG * hop < micro]
-        pairs = [(sections - 1 - hop, sections - 2 - hop) for hop in hops]
-        return lax.ppermute(value, "section", pairs)
+        return {
+            hop: lax.ppermute(value, "section", [(sections - 1 - hop, sections - 2 - hop)])
+            for hop in reversed(hops)
+        }
+
+    def receive(comes, *events):
+        value = None
+        for hop, come in comes.items():
+            come = after(come, *events)
+            events = (come,)
+            value = come if value is None else jnp.where(section == sections - 2 - hop, come, value)
+        return value
 
     def forward(block_in):
         pre = block_in.astype(jnp.float32) * norm_scale[0] + norm_shift[0]
@@ -311,8 +323,8 @@
             if gathered and now == FAR:
                 events.append(far_hidden)
             if gathered and now == ticks - 1:
-                events.append(near_grad[0])
-            received = after(sent[now - LAG], *events)
+                events += [near_grad[0], comes_early[0]]
+            received = receive(sent[now - LAG], *events)
         done.append(tick(now - LAG * (sections - 1 - section), received))
         if now + LAG < ticks:
             sent.append(send_down(done[now][2], now))
@@ -340,6 +352,9 @@
         if gathered and m >= 1:
             near_grad[m - 1] = jnp.concatenate(after(near_grad[m - 1], done[now]))
             far_grad[m - 1] = dp_swap(near_grad[m - 1])
+        if gathered and m == micro - 2:
+            early = jnp.stack([of_section(one, 2) for one in range(micro - 1)])
+            early, comes_early = from_residues(early, number)
 
     def add_conv(total, m, *events):
         if gathered:
@@ -360,22 +375,24 @@
         keep = choose(core == 0, quarters[:, 0], quarters[:, 1])
         send = choose(core == 0, quarters[:, 1], quarters[:, 0]).astype(jnp.bfloat16)
         come_out = seq_swap(send, 1)
-        far_grad[-2] = after(far_grad[-2], send, far_grad[0])
-        near_grad[-1] = jnp.concatenate(after(near_grad[-1], far_grad[-2]))
+        near_grad[-1] = jnp.concatenate(after(near_grad[-1], send))
         far_grad[-1] = dp_swap(near_grad[-1])
+        far_grad[-2] = after(far_grad[-2], near_grad[-1])
         come_out = after(come_out, near_grad[-1]).astype(jnp.float32)
         columns = [keep[0] + come_out[0], keep[1] + come_out[1]]
         send = choose(side == 0, columns[1], columns[0]).astype(jnp.bfloat16)
         keep = choose(side == 0, columns[0], columns[1])
         come = seq_swap(send, 2)
-        grads = jnp.stack([of_section(m, 2) for m in range(micro)])
-        grads_out, arrived_last = from_residues(after(grads, send), number)
+        late = after(of_section(micro - 1, 2)[None], send)
+        late, comes_late = from_residues(late, number)
+        grads_out = jnp.concatenate([early, late])
         for m in range(micro - 1):
-            conv_total = lax.optimization_barrier(add_conv(conv_total, m, send))
+            events = [send] if m == 0 else [send, comes_early[-1]]
+            conv_total = lax.optimization_barrier(add_conv(conv_total, m, *events))
         come = after(come, conv_total)
         columns = (keep + come.astype(jnp.float32)).astype(jnp.bfloat16)
         come_out = dp_swap(columns)
-        conv_total = add_conv(conv_total, micro - 1, columns, arrived_last)
+        conv_total = add_conv(conv_total, micro - 1, columns)
         out_sum = (columns.astype(jnp.float32) + come_out.astype(jnp.float32)).T
     else:
         for m in range(micro):
@@ -386,6 +403,7 @@
     if gathered:
         low, high = conv_total[:share], conv_total[share:]
         come = seq_swap(choose(core == 0, high, low).astype(jnp.bfloat16), 1)
+        come = after(come, comes_late[-1])
         conv_sum = choose(core == 0, low, high) + come.astype(jnp.float32)
         conv_sum = jnp.stack([conv_sum[:, k * inner : (k + 1) * inner] for k in range(3)])
     else:

time: 79.3 us -> 75.4 us (0.951)
  waiting for transfers between devices: 25.4 us -> 18.7 us
  starting transfers between devices: 28.2 us -> 30.8 us
    ppermute x14 -> x16, waiting for transfers between devices: 14.3 us -> 11 us  [seq_swap(): return lax.ppermute(value, 'seq', [(i, i ^ bit) for i in range(count)])]
    ppermute x7 -> x9, waiting for transfers between devices: 8.54 us -> 6.34 us  [send_down(): lax.ppermute(value, 'section', [(sections - 1 - hop, sections - 2 - hop)])]
    ppermute x14 -> x16, starting transfers between devices: 14.8 us -> 16.7 us  [seq_swap(): return lax.ppermute(value, 'seq', [(i, i ^ bit) for i in range(count)])]
    ppermute x7 -> x9, starting transfers between devices: 6.74 us -> 8.08 us  [send_down(): lax.ppermute(value, 'section', [(sections - 1 - hop, sections - 2 - hop)])]
    ppermute x5, waiting for transfers between devices: 2.5 us -> 1.38 us  [dp_swap(): return lax.ppermute(value, 'dp', [(0, 1), (1, 0)])]
    reshape x0 -> x1, other arithmetic: none -> 0.87 us  [on_device(): grads_out.reshape(section_inputs.shape)]
  transfers between devices with their start and end apart: 26 -> 30, of which waited for: 13 -> 13; matrix products, arithmetic and copies ran while one was open for 25% -> 27% of each run, Pallas kernels for 0% -> 0%
where the time goes in v5:
time: 75.4 us; the launch traced here: 75.1 us
  starting transfers between devices  30.8 us (41%)
  waiting for transfers between devices  18.7 us (25%)
  matrix products  13.4 us (18%)
  other arithmetic  6.49 us (9%)
  local copies, waits for them, and re-layouts  3.61 us (5%)
  between operations  1.83 us (2%)
    ppermute x16, starting transfers between devices, seq_swap(): return lax.ppermute(value, 'seq', [(i, i ^ bit) for i in range(count)])  16.7 us
    ppermute x16, waiting for transfers between devices, seq_swap(): return lax.ppermute(value, 'seq', [(i, i ^ bit) for i in range(count)])  11 us
    ppermute x9, starting transfers between devices, send_down(): lax.ppermute(value, 'section', [(sections - 1 - hop, sections - 2 - hop)])  8.08 us
    ppermute x9, waiting for transfers between devices, send_down(): lax.ppermute(value, 'section', [(sections - 1 - hop, sections - 2 - hop)])  6.34 us
    ppermute x5, starting transfers between devices, dp_swap(): return lax.ppermute(value, 'dp', [(0, 1), (1, 0)])  5.99 us
    dot_general x9, matrix products, tick(): grad_hidden = jnp.dot(back, back_kernel, preferred_element_type=jnp.float32)  4.09 us
    dot_general x9, matrix products, tick(): lax.dot_general(grad_top, out_w, (((1,), (1,)), ((), ())), preferred_elem...  2.85 us
    unnamed x21, local copies, waits for them, and re-layouts  2.27 us
  transfers between devices with their start and end apart: 30, of which 13 were waited for; matrix products, arithmetic and copies ran while one was open for 27% of the time, Pallas kernels for 0%

profile of v5, /device:TPU:0, one launch (start us, length us, event | category | flops | bytes accessed | tf_op | source)
XLA Modules:
  0.0 75.1 jit_solution(15724882442145724564)
XLA Ops:
  0.7 1.1 %copy-done.1 = bf16[1,3,1,128,768]{4,3,2,1,0:T(8,128)(2,1)S(1)} copy-done((bf16[1,3,1,128,768]{4,3,2,1,0:T(8,128)(2,1)S(1)}, bf16[1,3,1,128,768]{4,3,2,1,0:T(8,128)(2,1)}, u32[]{:S(2)}) %copy-start.1) | copy-done | bytes 589848
  1.8 1.1 %copy-done.2 = bf16[3,1,128,768]{3,2,1,0:T(8,128)(2,1)S(1)} copy-done((bf16[3,1,128,768]{3,2,1,0:T(8,128)(2,1)S(1)}, bf16[3,1,128,768]{3,2,1,0:T(8,128)(2,1)}, u32[]{:S(2)}) %copy-start.2) | copy-done | bytes 589848
  4.6 3.0 %collective-permute-start.2 = (bf16[2,2,32,768]{3,2,0,1:T(8,128)(2,1)S(1)}, bf16[2,2,32,768]{3,2,0,1:T(8,128)(2,1)S(1)}, u32[]{:S(2)}, u32[]{:S(2)}) collective-permute-start(bf16[2,2,32,768]{3,2,0,1:T(8,128)(2,1)S(1)} %pad_maximum_fusion.12), channel_id=1, source_target_pairs={{0,2},{1,3},{2,0},{3,1},{4,6},{5,7},{6,4},{7,5},{8,10},{9,11},{10,... | collective-permute-start | bytes 589832 | tf_op jit(solution)/shard_map/ppermute | solution.py:31
  9.3 1.2 %collective-permute-start.4 = (bf16[2,2,32,768]{3,2,0,1:T(8,128)(2,1)S(1)}, bf16[2,2,32,768]{3,2,0,1:T(8,128)(2,1)S(1)}, u32[]{:S(2)}, u32[]{:S(2)}) collective-permute-start(bf16[2,2,32,768]{3,2,0,1:T(8,128)(2,1)S(1)} %get-tuple-element.93), channel_id=1, source_target_pairs={{0,2},{1,3},{2,0},{3,1},{4,6},{5,7},{6,4},{7,5},{8,10},{9,11},{10,... | collective-permute-start | bytes 589832 | tf_op jit(solution)/shard_map/ppermute | solution.py:31
  10.7 2.6 %collective-permute-done.2 = bf16[2,2,32,768]{3,2,0,1:T(8,128)(2,1)S(1)} collective-permute-done((bf16[2,2,32,768]{3,2,0,1:T(8,128)(2,1)S(1)}, bf16[2,2,32,768]{3,2,0,1:T(8,128)(2,1)S(1)}, u32[]{:S(2)}, u32[]{:S(2)}) %collective-permute-start.2) | collective-permute-done | bytes 196640 | tf_op jit(solution)/shard_map/ppermute | solution.py:31
  15.9 2.1 %collective-permute-start.3 = (bf16[2,2,32,768]{3,2,0,1:T(8,128)(2,1)S(1)}, bf16[2,2,32,768]{3,2,0,1:T(8,128)(2,1)S(1)}, u32[]{:S(2)}, u32[]{:S(2)}) collective-permute-start(bf16[2,2,32,768]{3,2,0,1:T(8,128)(2,1)S(1)} %get-tuple-element.101), channel_id=1, source_target_pairs={{0,2},{1,3},{2,0},{3,1},{4,6},{5,7},{6,4},{7,5},{8,10},{9,11},{10,... | collective-permute-start | bytes 589832 | tf_op jit(solution)/shard_map/ppermute | solution.py:31
  20.8 1.2 %collective-permute-done.3 = bf16[2,2,32,768]{3,2,0,1:T(8,128)(2,1)S(1)} collective-permute-done((bf16[2,2,32,768]{3,2,0,1:T(8,128)(2,1)S(1)}, bf16[2,2,32,768]{3,2,0,1:T(8,128)(2,1)S(1)}, u32[]{:S(2)}, u32[]{:S(2)}) %collective-permute-start.3) | collective-permute-done | bytes 196640 | tf_op jit(solution)/shard_map/ppermute | solution.py:31
  25.5 1.8 %collective-permute-start.12 = (bf16[384,384]{1,0:T(8,128)(2,1)S(1)}, bf16[384,384]{1,0:T(8,128)(2,1)S(1)}, u32[]{:S(2)}, u32[]{:S(2)}) collective-permute-start(bf16[384,384]{1,0:T(8,128)(2,1)S(1)} %get-tuple-element.180), channel_id=1, source_target_pairs={{0,2},{1,3},{2,0},{3,1},{4,6},{5,7},{6,4},{7,5},{8,10},{9,11},{10,... | collective-permute-start | bytes 884744 | tf_op jit(solution)/shard_map/ppermute | solution.py:31
  29.9 1.3 %collective-permute-start.10 = (bf16[128,768]{1,0:T(8,128)(2,1)S(1)}, bf16[128,768]{1,0:T(8,128)(2,1)S(1)}, u32[]{:S(2)}, u32[]{:S(2)}) collective-permute-start(bf16[128,768]{1,0:T(8,128)(2,1)S(1)} %fusion.27), channel_id=1, source_target_pairs={{4,0},{5,1},{6,2},{7,3},{20,16},{21,17},{22,18},{23,19}} | collective-permute-start | bytes 589832 | tf_op jit(solution)/shard_map/ppermute | solution.py:166
  31.9 0.8 %collective-permute-done.12 = bf16[384,384]{1,0:T(8,128)(2,1)S(1)} collective-permute-done((bf16[384,384]{1,0:T(8,128)(2,1)S(1)}, bf16[384,384]{1,0:T(8,128)(2,1)S(1)}, u32[]{:S(2)}, u32[]{:S(2)}) %collective-permute-start.12) | collective-permute-done | bytes 294944 | tf_op jit(solution)/shard_map/ppermute | solution.py:31
  32.7 1.4 %collective-permute-start.17 = (bf16[3,256,384]{2,1,0:T(8,128)(2,1)S(1)}, bf16[3,256,384]{2,1,0:T(8,128)(2,1)S(1)}, u32[]{:S(2)}, u32[]{:S(2)}) collective-permute-start(bf16[3,256,384]{2,1,0:T(8,128)(2,1)S(1)} %pad_maximum_fusion.1), channel_id=1, source_target_pairs={{0,16},{16,0},{1,17},{17,1},{2,18},{18,2},{3,19},{19,3},{4,20},{20... | collective-permute-start | bytes 1769480 | tf_op jit(solution)/shard_map/ppermute | solution.py:35
  35.1 1.3 %collective-permute-start.13 = (bf16[128,768]{1,0:T(8,128)(2,1)S(1)}, bf16[128,768]{1,0:T(8,128)(2,1)S(1)}, u32[]{:S(2)}, u32[]{:S(2)}) collective-permute-start(bf16[128,768]{1,0:T(8,128)(2,1)S(1)} %add_convert_fusion.2), channel_id=1, source_target_pairs={{4,0},{5,1},{6,2},{7,3},{20,16},{21,17},{22,18},{23,19}} | collective-permute-start | bytes 589832 | tf_op jit(solution)/shard_map/ppermute | solution.py:166
  36.4 5.2 %collective-permute-done.10 = bf16[128,768]{1,0:T(8,128)(2,1)S(1)} collective-permute-done((bf16[128,768]{1,0:T(8,128)(2,1)S(1)}, bf16[128,768]{1,0:T(8,128)(2,1)S(1)}, u32[]{:S(2)}, u32[]{:S(2)}) %collective-permute-start.10) | collective-permute-done | bytes 196640 | tf_op jit(solution)/shard_map/ppermute | solution.py:166
  42.5 2.6 %collective-permute-start.18 = (bf16[128,384]{1,0:T(8,128)(2,1)S(1)}, bf16[128,384]{1,0:T(8,128)(2,1)S(1)}, u32[]{:S(2)}, u32[]{:S(2)}) collective-permute-start(bf16[128,384]{1,0:T(8,128)(2,1)S(1)} %select_select_fusion.4), channel_id=1, source_target_pairs={{0,2},{1,3},{2,0},{3,1},{4,6},{5,7},{6,4},{7,5},{8,10},{9,11},{10,... | collective-permute-start | bytes 294920 | tf_op jit(solution)/shard_map/ppermute | solution.py:31
  45.1 1.5 %collective-permute-start.16 = (bf16[128,768]{1,0:T(8,128)(2,1)S(1)}, bf16[128,768]{1,0:T(8,128)(2,1)S(1)}, u32[]{:S(2)}, u32[]{:S(2)}) collective-permute-start(bf16[128,768]{1,0:T(8,128)(2,1)S(1)} %fusion.26), channel_id=1, source_target_pairs={{4,0},{5,1},{6,2},{7,3},{20,16},{21,17},{22,18},{23,19}} | collective-permute-start | bytes 589832 | tf_op jit(solution)/shard_map/ppermute | solution.py:166
  47.0 1.2 %collective-permute-done.13 = bf16[128,768]{1,0:T(8,128)(2,1)S(1)} collective-permute-done((bf16[128,768]{1,0:T(8,128)(2,1)S(1)}, bf16[128,768]{1,0:T(8,128)(2,1)S(1)}, u32[]{:S(2)}, u32[]{:S(2)}) %collective-permute-start.13) | collective-permute-done | bytes 196640 | tf_op jit(solution)/shard_map/ppermute | solution.py:166
  49.3 1.3 %collective-permute-start.19 = (bf16[128,384]{1,0:T(8,128)(2,1)S(1)}, bf16[128,384]{1,0:T(8,128)(2,1)S(1)}, u32[]{:S(2)}, u32[]{:S(2)}) collective-permute-start(bf16[128,384]{1,0:T(8,128)(2,1)S(1)} %select_select_fusion.3), channel_id=1, source_target_pairs={{0,2},{1,3},{2,0},{3,1},{4,6},{5,7},{6,4},{7,5},{8,10},{9,11},{10,... | collective-permute-start | bytes 294920 | tf_op jit(solution)/shard_map/ppermute | solution.py:31
  50.6 0.8 %collective-permute-start.24 = (bf16[256,384]{1,0:T(8,128)(2,1)S(1)}, bf16[256,384]{1,0:T(8,128)(2,1)S(1)}, u32[]{:S(2)}, u32[]{:S(2)}) collective-permute-start(bf16[256,384]{1,0:T(8,128)(2,1)S(1)} %constant_dynamic-update-slice_fusion.3), channel_id=1, source_target_pairs={{0,16},{16,0},{1,17},{17,1},{2,18},{18,2},{3,19},{19,3},{4,20},{20... | collective-permute-start | bytes 589832 | tf_op jit(solution)/shard_map/ppermute | solution.py:35
  51.9 1.7 %collective-permute-start.15 = (bf16[2,2,4,1,8,768]{5,4,1,2,0,3:T(8,128)(2,1)S(1)}, bf16[2,2,4,1,8,768]{5,4,1,2,0,3:T(8,128)(2,1)S(1)}, u32[]{:S(2)}, u32[]{:S(2)}) collective-permute-start(bf16[2,2,4,1,8,768]{5,4,1,2,0,3:T(8,128)(2,1)S(1)} %bitcast.347), channel_id=1, source_target_pairs={{0,2},{1,3},{2,0},{3,1},{4,6},{5,7},{6,4},{7,5},{8,10},{9,11},{10,... | collective-permute-start | bytes 589832 | tf_op jit(solution)/shard_map/ppermute | solution.py:31
  55.3 1.6 %collective-permute-start.25 = (bf16[256,384]{1,0:T(8,128)(2,1)S(1)}, bf16[256,384]{1,0:T(8,128)(2,1)S(1)}, u32[]{:S(2)}, u32[]{:S(2)}) collective-permute-start(bf16[256,384]{1,0:T(8,128)(2,1)S(1)} %constant_dynamic-update-slice_fusion.5), channel_id=1, source_target_pairs={{0,16},{16,0},{1,17},{17,1},{2,18},{18,2},{3,19},{19,3},{4,20},{20... | collective-permute-start | bytes 589832 | tf_op jit(solution)/shard_map/ppermute | solution.py:35
  57.3 1.6 %collective-permute-done.15 = bf16[2,2,4,1,8,768]{5,4,1,2,0,3:T(8,128)(2,1)S(1)} collective-permute-done((bf16[2,2,4,1,8,768]{5,4,1,2,0,3:T(8,128)(2,1)S(1)}, bf16[2,2,4,1,8,768]{5,4,1,2,0,3:T(8,128)(2,1)S(1)}, u32[]{:S(2)}, u32[]{:S(2)}) %collective-permute-start.15) | collective-permute-done | bytes 196640 | tf_op jit(solution)/shard_map/ppermute | solution.py:31
  58.9 2.6 %collective-permute-done.21 = bf16[128,384]{1,0:T(8,128)(2,1)S(1)} collective-permute-done((bf16[128,384]{1,0:T(8,128)(2,1)S(1)}, bf16[128,384]{1,0:T(8,128)(2,1)S(1)}, u32[]{:S(2)}, u32[]{:S(2)}) %collective-permute-start.21) | collective-permute-done | bytes 98336 | tf_op jit(solution)/shard_map/ppermute | solution.py:31
  61.6 0.9 %collective-permute-start.26 = (bf16[256,384]{1,0:T(8,128)(2,1)S(1)}, bf16[256,384]{1,0:T(8,128)(2,1)S(1)}, u32[]{:S(2)}, u32[]{:S(2)}) collective-permute-start(bf16[256,384]{1,0:T(8,128)(2,1)S(1)} %constant_dynamic-update-slice_fusion.7), channel_id=1, source_target_pairs={{0,16},{16,0},{1,17},{17,1},{2,18},{18,2},{3,19},{19,3},{4,20},{20... | collective-permute-start | bytes 589832 | tf_op jit(solution)/shard_map/ppermute | solution.py:35
  62.6 0.7 collective-permute-start.27
  64.6 0.7 convolution_add_fusion.1
  66.0 1.4 %collective-permute-start.23 = (bf16[1,2,4,1,8,768]{5,4,1,2,3,0:T(8,128)(2,1)S(1)}, bf16[1,2,4,1,8,768]{5,4,1,2,3,0:T(8,128)(2,1)S(1)}, u32[]{:S(2)}, u32[]{:S(2)}) collective-permute-start(bf16[1,2,4,1,8,768]{5,4,1,2,3,0:T(8,128)(2,1)S(1)} %bitcast.348), channel_id=1, source_target_pairs={{0,2},{1,3},{2,0},{3,1},{4,6},{5,7},{6,4},{7,5},{8,10},{9,11},{10,... | collective-permute-start | bytes 294920 | tf_op jit(solution)/shard_map/ppermute | solution.py:31
  67.9 1.2 %collective-permute-start.29 = (bf16[192,384]{1,0:T(8,128)(2,1)S(1)}, bf16[192,384]{1,0:T(8,128)(2,1)S(1)}, u32[]{:S(2)}, u32[]{:S(2)}) collective-permute-start(bf16[192,384]{1,0:T(8,128)(2,1)S(1)} %fusion.190), channel_id=1, source_target_pairs={{0,16},{16,0},{1,17},{17,1},{2,18},{18,2},{3,19},{19,3},{4,20},{20... | collective-permute-start | bytes 442376 | tf_op jit(solution)/shard_map/ppermute | solution.py:35
  69.4 0.7 convolution_add_fusion
  70.9 0.9 %maximum_bitcast_fusion = bf16[1,3,1,128,768]{4,3,2,1,0:T(8,128)(2,1)} fusion(bf16[1,128,768]{2,1,0:T(8,128)(2,1)S(1)} %bitcast.335, bf16[2,128,768]{2,1,0:T(8,128)(2,1)S(1)} %bitcast.329), kind=kLoop, calls=%fused_computation.98 | loop fusion | flops 294912 | bytes 1179648 | tf_op jit(solution)/shard_map/reshape | solution.py:420
  71.8 1.4 %collective-permute-done.29 = bf16[192,384]{1,0:T(8,128)(2,1)S(1)} collective-permute-done((bf16[192,384]{1,0:T(8,128)(2,1)S(1)}, bf16[192,384]{1,0:T(8,128)(2,1)S(1)}, u32[]{:S(2)}, u32[]{:S(2)}) %collective-permute-start.29) | collective-permute-done | bytes 147488 | tf_op jit(solution)/shard_map/ppermute | solution.py:35
  73.2 0.8 %multiply_bitcast_fusion = f32[1,384,192]{1,2,0:T(8,128)} fusion(bf16[192,384]{1,0:T(8,128)(2,1)S(1)} %collective-permute-done.29, bf16[192,384]{1,0:T(8,128)(2,1)S(1)} %fusion.190), kind=kLoop, calls=%fused_computation.265 | loop fusion | flops 294912 | bytes 589824 | tf_op jit(solution)/shard_map/broadcast_in_dim | solution.py:422
  74.1 1.0 %maximum_multiply_fusion = f32[1,3,192,384]{3,2,1,0:T(8,128)} fusion(f32[1,1,192,384]{3,2,1,0:T(8,128)S(1)} %get-tuple-element.176, f32[1,1,192,384]{3,2,1,0:T(8,128)S(1)} %get-tuple-element.177, f32[1,1,192,384]{3,2,1,0:T(8,128)S(1)} %get-tuple-element.175), kind=kLoop, calls=%fused_computation.71 | loop fusion | flops 663552 | bytes 1769472 | tf_op jit(solution)/shard_map/mul | solution.py:421
  (175 shorter events, 24.8 us)
Async XLA Ops:
  0.6 13.7 %copy-start = (bf16[1,384,768]{2,1,0:T(8,128)(2,1)S(1)}, bf16[1,384,768]{2,1,0:T(8,128)(2,1)}, u32[]{:S(2)}) copy-start(bf16[1,384,768]{2,1,0:T(8,128)(2,1)} %param.11) | copy-start | bytes 1769476
  3.0 1.6 %collective-permute-start = (bf16[2,2,32,768]{3,2,0,1:T(8,128)(2,1)S(1)}, bf16[2,2,32,768]{3,2,0,1:T(8,128)(2,1)S(1)}, u32[]{:S(2)}, u32[]{:S(2)}) collective-permute-start(bf16[2,2,32,768]{3,2,0,1:T(8,128)(2,1)S(1)} %copy.12), channel_id=1, source_target_pairs={{0,1},{1,0},{2,3},{3,2},{4,5},{5,4},{6,7},{7,6},{8,9},{9,8},{10,11... | collective-permute-start | bytes 589832 | tf_op jit(solution)/shard_map/ppermute | solution.py:31
  3.7 3.9 %collective-permute-start.1 = (bf16[4,2,32,768]{3,2,0,1:T(8,128)(2,1)S(1)}, bf16[4,2,32,768]{3,2,0,1:T(8,128)(2,1)S(1)}, u32[]{:S(2)}, u32[]{:S(2)}) collective-permute-start(bf16[4,2,32,768]{3,2,0,1:T(8,128)(2,1)S(1)} %copy.14), channel_id=1, source_target_pairs={{0,1},{1,0},{2,3},{3,2},{4,5},{5,4},{6,7},{7,6},{8,9},{9,8},{10,11... | collective-permute-start | bytes 1179656 | tf_op jit(solution)/shard_map/ppermute | solution.py:31
  4.6 3.2 %copy-start.3 = (bf16[1,3,768,384]{3,2,1,0:T(8,128)(2,1)S(1)}, bf16[1,3,768,384]{3,2,1,0:T(8,128)(2,1)}, u32[]{:S(2)}) copy-start(bf16[1,3,768,384]{3,2,1,0:T(8,128)(2,1)} %param.10) | copy-start | bytes 5308420
  4.6 8.6 %collective-permute-start.2 = (bf16[2,2,32,768]{3,2,0,1:T(8,128)(2,1)S(1)}, bf16[2,2,32,768]{3,2,0,1:T(8,128)(2,1)S(1)}, u32[]{:S(2)}, u32[]{:S(2)}) collective-permute-start(bf16[2,2,32,768]{3,2,0,1:T(8,128)(2,1)S(1)} %pad_maximum_fusion.12), channel_id=1, source_target_pairs={{0,2},{1,3},{2,0},{3,1},{4,6},{5,7},{6,4},{7,5},{8,10},{9,11},{10,... | collective-permute-start | bytes 589832 | tf_op jit(solution)/shard_map/ppermute | solution.py:31
  9.3 8.8 %collective-permute-start.4 = (bf16[2,2,32,768]{3,2,0,1:T(8,128)(2,1)S(1)}, bf16[2,2,32,768]{3,2,0,1:T(8,128)(2,1)S(1)}, u32[]{:S(2)}, u32[]{:S(2)}) collective-permute-start(bf16[2,2,32,768]{3,2,0,1:T(8,128)(2,1)S(1)} %get-tuple-element.93), channel_id=1, source_target_pairs={{0,2},{1,3},{2,0},{3,1},{4,6},{5,7},{6,4},{7,5},{8,10},{9,11},{10,... | collective-permute-start | bytes 589832 | tf_op jit(solution)/shard_map/ppermute | solution.py:31
  15.2 7.8 %collective-permute-start.5 = (bf16[128,768]{1,0:T(8,128)(2,1)S(1)}, bf16[128,768]{1,0:T(8,128)(2,1)S(1)}, u32[]{:S(2)}, u32[]{:S(2)}) collective-permute-start(bf16[128,768]{1,0:T(8,128)(2,1)S(1)} %fusion.29), channel_id=1, source_target_pairs={{12,8},{13,9},{14,10},{15,11},{28,24},{29,25},{30,26},{31,27}} | collective-permute-start | bytes 589832 | tf_op jit(solution)/shard_map/ppermute | solution.py:166
  15.9 6.0 %collective-permute-start.3 = (bf16[2,2,32,768]{3,2,0,1:T(8,128)(2,1)S(1)}, bf16[2,2,32,768]{3,2,0,1:T(8,128)(2,1)S(1)}, u32[]{:S(2)}, u32[]{:S(2)}) collective-permute-start(bf16[2,2,32,768]{3,2,0,1:T(8,128)(2,1)S(1)} %get-tuple-element.101), channel_id=1, source_target_pairs={{0,2},{1,3},{2,0},{3,1},{4,6},{5,7},{6,4},{7,5},{8,10},{9,11},{10,... | collective-permute-start | bytes 589832 | tf_op jit(solution)/shard_map/ppermute | solution.py:31
  20.1 7.2 %collective-permute-start.8 = (bf16[128,768]{1,0:T(8,128)(2,1)S(1)}, bf16[128,768]{1,0:T(8,128)(2,1)S(1)}, u32[]{:S(2)}, u32[]{:S(2)}) collective-permute-start(bf16[128,768]{1,0:T(8,128)(2,1)S(1)} %fusion.28), channel_id=1, source_target_pairs={{12,8},{13,9},{14,10},{15,11},{28,24},{29,25},{30,26},{31,27}} | collective-permute-start | bytes 589832 | tf_op jit(solution)/shard_map/ppermute | solution.py:166
  24.0 5.0 %collective-permute-start.7 = (bf16[128,768]{1,0:T(8,128)(2,1)S(1)}, bf16[128,768]{1,0:T(8,128)(2,1)S(1)}, u32[]{:S(2)}, u32[]{:S(2)}) collective-permute-start(bf16[128,768]{1,0:T(8,128)(2,1)S(1)} %add_convert_fusion.4), channel_id=1, source_target_pairs={{8,4},{9,5},{10,6},{11,7},{24,20},{25,21},{26,22},{27,23}} | collective-permute-start | bytes 589832 | tf_op jit(solution)/shard_map/ppermute | solution.py:166
  24.6 4.3 %collective-permute-start.6 = (bf16[128,768]{1,0:T(8,128)(2,1)S(1)}, bf16[128,768]{1,0:T(8,128)(2,1)S(1)}, u32[]{:S(2)}, u32[]{:S(2)}) collective-permute-start(bf16[128,768]{1,0:T(8,128)(2,1)S(1)} %add_convert_fusion.4), channel_id=1, source_target_pairs={{12,8},{13,9},{14,10},{15,11},{28,24},{29,25},{30,26},{31,27}} | collective-permute-start | bytes 589832 | tf_op jit(solution)/shard_map/ppermute | solution.py:166
  25.5 7.2 %collective-permute-start.12 = (bf16[384,384]{1,0:T(8,128)(2,1)S(1)}, bf16[384,384]{1,0:T(8,128)(2,1)S(1)}, u32[]{:S(2)}, u32[]{:S(2)}) collective-permute-start(bf16[384,384]{1,0:T(8,128)(2,1)S(1)} %get-tuple-element.180), channel_id=1, source_target_pairs={{0,2},{1,3},{2,0},{3,1},{4,6},{5,7},{6,4},{7,5},{8,10},{9,11},{10,... | collective-permute-start | bytes 884744 | tf_op jit(solution)/shard_map/ppermute | solution.py:31
  28.2 5.9 %collective-permute-start.11 = (bf16[128,768]{1,0:T(8,128)(2,1)S(1)}, bf16[128,768]{1,0:T(8,128)(2,1)S(1)}, u32[]{:S(2)}, u32[]{:S(2)}) collective-permute-start(bf16[128,768]{1,0:T(8,128)(2,1)S(1)} %add_convert_fusion.3), channel_id=1, source_target_pairs={{8,4},{9,5},{10,6},{11,7},{24,20},{25,21},{26,22},{27,23}} | collective-permute-start | bytes 589832 | tf_op jit(solution)/shard_map/ppermute | solution.py:166
  29.9 11.7 %collective-permute-start.10 = (bf16[128,768]{1,0:T(8,128)(2,1)S(1)}, bf16[128,768]{1,0:T(8,128)(2,1)S(1)}, u32[]{:S(2)}, u32[]{:S(2)}) collective-permute-start(bf16[128,768]{1,0:T(8,128)(2,1)S(1)} %fusion.27), channel_id=1, source_target_pairs={{4,0},{5,1},{6,2},{7,3},{20,16},{21,17},{22,18},{23,19}} | collective-permute-start | bytes 589832 | tf_op jit(solution)/shard_map/ppermute | solution.py:166
  31.2 10.4 %collective-permute-start.9 = (bf16[128,768]{1,0:T(8,128)(2,1)S(1)}, bf16[128,768]{1,0:T(8,128)(2,1)S(1)}, u32[]{:S(2)}, u32[]{:S(2)}) collective-permute-start(bf16[128,768]{1,0:T(8,128)(2,1)S(1)} %fusion.27), channel_id=1, source_target_pairs={{8,4},{9,5},{10,6},{11,7},{24,20},{25,21},{26,22},{27,23}} | collective-permute-start | bytes 589832 | tf_op jit(solution)/shard_map/ppermute | solution.py:166
  32.7 20.9 %collective-permute-start.17 = (bf16[3,256,384]{2,1,0:T(8,128)(2,1)S(1)}, bf16[3,256,384]{2,1,0:T(8,128)(2,1)S(1)}, u32[]{:S(2)}, u32[]{:S(2)}) collective-permute-start(bf16[3,256,384]{2,1,0:T(8,128)(2,1)S(1)} %pad_maximum_fusion.1), channel_id=1, source_target_pairs={{0,16},{16,0},{1,17},{17,1},{2,18},{18,2},{3,19},{19,3},{4,20},{20... | collective-permute-start | bytes 1769480 | tf_op jit(solution)/shard_map/ppermute | solution.py:35
  35.1 13.1 %collective-permute-start.13 = (bf16[128,768]{1,0:T(8,128)(2,1)S(1)}, bf16[128,768]{1,0:T(8,128)(2,1)S(1)}, u32[]{:S(2)}, u32[]{:S(2)}) collective-permute-start(bf16[128,768]{1,0:T(8,128)(2,1)S(1)} %add_convert_fusion.2), channel_id=1, source_target_pairs={{4,0},{5,1},{6,2},{7,3},{20,16},{21,17},{22,18},{23,19}} | collective-permute-start | bytes 589832 | tf_op jit(solution)/shard_map/ppermute | solution.py:166
  42.5 6.8 %collective-permute-start.18 = (bf16[128,384]{1,0:T(8,128)(2,1)S(1)}, bf16[128,384]{1,0:T(8,128)(2,1)S(1)}, u32[]{:S(2)}, u32[]{:S(2)}) collective-permute-start(bf16[128,384]{1,0:T(8,128)(2,1)S(1)} %select_select_fusion.4), channel_id=1, source_target_pairs={{0,2},{1,3},{2,0},{3,1},{4,6},{5,7},{6,4},{7,5},{8,10},{9,11},{10,... | collective-permute-start | bytes 294920 | tf_op jit(solution)/shard_map/ppermute | solution.py:31
  45.1 8.5 %collective-permute-start.16 = (bf16[128,768]{1,0:T(8,128)(2,1)S(1)}, bf16[128,768]{1,0:T(8,128)(2,1)S(1)}, u32[]{:S(2)}, u32[]{:S(2)}) collective-permute-start(bf16[128,768]{1,0:T(8,128)(2,1)S(1)} %fusion.26), channel_id=1, source_target_pairs={{4,0},{5,1},{6,2},{7,3},{20,16},{21,17},{22,18},{23,19}} | collective-permute-start | bytes 589832 | tf_op jit(solution)/shard_map/ppermute | solution.py:166
  49.2 2.6 %collective-permute-start.14 = (bf16[2,1,4,2,8,768]{5,4,2,3,0,1:T(8,128)(2,1)S(1)}, bf16[2,1,4,2,8,768]{5,4,2,3,0,1:T(8,128)(2,1)S(1)}, u32[]{:S(2)}, u32[]{:S(2)}) collective-permute-start(bf16[2,1,4,2,8,768]{5,4,2,3,0,1:T(8,128)(2,1)S(1)} %dynamic-slice_bitcast_fusion), channel_id=1, source_target_pairs={{0,1},{1,0},{2,3},{3,2},{4,5},{5,4},{6,7},{7,6},{8,9},{9,8},{10,11... | collective-permute-start | bytes 589832 | tf_op jit(solution)/shard_map/ppermute | solution.py:31
  49.3 5.4 %collective-permute-start.19 = (bf16[128,384]{1,0:T(8,128)(2,1)S(1)}, bf16[128,384]{1,0:T(8,128)(2,1)S(1)}, u32[]{:S(2)}, u32[]{:S(2)}) collective-permute-start(bf16[128,384]{1,0:T(8,128)(2,1)S(1)} %select_select_fusion.3), channel_id=1, source_target_pairs={{0,2},{1,3},{2,0},{3,1},{4,6},{5,7},{6,4},{7,5},{8,10},{9,11},{10,... | collective-permute-start | bytes 294920 | tf_op jit(solution)/shard_map/ppermute | solution.py:31
  50.6 12.7 %collective-permute-start.24 = (bf16[256,384]{1,0:T(8,128)(2,1)S(1)}, bf16[256,384]{1,0:T(8,128)(2,1)S(1)}, u32[]{:S(2)}, u32[]{:S(2)}) collective-permute-start(bf16[256,384]{1,0:T(8,128)(2,1)S(1)} %constant_dynamic-update-slice_fusion.3), channel_id=1, source_target_pairs={{0,16},{16,0},{1,17},{17,1},{2,18},{18,2},{3,19},{19,3},{4,20},{20... | collective-permute-start | bytes 589832 | tf_op jit(solution)/shard_map/ppermute | solution.py:35
  51.9 7.0 %collective-permute-start.15 = (bf16[2,2,4,1,8,768]{5,4,1,2,0,3:T(8,128)(2,1)S(1)}, bf16[2,2,4,1,8,768]{5,4,1,2,0,3:T(8,128)(2,1)S(1)}, u32[]{:S(2)}, u32[]{:S(2)}) collective-permute-start(bf16[2,2,4,1,8,768]{5,4,1,2,0,3:T(8,128)(2,1)S(1)} %bitcast.347), channel_id=1, source_target_pairs={{0,2},{1,3},{2,0},{3,1},{4,6},{5,7},{6,4},{7,5},{8,10},{9,11},{10,... | collective-permute-start | bytes 589832 | tf_op jit(solution)/shard_map/ppermute | solution.py:31
  55.3 7.2 %collective-permute-start.25 = (bf16[256,384]{1,0:T(8,128)(2,1)S(1)}, bf16[256,384]{1,0:T(8,128)(2,1)S(1)}, u32[]{:S(2)}, u32[]{:S(2)}) collective-permute-start(bf16[256,384]{1,0:T(8,128)(2,1)S(1)} %constant_dynamic-update-slice_fusion.5), channel_id=1, source_target_pairs={{0,16},{16,0},{1,17},{17,1},{2,18},{18,2},{3,19},{19,3},{4,20},{20... | collective-permute-start | bytes 589832 | tf_op jit(solution)/shard_map/ppermute | solution.py:35
  56.9 4.6 %collective-permute-start.21 = (bf16[128,384]{1,0:T(8,128)(2,1)S(1)}, bf16[128,384]{1,0:T(8,128)(2,1)S(1)}, u32[]{:S(2)}, u32[]{:S(2)}) collective-permute-start(bf16[128,384]{1,0:T(8,128)(2,1)S(1)} %select_select_fusion.2), channel_id=1, source_target_pairs={{0,2},{1,3},{2,0},{3,1},{4,6},{5,7},{6,4},{7,5},{8,10},{9,11},{10,... | collective-permute-start | bytes 294920 | tf_op jit(solution)/shard_map/ppermute | solution.py:31
  57.0 5.5 %collective-permute-start.20 = (bf16[2,192,384]{2,1,0:T(8,128)(2,1)S(1)}, bf16[2,192,384]{2,1,0:T(8,128)(2,1)S(1)}, u32[]{:S(2)}, u32[]{:S(2)}) collective-permute-start(bf16[2,192,384]{2,1,0:T(8,128)(2,1)S(1)} %fusion.134), channel_id=1, source_target_pairs={{0,1},{1,0},{2,3},{3,2},{4,5},{5,4},{6,7},{7,6},{8,9},{9,8},{10,11... | collective-permute-start | bytes 884744 | tf_op jit(solution)/shard_map/ppermute | solution.py:31
  61.6 7.6 %collective-permute-start.26 = (bf16[256,384]{1,0:T(8,128)(2,1)S(1)}, bf16[256,384]{1,0:T(8,128)(2,1)S(1)}, u32[]{:S(2)}, u32[]{:S(2)}) collective-permute-start(bf16[256,384]{1,0:T(8,128)(2,1)S(1)} %constant_dynamic-update-slice_fusion.7), channel_id=1, source_target_pairs={{0,16},{16,0},{1,17},{17,1},{2,18},{18,2},{3,19},{19,3},{4,20},{20... | collective-permute-start | bytes 589832 | tf_op jit(solution)/shard_map/ppermute | solution.py:35
  62.6 5.2 %collective-permute-start.27 = (bf16[192,384]{1,0:T(8,128)(2,1)S(1)}, bf16[192,384]{1,0:T(8,128)(2,1)S(1)}, u32[]{:S(2)}, u32[]{:S(2)}) collective-permute-start(bf16[192,384]{1,0:T(8,128)(2,1)S(1)} %fusion.230), channel_id=1, source_target_pairs={{0,2},{1,3},{2,0},{3,1},{4,6},{5,7},{6,4},{7,5},{8,10},{9,11},{10,... | collective-permute-start | bytes 442376 | tf_op jit(solution)/shard_map/ppermute | solution.py:31
  64.5 1.4 %collective-permute-start.22 = (bf16[1,1,4,2,8,768]{5,4,2,3,1,0:T(8,128)(2,1)S(1)}, bf16[1,1,4,2,8,768]{5,4,2,3,1,0:T(8,128)(2,1)S(1)}, u32[]{:S(2)}, u32[]{:S(2)}) collective-permute-start(bf16[1,1,4,2,8,768]{5,4,2,3,1,0:T(8,128)(2,1)S(1)} %dynamic-slice_bitcast_fusion.2), channel_id=1, source_target_pairs={{0,1},{1,0},{2,3},{3,2},{4,5},{5,4},{6,7},{7,6},{8,9},{9,8},{10,11... | collective-permute-start | bytes 294920 | tf_op jit(solution)/shard_map/ppermute | solution.py:31
  66.0 4.9 %collective-permute-start.23 = (bf16[1,2,4,1,8,768]{5,4,1,2,3,0:T(8,128)(2,1)S(1)}, bf16[1,2,4,1,8,768]{5,4,1,2,3,0:T(8,128)(2,1)S(1)}, u32[]{:S(2)}, u32[]{:S(2)}) collective-permute-start(bf16[1,2,4,1,8,768]{5,4,1,2,3,0:T(8,128)(2,1)S(1)} %bitcast.348), channel_id=1, source_target_pairs={{0,2},{1,3},{2,0},{3,1},{4,6},{5,7},{6,4},{7,5},{8,10},{9,11},{10,... | collective-permute-start | bytes 294920 | tf_op jit(solution)/shard_map/ppermute | solution.py:31
  67.9 5.3 %collective-permute-start.29 = (bf16[192,384]{1,0:T(8,128)(2,1)S(1)}, bf16[192,384]{1,0:T(8,128)(2,1)S(1)}, u32[]{:S(2)}, u32[]{:S(2)}) collective-permute-start(bf16[192,384]{1,0:T(8,128)(2,1)S(1)} %fusion.190), channel_id=1, source_target_pairs={{0,16},{16,0},{1,17},{17,1},{2,18},{18,2},{3,19},{19,3},{4,20},{20... | collective-permute-start | bytes 442376 | tf_op jit(solution)/shard_map/ppermute | solution.py:35
  70.2 3.7 %collective-permute-start.28 = (bf16[192,1152]{1,0:T(8,128)(2,1)S(1)}, bf16[192,1152]{1,0:T(8,128)(2,1)S(1)}, u32[]{:S(2)}, u32[]{:S(2)}) collective-permute-start(bf16[192,1152]{1,0:T(8,128)(2,1)S(1)} %select_convert_fusion), channel_id=1, source_target_pairs={{0,1},{1,0},{2,3},{3,2},{4,5},{5,4},{6,7},{7,6},{8,9},{9,8},{10,11... | collective-permute-start | bytes 1327112 | tf_op jit(solution)/shard_map/ppermute | solution.py:31
  (6 other events, 6.6 us)

commit v6 on v5

--- a/solution.py
+++ b/solution.py
@@ -375,14 +375,14 @@
         keep = choose(core == 0, quarters[:, 0], quarters[:, 1])
         send = choose(core == 0, quarters[:, 1], quarters[:, 0]).astype(jnp.bfloat16)
         come_out = seq_swap(send, 1)
-        near_grad[-1] = jnp.concatenate(after(near_grad[-1], send))
-        far_grad[-1] = dp_swap(near_grad[-1])
-        far_grad[-2] = after(far_grad[-2], near_grad[-1])
-        come_out = after(come_out, near_grad[-1]).astype(jnp.float32)
+        come_out = after(come_out, near_grad[1]).astype(jnp.float32)
         columns = [keep[0] + come_out[0], keep[1] + come_out[1]]
         send = choose(side == 0, columns[1], columns[0]).astype(jnp.bfloat16)
         keep = choose(side == 0, columns[0], columns[1])
         come = seq_swap(send, 2)
+        near_grad[-1] = jnp.concatenate(after(near_grad[-1], send))
+        far_grad[-1] = dp_swap(near_grad[-1])
+        far_grad[-2] = after(far_grad[-2], near_grad[-1])
         late = after(of_section(micro - 1, 2)[None], send)
         late, comes_late = from_residues(late, number)
         grads_out = jnp.concatenate([early, late])
@@ -393,7 +393,6 @@
         columns = (keep + come.astype(jnp.float32)).astype(jnp.bfloat16)
         come_out = dp_swap(columns)
         conv_total = add_conv(conv_total, micro - 1, columns)
-        out_sum = (columns.astype(jnp.float32) + come_out.astype(jnp.float32)).T
     else:
         for m in range(micro):
             conv_total = add_conv(conv_total, m)
@@ -406,6 +405,9 @@
         come = after(come, comes_late[-1])
         conv_sum = choose(core == 0, low, high) + come.astype(jnp.float32)
         conv_sum = jnp.stack([conv_sum[:, k * inner : (k + 1) * inner] for k in range(3)])
+        conv_sum = conv_sum * factor
+        come_out = after(come_out, conv_sum)
+        out_sum = (columns.astype(jnp.float32) + come_out.astype(jnp.float32)).T
     else:
         out_part = out_part.T
         conv_part = conv_total.reshape(channels, 3, inner).transpose(1, 0, 2)
@@ -416,9 +418,10 @@
             ).astype(jnp.float32)
             for part in (conv_part, out_part)
         )
+        conv_sum = conv_sum * factor
     return (
         grads_out.reshape(section_inputs.shape),
-        (conv_sum * factor)[None],
+        conv_sum[None],
         (out_sum * factor)[None],
     )
 

time: 75.4 us -> 74.3 us (0.985)
  waiting for transfers between devices: 18.7 us -> 16.8 us
  starting transfers between devices: 30.8 us -> 31.6 us
    ppermute x16, waiting for transfers between devices: 11 us -> 8.99 us  [seq_swap(): return lax.ppermute(value, 'seq', [(i, i ^ bit) for i in range(count)])]
    ppermute x16, starting transfers between devices: 16.7 us -> 18.4 us  [seq_swap(): return lax.ppermute(value, 'seq', [(i, i ^ bit) for i in range(count)])]
    ppermute x5, starting transfers between devices: 5.99 us -> 5.17 us  [dp_swap(): return lax.ppermute(value, 'dp', [(0, 1), (1, 0)])]
  transfers between devices with their start and end apart: 30 -> 30, of which waited for: 13 -> 12; matrix products, arithmetic and copies ran while one was open for 27% -> 27% of each run, Pallas kernels for 0% -> 0%
where the time goes in v6:
time: 74.3 us; the launch traced here: 74 us
  starting transfers between devices  31.6 us (43%)
  waiting for transfers between devices  16.8 us (23%)
  matrix products  13.4 us (18%)
  other arithmetic  6.48 us (9%)
  local copies, waits for them, and re-layouts  3.61 us (5%)
  between operations  1.86 us (3%)
    ppermute x16, starting transfers between devices, seq_swap(): return lax.ppermute(value, 'seq', [(i, i ^ bit) for i in range(count)])  18.4 us
    ppermute x16, waiting for transfers between devices, seq_swap(): return lax.ppermute(value, 'seq', [(i, i ^ bit) for i in range(count)])  8.99 us
    ppermute x9, starting transfers between devices, send_down(): lax.ppermute(value, 'section', [(sections - 1 - hop, sections - 2 - hop)])  8.08 us
    ppermute x9, waiting for transfers between devices, send_down(): lax.ppermute(value, 'section', [(sections - 1 - hop, sections - 2 - hop)])  6.36 us
    ppermute x5, starting transfers between devices, dp_swap(): return lax.ppermute(value, 'dp', [(0, 1), (1, 0)])  5.17 us
    dot_general x9, matrix products, tick(): grad_hidden = jnp.dot(back, back_kernel, preferred_element_type=jnp.float32)  4.09 us
    dot_general x9, matrix products, tick(): lax.dot_general(grad_top, out_w, (((1,), (1,)), ((), ())), preferred_elem...  2.85 us
    unnamed x21, local copies, waits for them, and re-layouts  2.27 us
  transfers between devices with their start and end apart: 30, of which 12 were waited for; matrix products, arithmetic and copies ran while one was open for 27% of the time, Pallas kernels for 0%

profile of v6, /device:TPU:0, one launch (start us, length us, event | category | flops | bytes accessed | tf_op | source)
XLA Modules:
  0.0 74.0 jit_solution(6791586167642919228)
XLA Ops:
  0.7 1.1 %copy-done.1 = bf16[1,3,1,128,768]{4,3,2,1,0:T(8,128)(2,1)S(1)} copy-done((bf16[1,3,1,128,768]{4,3,2,1,0:T(8,128)(2,1)S(1)}, bf16[1,3,1,128,768]{4,3,2,1,0:T(8,128)(2,1)}, u32[]{:S(2)}) %copy-start.1) | copy-done | bytes 589848
  1.8 1.1 %copy-done.2 = bf16[3,1,128,768]{3,2,1,0:T(8,128)(2,1)S(1)} copy-done((bf16[3,1,128,768]{3,2,1,0:T(8,128)(2,1)S(1)}, bf16[3,1,128,768]{3,2,1,0:T(8,128)(2,1)}, u32[]{:S(2)}) %copy-start.2) | copy-done | bytes 589848
  4.6 3.0 %collective-permute-start.2 = (bf16[2,2,32,768]{3,2,0,1:T(8,128)(2,1)S(1)}, bf16[2,2,32,768]{3,2,0,1:T(8,128)(2,1)S(1)}, u32[]{:S(2)}, u32[]{:S(2)}) collective-permute-start(bf16[2,2,32,768]{3,2,0,1:T(8,128)(2,1)S(1)} %pad_maximum_fusion.12), channel_id=1, source_target_pairs={{0,2},{1,3},{2,0},{3,1},{4,6},{5,7},{6,4},{7,5},{8,10},{9,11},{10,... | collective-permute-start | bytes 589832 | tf_op jit(solution)/shard_map/ppermute | solution.py:31
  9.3 1.2 %collective-permute-start.4 = (bf16[2,2,32,768]{3,2,0,1:T(8,128)(2,1)S(1)}, bf16[2,2,32,768]{3,2,0,1:T(8,128)(2,1)S(1)}, u32[]{:S(2)}, u32[]{:S(2)}) collective-permute-start(bf16[2,2,32,768]{3,2,0,1:T(8,128)(2,1)S(1)} %get-tuple-element.93), channel_id=1, source_target_pairs={{0,2},{1,3},{2,0},{3,1},{4,6},{5,7},{6,4},{7,5},{8,10},{9,11},{10,... | collective-permute-start | bytes 589832 | tf_op jit(solution)/shard_map/ppermute | solution.py:31
  10.7 2.6 %collective-permute-done.2 = bf16[2,2,32,768]{3,2,0,1:T(8,128)(2,1)S(1)} collective-permute-done((bf16[2,2,32,768]{3,2,0,1:T(8,128)(2,1)S(1)}, bf16[2,2,32,768]{3,2,0,1:T(8,128)(2,1)S(1)}, u32[]{:S(2)}, u32[]{:S(2)}) %collective-permute-start.2) | collective-permute-done | bytes 196640 | tf_op jit(solution)/shard_map/ppermute | solution.py:31
  15.9 2.1 %collective-permute-start.3 = (bf16[2,2,32,768]{3,2,0,1:T(8,128)(2,1)S(1)}, bf16[2,2,32,768]{3,2,0,1:T(8,128)(2,1)S(1)}, u32[]{:S(2)}, u32[]{:S(2)}) collective-permute-start(bf16[2,2,32,768]{3,2,0,1:T(8,128)(2,1)S(1)} %get-tuple-element.101), channel_id=1, source_target_pairs={{0,2},{1,3},{2,0},{3,1},{4,6},{5,7},{6,4},{7,5},{8,10},{9,11},{10,... | collective-permute-start | bytes 589832 | tf_op jit(solution)/shard_map/ppermute | solution.py:31
  20.8 1.2 %collective-permute-done.3 = bf16[2,2,32,768]{3,2,0,1:T(8,128)(2,1)S(1)} collective-permute-done((bf16[2,2,32,768]{3,2,0,1:T(8,128)(2,1)S(1)}, bf16[2,2,32,768]{3,2,0,1:T(8,128)(2,1)S(1)}, u32[]{:S(2)}, u32[]{:S(2)}) %collective-permute-start.3) | collective-permute-done | bytes 196640 | tf_op jit(solution)/shard_map/ppermute | solution.py:31
  25.5 1.8 %collective-permute-start.12 = (bf16[384,384]{1,0:T(8,128)(2,1)S(1)}, bf16[384,384]{1,0:T(8,128)(2,1)S(1)}, u32[]{:S(2)}, u32[]{:S(2)}) collective-permute-start(bf16[384,384]{1,0:T(8,128)(2,1)S(1)} %get-tuple-element.180), channel_id=1, source_target_pairs={{0,2},{1,3},{2,0},{3,1},{4,6},{5,7},{6,4},{7,5},{8,10},{9,11},{10,... | collective-permute-start | bytes 884744 | tf_op jit(solution)/shard_map/ppermute | solution.py:31
  29.9 1.3 %collective-permute-start.10 = (bf16[128,768]{1,0:T(8,128)(2,1)S(1)}, bf16[128,768]{1,0:T(8,128)(2,1)S(1)}, u32[]{:S(2)}, u32[]{:S(2)}) collective-permute-start(bf16[128,768]{1,0:T(8,128)(2,1)S(1)} %fusion.27), channel_id=1, source_target_pairs={{4,0},{5,1},{6,2},{7,3},{20,16},{21,17},{22,18},{23,19}} | collective-permute-start | bytes 589832 | tf_op jit(solution)/shard_map/ppermute | solution.py:166
  31.9 0.8 %collective-permute-done.12 = bf16[384,384]{1,0:T(8,128)(2,1)S(1)} collective-permute-done((bf16[384,384]{1,0:T(8,128)(2,1)S(1)}, bf16[384,384]{1,0:T(8,128)(2,1)S(1)}, u32[]{:S(2)}, u32[]{:S(2)}) %collective-permute-start.12) | collective-permute-done | bytes 294944 | tf_op jit(solution)/shard_map/ppermute | solution.py:31
  32.7 1.4 %collective-permute-start.17 = (bf16[3,256,384]{2,1,0:T(8,128)(2,1)S(1)}, bf16[3,256,384]{2,1,0:T(8,128)(2,1)S(1)}, u32[]{:S(2)}, u32[]{:S(2)}) collective-permute-start(bf16[3,256,384]{2,1,0:T(8,128)(2,1)S(1)} %pad_maximum_fusion.1), channel_id=1, source_target_pairs={{0,16},{16,0},{1,17},{17,1},{2,18},{18,2},{3,19},{19,3},{4,20},{20... | collective-permute-start | bytes 1769480 | tf_op jit(solution)/shard_map/ppermute | solution.py:35
  35.1 1.3 %collective-permute-start.13 = (bf16[128,768]{1,0:T(8,128)(2,1)S(1)}, bf16[128,768]{1,0:T(8,128)(2,1)S(1)}, u32[]{:S(2)}, u32[]{:S(2)}) collective-permute-start(bf16[128,768]{1,0:T(8,128)(2,1)S(1)} %add_convert_fusion.2), channel_id=1, source_target_pairs={{4,0},{5,1},{6,2},{7,3},{20,16},{21,17},{22,18},{23,19}} | collective-permute-start | bytes 589832 | tf_op jit(solution)/shard_map/ppermute | solution.py:166
  36.4 5.2 %collective-permute-done.10 = bf16[128,768]{1,0:T(8,128)(2,1)S(1)} collective-permute-done((bf16[128,768]{1,0:T(8,128)(2,1)S(1)}, bf16[128,768]{1,0:T(8,128)(2,1)S(1)}, u32[]{:S(2)}, u32[]{:S(2)}) %collective-permute-start.10) | collective-permute-done | bytes 196640 | tf_op jit(solution)/shard_map/ppermute | solution.py:166
  42.5 2.6 %collective-permute-start.18 = (bf16[128,384]{1,0:T(8,128)(2,1)S(1)}, bf16[128,384]{1,0:T(8,128)(2,1)S(1)}, u32[]{:S(2)}, u32[]{:S(2)}) collective-permute-start(bf16[128,384]{1,0:T(8,128)(2,1)S(1)} %select_select_fusion.4), channel_id=1, source_target_pairs={{0,2},{1,3},{2,0},{3,1},{4,6},{5,7},{6,4},{7,5},{8,10},{9,11},{10,... | collective-permute-start | bytes 294920 | tf_op jit(solution)/shard_map/ppermute | solution.py:31
  45.1 1.5 %collective-permute-start.16 = (bf16[128,768]{1,0:T(8,128)(2,1)S(1)}, bf16[128,768]{1,0:T(8,128)(2,1)S(1)}, u32[]{:S(2)}, u32[]{:S(2)}) collective-permute-start(bf16[128,768]{1,0:T(8,128)(2,1)S(1)} %fusion.26), channel_id=1, source_target_pairs={{4,0},{5,1},{6,2},{7,3},{20,16},{21,17},{22,18},{23,19}} | collective-permute-start | bytes 589832 | tf_op jit(solution)/shard_map/ppermute | solution.py:166
  47.0 1.2 %collective-permute-done.13 = bf16[128,768]{1,0:T(8,128)(2,1)S(1)} collective-permute-done((bf16[128,768]{1,0:T(8,128)(2,1)S(1)}, bf16[128,768]{1,0:T(8,128)(2,1)S(1)}, u32[]{:S(2)}, u32[]{:S(2)}) %collective-permute-start.13) | collective-permute-done | bytes 196640 | tf_op jit(solution)/shard_map/ppermute | solution.py:166
  49.1 1.2 %collective-permute-start.19 = (bf16[128,384]{1,0:T(8,128)(2,1)S(1)}, bf16[128,384]{1,0:T(8,128)(2,1)S(1)}, u32[]{:S(2)}, u32[]{:S(2)}) collective-permute-start(bf16[128,384]{1,0:T(8,128)(2,1)S(1)} %select_select_fusion.3), channel_id=1, source_target_pairs={{0,2},{1,3},{2,0},{3,1},{4,6},{5,7},{6,4},{7,5},{8,10},{9,11},{10,... | collective-permute-start | bytes 294920 | tf_op jit(solution)/shard_map/ppermute | solution.py:31
  52.0 1.5 %collective-permute-start.15 = (bf16[2,2,4,1,8,768]{5,4,1,2,0,3:T(8,128)(2,1)S(1)}, bf16[2,2,4,1,8,768]{5,4,1,2,0,3:T(8,128)(2,1)S(1)}, u32[]{:S(2)}, u32[]{:S(2)}) collective-permute-start(bf16[2,2,4,1,8,768]{5,4,1,2,0,3:T(8,128)(2,1)S(1)} %bitcast.347), channel_id=1, source_target_pairs={{0,2},{1,3},{2,0},{3,1},{4,6},{5,7},{6,4},{7,5},{8,10},{9,11},{10,... | collective-permute-start | bytes 589832 | tf_op jit(solution)/shard_map/ppermute | solution.py:31
  55.1 1.0 %collective-permute-start.24 = (bf16[256,384]{1,0:T(8,128)(2,1)S(1)}, bf16[256,384]{1,0:T(8,128)(2,1)S(1)}, u32[]{:S(2)}, u32[]{:S(2)}) collective-permute-start(bf16[256,384]{1,0:T(8,128)(2,1)S(1)} %constant_dynamic-update-slice_fusion.5), channel_id=1, source_target_pairs={{0,16},{16,0},{1,17},{17,1},{2,18},{18,2},{3,19},{19,3},{4,20},{20... | collective-permute-start | bytes 589832 | tf_op jit(solution)/shard_map/ppermute | solution.py:35
  56.1 0.8 %collective-permute-start.25 = (bf16[128,384]{1,0:T(8,128)(2,1)S(1)}, bf16[128,384]{1,0:T(8,128)(2,1)S(1)}, u32[]{:S(2)}, u32[]{:S(2)}) collective-permute-start(bf16[128,384]{1,0:T(8,128)(2,1)S(1)} %select_select_fusion.2), channel_id=1, source_target_pairs={{0,2},{1,3},{2,0},{3,1},{4,6},{5,7},{6,4},{7,5},{8,10},{9,11},{10,... | collective-permute-start | bytes 294920 | tf_op jit(solution)/shard_map/ppermute | solution.py:31
  57.1 1.9 %collective-permute-done.15 = bf16[2,2,4,1,8,768]{5,4,1,2,0,3:T(8,128)(2,1)S(1)} collective-permute-done((bf16[2,2,4,1,8,768]{5,4,1,2,0,3:T(8,128)(2,1)S(1)}, bf16[2,2,4,1,8,768]{5,4,1,2,0,3:T(8,128)(2,1)S(1)}, u32[]{:S(2)}, u32[]{:S(2)}) %collective-permute-start.15) | collective-permute-done | bytes 196640 | tf_op jit(solution)/shard_map/ppermute | solution.py:31
  59.2 2.1 %collective-permute-start.27 = (bf16[192,384]{1,0:T(8,128)(2,1)S(1)}, bf16[192,384]{1,0:T(8,128)(2,1)S(1)}, u32[]{:S(2)}, u32[]{:S(2)}) collective-permute-start(bf16[192,384]{1,0:T(8,128)(2,1)S(1)} %fusion.230), channel_id=1, source_target_pairs={{0,2},{1,3},{2,0},{3,1},{4,6},{5,7},{6,4},{7,5},{8,10},{9,11},{10,... | collective-permute-start | bytes 442376 | tf_op jit(solution)/shard_map/ppermute | solution.py:31
  61.4 1.1 %collective-permute-start.26 = (bf16[256,384]{1,0:T(8,128)(2,1)S(1)}, bf16[256,384]{1,0:T(8,128)(2,1)S(1)}, u32[]{:S(2)}, u32[]{:S(2)}) collective-permute-start(bf16[256,384]{1,0:T(8,128)(2,1)S(1)} %constant_dynamic-update-slice_fusion.7), channel_id=1, source_target_pairs={{0,16},{16,0},{1,17},{17,1},{2,18},{18,2},{3,19},{19,3},{4,20},{20... | collective-permute-start | bytes 589832 | tf_op jit(solution)/shard_map/ppermute | solution.py:35
  63.8 0.7 convolution_add_fusion.1
  65.2 1.2 %collective-permute-start.22 = (bf16[1,2,4,1,8,768]{5,4,1,2,3,0:T(8,128)(2,1)S(1)}, bf16[1,2,4,1,8,768]{5,4,1,2,3,0:T(8,128)(2,1)S(1)}, u32[]{:S(2)}, u32[]{:S(2)}) collective-permute-start(bf16[1,2,4,1,8,768]{5,4,1,2,3,0:T(8,128)(2,1)S(1)} %bitcast.348), channel_id=1, source_target_pairs={{0,2},{1,3},{2,0},{3,1},{4,6},{5,7},{6,4},{7,5},{8,10},{9,11},{10,... | collective-permute-start | bytes 294920 | tf_op jit(solution)/shard_map/ppermute | solution.py:31
  66.4 1.2 %collective-permute-start.29 = (bf16[192,384]{1,0:T(8,128)(2,1)S(1)}, bf16[192,384]{1,0:T(8,128)(2,1)S(1)}, u32[]{:S(2)}, u32[]{:S(2)}) collective-permute-start(bf16[192,384]{1,0:T(8,128)(2,1)S(1)} %fusion.190), channel_id=1, source_target_pairs={{0,16},{16,0},{1,17},{17,1},{2,18},{18,2},{3,19},{19,3},{4,20},{20... | collective-permute-start | bytes 442376 | tf_op jit(solution)/shard_map/ppermute | solution.py:35
  68.2 0.7 convolution_add_fusion
  69.1 1.0 %collective-permute-done.22 = bf16[1,2,4,1,8,768]{5,4,1,2,3,0:T(8,128)(2,1)S(1)} collective-permute-done((bf16[1,2,4,1,8,768]{5,4,1,2,3,0:T(8,128)(2,1)S(1)}, bf16[1,2,4,1,8,768]{5,4,1,2,3,0:T(8,128)(2,1)S(1)}, u32[]{:S(2)}, u32[]{:S(2)}) %collective-permute-start.22) | collective-permute-done | bytes 98336 | tf_op jit(solution)/shard_map/ppermute | solution.py:31
  70.1 0.9 %maximum_bitcast_fusion = bf16[1,3,1,128,768]{4,3,2,1,0:T(8,128)(2,1)} fusion(bf16[1,128,768]{2,1,0:T(8,128)(2,1)S(1)} %bitcast.335, bf16[2,128,768]{2,1,0:T(8,128)(2,1)S(1)} %bitcast.329), kind=kLoop, calls=%fused_computation.98 | loop fusion | flops 294912 | bytes 1179648 | tf_op jit(solution)/shard_map/reshape | solution.py:423
  71.0 1.1 %collective-permute-done.29 = bf16[192,384]{1,0:T(8,128)(2,1)S(1)} collective-permute-done((bf16[192,384]{1,0:T(8,128)(2,1)S(1)}, bf16[192,384]{1,0:T(8,128)(2,1)S(1)}, u32[]{:S(2)}, u32[]{:S(2)}) %collective-permute-start.29) | collective-permute-done | bytes 147488 | tf_op jit(solution)/shard_map/ppermute | solution.py:35
  72.1 0.8 %multiply_bitcast_fusion = f32[1,384,192]{1,2,0:T(8,128)} fusion(bf16[192,384]{1,0:T(8,128)(2,1)S(1)} %collective-permute-done.29, bf16[192,384]{1,0:T(8,128)(2,1)S(1)} %fusion.190), kind=kLoop, calls=%fused_computation.265 | loop fusion | flops 294912 | bytes 589824 | tf_op jit(solution)/shard_map/broadcast_in_dim | solution.py:425
  73.1 1.0 %maximum_multiply_fusion = f32[1,3,192,384]{3,2,1,0:T(8,128)} fusion(f32[1,1,192,384]{3,2,1,0:T(8,128)S(1)} %get-tuple-element.176, f32[1,1,192,384]{3,2,1,0:T(8,128)S(1)} %get-tuple-element.177, f32[1,1,192,384]{3,2,1,0:T(8,128)S(1)} %get-tuple-element.175), kind=kLoop, calls=%fused_computation.71 | loop fusion | flops 663552 | bytes 1769472 | tf_op jit(solution)/shard_map/mul | solution.py:408
  (175 shorter events, 24.8 us)
Async XLA Ops:
  0.6 13.7 %copy-start = (bf16[1,384,768]{2,1,0:T(8,128)(2,1)S(1)}, bf16[1,384,768]{2,1,0:T(8,128)(2,1)}, u32[]{:S(2)}) copy-start(bf16[1,384,768]{2,1,0:T(8,128)(2,1)} %param.11) | copy-start | bytes 1769476
  3.0 1.6 %collective-permute-start = (bf16[2,2,32,768]{3,2,0,1:T(8,128)(2,1)S(1)}, bf16[2,2,32,768]{3,2,0,1:T(8,128)(2,1)S(1)}, u32[]{:S(2)}, u32[]{:S(2)}) collective-permute-start(bf16[2,2,32,768]{3,2,0,1:T(8,128)(2,1)S(1)} %copy.12), channel_id=1, source_target_pairs={{0,1},{1,0},{2,3},{3,2},{4,5},{5,4},{6,7},{7,6},{8,9},{9,8},{10,11... | collective-permute-start | bytes 589832 | tf_op jit(solution)/shard_map/ppermute | solution.py:31
  3.7 3.9 %collective-permute-start.1 = (bf16[4,2,32,768]{3,2,0,1:T(8,128)(2,1)S(1)}, bf16[4,2,32,768]{3,2,0,1:T(8,128)(2,1)S(1)}, u32[]{:S(2)}, u32[]{:S(2)}) collective-permute-start(bf16[4,2,32,768]{3,2,0,1:T(8,128)(2,1)S(1)} %copy.14), channel_id=1, source_target_pairs={{0,1},{1,0},{2,3},{3,2},{4,5},{5,4},{6,7},{7,6},{8,9},{9,8},{10,11... | collective-permute-start | bytes 1179656 | tf_op jit(solution)/shard_map/ppermute | solution.py:31
  4.6 3.2 %copy-start.3 = (bf16[1,3,768,384]{3,2,1,0:T(8,128)(2,1)S(1)}, bf16[1,3,768,384]{3,2,1,0:T(8,128)(2,1)}, u32[]{:S(2)}) copy-start(bf16[1,3,768,384]{3,2,1,0:T(8,128)(2,1)} %param.10) | copy-start | bytes 5308420
  4.6 8.6 %collective-permute-start.2 = (bf16[2,2,32,768]{3,2,0,1:T(8,128)(2,1)S(1)}, bf16[2,2,32,768]{3,2,0,1:T(8,128)(2,1)S(1)}, u32[]{:S(2)}, u32[]{:S(2)}) collective-permute-start(bf16[2,2,32,768]{3,2,0,1:T(8,128)(2,1)S(1)} %pad_maximum_fusion.12), channel_id=1, source_target_pairs={{0,2},{1,3},{2,0},{3,1},{4,6},{5,7},{6,4},{7,5},{8,10},{9,11},{10,... | collective-permute-start | bytes 589832 | tf_op jit(solution)/shard_map/ppermute | solution.py:31
  9.3 8.8 %collective-permute-start.4 = (bf16[2,2,32,768]{3,2,0,1:T(8,128)(2,1)S(1)}, bf16[2,2,32,768]{3,2,0,1:T(8,128)(2,1)S(1)}, u32[]{:S(2)}, u32[]{:S(2)}) collective-permute-start(bf16[2,2,32,768]{3,2,0,1:T(8,128)(2,1)S(1)} %get-tuple-element.93), channel_id=1, source_target_pairs={{0,2},{1,3},{2,0},{3,1},{4,6},{5,7},{6,4},{7,5},{8,10},{9,11},{10,... | collective-permute-start | bytes 589832 | tf_op jit(solution)/shard_map/ppermute | solution.py:31
  15.2 7.8 %collective-permute-start.5 = (bf16[128,768]{1,0:T(8,128)(2,1)S(1)}, bf16[128,768]{1,0:T(8,128)(2,1)S(1)}, u32[]{:S(2)}, u32[]{:S(2)}) collective-permute-start(bf16[128,768]{1,0:T(8,128)(2,1)S(1)} %fusion.29), channel_id=1, source_target_pairs={{12,8},{13,9},{14,10},{15,11},{28,24},{29,25},{30,26},{31,27}} | collective-permute-start | bytes 589832 | tf_op jit(solution)/shard_map/ppermute | solution.py:166
  15.9 6.0 %collective-permute-start.3 = (bf16[2,2,32,768]{3,2,0,1:T(8,128)(2,1)S(1)}, bf16[2,2,32,768]{3,2,0,1:T(8,128)(2,1)S(1)}, u32[]{:S(2)}, u32[]{:S(2)}) collective-permute-start(bf16[2,2,32,768]{3,2,0,1:T(8,128)(2,1)S(1)} %get-tuple-element.101), channel_id=1, source_target_pairs={{0,2},{1,3},{2,0},{3,1},{4,6},{5,7},{6,4},{7,5},{8,10},{9,11},{10,... | collective-permute-start | bytes 589832 | tf_op jit(solution)/shard_map/ppermute | solution.py:31
  20.1 7.2 %collective-permute-start.8 = (bf16[128,768]{1,0:T(8,128)(2,1)S(1)}, bf16[128,768]{1,0:T(8,128)(2,1)S(1)}, u32[]{:S(2)}, u32[]{:S(2)}) collective-permute-start(bf16[128,768]{1,0:T(8,128)(2,1)S(1)} %fusion.28), channel_id=1, source_target_pairs={{12,8},{13,9},{14,10},{15,11},{28,24},{29,25},{30,26},{31,27}} | collective-permute-start | bytes 589832 | tf_op jit(solution)/shard_map/ppermute | solution.py:166
  24.0 5.0 %collective-permute-start.7 = (bf16[128,768]{1,0:T(8,128)(2,1)S(1)}, bf16[128,768]{1,0:T(8,128)(2,1)S(1)}, u32[]{:S(2)}, u32[]{:S(2)}) collective-permute-start(bf16[128,768]{1,0:T(8,128)(2,1)S(1)} %add_convert_fusion.4), channel_id=1, source_target_pairs={{8,4},{9,5},{10,6},{11,7},{24,20},{25,21},{26,22},{27,23}} | collective-permute-start | bytes 589832 | tf_op jit(solution)/shard_map/ppermute | solution.py:166
  24.6 4.3 %collective-permute-start.6 = (bf16[128,768]{1,0:T(8,128)(2,1)S(1)}, bf16[128,768]{1,0:T(8,128)(2,1)S(1)}, u32[]{:S(2)}, u32[]{:S(2)}) collective-permute-start(bf16[128,768]{1,0:T(8,128)(2,1)S(1)} %add_convert_fusion.4), channel_id=1, source_target_pairs={{12,8},{13,9},{14,10},{15,11},{28,24},{29,25},{30,26},{31,27}} | collective-permute-start | bytes 589832 | tf_op jit(solution)/shard_map/ppermute | solution.py:166
  25.5 7.2 %collective-permute-start.12 = (bf16[384,384]{1,0:T(8,128)(2,1)S(1)}, bf16[384,384]{1,0:T(8,128)(2,1)S(1)}, u32[]{:S(2)}, u32[]{:S(2)}) collective-permute-start(bf16[384,384]{1,0:T(8,128)(2,1)S(1)} %get-tuple-element.180), channel_id=1, source_target_pairs={{0,2},{1,3},{2,0},{3,1},{4,6},{5,7},{6,4},{7,5},{8,10},{9,11},{10,... | collective-permute-start | bytes 884744 | tf_op jit(solution)/shard_map/ppermute | solution.py:31
  28.2 5.9 %collective-permute-start.11 = (bf16[128,768]{1,0:T(8,128)(2,1)S(1)}, bf16[128,768]{1,0:T(8,128)(2,1)S(1)}, u32[]{:S(2)}, u32[]{:S(2)}) collective-permute-start(bf16[128,768]{1,0:T(8,128)(2,1)S(1)} %add_convert_fusion.3), channel_id=1, source_target_pairs={{8,4},{9,5},{10,6},{11,7},{24,20},{25,21},{26,22},{27,23}} | collective-permute-start | bytes 589832 | tf_op jit(solution)/shard_map/ppermute | solution.py:166
  29.9 11.7 %collective-permute-start.10 = (bf16[128,768]{1,0:T(8,128)(2,1)S(1)}, bf16[128,768]{1,0:T(8,128)(2,1)S(1)}, u32[]{:S(2)}, u32[]{:S(2)}) collective-permute-start(bf16[128,768]{1,0:T(8,128)(2,1)S(1)} %fusion.27), channel_id=1, source_target_pairs={{4,0},{5,1},{6,2},{7,3},{20,16},{21,17},{22,18},{23,19}} | collective-permute-start | bytes 589832 | tf_op jit(solution)/shard_map/ppermute | solution.py:166
  31.2 10.4 %collective-permute-start.9 = (bf16[128,768]{1,0:T(8,128)(2,1)S(1)}, bf16[128,768]{1,0:T(8,128)(2,1)S(1)}, u32[]{:S(2)}, u32[]{:S(2)}) collective-permute-start(bf16[128,768]{1,0:T(8,128)(2,1)S(1)} %fusion.27), channel_id=1, source_target_pairs={{8,4},{9,5},{10,6},{11,7},{24,20},{25,21},{26,22},{27,23}} | collective-permute-start | bytes 589832 | tf_op jit(solution)/shard_map/ppermute | solution.py:166
  32.7 20.9 %collective-permute-start.17 = (bf16[3,256,384]{2,1,0:T(8,128)(2,1)S(1)}, bf16[3,256,384]{2,1,0:T(8,128)(2,1)S(1)}, u32[]{:S(2)}, u32[]{:S(2)}) collective-permute-start(bf16[3,256,384]{2,1,0:T(8,128)(2,1)S(1)} %pad_maximum_fusion.1), channel_id=1, source_target_pairs={{0,16},{16,0},{1,17},{17,1},{2,18},{18,2},{3,19},{19,3},{4,20},{20... | collective-permute-start | bytes 1769480 | tf_op jit(solution)/shard_map/ppermute | solution.py:35
  35.1 13.1 %collective-permute-start.13 = (bf16[128,768]{1,0:T(8,128)(2,1)S(1)}, bf16[128,768]{1,0:T(8,128)(2,1)S(1)}, u32[]{:S(2)}, u32[]{:S(2)}) collective-permute-start(bf16[128,768]{1,0:T(8,128)(2,1)S(1)} %add_convert_fusion.2), channel_id=1, source_target_pairs={{4,0},{5,1},{6,2},{7,3},{20,16},{21,17},{22,18},{23,19}} | collective-permute-start | bytes 589832 | tf_op jit(solution)/shard_map/ppermute | solution.py:166
  42.5 8.0 %collective-permute-start.18 = (bf16[128,384]{1,0:T(8,128)(2,1)S(1)}, bf16[128,384]{1,0:T(8,128)(2,1)S(1)}, u32[]{:S(2)}, u32[]{:S(2)}) collective-permute-start(bf16[128,384]{1,0:T(8,128)(2,1)S(1)} %select_select_fusion.4), channel_id=1, source_target_pairs={{0,2},{1,3},{2,0},{3,1},{4,6},{5,7},{6,4},{7,5},{8,10},{9,11},{10,... | collective-permute-start | bytes 294920 | tf_op jit(solution)/shard_map/ppermute | solution.py:31
  45.1 8.4 %collective-permute-start.16 = (bf16[128,768]{1,0:T(8,128)(2,1)S(1)}, bf16[128,768]{1,0:T(8,128)(2,1)S(1)}, u32[]{:S(2)}, u32[]{:S(2)}) collective-permute-start(bf16[128,768]{1,0:T(8,128)(2,1)S(1)} %fusion.26), channel_id=1, source_target_pairs={{4,0},{5,1},{6,2},{7,3},{20,16},{21,17},{22,18},{23,19}} | collective-permute-start | bytes 589832 | tf_op jit(solution)/shard_map/ppermute | solution.py:166
  49.1 5.4 %collective-permute-start.19 = (bf16[128,384]{1,0:T(8,128)(2,1)S(1)}, bf16[128,384]{1,0:T(8,128)(2,1)S(1)}, u32[]{:S(2)}, u32[]{:S(2)}) collective-permute-start(bf16[128,384]{1,0:T(8,128)(2,1)S(1)} %select_select_fusion.3), channel_id=1, source_target_pairs={{0,2},{1,3},{2,0},{3,1},{4,6},{5,7},{6,4},{7,5},{8,10},{9,11},{10,... | collective-permute-start | bytes 294920 | tf_op jit(solution)/shard_map/ppermute | solution.py:31
  50.4 1.5 %collective-permute-start.14 = (bf16[2,1,4,2,8,768]{5,4,2,3,0,1:T(8,128)(2,1)S(1)}, bf16[2,1,4,2,8,768]{5,4,2,3,0,1:T(8,128)(2,1)S(1)}, u32[]{:S(2)}, u32[]{:S(2)}) collective-permute-start(bf16[2,1,4,2,8,768]{5,4,2,3,0,1:T(8,128)(2,1)S(1)} %dynamic-slice_bitcast_fusion), channel_id=1, source_target_pairs={{0,1},{1,0},{2,3},{3,2},{4,5},{5,4},{6,7},{7,6},{8,9},{9,8},{10,11... | collective-permute-start | bytes 589832 | tf_op jit(solution)/shard_map/ppermute | solution.py:31
  50.5 10.8 %collective-permute-start.23 = (bf16[256,384]{1,0:T(8,128)(2,1)S(1)}, bf16[256,384]{1,0:T(8,128)(2,1)S(1)}, u32[]{:S(2)}, u32[]{:S(2)}) collective-permute-start(bf16[256,384]{1,0:T(8,128)(2,1)S(1)} %constant_dynamic-update-slice_fusion.3), channel_id=1, source_target_pairs={{0,16},{16,0},{1,17},{17,1},{2,18},{18,2},{3,19},{19,3},{4,20},{20... | collective-permute-start | bytes 589832 | tf_op jit(solution)/shard_map/ppermute | solution.py:35
  52.0 7.0 %collective-permute-start.15 = (bf16[2,2,4,1,8,768]{5,4,1,2,0,3:T(8,128)(2,1)S(1)}, bf16[2,2,4,1,8,768]{5,4,1,2,0,3:T(8,128)(2,1)S(1)}, u32[]{:S(2)}, u32[]{:S(2)}) collective-permute-start(bf16[2,2,4,1,8,768]{5,4,1,2,0,3:T(8,128)(2,1)S(1)} %bitcast.347), channel_id=1, source_target_pairs={{0,2},{1,3},{2,0},{3,1},{4,6},{5,7},{6,4},{7,5},{8,10},{9,11},{10,... | collective-permute-start | bytes 589832 | tf_op jit(solution)/shard_map/ppermute | solution.py:31
  55.1 7.5 %collective-permute-start.24 = (bf16[256,384]{1,0:T(8,128)(2,1)S(1)}, bf16[256,384]{1,0:T(8,128)(2,1)S(1)}, u32[]{:S(2)}, u32[]{:S(2)}) collective-permute-start(bf16[256,384]{1,0:T(8,128)(2,1)S(1)} %constant_dynamic-update-slice_fusion.5), channel_id=1, source_target_pairs={{0,16},{16,0},{1,17},{17,1},{2,18},{18,2},{3,19},{19,3},{4,20},{20... | collective-permute-start | bytes 589832 | tf_op jit(solution)/shard_map/ppermute | solution.py:35
  56.1 3.0 %collective-permute-start.20 = (bf16[2,192,384]{2,1,0:T(8,128)(2,1)S(1)}, bf16[2,192,384]{2,1,0:T(8,128)(2,1)S(1)}, u32[]{:S(2)}, u32[]{:S(2)}) collective-permute-start(bf16[2,192,384]{2,1,0:T(8,128)(2,1)S(1)} %fusion.134), channel_id=1, source_target_pairs={{0,1},{1,0},{2,3},{3,2},{4,5},{5,4},{6,7},{7,6},{8,9},{9,8},{10,11... | collective-permute-start | bytes 884744 | tf_op jit(solution)/shard_map/ppermute | solution.py:31
  56.1 5.3 %collective-permute-start.25 = (bf16[128,384]{1,0:T(8,128)(2,1)S(1)}, bf16[128,384]{1,0:T(8,128)(2,1)S(1)}, u32[]{:S(2)}, u32[]{:S(2)}) collective-permute-start(bf16[128,384]{1,0:T(8,128)(2,1)S(1)} %select_select_fusion.2), channel_id=1, source_target_pairs={{0,2},{1,3},{2,0},{3,1},{4,6},{5,7},{6,4},{7,5},{8,10},{9,11},{10,... | collective-permute-start | bytes 294920 | tf_op jit(solution)/shard_map/ppermute | solution.py:31
  59.2 7.1 %collective-permute-start.27 = (bf16[192,384]{1,0:T(8,128)(2,1)S(1)}, bf16[192,384]{1,0:T(8,128)(2,1)S(1)}, u32[]{:S(2)}, u32[]{:S(2)}) collective-permute-start(bf16[192,384]{1,0:T(8,128)(2,1)S(1)} %fusion.230), channel_id=1, source_target_pairs={{0,2},{1,3},{2,0},{3,1},{4,6},{5,7},{6,4},{7,5},{8,10},{9,11},{10,... | collective-permute-start | bytes 442376 | tf_op jit(solution)/shard_map/ppermute | solution.py:31
  61.4 6.5 %collective-permute-start.26 = (bf16[256,384]{1,0:T(8,128)(2,1)S(1)}, bf16[256,384]{1,0:T(8,128)(2,1)S(1)}, u32[]{:S(2)}, u32[]{:S(2)}) collective-permute-start(bf16[256,384]{1,0:T(8,128)(2,1)S(1)} %constant_dynamic-update-slice_fusion.7), channel_id=1, source_target_pairs={{0,16},{16,0},{1,17},{17,1},{2,18},{18,2},{3,19},{19,3},{4,20},{20... | collective-permute-start | bytes 589832 | tf_op jit(solution)/shard_map/ppermute | solution.py:35
  63.7 1.4 %collective-permute-start.21 = (bf16[1,1,4,2,8,768]{5,4,2,3,1,0:T(8,128)(2,1)S(1)}, bf16[1,1,4,2,8,768]{5,4,2,3,1,0:T(8,128)(2,1)S(1)}, u32[]{:S(2)}, u32[]{:S(2)}) collective-permute-start(bf16[1,1,4,2,8,768]{5,4,2,3,1,0:T(8,128)(2,1)S(1)} %dynamic-slice_bitcast_fusion.2), channel_id=1, source_target_pairs={{0,1},{1,0},{2,3},{3,2},{4,5},{5,4},{6,7},{7,6},{8,9},{9,8},{10,11... | collective-permute-start | bytes 294920 | tf_op jit(solution)/shard_map/ppermute | solution.py:31
  65.2 4.9 %collective-permute-start.22 = (bf16[1,2,4,1,8,768]{5,4,1,2,3,0:T(8,128)(2,1)S(1)}, bf16[1,2,4,1,8,768]{5,4,1,2,3,0:T(8,128)(2,1)S(1)}, u32[]{:S(2)}, u32[]{:S(2)}) collective-permute-start(bf16[1,2,4,1,8,768]{5,4,1,2,3,0:T(8,128)(2,1)S(1)} %bitcast.348), channel_id=1, source_target_pairs={{0,2},{1,3},{2,0},{3,1},{4,6},{5,7},{6,4},{7,5},{8,10},{9,11},{10,... | collective-permute-start | bytes 294920 | tf_op jit(solution)/shard_map/ppermute | solution.py:31
  66.4 5.7 %collective-permute-start.29 = (bf16[192,384]{1,0:T(8,128)(2,1)S(1)}, bf16[192,384]{1,0:T(8,128)(2,1)S(1)}, u32[]{:S(2)}, u32[]{:S(2)}) collective-permute-start(bf16[192,384]{1,0:T(8,128)(2,1)S(1)} %fusion.190), channel_id=1, source_target_pairs={{0,16},{16,0},{1,17},{17,1},{2,18},{18,2},{3,19},{19,3},{4,20},{20... | collective-permute-start | bytes 442376 | tf_op jit(solution)/shard_map/ppermute | solution.py:35
  69.0 3.9 %collective-permute-start.28 = (bf16[192,1152]{1,0:T(8,128)(2,1)S(1)}, bf16[192,1152]{1,0:T(8,128)(2,1)S(1)}, u32[]{:S(2)}, u32[]{:S(2)}) collective-permute-start(bf16[192,1152]{1,0:T(8,128)(2,1)S(1)} %select_convert_fusion), channel_id=1, source_target_pairs={{0,1},{1,0},{2,3},{3,2},{4,5},{5,4},{6,7},{7,6},{8,9},{9,8},{10,11... | collective-permute-start | bytes 1327112 | tf_op jit(solution)/shard_map/ppermute | solution.py:31
  (6 other events, 6.6 us)

commit v7 on v6

--- a/solution.py
+++ b/solution.py
@@ -232,7 +232,7 @@
             both = both.reshape(-1, rows, channels)
             return both[0], both[1]
 
-        send, keep = split_cores(section_inputs, cotangent, core, 0, 1)
+        send, keep = split_cores(section_inputs[:, :1], cotangent[:1], core, 0, 1)
         come = seq_swap(send, 1)
         later_core = after(core, send)
         later_send, later_keep = split_cores(section_inputs, cotangent, later_core, 1, micro - 1)

time: 74.3 us -> 74.2 us (level)
    unnamed x21, local copies, waits for them, and re-layouts: 2.27 us -> 0.11 us
    slice x0 -> x2, local copies, waits for them, and re-layouts: none -> 2 us  [on_device(): send, keep = split_cores(section_inputs[:, :1], cotangent[:1], core, 0, 1)]
where the time goes in v7:
time: 74.2 us; the launch traced here: 73.9 us
  starting transfers between devices  31.6 us (43%)
  waiting for transfers between devices  16.8 us (23%)
  matrix products  13.4 us (18%)
  other arithmetic  6.48 us (9%)
  local copies, waits for them, and re-layouts  3.45 us (5%)
  between operations  1.9 us (3%)
    ppermute x16, starting transfers between devices, seq_swap(): return lax.ppermute(value, 'seq', [(i, i ^ bit) for i in range(count)])  18.3 us
    ppermute x16, waiting for transfers between devices, seq_swap(): return lax.ppermute(value, 'seq', [(i, i ^ bit) for i in range(count)])  9.05 us
    ppermute x9, starting transfers between devices, send_down(): lax.ppermute(value, 'section', [(sections - 1 - hop, sections - 2 - hop)])  8.08 us
    ppermute x9, waiting for transfers between devices, send_down(): lax.ppermute(value, 'section', [(sections - 1 - hop, sections - 2 - hop)])  6.34 us
    ppermute x5, starting transfers between devices, dp_swap(): return lax.ppermute(value, 'dp', [(0, 1), (1, 0)])  5.18 us
    dot_general x9, matrix products, tick(): grad_hidden = jnp.dot(back, back_kernel, preferred_element_type=jnp.float32)  4.09 us
    dot_general x9, matrix products, tick(): lax.dot_general(grad_top, out_w, (((1,), (1,)), ((), ())), preferred_elem...  2.85 us
    dot_general x3, matrix products, add_conv(): lax.dot_general(all_hidden, back, (((0,), (0,)), ((), ())), preferred_ele...  2.14 us
  transfers between devices with their start and end apart: 30, of which 12 were waited for; matrix products, arithmetic and copies ran while one was open for 27% of the time, Pallas kernels for 0%

profile of v7, /device:TPU:0, one launch (start us, length us, event | category | flops | bytes accessed | tf_op | source)
XLA Modules:
  0.0 73.9 jit_solution(3855728824336935346)
XLA Ops:
  0.7 1.1 %slice.161.inputs_ref = bf16[1,1,1,128,768]{4,3,2,1,0:T(8,128)(2,1)S(1)} slice(bf16[1,3,1,128,768]{4,3,2,1,0:T(8,128)(2,1)} %inputs_ref.1), slice={[0:1], [0:1], [0:1], [0:128], [0:768]} | slice | bytes 393216 | tf_op jit(solution)/shard_map/slice | solution.py:235
  1.8 0.9 %slice.162.top_ref = bf16[1,1,128,768]{3,2,1,0:T(8,128)(2,1)S(1)} slice(bf16[3,1,128,768]{3,2,1,0:T(8,128)(2,1)} %top_ref.1), slice={[0:1], [0:1], [0:128], [0:768]} | slice | bytes 393216 | tf_op jit(solution)/shard_map/slice | solution.py:235
  4.5 3.0 %collective-permute-start.2 = (bf16[2,2,32,768]{3,2,0,1:T(8,128)(2,1)S(1)}, bf16[2,2,32,768]{3,2,0,1:T(8,128)(2,1)S(1)}, u32[]{:S(2)}, u32[]{:S(2)}) collective-permute-start(bf16[2,2,32,768]{3,2,0,1:T(8,128)(2,1)S(1)} %pad_maximum_fusion.12), channel_id=1, source_target_pairs={{0,2},{1,3},{2,0},{3,1},{4,6},{5,7},{6,4},{7,5},{8,10},{9,11},{10,... | collective-permute-start | bytes 589832 | tf_op jit(solution)/shard_map/ppermute | solution.py:31
  9.2 1.2 %collective-permute-start.4 = (bf16[2,2,32,768]{3,2,0,1:T(8,128)(2,1)S(1)}, bf16[2,2,32,768]{3,2,0,1:T(8,128)(2,1)S(1)}, u32[]{:S(2)}, u32[]{:S(2)}) collective-permute-start(bf16[2,2,32,768]{3,2,0,1:T(8,128)(2,1)S(1)} %get-tuple-element.93), channel_id=1, source_target_pairs={{0,2},{1,3},{2,0},{3,1},{4,6},{5,7},{6,4},{7,5},{8,10},{9,11},{10,... | collective-permute-start | bytes 589832 | tf_op jit(solution)/shard_map/ppermute | solution.py:31
  10.6 2.6 %collective-permute-done.2 = bf16[2,2,32,768]{3,2,0,1:T(8,128)(2,1)S(1)} collective-permute-done((bf16[2,2,32,768]{3,2,0,1:T(8,128)(2,1)S(1)}, bf16[2,2,32,768]{3,2,0,1:T(8,128)(2,1)S(1)}, u32[]{:S(2)}, u32[]{:S(2)}) %collective-permute-start.2) | collective-permute-done | bytes 196640 | tf_op jit(solution)/shard_map/ppermute | solution.py:31
  15.8 2.1 %collective-permute-start.3 = (bf16[2,2,32,768]{3,2,0,1:T(8,128)(2,1)S(1)}, bf16[2,2,32,768]{3,2,0,1:T(8,128)(2,1)S(1)}, u32[]{:S(2)}, u32[]{:S(2)}) collective-permute-start(bf16[2,2,32,768]{3,2,0,1:T(8,128)(2,1)S(1)} %get-tuple-element.101), channel_id=1, source_target_pairs={{0,2},{1,3},{2,0},{3,1},{4,6},{5,7},{6,4},{7,5},{8,10},{9,11},{10,... | collective-permute-start | bytes 589832 | tf_op jit(solution)/shard_map/ppermute | solution.py:31
  20.6 1.2 %collective-permute-done.3 = bf16[2,2,32,768]{3,2,0,1:T(8,128)(2,1)S(1)} collective-permute-done((bf16[2,2,32,768]{3,2,0,1:T(8,128)(2,1)S(1)}, bf16[2,2,32,768]{3,2,0,1:T(8,128)(2,1)S(1)}, u32[]{:S(2)}, u32[]{:S(2)}) %collective-permute-start.3) | collective-permute-done | bytes 196640 | tf_op jit(solution)/shard_map/ppermute | solution.py:31
  25.3 1.8 %collective-permute-start.12 = (bf16[384,384]{1,0:T(8,128)(2,1)S(1)}, bf16[384,384]{1,0:T(8,128)(2,1)S(1)}, u32[]{:S(2)}, u32[]{:S(2)}) collective-permute-start(bf16[384,384]{1,0:T(8,128)(2,1)S(1)} %get-tuple-element.180), channel_id=1, source_target_pairs={{0,2},{1,3},{2,0},{3,1},{4,6},{5,7},{6,4},{7,5},{8,10},{9,11},{10,... | collective-permute-start | bytes 884744 | tf_op jit(solution)/shard_map/ppermute | solution.py:31
  29.8 1.3 %collective-permute-start.10 = (bf16[128,768]{1,0:T(8,128)(2,1)S(1)}, bf16[128,768]{1,0:T(8,128)(2,1)S(1)}, u32[]{:S(2)}, u32[]{:S(2)}) collective-permute-start(bf16[128,768]{1,0:T(8,128)(2,1)S(1)} %fusion.27), channel_id=1, source_target_pairs={{4,0},{5,1},{6,2},{7,3},{20,16},{21,17},{22,18},{23,19}} | collective-permute-start | bytes 589832 | tf_op jit(solution)/shard_map/ppermute | solution.py:166
  31.7 0.8 %collective-permute-done.12 = bf16[384,384]{1,0:T(8,128)(2,1)S(1)} collective-permute-done((bf16[384,384]{1,0:T(8,128)(2,1)S(1)}, bf16[384,384]{1,0:T(8,128)(2,1)S(1)}, u32[]{:S(2)}, u32[]{:S(2)}) %collective-permute-start.12) | collective-permute-done | bytes 294944 | tf_op jit(solution)/shard_map/ppermute | solution.py:31
  32.6 1.4 %collective-permute-start.17 = (bf16[3,256,384]{2,1,0:T(8,128)(2,1)S(1)}, bf16[3,256,384]{2,1,0:T(8,128)(2,1)S(1)}, u32[]{:S(2)}, u32[]{:S(2)}) collective-permute-start(bf16[3,256,384]{2,1,0:T(8,128)(2,1)S(1)} %pad_maximum_fusion.1), channel_id=1, source_target_pairs={{0,16},{16,0},{1,17},{17,1},{2,18},{18,2},{3,19},{19,3},{4,20},{20... | collective-permute-start | bytes 1769480 | tf_op jit(solution)/shard_map/ppermute | solution.py:35
  34.9 1.3 %collective-permute-start.13 = (bf16[128,768]{1,0:T(8,128)(2,1)S(1)}, bf16[128,768]{1,0:T(8,128)(2,1)S(1)}, u32[]{:S(2)}, u32[]{:S(2)}) collective-permute-start(bf16[128,768]{1,0:T(8,128)(2,1)S(1)} %add_convert_fusion.2), channel_id=1, source_target_pairs={{4,0},{5,1},{6,2},{7,3},{20,16},{21,17},{22,18},{23,19}} | collective-permute-start | bytes 589832 | tf_op jit(solution)/shard_map/ppermute | solution.py:166
  36.2 5.2 %collective-permute-done.10 = bf16[128,768]{1,0:T(8,128)(2,1)S(1)} collective-permute-done((bf16[128,768]{1,0:T(8,128)(2,1)S(1)}, bf16[128,768]{1,0:T(8,128)(2,1)S(1)}, u32[]{:S(2)}, u32[]{:S(2)}) %collective-permute-start.10) | collective-permute-done | bytes 196640 | tf_op jit(solution)/shard_map/ppermute | solution.py:166
  42.4 2.6 %collective-permute-start.18 = (bf16[128,384]{1,0:T(8,128)(2,1)S(1)}, bf16[128,384]{1,0:T(8,128)(2,1)S(1)}, u32[]{:S(2)}, u32[]{:S(2)}) collective-permute-start(bf16[128,384]{1,0:T(8,128)(2,1)S(1)} %select_select_fusion.4), channel_id=1, source_target_pairs={{0,2},{1,3},{2,0},{3,1},{4,6},{5,7},{6,4},{7,5},{8,10},{9,11},{10,... | collective-permute-start | bytes 294920 | tf_op jit(solution)/shard_map/ppermute | solution.py:31
  45.0 1.5 %collective-permute-start.16 = (bf16[128,768]{1,0:T(8,128)(2,1)S(1)}, bf16[128,768]{1,0:T(8,128)(2,1)S(1)}, u32[]{:S(2)}, u32[]{:S(2)}) collective-permute-start(bf16[128,768]{1,0:T(8,128)(2,1)S(1)} %fusion.26), channel_id=1, source_target_pairs={{4,0},{5,1},{6,2},{7,3},{20,16},{21,17},{22,18},{23,19}} | collective-permute-start | bytes 589832 | tf_op jit(solution)/shard_map/ppermute | solution.py:166
  46.9 1.2 %collective-permute-done.13 = bf16[128,768]{1,0:T(8,128)(2,1)S(1)} collective-permute-done((bf16[128,768]{1,0:T(8,128)(2,1)S(1)}, bf16[128,768]{1,0:T(8,128)(2,1)S(1)}, u32[]{:S(2)}, u32[]{:S(2)}) %collective-permute-start.13) | collective-permute-done | bytes 196640 | tf_op jit(solution)/shard_map/ppermute | solution.py:166
  49.0 1.3 %collective-permute-start.19 = (bf16[128,384]{1,0:T(8,128)(2,1)S(1)}, bf16[128,384]{1,0:T(8,128)(2,1)S(1)}, u32[]{:S(2)}, u32[]{:S(2)}) collective-permute-start(bf16[128,384]{1,0:T(8,128)(2,1)S(1)} %select_select_fusion.3), channel_id=1, source_target_pairs={{0,2},{1,3},{2,0},{3,1},{4,6},{5,7},{6,4},{7,5},{8,10},{9,11},{10,... | collective-permute-start | bytes 294920 | tf_op jit(solution)/shard_map/ppermute | solution.py:31
  52.0 1.5 %collective-permute-start.15 = (bf16[2,2,4,1,8,768]{5,4,1,2,0,3:T(8,128)(2,1)S(1)}, bf16[2,2,4,1,8,768]{5,4,1,2,0,3:T(8,128)(2,1)S(1)}, u32[]{:S(2)}, u32[]{:S(2)}) collective-permute-start(bf16[2,2,4,1,8,768]{5,4,1,2,0,3:T(8,128)(2,1)S(1)} %bitcast.347), channel_id=1, source_target_pairs={{0,2},{1,3},{2,0},{3,1},{4,6},{5,7},{6,4},{7,5},{8,10},{9,11},{10,... | collective-permute-start | bytes 589832 | tf_op jit(solution)/shard_map/ppermute | solution.py:31
  55.0 1.0 %collective-permute-start.24 = (bf16[256,384]{1,0:T(8,128)(2,1)S(1)}, bf16[256,384]{1,0:T(8,128)(2,1)S(1)}, u32[]{:S(2)}, u32[]{:S(2)}) collective-permute-start(bf16[256,384]{1,0:T(8,128)(2,1)S(1)} %constant_dynamic-update-slice_fusion.5), channel_id=1, source_target_pairs={{0,16},{16,0},{1,17},{17,1},{2,18},{18,2},{3,19},{19,3},{4,20},{20... | collective-permute-start | bytes 589832 | tf_op jit(solution)/shard_map/ppermute | solution.py:35
  56.0 0.8 %collective-permute-start.25 = (bf16[128,384]{1,0:T(8,128)(2,1)S(1)}, bf16[128,384]{1,0:T(8,128)(2,1)S(1)}, u32[]{:S(2)}, u32[]{:S(2)}) collective-permute-start(bf16[128,384]{1,0:T(8,128)(2,1)S(1)} %select_select_fusion.2), channel_id=1, source_target_pairs={{0,2},{1,3},{2,0},{3,1},{4,6},{5,7},{6,4},{7,5},{8,10},{9,11},{10,... | collective-permute-start | bytes 294920 | tf_op jit(solution)/shard_map/ppermute | solution.py:31
  57.1 1.9 %collective-permute-done.15 = bf16[2,2,4,1,8,768]{5,4,1,2,0,3:T(8,128)(2,1)S(1)} collective-permute-done((bf16[2,2,4,1,8,768]{5,4,1,2,0,3:T(8,128)(2,1)S(1)}, bf16[2,2,4,1,8,768]{5,4,1,2,0,3:T(8,128)(2,1)S(1)}, u32[]{:S(2)}, u32[]{:S(2)}) %collective-permute-start.15) | collective-permute-done | bytes 196640 | tf_op jit(solution)/shard_map/ppermute | solution.py:31
  59.2 2.0 %collective-permute-start.27 = (bf16[192,384]{1,0:T(8,128)(2,1)S(1)}, bf16[192,384]{1,0:T(8,128)(2,1)S(1)}, u32[]{:S(2)}, u32[]{:S(2)}) collective-permute-start(bf16[192,384]{1,0:T(8,128)(2,1)S(1)} %fusion.230), channel_id=1, source_target_pairs={{0,2},{1,3},{2,0},{3,1},{4,6},{5,7},{6,4},{7,5},{8,10},{9,11},{10,... | collective-permute-start | bytes 442376 | tf_op jit(solution)/shard_map/ppermute | solution.py:31
  61.2 1.1 %collective-permute-start.26 = (bf16[256,384]{1,0:T(8,128)(2,1)S(1)}, bf16[256,384]{1,0:T(8,128)(2,1)S(1)}, u32[]{:S(2)}, u32[]{:S(2)}) collective-permute-start(bf16[256,384]{1,0:T(8,128)(2,1)S(1)} %constant_dynamic-update-slice_fusion.7), channel_id=1, source_target_pairs={{0,16},{16,0},{1,17},{17,1},{2,18},{18,2},{3,19},{19,3},{4,20},{20... | collective-permute-start | bytes 589832 | tf_op jit(solution)/shard_map/ppermute | solution.py:35
  63.7 0.7 convolution_add_fusion.1
  65.0 1.2 %collective-permute-start.22 = (bf16[1,2,4,1,8,768]{5,4,1,2,3,0:T(8,128)(2,1)S(1)}, bf16[1,2,4,1,8,768]{5,4,1,2,3,0:T(8,128)(2,1)S(1)}, u32[]{:S(2)}, u32[]{:S(2)}) collective-permute-start(bf16[1,2,4,1,8,768]{5,4,1,2,3,0:T(8,128)(2,1)S(1)} %bitcast.348), channel_id=1, source_target_pairs={{0,2},{1,3},{2,0},{3,1},{4,6},{5,7},{6,4},{7,5},{8,10},{9,11},{10,... | collective-permute-start | bytes 294920 | tf_op jit(solution)/shard_map/ppermute | solution.py:31
  66.3 1.2 %collective-permute-start.29 = (bf16[192,384]{1,0:T(8,128)(2,1)S(1)}, bf16[192,384]{1,0:T(8,128)(2,1)S(1)}, u32[]{:S(2)}, u32[]{:S(2)}) collective-permute-start(bf16[192,384]{1,0:T(8,128)(2,1)S(1)} %fusion.190), channel_id=1, source_target_pairs={{0,16},{16,0},{1,17},{17,1},{2,18},{18,2},{3,19},{19,3},{4,20},{20... | collective-permute-start | bytes 442376 | tf_op jit(solution)/shard_map/ppermute | solution.py:35
  68.0 0.7 convolution_add_fusion
  68.9 1.0 %collective-permute-done.22 = bf16[1,2,4,1,8,768]{5,4,1,2,3,0:T(8,128)(2,1)S(1)} collective-permute-done((bf16[1,2,4,1,8,768]{5,4,1,2,3,0:T(8,128)(2,1)S(1)}, bf16[1,2,4,1,8,768]{5,4,1,2,3,0:T(8,128)(2,1)S(1)}, u32[]{:S(2)}, u32[]{:S(2)}) %collective-permute-start.22) | collective-permute-done | bytes 98336 | tf_op jit(solution)/shard_map/ppermute | solution.py:31
  70.0 0.9 %maximum_bitcast_fusion = bf16[1,3,1,128,768]{4,3,2,1,0:T(8,128)(2,1)} fusion(bf16[1,128,768]{2,1,0:T(8,128)(2,1)S(1)} %bitcast.335, bf16[2,128,768]{2,1,0:T(8,128)(2,1)S(1)} %bitcast.329), kind=kLoop, calls=%fused_computation.98 | loop fusion | flops 294912 | bytes 1179648 | tf_op jit(solution)/shard_map/reshape | solution.py:423
  70.9 1.1 %collective-permute-done.29 = bf16[192,384]{1,0:T(8,128)(2,1)S(1)} collective-permute-done((bf16[192,384]{1,0:T(8,128)(2,1)S(1)}, bf16[192,384]{1,0:T(8,128)(2,1)S(1)}, u32[]{:S(2)}, u32[]{:S(2)}) %collective-permute-start.29) | collective-permute-done | bytes 147488 | tf_op jit(solution)/shard_map/ppermute | solution.py:35
  72.0 0.8 %multiply_bitcast_fusion = f32[1,384,192]{1,2,0:T(8,128)} fusion(bf16[192,384]{1,0:T(8,128)(2,1)S(1)} %collective-permute-done.29, bf16[192,384]{1,0:T(8,128)(2,1)S(1)} %fusion.190), kind=kLoop, calls=%fused_computation.265 | loop fusion | flops 294912 | bytes 589824 | tf_op jit(solution)/shard_map/broadcast_in_dim | solution.py:425
  72.9 1.0 %maximum_multiply_fusion = f32[1,3,192,384]{3,2,1,0:T(8,128)} fusion(f32[1,1,192,384]{3,2,1,0:T(8,128)S(1)} %get-tuple-element.176, f32[1,1,192,384]{3,2,1,0:T(8,128)S(1)} %get-tuple-element.177, f32[1,1,192,384]{3,2,1,0:T(8,128)S(1)} %get-tuple-element.175), kind=kLoop, calls=%fused_computation.71 | loop fusion | flops 663552 | bytes 1769472 | tf_op jit(solution)/shard_map/mul | solution.py:408
  (177 shorter events, 24.8 us)
Async XLA Ops:
  0.6 13.6 %copy-start = (bf16[1,384,768]{2,1,0:T(8,128)(2,1)S(1)}, bf16[1,384,768]{2,1,0:T(8,128)(2,1)}, u32[]{:S(2)}) copy-start(bf16[1,384,768]{2,1,0:T(8,128)(2,1)} %param.11) | copy-start | bytes 1769476
  2.8 1.6 %collective-permute-start = (bf16[2,2,32,768]{3,2,0,1:T(8,128)(2,1)S(1)}, bf16[2,2,32,768]{3,2,0,1:T(8,128)(2,1)S(1)}, u32[]{:S(2)}, u32[]{:S(2)}) collective-permute-start(bf16[2,2,32,768]{3,2,0,1:T(8,128)(2,1)S(1)} %copy.12), channel_id=1, source_target_pairs={{0,1},{1,0},{2,3},{3,2},{4,5},{5,4},{6,7},{7,6},{8,9},{9,8},{10,11... | collective-permute-start | bytes 589832 | tf_op jit(solution)/shard_map/ppermute | solution.py:31
  3.6 3.9 %collective-permute-start.1 = (bf16[4,2,32,768]{3,2,0,1:T(8,128)(2,1)S(1)}, bf16[4,2,32,768]{3,2,0,1:T(8,128)(2,1)S(1)}, u32[]{:S(2)}, u32[]{:S(2)}) collective-permute-start(bf16[4,2,32,768]{3,2,0,1:T(8,128)(2,1)S(1)} %copy.14), channel_id=1, source_target_pairs={{0,1},{1,0},{2,3},{3,2},{4,5},{5,4},{6,7},{7,6},{8,9},{9,8},{10,11... | collective-permute-start | bytes 1179656 | tf_op jit(solution)/shard_map/ppermute | solution.py:31
  4.5 3.2 %copy-start.3 = (bf16[1,3,768,384]{3,2,1,0:T(8,128)(2,1)S(1)}, bf16[1,3,768,384]{3,2,1,0:T(8,128)(2,1)}, u32[]{:S(2)}) copy-start(bf16[1,3,768,384]{3,2,1,0:T(8,128)(2,1)} %param.10) | copy-start | bytes 5308420
  4.5 8.6 %collective-permute-start.2 = (bf16[2,2,32,768]{3,2,0,1:T(8,128)(2,1)S(1)}, bf16[2,2,32,768]{3,2,0,1:T(8,128)(2,1)S(1)}, u32[]{:S(2)}, u32[]{:S(2)}) collective-permute-start(bf16[2,2,32,768]{3,2,0,1:T(8,128)(2,1)S(1)} %pad_maximum_fusion.12), channel_id=1, source_target_pairs={{0,2},{1,3},{2,0},{3,1},{4,6},{5,7},{6,4},{7,5},{8,10},{9,11},{10,... | collective-permute-start | bytes 589832 | tf_op jit(solution)/shard_map/ppermute | solution.py:31
  9.2 8.8 %collective-permute-start.4 = (bf16[2,2,32,768]{3,2,0,1:T(8,128)(2,1)S(1)}, bf16[2,2,32,768]{3,2,0,1:T(8,128)(2,1)S(1)}, u32[]{:S(2)}, u32[]{:S(2)}) collective-permute-start(bf16[2,2,32,768]{3,2,0,1:T(8,128)(2,1)S(1)} %get-tuple-element.93), channel_id=1, source_target_pairs={{0,2},{1,3},{2,0},{3,1},{4,6},{5,7},{6,4},{7,5},{8,10},{9,11},{10,... | collective-permute-start | bytes 589832 | tf_op jit(solution)/shard_map/ppermute | solution.py:31
  15.1 7.8 %collective-permute-start.5 = (bf16[128,768]{1,0:T(8,128)(2,1)S(1)}, bf16[128,768]{1,0:T(8,128)(2,1)S(1)}, u32[]{:S(2)}, u32[]{:S(2)}) collective-permute-start(bf16[128,768]{1,0:T(8,128)(2,1)S(1)} %fusion.29), channel_id=1, source_target_pairs={{12,8},{13,9},{14,10},{15,11},{28,24},{29,25},{30,26},{31,27}} | collective-permute-start | bytes 589832 | tf_op jit(solution)/shard_map/ppermute | solution.py:166
  15.8 6.0 %collective-permute-start.3 = (bf16[2,2,32,768]{3,2,0,1:T(8,128)(2,1)S(1)}, bf16[2,2,32,768]{3,2,0,1:T(8,128)(2,1)S(1)}, u32[]{:S(2)}, u32[]{:S(2)}) collective-permute-start(bf16[2,2,32,768]{3,2,0,1:T(8,128)(2,1)S(1)} %get-tuple-element.101), channel_id=1, source_target_pairs={{0,2},{1,3},{2,0},{3,1},{4,6},{5,7},{6,4},{7,5},{8,10},{9,11},{10,... | collective-permute-start | bytes 589832 | tf_op jit(solution)/shard_map/ppermute | solution.py:31
  20.0 7.2 %collective-permute-start.8 = (bf16[128,768]{1,0:T(8,128)(2,1)S(1)}, bf16[128,768]{1,0:T(8,128)(2,1)S(1)}, u32[]{:S(2)}, u32[]{:S(2)}) collective-permute-start(bf16[128,768]{1,0:T(8,128)(2,1)S(1)} %fusion.28), channel_id=1, source_target_pairs={{12,8},{13,9},{14,10},{15,11},{28,24},{29,25},{30,26},{31,27}} | collective-permute-start | bytes 589832 | tf_op jit(solution)/shard_map/ppermute | solution.py:166
  23.8 5.0 %collective-permute-start.7 = (bf16[128,768]{1,0:T(8,128)(2,1)S(1)}, bf16[128,768]{1,0:T(8,128)(2,1)S(1)}, u32[]{:S(2)}, u32[]{:S(2)}) collective-permute-start(bf16[128,768]{1,0:T(8,128)(2,1)S(1)} %add_convert_fusion.4), channel_id=1, source_target_pairs={{8,4},{9,5},{10,6},{11,7},{24,20},{25,21},{26,22},{27,23}} | collective-permute-start | bytes 589832 | tf_op jit(solution)/shard_map/ppermute | solution.py:166
  24.5 4.3 %collective-permute-start.6 = (bf16[128,768]{1,0:T(8,128)(2,1)S(1)}, bf16[128,768]{1,0:T(8,128)(2,1)S(1)}, u32[]{:S(2)}, u32[]{:S(2)}) collective-permute-start(bf16[128,768]{1,0:T(8,128)(2,1)S(1)} %add_convert_fusion.4), channel_id=1, source_target_pairs={{12,8},{13,9},{14,10},{15,11},{28,24},{29,25},{30,26},{31,27}} | collective-permute-start | bytes 589832 | tf_op jit(solution)/shard_map/ppermute | solution.py:166
  25.3 7.2 %collective-permute-start.12 = (bf16[384,384]{1,0:T(8,128)(2,1)S(1)}, bf16[384,384]{1,0:T(8,128)(2,1)S(1)}, u32[]{:S(2)}, u32[]{:S(2)}) collective-permute-start(bf16[384,384]{1,0:T(8,128)(2,1)S(1)} %get-tuple-element.180), channel_id=1, source_target_pairs={{0,2},{1,3},{2,0},{3,1},{4,6},{5,7},{6,4},{7,5},{8,10},{9,11},{10,... | collective-permute-start | bytes 884744 | tf_op jit(solution)/shard_map/ppermute | solution.py:31
  28.1 5.9 %collective-permute-start.11 = (bf16[128,768]{1,0:T(8,128)(2,1)S(1)}, bf16[128,768]{1,0:T(8,128)(2,1)S(1)}, u32[]{:S(2)}, u32[]{:S(2)}) collective-permute-start(bf16[128,768]{1,0:T(8,128)(2,1)S(1)} %add_convert_fusion.3), channel_id=1, source_target_pairs={{8,4},{9,5},{10,6},{11,7},{24,20},{25,21},{26,22},{27,23}} | collective-permute-start | bytes 589832 | tf_op jit(solution)/shard_map/ppermute | solution.py:166
  29.8 11.7 %collective-permute-start.10 = (bf16[128,768]{1,0:T(8,128)(2,1)S(1)}, bf16[128,768]{1,0:T(8,128)(2,1)S(1)}, u32[]{:S(2)}, u32[]{:S(2)}) collective-permute-start(bf16[128,768]{1,0:T(8,128)(2,1)S(1)} %fusion.27), channel_id=1, source_target_pairs={{4,0},{5,1},{6,2},{7,3},{20,16},{21,17},{22,18},{23,19}} | collective-permute-start | bytes 589832 | tf_op jit(solution)/shard_map/ppermute | solution.py:166
  31.1 10.4 %collective-permute-start.9 = (bf16[128,768]{1,0:T(8,128)(2,1)S(1)}, bf16[128,768]{1,0:T(8,128)(2,1)S(1)}, u32[]{:S(2)}, u32[]{:S(2)}) collective-permute-start(bf16[128,768]{1,0:T(8,128)(2,1)S(1)} %fusion.27), channel_id=1, source_target_pairs={{8,4},{9,5},{10,6},{11,7},{24,20},{25,21},{26,22},{27,23}} | collective-permute-start | bytes 589832 | tf_op jit(solution)/shard_map/ppermute | solution.py:166
  32.6 20.9 %collective-permute-start.17 = (bf16[3,256,384]{2,1,0:T(8,128)(2,1)S(1)}, bf16[3,256,384]{2,1,0:T(8,128)(2,1)S(1)}, u32[]{:S(2)}, u32[]{:S(2)}) collective-permute-start(bf16[3,256,384]{2,1,0:T(8,128)(2,1)S(1)} %pad_maximum_fusion.1), channel_id=1, source_target_pairs={{0,16},{16,0},{1,17},{17,1},{2,18},{18,2},{3,19},{19,3},{4,20},{20... | collective-permute-start | bytes 1769480 | tf_op jit(solution)/shard_map/ppermute | solution.py:35
  34.9 13.1 %collective-permute-start.13 = (bf16[128,768]{1,0:T(8,128)(2,1)S(1)}, bf16[128,768]{1,0:T(8,128)(2,1)S(1)}, u32[]{:S(2)}, u32[]{:S(2)}) collective-permute-start(bf16[128,768]{1,0:T(8,128)(2,1)S(1)} %add_convert_fusion.2), channel_id=1, source_target_pairs={{4,0},{5,1},{6,2},{7,3},{20,16},{21,17},{22,18},{23,19}} | collective-permute-start | bytes 589832 | tf_op jit(solution)/shard_map/ppermute | solution.py:166
  42.4 8.0 %collective-permute-start.18 = (bf16[128,384]{1,0:T(8,128)(2,1)S(1)}, bf16[128,384]{1,0:T(8,128)(2,1)S(1)}, u32[]{:S(2)}, u32[]{:S(2)}) collective-permute-start(bf16[128,384]{1,0:T(8,128)(2,1)S(1)} %select_select_fusion.4), channel_id=1, source_target_pairs={{0,2},{1,3},{2,0},{3,1},{4,6},{5,7},{6,4},{7,5},{8,10},{9,11},{10,... | collective-permute-start | bytes 294920 | tf_op jit(solution)/shard_map/ppermute | solution.py:31
  45.0 8.4 %collective-permute-start.16 = (bf16[128,768]{1,0:T(8,128)(2,1)S(1)}, bf16[128,768]{1,0:T(8,128)(2,1)S(1)}, u32[]{:S(2)}, u32[]{:S(2)}) collective-permute-start(bf16[128,768]{1,0:T(8,128)(2,1)S(1)} %fusion.26), channel_id=1, source_target_pairs={{4,0},{5,1},{6,2},{7,3},{20,16},{21,17},{22,18},{23,19}} | collective-permute-start | bytes 589832 | tf_op jit(solution)/shard_map/ppermute | solution.py:166
  49.0 5.4 %collective-permute-start.19 = (bf16[128,384]{1,0:T(8,128)(2,1)S(1)}, bf16[128,384]{1,0:T(8,128)(2,1)S(1)}, u32[]{:S(2)}, u32[]{:S(2)}) collective-permute-start(bf16[128,384]{1,0:T(8,128)(2,1)S(1)} %select_select_fusion.3), channel_id=1, source_target_pairs={{0,2},{1,3},{2,0},{3,1},{4,6},{5,7},{6,4},{7,5},{8,10},{9,11},{10,... | collective-permute-start | bytes 294920 | tf_op jit(solution)/shard_map/ppermute | solution.py:31
  50.4 1.5 %collective-permute-start.14 = (bf16[2,1,4,2,8,768]{5,4,2,3,0,1:T(8,128)(2,1)S(1)}, bf16[2,1,4,2,8,768]{5,4,2,3,0,1:T(8,128)(2,1)S(1)}, u32[]{:S(2)}, u32[]{:S(2)}) collective-permute-start(bf16[2,1,4,2,8,768]{5,4,2,3,0,1:T(8,128)(2,1)S(1)} %dynamic-slice_bitcast_fusion), channel_id=1, source_target_pairs={{0,1},{1,0},{2,3},{3,2},{4,5},{5,4},{6,7},{7,6},{8,9},{9,8},{10,11... | collective-permute-start | bytes 589832 | tf_op jit(solution)/shard_map/ppermute | solution.py:31
  50.5 10.7 %collective-permute-start.23 = (bf16[256,384]{1,0:T(8,128)(2,1)S(1)}, bf16[256,384]{1,0:T(8,128)(2,1)S(1)}, u32[]{:S(2)}, u32[]{:S(2)}) collective-permute-start(bf16[256,384]{1,0:T(8,128)(2,1)S(1)} %constant_dynamic-update-slice_fusion.3), channel_id=1, source_target_pairs={{0,16},{16,0},{1,17},{17,1},{2,18},{18,2},{3,19},{19,3},{4,20},{20... | collective-permute-start | bytes 589832 | tf_op jit(solution)/shard_map/ppermute | solution.py:35
  52.0 7.0 %collective-permute-start.15 = (bf16[2,2,4,1,8,768]{5,4,1,2,0,3:T(8,128)(2,1)S(1)}, bf16[2,2,4,1,8,768]{5,4,1,2,0,3:T(8,128)(2,1)S(1)}, u32[]{:S(2)}, u32[]{:S(2)}) collective-permute-start(bf16[2,2,4,1,8,768]{5,4,1,2,0,3:T(8,128)(2,1)S(1)} %bitcast.347), channel_id=1, source_target_pairs={{0,2},{1,3},{2,0},{3,1},{4,6},{5,7},{6,4},{7,5},{8,10},{9,11},{10,... | collective-permute-start | bytes 589832 | tf_op jit(solution)/shard_map/ppermute | solution.py:31
  55.0 7.5 %collective-permute-start.24 = (bf16[256,384]{1,0:T(8,128)(2,1)S(1)}, bf16[256,384]{1,0:T(8,128)(2,1)S(1)}, u32[]{:S(2)}, u32[]{:S(2)}) collective-permute-start(bf16[256,384]{1,0:T(8,128)(2,1)S(1)} %constant_dynamic-update-slice_fusion.5), channel_id=1, source_target_pairs={{0,16},{16,0},{1,17},{17,1},{2,18},{18,2},{3,19},{19,3},{4,20},{20... | collective-permute-start | bytes 589832 | tf_op jit(solution)/shard_map/ppermute | solution.py:35
  56.0 3.1 %collective-permute-start.20 = (bf16[2,192,384]{2,1,0:T(8,128)(2,1)S(1)}, bf16[2,192,384]{2,1,0:T(8,128)(2,1)S(1)}, u32[]{:S(2)}, u32[]{:S(2)}) collective-permute-start(bf16[2,192,384]{2,1,0:T(8,128)(2,1)S(1)} %fusion.134), channel_id=1, source_target_pairs={{0,1},{1,0},{2,3},{3,2},{4,5},{5,4},{6,7},{7,6},{8,9},{9,8},{10,11... | collective-permute-start | bytes 884744 | tf_op jit(solution)/shard_map/ppermute | solution.py:31
  56.0 5.2 %collective-permute-start.25 = (bf16[128,384]{1,0:T(8,128)(2,1)S(1)}, bf16[128,384]{1,0:T(8,128)(2,1)S(1)}, u32[]{:S(2)}, u32[]{:S(2)}) collective-permute-start(bf16[128,384]{1,0:T(8,128)(2,1)S(1)} %select_select_fusion.2), channel_id=1, source_target_pairs={{0,2},{1,3},{2,0},{3,1},{4,6},{5,7},{6,4},{7,5},{8,10},{9,11},{10,... | collective-permute-start | bytes 294920 | tf_op jit(solution)/shard_map/ppermute | solution.py:31
  59.2 7.0 %collective-permute-start.27 = (bf16[192,384]{1,0:T(8,128)(2,1)S(1)}, bf16[192,384]{1,0:T(8,128)(2,1)S(1)}, u32[]{:S(2)}, u32[]{:S(2)}) collective-permute-start(bf16[192,384]{1,0:T(8,128)(2,1)S(1)} %fusion.230), channel_id=1, source_target_pairs={{0,2},{1,3},{2,0},{3,1},{4,6},{5,7},{6,4},{7,5},{8,10},{9,11},{10,... | collective-permute-start | bytes 442376 | tf_op jit(solution)/shard_map/ppermute | solution.py:31
  61.2 6.6 %collective-permute-start.26 = (bf16[256,384]{1,0:T(8,128)(2,1)S(1)}, bf16[256,384]{1,0:T(8,128)(2,1)S(1)}, u32[]{:S(2)}, u32[]{:S(2)}) collective-permute-start(bf16[256,384]{1,0:T(8,128)(2,1)S(1)} %constant_dynamic-update-slice_fusion.7), channel_id=1, source_target_pairs={{0,16},{16,0},{1,17},{17,1},{2,18},{18,2},{3,19},{19,3},{4,20},{20... | collective-permute-start | bytes 589832 | tf_op jit(solution)/shard_map/ppermute | solution.py:35
  63.6 1.4 %collective-permute-start.21 = (bf16[1,1,4,2,8,768]{5,4,2,3,1,0:T(8,128)(2,1)S(1)}, bf16[1,1,4,2,8,768]{5,4,2,3,1,0:T(8,128)(2,1)S(1)}, u32[]{:S(2)}, u32[]{:S(2)}) collective-permute-start(bf16[1,1,4,2,8,768]{5,4,2,3,1,0:T(8,128)(2,1)S(1)} %dynamic-slice_bitcast_fusion.2), channel_id=1, source_target_pairs={{0,1},{1,0},{2,3},{3,2},{4,5},{5,4},{6,7},{7,6},{8,9},{9,8},{10,11... | collective-permute-start | bytes 294920 | tf_op jit(solution)/shard_map/ppermute | solution.py:31
  65.0 4.9 %collective-permute-start.22 = (bf16[1,2,4,1,8,768]{5,4,1,2,3,0:T(8,128)(2,1)S(1)}, bf16[1,2,4,1,8,768]{5,4,1,2,3,0:T(8,128)(2,1)S(1)}, u32[]{:S(2)}, u32[]{:S(2)}) collective-permute-start(bf16[1,2,4,1,8,768]{5,4,1,2,3,0:T(8,128)(2,1)S(1)} %bitcast.348), channel_id=1, source_target_pairs={{0,2},{1,3},{2,0},{3,1},{4,6},{5,7},{6,4},{7,5},{8,10},{9,11},{10,... | collective-permute-start | bytes 294920 | tf_op jit(solution)/shard_map/ppermute | solution.py:31
  66.3 5.7 %collective-permute-start.29 = (bf16[192,384]{1,0:T(8,128)(2,1)S(1)}, bf16[192,384]{1,0:T(8,128)(2,1)S(1)}, u32[]{:S(2)}, u32[]{:S(2)}) collective-permute-start(bf16[192,384]{1,0:T(8,128)(2,1)S(1)} %fusion.190), channel_id=1, source_target_pairs={{0,16},{16,0},{1,17},{17,1},{2,18},{18,2},{3,19},{19,3},{4,20},{20... | collective-permute-start | bytes 442376 | tf_op jit(solution)/shard_map/ppermute | solution.py:35
  68.9 3.9 %collective-permute-start.28 = (bf16[192,1152]{1,0:T(8,128)(2,1)S(1)}, bf16[192,1152]{1,0:T(8,128)(2,1)S(1)}, u32[]{:S(2)}, u32[]{:S(2)}) collective-permute-start(bf16[192,1152]{1,0:T(8,128)(2,1)S(1)} %select_convert_fusion), channel_id=1, source_target_pairs={{0,1},{1,0},{2,3},{3,2},{4,5},{5,4},{6,7},{7,6},{8,9},{9,8},{10,11... | collective-permute-start | bytes 1327112 | tf_op jit(solution)/shard_map/ppermute | solution.py:31
  (6 other events, 16.9 us)

commit v8 on v6

--- a/solution.py
+++ b/solution.py
@@ -392,7 +392,7 @@
         come = after(come, conv_total)
         columns = (keep + come.astype(jnp.float32)).astype(jnp.bfloat16)
         come_out = dp_swap(columns)
-        conv_total = add_conv(conv_total, micro - 1, columns)
+        conv_total = add_conv(conv_total, micro - 1, columns, comes_late[0])
     else:
         for m in range(micro):
             conv_total = add_conv(conv_total, m)

time: 74.3 us -> 74.3 us (level)
  no operation moved by 1% of the time
where the time goes in v8:
time: 74.3 us; the launch traced here: 74 us
  starting transfers between devices  31.6 us (43%)
  waiting for transfers between devices  16.8 us (23%)
  matrix products  13.4 us (18%)
  other arithmetic  6.48 us (9%)
  local copies, waits for them, and re-layouts  3.61 us (5%)
  between operations  1.86 us (3%)
    ppermute x16, starting transfers between devices, seq_swap(): return lax.ppermute(value, 'seq', [(i, i ^ bit) for i in range(count)])  18.4 us
    ppermute x16, waiting for transfers between devices, seq_swap(): return lax.ppermute(value, 'seq', [(i, i ^ bit) for i in range(count)])  8.99 us
    ppermute x9, starting transfers between devices, send_down(): lax.ppermute(value, 'section', [(sections - 1 - hop, sections - 2 - hop)])  8.08 us
    ppermute x9, waiting for transfers between devices, send_down(): lax.ppermute(value, 'section', [(sections - 1 - hop, sections - 2 - hop)])  6.36 us
    ppermute x5, starting transfers between devices, dp_swap(): return lax.ppermute(value, 'dp', [(0, 1), (1, 0)])  5.17 us
    dot_general x9, matrix products, tick(): grad_hidden = jnp.dot(back, back_kernel, preferred_element_type=jnp.float32)  4.09 us
    dot_general x9, matrix products, tick(): lax.dot_general(grad_top, out_w, (((1,), (1,)), ((), ())), preferred_elem...  2.85 us
    unnamed x21, local copies, waits for them, and re-layouts  2.27 us
  transfers between devices with their start and end apart: 30, of which 12 were waited for; matrix products, arithmetic and copies ran while one was open for 27% of the time, Pallas kernels for 0%

profile of v8, /device:TPU:0, one launch (start us, length us, event | category | flops | bytes accessed | tf_op | source)
XLA Modules:
  0.0 74.0 jit_solution(6791586167642919228)
XLA Ops:
  0.7 1.1 %copy-done.1 = bf16[1,3,1,128,768]{4,3,2,1,0:T(8,128)(2,1)S(1)} copy-done((bf16[1,3,1,128,768]{4,3,2,1,0:T(8,128)(2,1)S(1)}, bf16[1,3,1,128,768]{4,3,2,1,0:T(8,128)(2,1)}, u32[]{:S(2)}) %copy-start.1) | copy-done | bytes 589848
  1.8 1.1 %copy-done.2 = bf16[3,1,128,768]{3,2,1,0:T(8,128)(2,1)S(1)} copy-done((bf16[3,1,128,768]{3,2,1,0:T(8,128)(2,1)S(1)}, bf16[3,1,128,768]{3,2,1,0:T(8,128)(2,1)}, u32[]{:S(2)}) %copy-start.2) | copy-done | bytes 589848
  4.6 3.0 %collective-permute-start.2 = (bf16[2,2,32,768]{3,2,0,1:T(8,128)(2,1)S(1)}, bf16[2,2,32,768]{3,2,0,1:T(8,128)(2,1)S(1)}, u32[]{:S(2)}, u32[]{:S(2)}) collective-permute-start(bf16[2,2,32,768]{3,2,0,1:T(8,128)(2,1)S(1)} %pad_maximum_fusion.12), channel_id=1, source_target_pairs={{0,2},{1,3},{2,0},{3,1},{4,6},{5,7},{6,4},{7,5},{8,10},{9,11},{10,... | collective-permute-start | bytes 589832 | tf_op jit(solution)/shard_map/ppermute | solution.py:31
  9.3 1.2 %collective-permute-start.4 = (bf16[2,2,32,768]{3,2,0,1:T(8,128)(2,1)S(1)}, bf16[2,2,32,768]{3,2,0,1:T(8,128)(2,1)S(1)}, u32[]{:S(2)}, u32[]{:S(2)}) collective-permute-start(bf16[2,2,32,768]{3,2,0,1:T(8,128)(2,1)S(1)} %get-tuple-element.93), channel_id=1, source_target_pairs={{0,2},{1,3},{2,0},{3,1},{4,6},{5,7},{6,4},{7,5},{8,10},{9,11},{10,... | collective-permute-start | bytes 589832 | tf_op jit(solution)/shard_map/ppermute | solution.py:31
  10.7 2.6 %collective-permute-done.2 = bf16[2,2,32,768]{3,2,0,1:T(8,128)(2,1)S(1)} collective-permute-done((bf16[2,2,32,768]{3,2,0,1:T(8,128)(2,1)S(1)}, bf16[2,2,32,768]{3,2,0,1:T(8,128)(2,1)S(1)}, u32[]{:S(2)}, u32[]{:S(2)}) %collective-permute-start.2) | collective-permute-done | bytes 196640 | tf_op jit(solution)/shard_map/ppermute | solution.py:31
  15.9 2.1 %collective-permute-start.3 = (bf16[2,2,32,768]{3,2,0,1:T(8,128)(2,1)S(1)}, bf16[2,2,32,768]{3,2,0,1:T(8,128)(2,1)S(1)}, u32[]{:S(2)}, u32[]{:S(2)}) collective-permute-start(bf16[2,2,32,768]{3,2,0,1:T(8,128)(2,1)S(1)} %get-tuple-element.101), channel_id=1, source_target_pairs={{0,2},{1,3},{2,0},{3,1},{4,6},{5,7},{6,4},{7,5},{8,10},{9,11},{10,... | collective-permute-start | bytes 589832 | tf_op jit(solution)/shard_map/ppermute | solution.py:31
  20.8 1.2 %collective-permute-done.3 = bf16[2,2,32,768]{3,2,0,1:T(8,128)(2,1)S(1)} collective-permute-done((bf16[2,2,32,768]{3,2,0,1:T(8,128)(2,1)S(1)}, bf16[2,2,32,768]{3,2,0,1:T(8,128)(2,1)S(1)}, u32[]{:S(2)}, u32[]{:S(2)}) %collective-permute-start.3) | collective-permute-done | bytes 196640 | tf_op jit(solution)/shard_map/ppermute | solution.py:31
  25.5 1.8 %collective-permute-start.12 = (bf16[384,384]{1,0:T(8,128)(2,1)S(1)}, bf16[384,384]{1,0:T(8,128)(2,1)S(1)}, u32[]{:S(2)}, u32[]{:S(2)}) collective-permute-start(bf16[384,384]{1,0:T(8,128)(2,1)S(1)} %get-tuple-element.180), channel_id=1, source_target_pairs={{0,2},{1,3},{2,0},{3,1},{4,6},{5,7},{6,4},{7,5},{8,10},{9,11},{10,... | collective-permute-start | bytes 884744 | tf_op jit(solution)/shard_map/ppermute | solution.py:31
  29.9 1.3 %collective-permute-start.10 = (bf16[128,768]{1,0:T(8,128)(2,1)S(1)}, bf16[128,768]{1,0:T(8,128)(2,1)S(1)}, u32[]{:S(2)}, u32[]{:S(2)}) collective-permute-start(bf16[128,768]{1,0:T(8,128)(2,1)S(1)} %fusion.27), channel_id=1, source_target_pairs={{4,0},{5,1},{6,2},{7,3},{20,16},{21,17},{22,18},{23,19}} | collective-permute-start | bytes 589832 | tf_op jit(solution)/shard_map/ppermute | solution.py:166
  31.9 0.8 %collective-permute-done.12 = bf16[384,384]{1,0:T(8,128)(2,1)S(1)} collective-permute-done((bf16[384,384]{1,0:T(8,128)(2,1)S(1)}, bf16[384,384]{1,0:T(8,128)(2,1)S(1)}, u32[]{:S(2)}, u32[]{:S(2)}) %collective-permute-start.12) | collective-permute-done | bytes 294944 | tf_op jit(solution)/shard_map/ppermute | solution.py:31
  32.7 1.4 %collective-permute-start.17 = (bf16[3,256,384]{2,1,0:T(8,128)(2,1)S(1)}, bf16[3,256,384]{2,1,0:T(8,128)(2,1)S(1)}, u32[]{:S(2)}, u32[]{:S(2)}) collective-permute-start(bf16[3,256,384]{2,1,0:T(8,128)(2,1)S(1)} %pad_maximum_fusion.1), channel_id=1, source_target_pairs={{0,16},{16,0},{1,17},{17,1},{2,18},{18,2},{3,19},{19,3},{4,20},{20... | collective-permute-start | bytes 1769480 | tf_op jit(solution)/shard_map/ppermute | solution.py:35
  35.1 1.3 %collective-permute-start.13 = (bf16[128,768]{1,0:T(8,128)(2,1)S(1)}, bf16[128,768]{1,0:T(8,128)(2,1)S(1)}, u32[]{:S(2)}, u32[]{:S(2)}) collective-permute-start(bf16[128,768]{1,0:T(8,128)(2,1)S(1)} %add_convert_fusion.2), channel_id=1, source_target_pairs={{4,0},{5,1},{6,2},{7,3},{20,16},{21,17},{22,18},{23,19}} | collective-permute-start | bytes 589832 | tf_op jit(solution)/shard_map/ppermute | solution.py:166
  36.4 5.2 %collective-permute-done.10 = bf16[128,768]{1,0:T(8,128)(2,1)S(1)} collective-permute-done((bf16[128,768]{1,0:T(8,128)(2,1)S(1)}, bf16[128,768]{1,0:T(8,128)(2,1)S(1)}, u32[]{:S(2)}, u32[]{:S(2)}) %collective-permute-start.10) | collective-permute-done | bytes 196640 | tf_op jit(solution)/shard_map/ppermute | solution.py:166
  42.5 2.6 %collective-permute-start.18 = (bf16[128,384]{1,0:T(8,128)(2,1)S(1)}, bf16[128,384]{1,0:T(8,128)(2,1)S(1)}, u32[]{:S(2)}, u32[]{:S(2)}) collective-permute-start(bf16[128,384]{1,0:T(8,128)(2,1)S(1)} %select_select_fusion.4), channel_id=1, source_target_pairs={{0,2},{1,3},{2,0},{3,1},{4,6},{5,7},{6,4},{7,5},{8,10},{9,11},{10,... | collective-permute-start | bytes 294920 | tf_op jit(solution)/shard_map/ppermute | solution.py:31
  45.1 1.5 %collective-permute-start.16 = (bf16[128,768]{1,0:T(8,128)(2,1)S(1)}, bf16[128,768]{1,0:T(8,128)(2,1)S(1)}, u32[]{:S(2)}, u32[]{:S(2)}) collective-permute-start(bf16[128,768]{1,0:T(8,128)(2,1)S(1)} %fusion.26), channel_id=1, source_target_pairs={{4,0},{5,1},{6,2},{7,3},{20,16},{21,17},{22,18},{23,19}} | collective-permute-start | bytes 589832 | tf_op jit(solution)/shard_map/ppermute | solution.py:166
  47.0 1.2 %collective-permute-done.13 = bf16[128,768]{1,0:T(8,128)(2,1)S(1)} collective-permute-done((bf16[128,768]{1,0:T(8,128)(2,1)S(1)}, bf16[128,768]{1,0:T(8,128)(2,1)S(1)}, u32[]{:S(2)}, u32[]{:S(2)}) %collective-permute-start.13) | collective-permute-done | bytes 196640 | tf_op jit(solution)/shard_map/ppermute | solution.py:166
  49.1 1.2 %collective-permute-start.19 = (bf16[128,384]{1,0:T(8,128)(2,1)S(1)}, bf16[128,384]{1,0:T(8,128)(2,1)S(1)}, u32[]{:S(2)}, u32[]{:S(2)}) collective-permute-start(bf16[128,384]{1,0:T(8,128)(2,1)S(1)} %select_select_fusion.3), channel_id=1, source_target_pairs={{0,2},{1,3},{2,0},{3,1},{4,6},{5,7},{6,4},{7,5},{8,10},{9,11},{10,... | collective-permute-start | bytes 294920 | tf_op jit(solution)/shard_map/ppermute | solution.py:31
  52.0 1.5 %collective-permute-start.15 = (bf16[2,2,4,1,8,768]{5,4,1,2,0,3:T(8,128)(2,1)S(1)}, bf16[2,2,4,1,8,768]{5,4,1,2,0,3:T(8,128)(2,1)S(1)}, u32[]{:S(2)}, u32[]{:S(2)}) collective-permute-start(bf16[2,2,4,1,8,768]{5,4,1,2,0,3:T(8,128)(2,1)S(1)} %bitcast.347), channel_id=1, source_target_pairs={{0,2},{1,3},{2,0},{3,1},{4,6},{5,7},{6,4},{7,5},{8,10},{9,11},{10,... | collective-permute-start | bytes 589832 | tf_op jit(solution)/shard_map/ppermute | solution.py:31
  55.1 1.0 %collective-permute-start.24 = (bf16[256,384]{1,0:T(8,128)(2,1)S(1)}, bf16[256,384]{1,0:T(8,128)(2,1)S(1)}, u32[]{:S(2)}, u32[]{:S(2)}) collective-permute-start(bf16[256,384]{1,0:T(8,128)(2,1)S(1)} %constant_dynamic-update-slice_fusion.5), channel_id=1, source_target_pairs={{0,16},{16,0},{1,17},{17,1},{2,18},{18,2},{3,19},{19,3},{4,20},{20... | collective-permute-start | bytes 589832 | tf_op jit(solution)/shard_map/ppermute | solution.py:35
  56.1 0.8 %collective-permute-start.25 = (bf16[128,384]{1,0:T(8,128)(2,1)S(1)}, bf16[128,384]{1,0:T(8,128)(2,1)S(1)}, u32[]{:S(2)}, u32[]{:S(2)}) collective-permute-start(bf16[128,384]{1,0:T(8,128)(2,1)S(1)} %select_select_fusion.2), channel_id=1, source_target_pairs={{0,2},{1,3},{2,0},{3,1},{4,6},{5,7},{6,4},{7,5},{8,10},{9,11},{10,... | collective-permute-start | bytes 294920 | tf_op jit(solution)/shard_map/ppermute | solution.py:31
  57.1 1.9 %collective-permute-done.15 = bf16[2,2,4,1,8,768]{5,4,1,2,0,3:T(8,128)(2,1)S(1)} collective-permute-done((bf16[2,2,4,1,8,768]{5,4,1,2,0,3:T(8,128)(2,1)S(1)}, bf16[2,2,4,1,8,768]{5,4,1,2,0,3:T(8,128)(2,1)S(1)}, u32[]{:S(2)}, u32[]{:S(2)}) %collective-permute-start.15) | collective-permute-done | bytes 196640 | tf_op jit(solution)/shard_map/ppermute | solution.py:31
  59.2 2.1 %collective-permute-start.27 = (bf16[192,384]{1,0:T(8,128)(2,1)S(1)}, bf16[192,384]{1,0:T(8,128)(2,1)S(1)}, u32[]{:S(2)}, u32[]{:S(2)}) collective-permute-start(bf16[192,384]{1,0:T(8,128)(2,1)S(1)} %fusion.230), channel_id=1, source_target_pairs={{0,2},{1,3},{2,0},{3,1},{4,6},{5,7},{6,4},{7,5},{8,10},{9,11},{10,... | collective-permute-start | bytes 442376 | tf_op jit(solution)/shard_map/ppermute | solution.py:31
  61.4 1.1 %collective-permute-start.26 = (bf16[256,384]{1,0:T(8,128)(2,1)S(1)}, bf16[256,384]{1,0:T(8,128)(2,1)S(1)}, u32[]{:S(2)}, u32[]{:S(2)}) collective-permute-start(bf16[256,384]{1,0:T(8,128)(2,1)S(1)} %constant_dynamic-update-slice_fusion.7), channel_id=1, source_target_pairs={{0,16},{16,0},{1,17},{17,1},{2,18},{18,2},{3,19},{19,3},{4,20},{20... | collective-permute-start | bytes 589832 | tf_op jit(solution)/shard_map/ppermute | solution.py:35
  63.8 0.7 convolution_add_fusion.1
  65.2 1.2 %collective-permute-start.22 = (bf16[1,2,4,1,8,768]{5,4,1,2,3,0:T(8,128)(2,1)S(1)}, bf16[1,2,4,1,8,768]{5,4,1,2,3,0:T(8,128)(2,1)S(1)}, u32[]{:S(2)}, u32[]{:S(2)}) collective-permute-start(bf16[1,2,4,1,8,768]{5,4,1,2,3,0:T(8,128)(2,1)S(1)} %bitcast.348), channel_id=1, source_target_pairs={{0,2},{1,3},{2,0},{3,1},{4,6},{5,7},{6,4},{7,5},{8,10},{9,11},{10,... | collective-permute-start | bytes 294920 | tf_op jit(solution)/shard_map/ppermute | solution.py:31
  66.4 1.2 %collective-permute-start.29 = (bf16[192,384]{1,0:T(8,128)(2,1)S(1)}, bf16[192,384]{1,0:T(8,128)(2,1)S(1)}, u32[]{:S(2)}, u32[]{:S(2)}) collective-permute-start(bf16[192,384]{1,0:T(8,128)(2,1)S(1)} %fusion.190), channel_id=1, source_target_pairs={{0,16},{16,0},{1,17},{17,1},{2,18},{18,2},{3,19},{19,3},{4,20},{20... | collective-permute-start | bytes 442376 | tf_op jit(solution)/shard_map/ppermute | solution.py:35
  68.2 0.7 convolution_add_fusion
  69.1 1.0 %collective-permute-done.22 = bf16[1,2,4,1,8,768]{5,4,1,2,3,0:T(8,128)(2,1)S(1)} collective-permute-done((bf16[1,2,4,1,8,768]{5,4,1,2,3,0:T(8,128)(2,1)S(1)}, bf16[1,2,4,1,8,768]{5,4,1,2,3,0:T(8,128)(2,1)S(1)}, u32[]{:S(2)}, u32[]{:S(2)}) %collective-permute-start.22) | collective-permute-done | bytes 98336 | tf_op jit(solution)/shard_map/ppermute | solution.py:31
  70.1 0.9 %maximum_bitcast_fusion = bf16[1,3,1,128,768]{4,3,2,1,0:T(8,128)(2,1)} fusion(bf16[1,128,768]{2,1,0:T(8,128)(2,1)S(1)} %bitcast.335, bf16[2,128,768]{2,1,0:T(8,128)(2,1)S(1)} %bitcast.329), kind=kLoop, calls=%fused_computation.98 | loop fusion | flops 294912 | bytes 1179648 | tf_op jit(solution)/shard_map/reshape | solution.py:423
  71.0 1.1 %collective-permute-done.29 = bf16[192,384]{1,0:T(8,128)(2,1)S(1)} collective-permute-done((bf16[192,384]{1,0:T(8,128)(2,1)S(1)}, bf16[192,384]{1,0:T(8,128)(2,1)S(1)}, u32[]{:S(2)}, u32[]{:S(2)}) %collective-permute-start.29) | collective-permute-done | bytes 147488 | tf_op jit(solution)/shard_map/ppermute | solution.py:35
  72.1 0.8 %multiply_bitcast_fusion = f32[1,384,192]{1,2,0:T(8,128)} fusion(bf16[192,384]{1,0:T(8,128)(2,1)S(1)} %collective-permute-done.29, bf16[192,384]{1,0:T(8,128)(2,1)S(1)} %fusion.190), kind=kLoop, calls=%fused_computation.265 | loop fusion | flops 294912 | bytes 589824 | tf_op jit(solution)/shard_map/broadcast_in_dim | solution.py:425
  73.1 1.0 %maximum_multiply_fusion = f32[1,3,192,384]{3,2,1,0:T(8,128)} fusion(f32[1,1,192,384]{3,2,1,0:T(8,128)S(1)} %get-tuple-element.176, f32[1,1,192,384]{3,2,1,0:T(8,128)S(1)} %get-tuple-element.177, f32[1,1,192,384]{3,2,1,0:T(8,128)S(1)} %get-tuple-element.175), kind=kLoop, calls=%fused_computation.71 | loop fusion | flops 663552 | bytes 1769472 | tf_op jit(solution)/shard_map/mul | solution.py:408
  (175 shorter events, 24.8 us)
Async XLA Ops:
  0.6 13.7 %copy-start = (bf16[1,384,768]{2,1,0:T(8,128)(2,1)S(1)}, bf16[1,384,768]{2,1,0:T(8,128)(2,1)}, u32[]{:S(2)}) copy-start(bf16[1,384,768]{2,1,0:T(8,128)(2,1)} %param.11) | copy-start | bytes 1769476
  3.0 1.6 %collective-permute-start = (bf16[2,2,32,768]{3,2,0,1:T(8,128)(2,1)S(1)}, bf16[2,2,32,768]{3,2,0,1:T(8,128)(2,1)S(1)}, u32[]{:S(2)}, u32[]{:S(2)}) collective-permute-start(bf16[2,2,32,768]{3,2,0,1:T(8,128)(2,1)S(1)} %copy.12), channel_id=1, source_target_pairs={{0,1},{1,0},{2,3},{3,2},{4,5},{5,4},{6,7},{7,6},{8,9},{9,8},{10,11... | collective-permute-start | bytes 589832 | tf_op jit(solution)/shard_map/ppermute | solution.py:31
  3.7 3.9 %collective-permute-start.1 = (bf16[4,2,32,768]{3,2,0,1:T(8,128)(2,1)S(1)}, bf16[4,2,32,768]{3,2,0,1:T(8,128)(2,1)S(1)}, u32[]{:S(2)}, u32[]{:S(2)}) collective-permute-start(bf16[4,2,32,768]{3,2,0,1:T(8,128)(2,1)S(1)} %copy.14), channel_id=1, source_target_pairs={{0,1},{1,0},{2,3},{3,2},{4,5},{5,4},{6,7},{7,6},{8,9},{9,8},{10,11... | collective-permute-start | bytes 1179656 | tf_op jit(solution)/shard_map/ppermute | solution.py:31
  4.6 3.2 %copy-start.3 = (bf16[1,3,768,384]{3,2,1,0:T(8,128)(2,1)S(1)}, bf16[1,3,768,384]{3,2,1,0:T(8,128)(2,1)}, u32[]{:S(2)}) copy-start(bf16[1,3,768,384]{3,2,1,0:T(8,128)(2,1)} %param.10) | copy-start | bytes 5308420
  4.6 8.6 %collective-permute-start.2 = (bf16[2,2,32,768]{3,2,0,1:T(8,128)(2,1)S(1)}, bf16[2,2,32,768]{3,2,0,1:T(8,128)(2,1)S(1)}, u32[]{:S(2)}, u32[]{:S(2)}) collective-permute-start(bf16[2,2,32,768]{3,2,0,1:T(8,128)(2,1)S(1)} %pad_maximum_fusion.12), channel_id=1, source_target_pairs={{0,2},{1,3},{2,0},{3,1},{4,6},{5,7},{6,4},{7,5},{8,10},{9,11},{10,... | collective-permute-start | bytes 589832 | tf_op jit(solution)/shard_map/ppermute | solution.py:31
  9.3 8.8 %collective-permute-start.4 = (bf16[2,2,32,768]{3,2,0,1:T(8,128)(2,1)S(1)}, bf16[2,2,32,768]{3,2,0,1:T(8,128)(2,1)S(1)}, u32[]{:S(2)}, u32[]{:S(2)}) collective-permute-start(bf16[2,2,32,768]{3,2,0,1:T(8,128)(2,1)S(1)} %get-tuple-element.93), channel_id=1, source_target_pairs={{0,2},{1,3},{2,0},{3,1},{4,6},{5,7},{6,4},{7,5},{8,10},{9,11},{10,... | collective-permute-start | bytes 589832 | tf_op jit(solution)/shard_map/ppermute | solution.py:31
  15.2 7.8 %collective-permute-start.5 = (bf16[128,768]{1,0:T(8,128)(2,1)S(1)}, bf16[128,768]{1,0:T(8,128)(2,1)S(1)}, u32[]{:S(2)}, u32[]{:S(2)}) collective-permute-start(bf16[128,768]{1,0:T(8,128)(2,1)S(1)} %fusion.29), channel_id=1, source_target_pairs={{12,8},{13,9},{14,10},{15,11},{28,24},{29,25},{30,26},{31,27}} | collective-permute-start | bytes 589832 | tf_op jit(solution)/shard_map/ppermute | solution.py:166
  15.9 6.0 %collective-permute-start.3 = (bf16[2,2,32,768]{3,2,0,1:T(8,128)(2,1)S(1)}, bf16[2,2,32,768]{3,2,0,1:T(8,128)(2,1)S(1)}, u32[]{:S(2)}, u32[]{:S(2)}) collective-permute-start(bf16[2,2,32,768]{3,2,0,1:T(8,128)(2,1)S(1)} %get-tuple-element.101), channel_id=1, source_target_pairs={{0,2},{1,3},{2,0},{3,1},{4,6},{5,7},{6,4},{7,5},{8,10},{9,11},{10,... | collective-permute-start | bytes 589832 | tf_op jit(solution)/shard_map/ppermute | solution.py:31
  20.1 7.2 %collective-permute-start.8 = (bf16[128,768]{1,0:T(8,128)(2,1)S(1)}, bf16[128,768]{1,0:T(8,128)(2,1)S(1)}, u32[]{:S(2)}, u32[]{:S(2)}) collective-permute-start(bf16[128,768]{1,0:T(8,128)(2,1)S(1)} %fusion.28), channel_id=1, source_target_pairs={{12,8},{13,9},{14,10},{15,11},{28,24},{29,25},{30,26},{31,27}} | collective-permute-start | bytes 589832 | tf_op jit(solution)/shard_map/ppermute | solution.py:166
  24.0 5.0 %collective-permute-start.7 = (bf16[128,768]{1,0:T(8,128)(2,1)S(1)}, bf16[128,768]{1,0:T(8,128)(2,1)S(1)}, u32[]{:S(2)}, u32[]{:S(2)}) collective-permute-start(bf16[128,768]{1,0:T(8,128)(2,1)S(1)} %add_convert_fusion.4), channel_id=1, source_target_pairs={{8,4},{9,5},{10,6},{11,7},{24,20},{25,21},{26,22},{27,23}} | collective-permute-start | bytes 589832 | tf_op jit(solution)/shard_map/ppermute | solution.py:166
  24.6 4.3 %collective-permute-start.6 = (bf16[128,768]{1,0:T(8,128)(2,1)S(1)}, bf16[128,768]{1,0:T(8,128)(2,1)S(1)}, u32[]{:S(2)}, u32[]{:S(2)}) collective-permute-start(bf16[128,768]{1,0:T(8,128)(2,1)S(1)} %add_convert_fusion.4), channel_id=1, source_target_pairs={{12,8},{13,9},{14,10},{15,11},{28,24},{29,25},{30,26},{31,27}} | collective-permute-start | bytes 589832 | tf_op jit(solution)/shard_map/ppermute | solution.py:166
  25.5 7.2 %collective-permute-start.12 = (bf16[384,384]{1,0:T(8,128)(2,1)S(1)}, bf16[384,384]{1,0:T(8,128)(2,1)S(1)}, u32[]{:S(2)}, u32[]{:S(2)}) collective-permute-start(bf16[384,384]{1,0:T(8,128)(2,1)S(1)} %get-tuple-element.180), channel_id=1, source_target_pairs={{0,2},{1,3},{2,0},{3,1},{4,6},{5,7},{6,4},{7,5},{8,10},{9,11},{10,... | collective-permute-start | bytes 884744 | tf_op jit(solution)/shard_map/ppermute | solution.py:31
  28.2 5.9 %collective-permute-start.11 = (bf16[128,768]{1,0:T(8,128)(2,1)S(1)}, bf16[128,768]{1,0:T(8,128)(2,1)S(1)}, u32[]{:S(2)}, u32[]{:S(2)}) collective-permute-start(bf16[128,768]{1,0:T(8,128)(2,1)S(1)} %add_convert_fusion.3), channel_id=1, source_target_pairs={{8,4},{9,5},{10,6},{11,7},{24,20},{25,21},{26,22},{27,23}} | collective-permute-start | bytes 589832 | tf_op jit(solution)/shard_map/ppermute | solution.py:166
  29.9 11.7 %collective-permute-start.10 = (bf16[128,768]{1,0:T(8,128)(2,1)S(1)}, bf16[128,768]{1,0:T(8,128)(2,1)S(1)}, u32[]{:S(2)}, u32[]{:S(2)}) collective-permute-start(bf16[128,768]{1,0:T(8,128)(2,1)S(1)} %fusion.27), channel_id=1, source_target_pairs={{4,0},{5,1},{6,2},{7,3},{20,16},{21,17},{22,18},{23,19}} | collective-permute-start | bytes 589832 | tf_op jit(solution)/shard_map/ppermute | solution.py:166
  31.2 10.4 %collective-permute-start.9 = (bf16[128,768]{1,0:T(8,128)(2,1)S(1)}, bf16[128,768]{1,0:T(8,128)(2,1)S(1)}, u32[]{:S(2)}, u32[]{:S(2)}) collective-permute-start(bf16[128,768]{1,0:T(8,128)(2,1)S(1)} %fusion.27), channel_id=1, source_target_pairs={{8,4},{9,5},{10,6},{11,7},{24,20},{25,21},{26,22},{27,23}} | collective-permute-start | bytes 589832 | tf_op jit(solution)/shard_map/ppermute | solution.py:166
  32.7 20.9 %collective-permute-start.17 = (bf16[3,256,384]{2,1,0:T(8,128)(2,1)S(1)}, bf16[3,256,384]{2,1,0:T(8,128)(2,1)S(1)}, u32[]{:S(2)}, u32[]{:S(2)}) collective-permute-start(bf16[3,256,384]{2,1,0:T(8,128)(2,1)S(1)} %pad_maximum_fusion.1), channel_id=1, source_target_pairs={{0,16},{16,0},{1,17},{17,1},{2,18},{18,2},{3,19},{19,3},{4,20},{20... | collective-permute-start | bytes 1769480 | tf_op jit(solution)/shard_map/ppermute | solution.py:35
  35.1 13.1 %collective-permute-start.13 = (bf16[128,768]{1,0:T(8,128)(2,1)S(1)}, bf16[128,768]{1,0:T(8,128)(2,1)S(1)}, u32[]{:S(2)}, u32[]{:S(2)}) collective-permute-start(bf16[128,768]{1,0:T(8,128)(2,1)S(1)} %add_convert_fusion.2), channel_id=1, source_target_pairs={{4,0},{5,1},{6,2},{7,3},{20,16},{21,17},{22,18},{23,19}} | collective-permute-start | bytes 589832 | tf_op jit(solution)/shard_map/ppermute | solution.py:166
  42.5 8.0 %collective-permute-start.18 = (bf16[128,384]{1,0:T(8,128)(2,1)S(1)}, bf16[128,384]{1,0:T(8,128)(2,1)S(1)}, u32[]{:S(2)}, u32[]{:S(2)}) collective-permute-start(bf16[128,384]{1,0:T(8,128)(2,1)S(1)} %select_select_fusion.4), channel_id=1, source_target_pairs={{0,2},{1,3},{2,0},{3,1},{4,6},{5,7},{6,4},{7,5},{8,10},{9,11},{10,... | collective-permute-start | bytes 294920 | tf_op jit(solution)/shard_map/ppermute | solution.py:31
  45.1 8.4 %collective-permute-start.16 = (bf16[128,768]{1,0:T(8,128)(2,1)S(1)}, bf16[128,768]{1,0:T(8,128)(2,1)S(1)}, u32[]{:S(2)}, u32[]{:S(2)}) collective-permute-start(bf16[128,768]{1,0:T(8,128)(2,1)S(1)} %fusion.26), channel_id=1, source_target_pairs={{4,0},{5,1},{6,2},{7,3},{20,16},{21,17},{22,18},{23,19}} | collective-permute-start | bytes 589832 | tf_op jit(solution)/shard_map/ppermute | solution.py:166
  49.1 5.4 %collective-permute-start.19 = (bf16[128,384]{1,0:T(8,128)(2,1)S(1)}, bf16[128,384]{1,0:T(8,128)(2,1)S(1)}, u32[]{:S(2)}, u32[]{:S(2)}) collective-permute-start(bf16[128,384]{1,0:T(8,128)(2,1)S(1)} %select_select_fusion.3), channel_id=1, source_target_pairs={{0,2},{1,3},{2,0},{3,1},{4,6},{5,7},{6,4},{7,5},{8,10},{9,11},{10,... | collective-permute-start | bytes 294920 | tf_op jit(solution)/shard_map/ppermute | solution.py:31
  50.4 1.5 %collective-permute-start.14 = (bf16[2,1,4,2,8,768]{5,4,2,3,0,1:T(8,128)(2,1)S(1)}, bf16[2,1,4,2,8,768]{5,4,2,3,0,1:T(8,128)(2,1)S(1)}, u32[]{:S(2)}, u32[]{:S(2)}) collective-permute-start(bf16[2,1,4,2,8,768]{5,4,2,3,0,1:T(8,128)(2,1)S(1)} %dynamic-slice_bitcast_fusion), channel_id=1, source_target_pairs={{0,1},{1,0},{2,3},{3,2},{4,5},{5,4},{6,7},{7,6},{8,9},{9,8},{10,11... | collective-permute-start | bytes 589832 | tf_op jit(solution)/shard_map/ppermute | solution.py:31
  50.5 10.8 %collective-permute-start.23 = (bf16[256,384]{1,0:T(8,128)(2,1)S(1)}, bf16[256,384]{1,0:T(8,128)(2,1)S(1)}, u32[]{:S(2)}, u32[]{:S(2)}) collective-permute-start(bf16[256,384]{1,0:T(8,128)(2,1)S(1)} %constant_dynamic-update-slice_fusion.3), channel_id=1, source_target_pairs={{0,16},{16,0},{1,17},{17,1},{2,18},{18,2},{3,19},{19,3},{4,20},{20... | collective-permute-start | bytes 589832 | tf_op jit(solution)/shard_map/ppermute | solution.py:35
  52.0 7.0 %collective-permute-start.15 = (bf16[2,2,4,1,8,768]{5,4,1,2,0,3:T(8,128)(2,1)S(1)}, bf16[2,2,4,1,8,768]{5,4,1,2,0,3:T(8,128)(2,1)S(1)}, u32[]{:S(2)}, u32[]{:S(2)}) collective-permute-start(bf16[2,2,4,1,8,768]{5,4,1,2,0,3:T(8,128)(2,1)S(1)} %bitcast.347), channel_id=1, source_target_pairs={{0,2},{1,3},{2,0},{3,1},{4,6},{5,7},{6,4},{7,5},{8,10},{9,11},{10,... | collective-permute-start | bytes 589832 | tf_op jit(solution)/shard_map/ppermute | solution.py:31
  55.1 7.5 %collective-permute-start.24 = (bf16[256,384]{1,0:T(8,128)(2,1)S(1)}, bf16[256,384]{1,0:T(8,128)(2,1)S(1)}, u32[]{:S(2)}, u32[]{:S(2)}) collective-permute-start(bf16[256,384]{1,0:T(8,128)(2,1)S(1)} %constant_dynamic-update-slice_fusion.5), channel_id=1, source_target_pairs={{0,16},{16,0},{1,17},{17,1},{2,18},{18,2},{3,19},{19,3},{4,20},{20... | collective-permute-start | bytes 589832 | tf_op jit(solution)/shard_map/ppermute | solution.py:35
  56.1 3.0 %collective-permute-start.20 = (bf16[2,192,384]{2,1,0:T(8,128)(2,1)S(1)}, bf16[2,192,384]{2,1,0:T(8,128)(2,1)S(1)}, u32[]{:S(2)}, u32[]{:S(2)}) collective-permute-start(bf16[2,192,384]{2,1,0:T(8,128)(2,1)S(1)} %fusion.134), channel_id=1, source_target_pairs={{0,1},{1,0},{2,3},{3,2},{4,5},{5,4},{6,7},{7,6},{8,9},{9,8},{10,11... | collective-permute-start | bytes 884744 | tf_op jit(solution)/shard_map/ppermute | solution.py:31
  56.1 5.3 %collective-permute-start.25 = (bf16[128,384]{1,0:T(8,128)(2,1)S(1)}, bf16[128,384]{1,0:T(8,128)(2,1)S(1)}, u32[]{:S(2)}, u32[]{:S(2)}) collective-permute-start(bf16[128,384]{1,0:T(8,128)(2,1)S(1)} %select_select_fusion.2), channel_id=1, source_target_pairs={{0,2},{1,3},{2,0},{3,1},{4,6},{5,7},{6,4},{7,5},{8,10},{9,11},{10,... | collective-permute-start | bytes 294920 | tf_op jit(solution)/shard_map/ppermute | solution.py:31
  59.2 7.1 %collective-permute-start.27 = (bf16[192,384]{1,0:T(8,128)(2,1)S(1)}, bf16[192,384]{1,0:T(8,128)(2,1)S(1)}, u32[]{:S(2)}, u32[]{:S(2)}) collective-permute-start(bf16[192,384]{1,0:T(8,128)(2,1)S(1)} %fusion.230), channel_id=1, source_target_pairs={{0,2},{1,3},{2,0},{3,1},{4,6},{5,7},{6,4},{7,5},{8,10},{9,11},{10,... | collective-permute-start | bytes 442376 | tf_op jit(solution)/shard_map/ppermute | solution.py:31
  61.4 6.5 %collective-permute-start.26 = (bf16[256,384]{1,0:T(8,128)(2,1)S(1)}, bf16[256,384]{1,0:T(8,128)(2,1)S(1)}, u32[]{:S(2)}, u32[]{:S(2)}) collective-permute-start(bf16[256,384]{1,0:T(8,128)(2,1)S(1)} %constant_dynamic-update-slice_fusion.7), channel_id=1, source_target_pairs={{0,16},{16,0},{1,17},{17,1},{2,18},{18,2},{3,19},{19,3},{4,20},{20... | collective-permute-start | bytes 589832 | tf_op jit(solution)/shard_map/ppermute | solution.py:35
  63.7 1.4 %collective-permute-start.21 = (bf16[1,1,4,2,8,768]{5,4,2,3,1,0:T(8,128)(2,1)S(1)}, bf16[1,1,4,2,8,768]{5,4,2,3,1,0:T(8,128)(2,1)S(1)}, u32[]{:S(2)}, u32[]{:S(2)}) collective-permute-start(bf16[1,1,4,2,8,768]{5,4,2,3,1,0:T(8,128)(2,1)S(1)} %dynamic-slice_bitcast_fusion.2), channel_id=1, source_target_pairs={{0,1},{1,0},{2,3},{3,2},{4,5},{5,4},{6,7},{7,6},{8,9},{9,8},{10,11... | collective-permute-start | bytes 294920 | tf_op jit(solution)/shard_map/ppermute | solution.py:31
  65.2 4.9 %collective-permute-start.22 = (bf16[1,2,4,1,8,768]{5,4,1,2,3,0:T(8,128)(2,1)S(1)}, bf16[1,2,4,1,8,768]{5,4,1,2,3,0:T(8,128)(2,1)S(1)}, u32[]{:S(2)}, u32[]{:S(2)}) collective-permute-start(bf16[1,2,4,1,8,768]{5,4,1,2,3,0:T(8,128)(2,1)S(1)} %bitcast.348), channel_id=1, source_target_pairs={{0,2},{1,3},{2,0},{3,1},{4,6},{5,7},{6,4},{7,5},{8,10},{9,11},{10,... | collective-permute-start | bytes 294920 | tf_op jit(solution)/shard_map/ppermute | solution.py:31
  66.4 5.7 %collective-permute-start.29 = (bf16[192,384]{1,0:T(8,128)(2,1)S(1)}, bf16[192,384]{1,0:T(8,128)(2,1)S(1)}, u32[]{:S(2)}, u32[]{:S(2)}) collective-permute-start(bf16[192,384]{1,0:T(8,128)(2,1)S(1)} %fusion.190), channel_id=1, source_target_pairs={{0,16},{16,0},{1,17},{17,1},{2,18},{18,2},{3,19},{19,3},{4,20},{20... | collective-permute-start | bytes 442376 | tf_op jit(solution)/shard_map/ppermute | solution.py:35
  69.0 3.9 %collective-permute-start.28 = (bf16[192,1152]{1,0:T(8,128)(2,1)S(1)}, bf16[192,1152]{1,0:T(8,128)(2,1)S(1)}, u32[]{:S(2)}, u32[]{:S(2)}) collective-permute-start(bf16[192,1152]{1,0:T(8,128)(2,1)S(1)} %select_convert_fusion), channel_id=1, source_target_pairs={{0,1},{1,0},{2,3},{3,2},{4,5},{5,4},{6,7},{7,6},{8,9},{9,8},{10,11... | collective-permute-start | bytes 1327112 | tf_op jit(solution)/shard_map/ppermute | solution.py:31
  (6 other events, 6.6 us)
